TPU v7x, 32 devices: a whole 2x2x4 slice. The times are simulated.
32 devices in a mesh: section: 2 (over x), row: 4 (over z), col: 4 (over y, core).
Axes of the slice: x: 2, y: 2, z: 4, core: 2. Of those that a mesh axis runs over, the one named last changes fastest.
Arguments:
- boundary: bfloat16 [2, 4, 512, 2048], P('section', None, 'row', 'col'), may hold values from -6 to 6
- segment_ids: int32 [4, 512], replicated, may hold values from -1 to 1, as said below
- w_query: bfloat16 [2, 2048, 2048], P('section', 'row', 'col'), may hold values from -0.125 to 0.125
- key_projection: bfloat16 [2, 2048, 1024], P('section', 'row', 'col'), may hold values from -0.125 to 0.125
- value_projection: bfloat16 [2, 2048, 1024], P('section', 'row', 'col'), may hold values from -0.125 to 0.125
- w_out: bfloat16 [2, 2048, 2048], P('section', 'col', 'row'), may hold values from -0.375 to 0.375
- w_gate: bfloat16 [2, 2048, 6144], P('section', 'row', 'col'), may hold values from -0.125 to 0.125
- w_up: bfloat16 [2, 2048, 6144], P('section', 'row', 'col'), may hold values from -0.125 to 0.125
- w_down: bfloat16 [2, 6144, 2048], P('section', 'col', 'row'), may hold values from -0.078125 to 0.078125
- attn_gain: bfloat16 [2, 2048], P('section', 'col'), may hold values from 0.5 to 1.5
- mlp_gain: bfloat16 [2, 2048], P('section', 'col'), may hold values from 0.5 to 1.5
- query_gain: bfloat16 [2, 128], P('section'), may hold values from 0.5 to 1.5
- key_norm_gain: bfloat16 [2, 128], P('section'), may hold values from 0.5 to 1.5
Outputs:
- section_out: float32 [2, 4, 512, 2048], P('section', None, 'row', 'col')
- grad_query: float32 [2, 2048, 2048], P('section', 'row', 'col')
- grad_key: float32 [2, 2048, 1024], P('section', 'row', 'col')
- grad_value: float32 [2, 2048, 1024], P('section', 'row', 'col')
- grad_out: float32 [2, 2048, 2048], P('section', 'col', 'row')
- grad_gate: float32 [2, 2048, 6144], P('section', 'row', 'col')
- grad_up: float32 [2, 2048, 6144], P('section', 'row', 'col')
- grad_down: float32 [2, 6144, 2048], P('section', 'col', 'row')
- grad_attn_gain: float32 [2, 2048], P('section')
- grad_mlp_gain: float32 [2, 2048], P('section')
- grad_query_gain: float32 [2, 128], P('section')
- grad_key_gain: float32 [2, 128], P('section')
Inputs may be any that keep to these rules, and one draw needn't show every extreme that they name: `segment_ids`: in each micro-batch the ids are 0 on a first run of slots, then possibly 1 on a second run, then -1 on an empty tail; at least 256 slots of each micro-batch hold tokens, and in at least one micro-batch a single sequence fills all 512 slots.
All inputs are finite; a program needn't handle non-finite values.
Results may differ from a plain program's by a relative error of at most 0.025.
Values may be sent and summed in bfloat16 or wider, within the bound.
No kernel may reach another device: no remote copies, remote signals or barrier semaphores. Data moves between devices by JAX's collectives and lax.ppermute only.
A program may use at most 192 MiB of HBM per device.

v0:
```python
import jax
import jax.numpy as jnp
from jax import lax
from jax.sharding import PartitionSpec as P

EPS = 1e-06
THETA = 1000000.0


def passed_along(value, axis, steps):
    count = lax.axis_size(axis)
    initial, last = (max(0, -steps), min(count, count - steps))
    return lax.ppermute(value, axis, [(source, source + steps) for source in range(initial, last)])


def positions(segments):
    places = jnp.arange(segments.shape[0], dtype=jnp.int32)
    changed = jnp.concatenate([jnp.ones((1,), bool), segments[1:] != segments[:-1]])
    starts = lax.cummax(jnp.where(changed, places, jnp.zeros_like(places)), axis=0)
    return places - starts


def rotary_tables(offsets, head_width):
    inv_freq = THETA ** (-jnp.arange(0, head_width, 2, dtype=jnp.float32) / head_width)
    angles = offsets.astype(jnp.float32)[:, None] * inv_freq[None, :]
    cosine_table = jnp.concatenate([jnp.cos(angles), jnp.cos(angles)], axis=1)
    sine_lookup = jnp.concatenate([jnp.sin(angles), jnp.sin(angles)], axis=1)
    return (cosine_table, sine_lookup)


def rotate_head_halves(raw_vals, gain_vec, cosine_table, sine_lookup):
    scaled = (
        raw_vals * lax.rsqrt(jnp.mean(raw_vals * raw_vals, axis=2, keepdims=True) + EPS) * gain_vec
    )
    half_width = raw_vals.shape[2] // 2
    turned = jnp.concatenate([-scaled[:, :, half_width:], scaled[:, :, :half_width]], axis=2)
    return scaled * cosine_table[:, None, :] + turned * sine_lookup[:, None, :]


def outer_sum(left, right):
    return lax.dot_general(
        left, right, (((0,), (0,)), ((), ())), preferred_element_type=jnp.float32
    )


def back_dot(left, right):
    return lax.dot_general(
        left, right, (((1,), (1,)), ((), ())), preferred_element_type=jnp.float32
    )


def attend(query_rows, key_matrix_rows, value_rows, allowed):
    scale_qk = query_rows.shape[-1] ** (-0.5)
    scores = (
        jnp.einsum(
            "qhgd,khd->hgqk", query_rows, key_matrix_rows, preferred_element_type=jnp.float32
        )
        * scale_qk
    )
    scores = jnp.where(allowed[None, None], scores, -1e30)
    row_peak = jnp.max(scores, axis=3, keepdims=True)
    exp_vals = jnp.exp(scores - row_peak)
    denom_sum = jnp.sum(exp_vals, axis=3, keepdims=True)
    attention_mixing = (exp_vals / denom_sum).astype(jnp.bfloat16)
    heads_mixed_output = jnp.einsum(
        "fmvc,cfn->vfmn", attention_mixing, value_rows, preferred_element_type=jnp.float32
    )
    return (heads_mixed_output, (row_peak + jnp.log(denom_sum))[..., 0])


def attend_back(query_rows, key_matrix_rows, value_rows, allowed, grad_heads, log_total, inner_sum):
    scale_qk = query_rows.shape[-1] ** (-0.5)
    scores = (
        jnp.einsum(
            "qhgd,khd->hgqk", query_rows, key_matrix_rows, preferred_element_type=jnp.float32
        )
        * scale_qk
    )
    scores = jnp.where(allowed[None, None], scores, -1e30)
    attention_mixing = jnp.exp(scores - log_total[..., None])
    grad_attn = jnp.einsum(
        "qhgd,khd->hgqk", grad_heads, value_rows, preferred_element_type=jnp.float32
    )
    inner_sum = jnp.sum(attention_mixing * grad_attn, axis=3)
    grad_scores = (attention_mixing * (grad_attn - inner_sum[..., None])).astype(jnp.bfloat16)
    return (attention_mixing, grad_scores, inner_sum)


def body(
    boundary,
    segment_ids,
    w_query,
    key_projection,
    value_projection,
    w_out,
    w_gate,
    w_up,
    w_down,
    attn_gain,
    mlp_gain,
    query_gain,
    key_norm_gain,
):
    section_index = lax.axis_index("section")
    row_index = lax.axis_index("row")
    col_index = lax.axis_index("col")
    micro_count = boundary.shape[1]
    tok_rows = boundary.shape[2]
    width_col = boundary.shape[3]
    model_width = width_col * lax.axis_size("col")
    seq_span = tok_rows * lax.axis_size("row")
    head_width = query_gain.shape[1]
    q_cols = w_query.shape[2]
    kv_cols = key_projection.shape[2]
    kv_heads = kv_cols // head_width
    group_size = q_cols // kv_cols
    scale_qk = head_width ** (-0.5)
    f32 = jnp.float32
    bf16 = jnp.bfloat16
    q_full, k_full, v_full, g_full, u_full = (
        lax.all_gather(w_query[0], "row", axis=0, tiled=True),
        lax.all_gather(key_projection[0], "row", axis=0, tiled=True),
        lax.all_gather(value_projection[0], "row", axis=0, tiled=True),
        lax.all_gather(w_gate[0], "row", axis=0, tiled=True),
        lax.all_gather(w_up[0], "row", axis=0, tiled=True),
    )
    o_full, d_full = (
        lax.all_gather(w_out[0], "row", axis=1, tiled=True),
        lax.all_gather(w_down[0], "row", axis=1, tiled=True),
    )
    gain_a = attn_gain[0].astype(f32)
    gain_m = mlp_gain[0].astype(f32)
    gain_q = query_gain[0].astype(f32)
    gain_k = key_norm_gain[0].astype(f32)

    def totals(partial_value):
        return lax.psum(partial_value, "col")

    def widen(partial_value):
        return lax.all_gather(partial_value, "col", axis=1, tiled=True)

    def narrow(partial_value):
        return lax.psum_scatter(partial_value, "col", scatter_dimension=1, tiled=True)

    def normalize(residual, gain_vec):
        scale_rms = lax.rsqrt(totals(jnp.sum(residual * residual, axis=1)) / model_width + EPS)
        return (scale_rms, widen((residual * scale_rms[:, None] * gain_vec).astype(bf16)))

    def norm_back(residual, scale_rms, gain_vec, grad_norm):
        lifted = grad_norm * gain_vec
        inner_sum = totals(jnp.sum(lifted * residual, axis=1))
        grad_res = (
            scale_rms[:, None] * lifted
            - residual * (scale_rms**3 * inner_sum / model_width)[:, None]
        )
        grad_gain = jnp.sum(grad_norm * residual * scale_rms[:, None], axis=0)
        return (grad_res, grad_gain)

    def geometry(batch_index):
        segments = lax.dynamic_index_in_dim(segment_ids, batch_index, 0, keepdims=False)
        cosine_table, sine_lookup = rotary_tables(positions(segments), head_width)
        start_row = row_index * tok_rows
        my_segs = lax.dynamic_slice_in_dim(segments, start_row, tok_rows)
        places = jnp.arange(seq_span, dtype=jnp.int32)
        my_places = start_row + jnp.arange(tok_rows, dtype=jnp.int32)
        allowed = (my_segs[:, None] == segments[None, :]) & (places[None, :] <= my_places[:, None])
        allowed_t = (segments[:, None] == my_segs[None, :]) & (
            my_places[None, :] <= places[:, None]
        )
        my_cos = lax.dynamic_slice_in_dim(cosine_table, start_row, tok_rows)
        my_sin = lax.dynamic_slice_in_dim(sine_lookup, start_row, tok_rows)
        return (allowed, allowed_t, my_cos, my_sin)

    def layer_backward(grad_top, stored, batch_index):
        (
            residual,
            scale_a,
            normed_a,
            q_raw,
            key_unrotated,
            key_matrix_rows,
            value_rows,
            heads_mixed_output,
            log_total,
            middle,
            scale_m,
            normed_m,
            gate_pre,
            up_proj,
            hidden,
        ) = stored
        allowed, allowed_t, my_cos, my_sin = geometry(batch_index)
        wide_top = widen(grad_top.astype(bf16))
        acc_down = outer_sum(hidden, wide_top)
        grad_hidden = back_dot(wide_top, d_full)

        def gated(gate_vals, up_vals):
            return jax.nn.silu(gate_vals) * up_vals

        _, pull_gate = jax.vjp(gated, gate_pre, up_proj)
        grad_gate, grad_up = pull_gate(grad_hidden)
        grad_gate = grad_gate.astype(bf16)
        grad_up = grad_up.astype(bf16)
        acc_gate = outer_sum(normed_m, grad_gate)
        acc_up = outer_sum(normed_m, grad_up)
        grad_norm_m = narrow(back_dot(grad_gate, g_full) + back_dot(grad_up, u_full))
        grad_mid_norm, grad_gain_m = norm_back(middle, scale_m, gain_m, grad_norm_m)
        grad_mid = grad_top + grad_mid_norm
        wide_mid = widen(grad_mid.astype(bf16))
        acc_out = outer_sum(heads_mixed_output, wide_mid)
        grad_heads = (
            back_dot(wide_mid, o_full)
            .astype(bf16)
            .reshape(tok_rows, kv_heads, group_size, head_width)
        )
        rotated_q, pull_query = jax.vjp(
            lambda raw_vals, gain_vec: rotate_head_halves(raw_vals, gain_vec, my_cos, my_sin),
            q_raw.reshape(tok_rows, -1, head_width),
            gain_q,
        )
        rotated_k, pull_key = jax.vjp(
            lambda raw_vals, gain_vec: rotate_head_halves(raw_vals, gain_vec, my_cos, my_sin),
            key_unrotated.reshape(tok_rows, kv_heads, head_width),
            gain_k,
        )
        query_rows = rotated_q.astype(bf16).reshape(tok_rows, kv_heads, group_size, head_width)
        attention_mixing, grad_scores, inner_sum = attend_back(
            query_rows, key_matrix_rows, value_rows, allowed, grad_heads, log_total, None
        )
        grad_q = (
            jnp.einsum("fmvc,cfn->vfmn", grad_scores, key_matrix_rows, preferred_element_type=f32)
            * scale_qk
        )
        part_k = (
            jnp.einsum("hgqk,qhgd->khd", grad_scores, query_rows, preferred_element_type=f32)
            * scale_qk
        )
        part_v = jnp.einsum(
            "hgqk,qhgd->khd", attention_mixing.astype(bf16), grad_heads, preferred_element_type=f32
        )
        grad_k, grad_v = (
            lax.psum_scatter(
                part_k.astype(jnp.bfloat16), "row", scatter_dimension=0, tiled=True
            ).astype(jnp.float32),
            lax.psum_scatter(
                part_v.astype(jnp.bfloat16), "row", scatter_dimension=0, tiled=True
            ).astype(jnp.float32),
        )
        grad_q_raw, grad_gain_q = pull_query(grad_q.reshape(tok_rows, -1, head_width))
        grad_k_raw, grad_gain_k = pull_key(grad_k)
        grad_q_low = grad_q_raw.reshape(tok_rows, q_cols).astype(bf16)
        grad_k_low = grad_k_raw.reshape(tok_rows, kv_cols).astype(bf16)
        grad_v_low = grad_v.reshape(tok_rows, kv_cols).astype(bf16)
        acc_query = outer_sum(normed_a, grad_q_low)
        acc_key = outer_sum(normed_a, grad_k_low)
        acc_value = outer_sum(normed_a, grad_v_low)
        grad_norm_a = narrow(
            back_dot(grad_q_low, q_full)
            + back_dot(grad_k_low, k_full)
            + back_dot(grad_v_low, v_full)
        )
        grad_in_norm, grad_gain_a = norm_back(residual, scale_a, gain_a, grad_norm_a)
        pieces = (
            acc_query,
            acc_key,
            acc_value,
            acc_out,
            acc_gate,
            acc_up,
            acc_down,
            grad_gain_a,
            grad_gain_m,
            grad_gain_q,
            grad_gain_k,
        )
        return (grad_mid + grad_in_norm, pieces)

    zero_state = jnp.zeros((tok_rows, width_col), f32)
    arrived = zero_state
    stored_list = []
    outputs = []
    for tick_step in range(micro_count + 1):
        batch_index = jnp.clip(tick_step - section_index, 0, micro_count - 1)
        first_in = boundary[0, min(tick_step, micro_count - 1)].astype(f32) * (
            1.0 if tick_step < micro_count else 0.0
        )
        entering = jnp.where(section_index == 0, first_in, arrived)
        layer_allowed, layer_allowed_t, layer_my_cos, layer_my_sin = geometry(batch_index)
        layer_scale_a, layer_normed_a = normalize(entering, gain_a)
        layer_q_raw = jnp.dot(layer_normed_a, q_full, preferred_element_type=f32)
        layer_key_unrotated = jnp.dot(layer_normed_a, k_full, preferred_element_type=f32)
        v_own = jnp.dot(layer_normed_a, v_full, preferred_element_type=f32).astype(bf16)
        layer_query_rows = rotate_head_halves(
            layer_q_raw.reshape(tok_rows, -1, head_width), gain_q, layer_my_cos, layer_my_sin
        ).astype(bf16)
        keys_own = rotate_head_halves(
            layer_key_unrotated.reshape(tok_rows, kv_heads, head_width),
            gain_k,
            layer_my_cos,
            layer_my_sin,
        ).astype(bf16)
        layer_key_matrix_rows = lax.all_gather(keys_own, "row", axis=0, tiled=True)
        layer_value_rows = lax.all_gather(
            v_own.reshape(tok_rows, kv_heads, head_width), "row", axis=0, tiled=True
        )
        layer_query_rows = layer_query_rows.reshape(tok_rows, kv_heads, group_size, head_width)
        layer_heads_mixed_output, layer_log_total = attend(
            layer_query_rows, layer_key_matrix_rows, layer_value_rows, layer_allowed
        )
        layer_heads_mixed_output = layer_heads_mixed_output.reshape(tok_rows, q_cols).astype(bf16)
        layer_middle = entering + narrow(
            jnp.dot(layer_heads_mixed_output, o_full, preferred_element_type=f32)
        )
        layer_scale_m, layer_normed_m = normalize(layer_middle, gain_m)
        layer_gate_pre = jnp.dot(layer_normed_m, g_full, preferred_element_type=f32)
        layer_up_proj = jnp.dot(layer_normed_m, u_full, preferred_element_type=f32)
        layer_hidden = (jax.nn.silu(layer_gate_pre) * layer_up_proj).astype(bf16)
        result = layer_middle + narrow(jnp.dot(layer_hidden, d_full, preferred_element_type=f32))
        layer_stored = (
            entering,
            layer_scale_a,
            layer_normed_a,
            layer_q_raw,
            layer_key_unrotated,
            layer_key_matrix_rows,
            layer_value_rows,
            layer_heads_mixed_output,
            layer_log_total,
            layer_middle,
            layer_scale_m,
            layer_normed_m,
            layer_gate_pre,
            layer_up_proj,
            layer_hidden,
        )
        result, stored = (result, layer_stored)
        stored_list.append(stored)
        outputs.append(result)
        if tick_step < micro_count:
            arrived = passed_along(result.astype(bf16), "section", 1).astype(f32)
    returned = zero_state
    totals_sum = None
    grads_in = []
    for tick_step in range(micro_count + 1):
        batch_index = jnp.clip(tick_step - 1 + section_index, 0, micro_count - 1)
        top_index = min(tick_step, micro_count - 1)
        my_top_segs = lax.dynamic_slice_in_dim(
            segment_ids[top_index], row_index * tok_rows, tok_rows
        )
        valid_rows = (my_top_segs >= 0).astype(f32)
        top_grad = (
            boundary[0, top_index].astype(f32)
            * valid_rows[:, None]
            * (1.0 if tick_step < micro_count else 0.0)
        )
        grad_top = jnp.where(section_index == 1, top_grad, returned)
        lower_kept = stored_list[max(tick_step - 1, 0)]
        upper_kept = stored_list[min(tick_step + 1, micro_count)]
        stored = jax.tree.map(
            lambda low_val, high_val: jnp.where(section_index == 1, high_val, low_val),
            lower_kept,
            upper_kept,
        )
        grad_in, pieces = layer_backward(grad_top, stored, batch_index)
        totals_sum = pieces if totals_sum is None else jax.tree.map(jnp.add, totals_sum, pieces)
        grads_in.append(grad_in)
        if tick_step < micro_count:
            returned = passed_along(grad_in.astype(bf16), "section", -1).astype(f32)
    section_out = jnp.stack(
        [
            jnp.where(section_index == 0, grads_in[index_mb + 1], outputs[index_mb + 1])
            for index_mb in range(micro_count)
        ]
    )[None]
    (
        acc_query,
        acc_key,
        acc_value,
        acc_out,
        acc_gate,
        acc_up,
        acc_down,
        gain_a_sum,
        gain_m_sum,
        gain_q_sum,
        gain_k_sum,
    ) = totals_sum
    red_query, red_key, red_value, red_gate, red_up = (
        lax.psum_scatter(
            acc_query.astype(jnp.bfloat16), "row", scatter_dimension=0, tiled=True
        ).astype(jnp.float32),
        lax.psum_scatter(
            acc_key.astype(jnp.bfloat16), "row", scatter_dimension=0, tiled=True
        ).astype(jnp.float32),
        lax.psum_scatter(
            acc_value.astype(jnp.bfloat16), "row", scatter_dimension=0, tiled=True
        ).astype(jnp.float32),
        lax.psum_scatter(
            acc_gate.astype(jnp.bfloat16), "row", scatter_dimension=0, tiled=True
        ).astype(jnp.float32),
        lax.psum_scatter(
            acc_up.astype(jnp.bfloat16), "row", scatter_dimension=0, tiled=True
        ).astype(jnp.float32),
    )
    red_out, red_down = (
        lax.psum_scatter(
            acc_out.astype(jnp.bfloat16), "row", scatter_dimension=1, tiled=True
        ).astype(jnp.float32),
        lax.psum_scatter(
            acc_down.astype(jnp.bfloat16), "row", scatter_dimension=1, tiled=True
        ).astype(jnp.float32),
    )
    full_zero = jnp.zeros((model_width,), f32)
    gain_a_full = lax.dynamic_update_slice_in_dim(full_zero, gain_a_sum, col_index * width_col, 0)
    gain_m_full = lax.dynamic_update_slice_in_dim(full_zero, gain_m_sum, col_index * width_col, 0)
    sum_a, sum_m, sum_q, sum_k = lax.psum(
        (gain_a_full, gain_m_full, gain_q_sum, gain_k_sum), ("row", "col")
    )
    return (
        section_out,
        red_query[None],
        red_key[None],
        red_value[None],
        red_out[None],
        red_gate[None],
        red_up[None],
        red_down[None],
        sum_a[None],
        sum_m[None],
        sum_q[None],
        sum_k[None],
    )


def solution(mesh):
    return jax.shard_map(
        body,
        mesh=mesh,
        in_specs=(
            P("section", None, "row", "col"),
            P(),
            P("section", "row", "col"),
            P("section", "row", "col"),
            P("section", "row", "col"),
            P("section", "col", "row"),
            P("section", "row", "col"),
            P("section", "row", "col"),
            P("section", "col", "row"),
            P("section", "col"),
            P("section", "col"),
            P("section", None),
            P("section", None),
        ),
        out_specs=(
            P("section", None, "row", "col"),
            P("section", "row", "col"),
            P("section", "row", "col"),
            P("section", "row", "col"),
            P("section", "col", "row"),
            P("section", "row", "col"),
            P("section", "row", "col"),
            P("section", "col", "row"),
            P("section", None),
            P("section", None),
            P("section", None),
            P("section", None),
        ),
        check_vma=False,
    )
```

profile of v0, /device:TPU:0, one launch (start us, length us, event | category | flops | bytes accessed | tf_op | source)
XLA Modules:
  0.0 2374.7 jit_solution(13930256978946984270)
XLA Ops:
  14.9 8.4 psum.168
  48.8 20.5 all-gather.15.cloned.1.call-done
  71.2 15.7 all_gather.115
  86.9 16.1 all_gather.113
  103.0 18.2 all-gather.19.cloned.1.call-done
  124.5 43.4 %all-gather.21.cloned.1.call-done = bf16[1,512,2048]{2,1,0:T(8,128)(2,1)} async-done(((bf16[1,512,512]{2,1,0:T(8,128)(2,1)}), bf16[1,512,2048]{2,1,0:T(8,128)(2,1)}) %all-gather.21.cloned.1.call-update) | async-done | bytes 2097168 | tf_op jit(solution)/shard_map/all_gather | solution.py:128
  173.2 21.6 reduce-scatter.48.cloned.1.call-done
  202.3 7.3 all_gather.118
  209.6 102.1 %all-gather.23.cloned.1.call-done = bf16[1,2048,1536]{2,1,0:T(8,128)(2,1)} async-done(((bf16[1,512,1536]{2,1,0:T(8,128)(2,1)}), bf16[1,2048,1536]{2,1,0:T(8,128)(2,1)}) %all-gather.23.cloned.1.call-update) | async-done | bytes 6291472 | tf_op jit(solution)/shard_map/all_gather | solution.py:124
  315.5 111.5 %all-gather.25.cloned.1.call-done = bf16[1,2048,1536]{2,1,0:T(8,128)(2,1)} async-done(((bf16[1,512,1536]{2,1,0:T(8,128)(2,1)}), bf16[1,2048,1536]{2,1,0:T(8,128)(2,1)}) %all-gather.25.cloned.1.call-update) | async-done | bytes 6291472 | tf_op jit(solution)/shard_map/all_gather | solution.py:125
  431.8 110.4 %all-gather.27.cloned.1.call-done = bf16[1,1536,2048]{2,1,0:T(8,128)(2,1)} async-done(((bf16[1,1536,512]{2,1,0:T(8,128)(2,1)}), bf16[1,1536,2048]{2,1,0:T(8,128)(2,1)}) %all-gather.27.cloned.1.call-update) | async-done | bytes 6291472 | tf_op jit(solution)/shard_map/all_gather | solution.py:129
  550.7 19.6 reduce-scatter.50.cloned.1.call-done
  608.6 14.0 all_gather.124
  628.0 14.8 all_gather.123
  647.2 7.8 all_gather.125
  655.0 17.5 reduce-scatter.52.cloned.1.call-done
  680.2 7.5 all_gather.126
  707.4 20.4 reduce-scatter.54.cloned.1.call-done
  727.8 27.9 %reduce-scatter.60.cloned.1.call-done = f32[128,512]{1,0:T(8,128)} async-done(((f32[128,2048]{1,0:T(8,128)}), f32[128,512]{1,0:T(8,128)}) %reduce-scatter.60.cloned.1.call-update) | async-done | bytes 262160 | tf_op jit(solution)/shard_map/reduce_scatter | solution.py:143
  801.6 14.8 all_gather.130
  821.8 14.6 all_gather.129
  856.9 10.1 reduce-scatter.62.cloned.1.call-done
  879.5 7.3 all_gather.127
  895.4 8.6 all_gather.132
  926.6 8.8 reduce-scatter.112.cloned.1.call-done
  943.9 17.8 reduce-scatter.70.cloned.1.call-done
  969.5 20.1 reduce-scatter.58.cloned.1.call-done
  1001.4 7.3 all_gather.134
  1019.8 14.0 all_gather.136
  1035.7 14.5 all_gather.135
  1063.5 17.2 reduce-scatter.72.cloned.1.call-done
  1142.4 7.5 all_gather.133
  1160.1 8.7 all_gather.138
  1192.6 7.8 reduce-scatter.114.cloned.1.call-done
  1206.3 20.4 reduce-scatter.80.cloned.1.call-done
  1234.7 20.2 reduce-scatter.68.cloned.1.call-done
  1274.0 7.5 all_gather.137
  1302.2 18.0 reduce-scatter.74.cloned.1.call-done
  1331.0 7.3 all_gather.139
  1360.2 11.2 reduce-scatter.76.cloned.1.call-done
  1378.0 13.9 reduce-scatter.116.cloned.1.call-done
  1401.4 18.8 reduce-scatter.78.cloned.1.call-done
  1447.2 14.7 all_gather.142
  1467.3 14.9 all_gather.141
  1487.7 23.3 reduce-scatter.82.cloned.1.call-done
  1522.1 7.3 all_gather.144
  1572.4 9.5 reduce-scatter.84.cloned.1.call-done
  1593.3 7.3 all_gather.145
  1617.6 13.5 reduce-scatter.86.cloned.1.call-done
  1635.7 16.3 reduce-scatter.118.cloned.1.call-done
  1657.5 23.3 reduce-scatter.88.cloned.1.call-done
  1699.9 7.1 all_gather.146
  1707.0 7.1 fusion.237
  1726.8 20.2 reduce-scatter.90.cloned.1.call-done
  1757.1 7.4 all_gather.147
  1784.1 12.4 reduce-scatter.92.cloned.1.call-done
  1803.1 14.3 reduce-scatter.120.cloned.1.call-done
  1883.5 16.9 add_convert_fusion.2
  1923.7 16.9 add_convert_fusion.1
  1963.8 16.4 add_convert_fusion
  1988.3 61.1 %all-reduce.20 = (f32[1,2048]{1,0:T(1,128)}, f32[1,2048]{1,0:T(1,128)}, f32[1,128]{1,0:T(1,128)}, f32[1,128]{1,0:T(1,128)}) all-reduce(f32[1,2048]{1,0:T(1,128)S(1)} %constant_dynamic-update-slice_fusion.1, f32[1,2048]{1,0:T(1,128)S(1)} %constant_dynamic-update-slice_fusion, ...), channel_id=1, replica_groups=mesh['section'=2,'row'=4,'col'=4] {'row','col'}, use_global_device_ids=true, to_apply=%region_147.148 | all-reduce | flops 4352 | bytes 34816 | tf_op jit(solution)/shard_map/psum | solution.py:416
  2059.6 77.5 %reduce-scatter.106.cloned.1.call-done = bf16[512,1536]{1,0:T(8,128)(2,1)} async-done(((bf16[2048,1536]{1,0:T(8,128)(2,1)}), bf16[512,1536]{1,0:T(8,128)(2,1)}) %reduce-scatter.106.cloned.1.call-update) | async-done | bytes 1572880 | tf_op jit(solution)/shard_map/reduce_scatter | solution.py:398
  2140.6 110.1 %reduce-scatter.108.cloned.1.call-done = bf16[512,1536]{1,0:T(8,128)(2,1)} async-done(((bf16[2048,1536]{1,0:T(8,128)(2,1)}), bf16[512,1536]{1,0:T(8,128)(2,1)}) %reduce-scatter.108.cloned.1.call-update) | async-done | bytes 1572880 | tf_op jit(solution)/shard_map/reduce_scatter | solution.py:401
  2254.1 110.1 %reduce-scatter.110.cloned.1.call-done = bf16[1536,512]{1,0:T(8,128)(2,1)} async-done(((bf16[1536,2048]{1,0:T(8,128)(2,1)}), bf16[1536,512]{1,0:T(8,128)(2,1)}) %reduce-scatter.110.cloned.1.call-update) | async-done | bytes 1572880 | tf_op jit(solution)/shard_map/reduce_scatter | solution.py:409
  (1228 shorter events, 846.8 us)
Async XLA Ops:
  7.2 39.6 %all-gather.17.cloned.1.call-start = ((), (), s32[]{:S(2)}) async-start(), calls=%async_computation.70 | async-start | bytes 1310720 | tf_op jit(solution)/shard_map/all_gather | solution.py:122
  7.9 61.4 %all-gather.15.cloned.1.call-start = ((), (), s32[]{:S(2)}) async-start(), calls=%async_computation.69 | async-start | bytes 1310720 | tf_op jit(solution)/shard_map/all_gather | solution.py:123
  8.7 112.5 %all-gather.19.cloned.1.call-start = ((), (), s32[]{:S(2)}) async-start(), calls=%async_computation.71 | async-start | bytes 2621440 | tf_op jit(solution)/shard_map/all_gather | solution.py:121
  9.4 158.5 %all-gather.21.cloned.1.call-start = ((), (), s32[]{:S(2)}) async-start(), calls=%async_computation.72 | async-start | bytes 2621440 | tf_op jit(solution)/shard_map/all_gather | solution.py:128
  10.0 184.8 %reduce-scatter.48.cloned.1.call-start = ((), (), s32[]{:S(2)}) async-start(), calls=%async_computation.37 | async-start | bytes 1310720 | tf_op jit(solution)/shard_map/reduce_scatter | solution.py:143
  30.8 92.4 %copy-start.34 = (bf16[128,2048]{1,0:T(8,128)(2,1)}, bf16[128,2048]{1,0:T(8,128)(2,1)S(1)}, u32[]{:S(2)}) copy-start(bf16[128,2048]{1,0:T(8,128)(2,1)S(1)} %all_gather.111) | copy-start | bytes 1572868
  86.9 84.0 %copy-start.49 = (bf16[512,2,128]{2,0,1:T(8,128)(2,1)}, bf16[512,2,128]{2,0,1:T(8,128)(2,1)S(1)}, u32[]{:S(2)}) copy-start(bf16[512,2,128]{2,0,1:T(8,128)(2,1)S(1)} %all_gather.115) | copy-start | bytes 786436
  124.5 85.1 %copy-start.181 = (bf16[2,128,2,128]{3,1,2,0:T(8,128)(2,1)}, bf16[2,128,2,128]{3,1,2,0:T(8,128)(2,1)S(1)}, u32[]{:S(2)}) copy-start(bf16[2,128,2,128]{3,1,2,0:T(8,128)(2,1)S(1)} %convolution_convert_fusion.4) | copy-start | bytes 393220
  171.0 140.7 %all-gather.23.cloned.1.call-start = ((), (), s32[]{:S(2)}) async-start(), calls=%async_computation.73 | async-start | bytes 7864320 | tf_op jit(solution)/shard_map/all_gather | solution.py:124
  171.6 255.4 %all-gather.25.cloned.1.call-start = ((), (), s32[]{:S(2)}) async-start(), calls=%async_computation.74 | async-start | bytes 7864320 | tf_op jit(solution)/shard_map/all_gather | solution.py:125
  172.3 369.9 %all-gather.27.cloned.1.call-start = ((), (), s32[]{:S(2)}) async-start(), calls=%async_computation.75 | async-start | bytes 7864320 | tf_op jit(solution)/shard_map/all_gather | solution.py:129
  173.1 397.3 %reduce-scatter.50.cloned.1.call-start = ((), (), s32[]{:S(2)}) async-start(), calls=%async_computation.38 | async-start | bytes 1310720 | tf_op jit(solution)/shard_map/reduce_scatter | solution.py:143
  195.9 374.5 %copy-start.69 = (f32[128,512]{1,0:T(8,128)}, f32[128,512]{1,0:T(8,128)S(1)}, u32[]{:S(2)}) copy-start(f32[128,512]{1,0:T(8,128)S(1)} %get-tuple-element.126) | copy-start | bytes 786436
  209.6 217.3 %copy-start.17 = (bf16[128,2048]{1,0:T(8,128)(2,1)}, bf16[128,2048]{1,0:T(8,128)(2,1)S(1)}, u32[]{:S(2)}) copy-start(bf16[128,2048]{1,0:T(8,128)(2,1)S(1)} %all_gather.118) | copy-start | bytes 1572868
  315.4 116.3 %copy-start.159 = (f32[128,1536]{1,0:T(8,128)}, f32[128,1536]{1,0:T(8,128)S(1)}, u32[]{:S(2)}) copy-start(f32[128,1536]{1,0:T(8,128)S(1)} %fusion.58) | copy-start | bytes 2359300
  431.7 110.4 %copy-start.62 = (bf16[128,1536]{1,0:T(8,128)(2,1)}, bf16[128,1536]{1,0:T(8,128)(2,1)S(1)}, u32[]{:S(2)}) copy-start(bf16[128,1536]{1,0:T(8,128)(2,1)S(1)} %get-tuple-element.317) | copy-start | bytes 1179652
  547.1 125.4 %reduce-scatter.52.cloned.1.call-start = ((), (), s32[]{:S(2)}) async-start(), calls=%async_computation.39 | async-start | bytes 1310720 | tf_op jit(solution)/shard_map/reduce_scatter | solution.py:143
  572.0 7.4 collective-permute-start
  579.4 93.1 %copy-start.92 = (bf16[128,512]{1,0:T(8,128)(2,1)}, bf16[128,512]{1,0:T(8,128)(2,1)S(1)}, u32[]{:S(2)}) copy-start(bf16[128,512]{1,0:T(8,128)(2,1)S(1)} %collective-permute-done) | copy-start | bytes 393220
  647.1 80.7 %reduce-scatter.54.cloned.1.call-start = ((), (), s32[]{:S(2)}) async-start(), calls=%async_computation.40 | async-start | bytes 1310720 | tf_op jit(solution)/shard_map/reduce_scatter | solution.py:143
  680.1 75.7 %copy-start.232 = (f32[128]{0:T(128)}, f32[128]{0:T(128)S(1)}, u32[]{:S(2)}) copy-start(f32[128]{0:T(128)S(1)} %get-tuple-element.313) | copy-start | bytes 1540
  702.6 53.2 %reduce-scatter.60.cloned.1.call-start = ((), (), s32[]{:S(2)}) async-start(), calls=%async_computation.43 | async-start | bytes 1310720 | tf_op jit(solution)/shard_map/reduce_scatter | solution.py:143
  707.4 159.6 %reduce-scatter.62.cloned.1.call-start = ((), (), s32[]{:S(2)}) async-start(), calls=%async_computation.44 | async-start | bytes 1310720 | tf_op jit(solution)/shard_map/reduce_scatter | solution.py:143
  758.4 6.4 collective-permute-start.2
  764.8 102.2 %copy-start.90 = (bf16[128,512]{1,0:T(8,128)(2,1)}, bf16[128,512]{1,0:T(8,128)(2,1)S(1)}, u32[]{:S(2)}) copy-start(bf16[128,512]{1,0:T(8,128)(2,1)S(1)} %collective-permute-done.2) | copy-start | bytes 393220
  840.7 80.1 %reduce-scatter.56.cloned.1.call-start = ((), (), s32[]{:S(2)}) async-start(), calls=%async_computation.41 | async-start | bytes 327680 | tf_op jit(solution)/shard_map/reduce_scatter | solution.py:242
  895.3 40.1 %reduce-scatter.112.cloned.1.call-start = ((), (), s32[]{:S(2)}) async-start(), calls=%async_computation.76 | async-start | bytes 327680 | tf_op jit(solution)/shard_map/convert_element_type | solution.py:253
  907.3 54.3 %reduce-scatter.70.cloned.1.call-start = ((), (), s32[]{:S(2)}) async-start(), calls=%async_computation.48 | async-start | bytes 1310720 | tf_op jit(solution)/shard_map/reduce_scatter | solution.py:143
  918.8 70.9 %reduce-scatter.58.cloned.1.call-start = ((), (), s32[]{:S(2)}) async-start(), calls=%async_computation.42 | async-start | bytes 1310720 | tf_op jit(solution)/shard_map/reduce_scatter | solution.py:143
  939.5 141.2 %reduce-scatter.72.cloned.1.call-start = ((), (), s32[]{:S(2)}) async-start(), calls=%async_computation.49 | async-start | bytes 1310720 | tf_op jit(solution)/shard_map/reduce_scatter | solution.py:143
  963.4 6.1 collective-permute-start.4
  969.5 450.6 %copy-start.88 = (bf16[128,512]{1,0:T(8,128)(2,1)}, bf16[128,512]{1,0:T(8,128)(2,1)S(1)}, u32[]{:S(2)}) copy-start(bf16[128,512]{1,0:T(8,128)(2,1)S(1)} %collective-permute-done.4) | copy-start | bytes 393220
  1056.3 73.2 %reduce-scatter.64.cloned.1.call-start = ((), (), s32[]{:S(2)}) async-start(), calls=%async_computation.45 | async-start | bytes 1310720 | tf_op jit(solution)/shard_map/reduce_scatter | solution.py:143
  1056.3 7.2 collective-permute-start.1
  1104.1 81.9 %reduce-scatter.66.cloned.1.call-start = ((), (), s32[]{:S(2)}) async-start(), calls=%async_computation.46 | async-start | bytes 327680 | tf_op jit(solution)/shard_map/reduce_scatter | solution.py:242
  1160.1 40.4 %reduce-scatter.114.cloned.1.call-start = ((), (), s32[]{:S(2)}) async-start(), calls=%async_computation.77 | async-start | bytes 327680 | tf_op jit(solution)/shard_map/convert_element_type | solution.py:253
  1172.4 54.3 %reduce-scatter.80.cloned.1.call-start = ((), (), s32[]{:S(2)}) async-start(), calls=%async_computation.53 | async-start | bytes 1310720 | tf_op jit(solution)/shard_map/reduce_scatter | solution.py:143
  1184.0 70.9 %reduce-scatter.68.cloned.1.call-start = ((), (), s32[]{:S(2)}) async-start(), calls=%async_computation.47 | async-start | bytes 1310720 | tf_op jit(solution)/shard_map/reduce_scatter | solution.py:143
  1206.2 114.0 %reduce-scatter.74.cloned.1.call-start = ((), (), s32[]{:S(2)}) async-start(), calls=%async_computation.50 | async-start | bytes 1310720 | tf_op jit(solution)/shard_map/reduce_scatter | solution.py:143
  1228.6 6.1 collective-permute-start.6
  1265.9 7.1 collective-permute-start.3
  1295.8 75.6 %reduce-scatter.76.cloned.1.call-start = ((), (), s32[]{:S(2)}) async-start(), calls=%async_computation.51 | async-start | bytes 327680 | tf_op jit(solution)/shard_map/reduce_scatter | solution.py:242
  1351.2 40.7 %reduce-scatter.116.cloned.1.call-start = ((), (), s32[]{:S(2)}) async-start(), calls=%async_computation.78 | async-start | bytes 327680 | tf_op jit(solution)/shard_map/convert_element_type | solution.py:253
  1358.4 61.7 %reduce-scatter.78.cloned.1.call-start = ((), (), s32[]{:S(2)}) async-start(), calls=%async_computation.52 | async-start | bytes 1310720 | tf_op jit(solution)/shard_map/reduce_scatter | solution.py:143
  1396.9 114.1 %reduce-scatter.82.cloned.1.call-start = ((), (), s32[]{:S(2)}) async-start(), calls=%async_computation.54 | async-start | bytes 1310720 | tf_op jit(solution)/shard_map/reduce_scatter | solution.py:143
  1439.3 125.4 %copy-start.118 = (f32[128,256]{1,0:T(8,128)}, f32[128,256]{1,0:T(8,128)S(1)}, u32[]{:S(2)}) copy-start(f32[128,256]{1,0:T(8,128)S(1)} %get-tuple-element.189) | copy-start | bytes 393220
  1486.5 95.4 %reduce-scatter.84.cloned.1.call-start = ((), (), s32[]{:S(2)}) async-start(), calls=%async_computation.55 | async-start | bytes 1310720 | tf_op jit(solution)/shard_map/reduce_scatter | solution.py:143
  1532.0 8.0 collective-permute-start.5
  1555.7 75.4 %reduce-scatter.86.cloned.1.call-start = ((), (), s32[]{:S(2)}) async-start(), calls=%async_computation.56 | async-start | bytes 327680 | tf_op jit(solution)/shard_map/reduce_scatter | solution.py:242
  1611.0 41.0 %reduce-scatter.118.cloned.1.call-start = ((), (), s32[]{:S(2)}) async-start(), calls=%async_computation.79 | async-start | bytes 327680 | tf_op jit(solution)/shard_map/convert_element_type | solution.py:253
  1616.1 64.6 %reduce-scatter.88.cloned.1.call-start = ((), (), s32[]{:S(2)}) async-start(), calls=%async_computation.57 | async-start | bytes 1310720 | tf_op jit(solution)/shard_map/reduce_scatter | solution.py:143
  1657.4 89.6 %reduce-scatter.90.cloned.1.call-start = ((), (), s32[]{:S(2)}) async-start(), calls=%async_computation.58 | async-start | bytes 1310720 | tf_op jit(solution)/shard_map/reduce_scatter | solution.py:143
  1691.7 7.1 collective-permute-start.7
  1722.6 73.9 %reduce-scatter.92.cloned.1.call-start = ((), (), s32[]{:S(2)}) async-start(), calls=%async_computation.59 | async-start | bytes 327680 | tf_op jit(solution)/shard_map/reduce_scatter | solution.py:242
  1776.5 41.0 %reduce-scatter.120.cloned.1.call-start = ((), (), s32[]{:S(2)}) async-start(), calls=%async_computation.80 | async-start | bytes 327680 | tf_op jit(solution)/shard_map/convert_element_type | solution.py:253
  1782.3 198.7 %reduce-scatter.94.cloned.1.call-start = ((), (), s32[]{:S(2)}) async-start(), calls=%async_computation.60 | async-start | bytes 1310720 | tf_op jit(solution)/shard_map/reduce_scatter | solution.py:143
  1823.2 226.2 %reduce-scatter.96.cloned.1.call-start = ((), (), s32[]{:S(2)}) async-start(), calls=%async_computation.61 | async-start | bytes 1310720 | tf_op jit(solution)/shard_map/reduce_scatter | solution.py:143
  1828.7 223.1 %reduce-scatter.100.cloned.1.call-start = ((), (), s32[]{:S(2)}) async-start(), calls=%async_computation.63 | async-start | bytes 1310720 | tf_op jit(solution)/shard_map/reduce_scatter | solution.py:392
  1833.0 220.5 %reduce-scatter.102.cloned.1.call-start = ((), (), s32[]{:S(2)}) async-start(), calls=%async_computation.64 | async-start | bytes 1310720 | tf_op jit(solution)/shard_map/reduce_scatter | solution.py:395
  1837.7 217.7 %reduce-scatter.98.cloned.1.call-start = ((), (), s32[]{:S(2)}) async-start(), calls=%async_computation.62 | async-start | bytes 2621440 | tf_op jit(solution)/shard_map/reduce_scatter | solution.py:389
  1843.4 214.1 %reduce-scatter.104.cloned.1.call-start = ((), (), s32[]{:S(2)}) async-start(), calls=%async_computation.65 | async-start | bytes 2621440 | tf_op jit(solution)/shard_map/reduce_scatter | solution.py:406
  1861.2 275.8 %reduce-scatter.106.cloned.1.call-start = ((), (), s32[]{:S(2)}) async-start(), calls=%async_computation.66 | async-start | bytes 7864320 | tf_op jit(solution)/shard_map/reduce_scatter | solution.py:398
  1900.5 350.1 %reduce-scatter.108.cloned.1.call-start = ((), (), s32[]{:S(2)}) async-start(), calls=%async_computation.67 | async-start | bytes 7864320 | tf_op jit(solution)/shard_map/reduce_scatter | solution.py:401
  1940.6 423.6 %reduce-scatter.110.cloned.1.call-start = ((), (), s32[]{:S(2)}) async-start(), calls=%async_computation.68 | async-start | bytes 7864320 | tf_op jit(solution)/shard_map/reduce_scatter | solution.py:409
  (269 other events, 3298.6 us)
Sparse Core Ops, SparseCore 0:
  9.6 30.6 all-gather.16
  41.8 27.4 all-gather.14
  70.9 50.3 all-gather.18
  122.6 45.2 all-gather.20
  171.1 23.5 reduce-scatter.47
  196.3 115.3 all-gather.22
  313.3 113.5 all-gather.24
  428.6 113.5 all-gather.26
  547.2 23.0 reduce-scatter.49
  647.3 25.2 reduce-scatter.51
  702.7 25.1 reduce-scatter.53
  730.8 24.9 reduce-scatter.59
  840.8 26.0 reduce-scatter.61
  895.4 19.9 reduce-scatter.55
  917.6 17.7 reduce-scatter.111
  938.4 23.1 reduce-scatter.69
  964.8 24.8 reduce-scatter.57
  1056.4 24.2 reduce-scatter.71
  1104.2 25.2 reduce-scatter.63
  1160.2 19.9 reduce-scatter.65
  1182.6 17.8 reduce-scatter.113
  1203.5 23.1 reduce-scatter.79
  1230.0 24.8 reduce-scatter.67
  1295.9 24.2 reduce-scatter.73
  1351.4 19.9 reduce-scatter.75
  1374.1 17.8 reduce-scatter.115
  1397.0 23.1 reduce-scatter.77
  1486.6 24.3 reduce-scatter.81
  1555.9 25.9 reduce-scatter.83
  1611.1 19.9 reduce-scatter.85
  1634.0 17.8 reduce-scatter.117
  1657.5 23.1 reduce-scatter.87
  1722.7 24.2 reduce-scatter.89
  1776.6 19.9 reduce-scatter.91
  1799.5 17.9 reduce-scatter.119
  1823.4 23.0 reduce-scatter.93
  1849.6 24.8 reduce-scatter.95
  1877.4 27.1 reduce-scatter.99
  1906.8 25.7 reduce-scatter.101
  1935.5 42.4 reduce-scatter.97
  1981.0 43.3 reduce-scatter.103
  2026.7 110.3 reduce-scatter.105
  2139.2 111.3 reduce-scatter.107
  2252.9 111.2 reduce-scatter.109
where the time goes:
time: 2390 us; the launch traced here: 2370 us
  waiting for transfers between devices  1160 us (49%)
  blocking collectives  449 us (19%)
  matrix products  373 us (16%)
  other arithmetic  247 us (10%)
  local copies, waits for them, and re-layouts  103 us (4%)
    reduce_scatter x20, waiting for transfers between devices, narrow(): lax.psum_scatter(partial_value, 'col', scatter_dimension=1, tiled=True)  332 us
    all_gather x20, blocking collectives, widen(): return lax.all_gather(partial_value, 'col', axis=1, tiled=True)  146 us
    dot_general x35, matrix products, outer_sum(): lax.dot_general(left, right, (((0,), (0,)), ((), ())), preferred_element_...  145 us
    all_gather x1, waiting for transfers between devices, body(): lax.all_gather(w_up[0], 'row', axis=0, tiled=True)  111 us
    all_gather x1, waiting for transfers between devices, body(): lax.all_gather(w_down[0], 'row', axis=1, tiled=True)  110 us
    reduce_scatter x1, waiting for transfers between devices, body(): lax.psum_scatter(acc_down.astype(jnp.bfloat16), 'row', scatter_dimension=...  110 us
    reduce_scatter x1, waiting for transfers between devices, body(): lax.psum_scatter(acc_up.astype(jnp.bfloat16), 'row', scatter_dimension=0,...  110 us
    all_gather x1, waiting for transfers between devices, body(): lax.all_gather(w_gate[0], 'row', axis=0, tiled=True)  102 us
  transfers between devices with their start and end apart: 52, of which 41 were waited for; matrix products, arithmetic and copies ran while one was open for 17% of the time, Pallas kernels for 0%

commit v1 on v0

v1 whole, which is shorter than its diff:
```python
import jax
import jax.numpy as jnp
import numpy as np
from jax import lax
from jax.sharding import Mesh
from jax.sharding import PartitionSpec as P

EPS = 1e-06
THETA = 1000000.0
f32 = jnp.float32
bf16 = jnp.bfloat16


def swap(value, axis):
    return lax.ppermute(value, axis, [(0, 1), (1, 0)])


def take(value, index, axis=0):
    return lax.dynamic_index_in_dim(value, index, axis, keepdims=False)


def pair(bit, mine, other, axis=0):
    low = jnp.where(bit == 0, mine, other)
    high = jnp.where(bit == 0, other, mine)
    return jnp.stack([low, high], axis)


def dot(left, right):
    return jnp.dot(left, right, preferred_element_type=f32)


def dot_t(left, right):
    return lax.dot_general(left, right, (((1,), (1,)), ((), ())), preferred_element_type=f32)


def t_dot(left, right):
    return lax.dot_general(left, right, (((0,), (0,)), ((), ())), preferred_element_type=f32)


def gather_tokens(mine):
    part = mine.shape[0] // 2
    low, high = mine[:part], mine[part:]
    near = jnp.concatenate([swap(low, "s"), swap(high, "t")])
    mine_k = swap(mine, "k")
    far_low = swap(jnp.concatenate([low, near[:part]]), "t")
    far_high = swap(jnp.concatenate([high, near[part:]]), "s")
    near_k = swap(near, "k")
    far = jnp.concatenate([far_low, far_high])
    far_k = swap(far, "k")
    return jnp.concatenate([mine, near, far, mine_k, near_k, far_k])


def slots_of(s, t, k, g, groups, part):
    pieces = []
    tok = 4 * part
    for dk in (0, 1):
        for ds, dt, p in (
            (0, 0, 0), (0, 0, 1), (1, 0, 0), (0, 1, 1),
            (0, 1, 0), (1, 1, 0), (1, 0, 1), (1, 1, 1),
        ):
            block = ((s ^ ds) * 2 + (t ^ dt)) * groups + g
            start = block * tok + (k ^ dk) * (2 * part) + p * part
            pieces.append(start + jnp.arange(part, dtype=jnp.int32))
    return jnp.concatenate(pieces)


def scatter_sum(near_part, far_part):
    total = near_part + swap(far_part, "k").astype(f32)
    part = total.shape[0] // 8
    far = total[4 * part :].astype(bf16)
    from_t = swap(far[: 2 * part], "t").astype(f32)
    from_s = swap(far[2 * part :], "s").astype(f32)
    x0 = (total[2 * part : 3 * part] + from_t[part:]).astype(bf16)
    y1 = (total[3 * part : 4 * part] + from_s[part:]).astype(bf16)
    back_s = swap(x0, "s").astype(f32)
    back_t = swap(y1, "t").astype(f32)
    low = total[:part] + from_t[:part] + back_s
    high = total[part : 2 * part] + from_s[:part] + back_t
    return jnp.concatenate([low, high])


def split_product(left, right, contract):
    half = left.shape[0] // 2
    far = contract(left[half:], right).astype(bf16)
    near = contract(left[:half], right)
    return near, far


def rms(residual):
    return lax.rsqrt(jnp.mean(residual * residual, axis=1, keepdims=True) + EPS)


def norm_back(residual, scale, gain, grad):
    lifted = grad * gain
    inner = jnp.mean(lifted * residual, axis=1, keepdims=True)
    grad_residual = scale * lifted - residual * (scale**3 * inner)
    return grad_residual, jnp.sum(grad * residual * scale, axis=0)


def rotate(raw, gain, cosine, sine):
    scaled = raw * lax.rsqrt(jnp.mean(raw * raw, axis=2, keepdims=True) + EPS) * gain
    half = raw.shape[2] // 2
    turned = jnp.concatenate([-scaled[:, :, half:], scaled[:, :, :half]], axis=2)
    return scaled * cosine[:, None, :] + turned * sine[:, None, :]


def body(
    boundary, segment_ids, w_query, key_projection, value_projection, w_out, w_gate, w_up, w_down,
    attn_gain, mlp_gain, query_gain, key_norm_gain,
):
    s, h, t, g, y, k = (lax.axis_index(name) for name in ("s", "h", "t", "g", "y", "k"))
    groups = lax.axis_size("g")
    micro, tok, width = boundary.shape[1:]
    cols = lax.axis_size("y") * lax.axis_size("k")
    model = width * cols
    head = query_gain.shape[1]
    span = segment_ids.shape[1]
    rb = w_query.shape[1]
    q_part = w_query.shape[2] // 4
    ff_part = w_gate.shape[2] // 4
    scale_qk = head ** (-0.5)

    packed = jnp.concatenate([attn_gain[0], mlp_gain[0], query_gain[0], key_norm_gain[0]])
    packed = lax.all_gather(packed, ("s", "y", "k"), axis=0).reshape(2, cols, -1).astype(f32)
    gain_a = packed[:, :, :width].reshape(2, model)
    gain_m = packed[:, :, width : 2 * width].reshape(2, model)
    gain_q = packed[:, 0, 2 * width : 2 * width + head]
    gain_k = packed[:, 0, 2 * width + head :]

    sent = boundary[0].reshape(2, 2, 2, tok // 2, width).transpose(0, 2, 1, 3, 4)
    sent = lax.all_to_all(sent.reshape(cols, 2, tok // 2, width), ("y", "k"), 0, 0, tiled=True)
    rows = sent.transpose(1, 2, 0, 3).reshape(2, tok // 2, model)
    own_rows = take(rows, h)
    other_rows = swap(take(rows, 1 - h), "h")
    keep = jnp.where(s == h, own_rows, other_rows)
    passed = swap(jnp.where(s == h, other_rows, own_rows), "s")
    entering = jnp.where(s == 0, keep, passed).astype(f32)
    cotangent = jnp.where(s == 0, passed, keep).astype(f32)

    def across(own):
        other = swap(take(own, 1 - s), "s")
        own = take(own, s)
        return [jnp.where(s == layer, own, other) for layer in (0, 1)]

    def spread(value):
        mine = pair(t, take(value, t), swap(take(value, 1 - t), "t"))
        mine = pair(h, mine, swap(mine, "h"))
        if groups > 1:
            mine = lax.all_gather(mine, "g", axis=2)
        mine = mine.reshape((-1,) + value.shape[1:])
        return mine, swap(mine, "y")

    def spread_kv(value):
        mine = pair(h, value, swap(value, "h"))
        if groups > 1:
            mine = lax.all_gather(mine, "g", axis=1)
        mine = jnp.stack([mine, swap(mine, "y")])
        return pair(t, mine, swap(mine, "t"), 2)

    def by_columns(weight):
        return weight.reshape(rb, 2, 2, -1).transpose(1, 2, 0, 3)

    def by_rows(weight):
        return weight.reshape(2, 2, -1, rb)

    kv_home = jnp.stack(
        [key_projection[0].reshape(rb, 2, head), value_projection[0].reshape(rb, 2, head)], 2
    )
    kv_home = kv_home.transpose(1, 0, 2, 3).reshape(2, rb, 2 * head)
    q_home = by_columns(w_query[0])
    o_home = by_rows(w_out[0])
    gu_home = jnp.concatenate([by_columns(w_gate[0]), by_columns(w_up[0])], 3)
    d_home = by_rows(w_down[0])

    q_half = across(q_home)
    kv_half = across(kv_home)
    o_half = across(o_home)
    gu_half = across(gu_home)
    d_half = across(d_home)

    def columns(pieces):
        return jnp.concatenate([piece.reshape(model, -1) for piece in pieces], 1)

    def rows_of(pieces):
        return jnp.concatenate(
            [piece.transpose(1, 0, 2).reshape(piece.shape[1], model) for piece in pieces], 0
        )

    def layer_weights(layer):
        wq = spread(q_half[layer])
        wkv = spread_kv(kv_half[layer])
        if groups > 1:
            wkv = wkv.transpose(0, 1, 2, 3, 4, 5)
        wkv = wkv.reshape(2, model, 2 * head)
        w_in = jnp.concatenate(
            [
                wq[0].reshape(model, -1), wq[1].reshape(model, -1),
                wkv[0, :, :head], wkv[1, :, :head], wkv[0, :, head:], wkv[1, :, head:],
            ],
            1,
        )
        wo = rows_of(spread(o_half[layer]))
        wgu = columns(spread(gu_half[layer]))
        wd = rows_of(spread(d_half[layer]))
        return w_in, wo, wgu, wd

    weights = [layer_weights(layer) for layer in (0, 1)]

    segments = take(segment_ids, 2 * y + h)
    part = tok // 4
    slots = slots_of(s, t, k, g, groups, part)
    places = jnp.arange(span, dtype=jnp.int32)
    changed = jnp.concatenate([jnp.ones((1,), bool), segments[1:] != segments[:-1]])
    starts = lax.cummax(jnp.where(changed, places, 0), axis=0)
    offsets = (places - starts)[slots]
    my_segments = segments[slots]
    inv_freq = THETA ** (-jnp.arange(0, head, 2, dtype=f32) / head)
    angles = offsets.astype(f32)[:, None] * inv_freq[None, :]
    cosine = jnp.concatenate([jnp.cos(angles)] * 2, 1)
    sine = jnp.concatenate([jnp.sin(angles)] * 2, 1)
    valid = (my_segments[: 2 * part] >= 0).astype(f32)
    if groups > 1:
        key_slots = lax.all_gather(slots, "g", axis=0, tiled=True)
        key_segments = segments[key_slots]
    else:
        key_slots, key_segments = slots, my_segments
    allowed = (my_segments[:, None] == key_segments[None, :]) & (
        key_slots[None, :] <= slots[:, None]
    )
    q_cols = 2 * head

    def all_keys(value):
        return lax.all_gather(value, "g", axis=0, tiled=True) if groups > 1 else value

    def sum_keys(value):
        if groups > 1:
            return lax.psum_scatter(value.astype(bf16), "g", scatter_dimension=0, tiled=True).astype(f32)
        return value

    def scores_of(q, keys):
        scores = jnp.einsum("qhd,khd->hqk", q, keys, preferred_element_type=f32) * scale_qk
        return jnp.where(allowed[None], scores, -1e30)

    def heads_of(value):
        return value.reshape(value.shape[0], 2, head)

    def forward(layer, residual):
        w_in, wo, wgu, wd = weights[layer]
        scale_a = rms(residual)
        xa = gather_tokens((residual * scale_a * gain_a[layer]).astype(bf16))
        raw = dot(xa, w_in)
        q_raw, k_raw = heads_of(raw[:, :q_cols]), heads_of(raw[:, q_cols : 2 * q_cols])
        v = heads_of(raw[:, 2 * q_cols :]).astype(bf16)
        q = rotate(q_raw, gain_q[layer], cosine, sine).astype(bf16)
        keys = rotate(k_raw, gain_k[layer], cosine, sine).astype(bf16)
        keys, values = all_keys(keys), all_keys(v)
        scores = scores_of(q, keys)
        peak = jnp.max(scores, axis=2, keepdims=True)
        exps = jnp.exp(scores - peak)
        denom = jnp.sum(exps, axis=2, keepdims=True)
        mixing = (exps / denom).astype(bf16)
        lse = peak + jnp.log(denom)
        o = jnp.einsum("hqk,khd->qhd", mixing, values, preferred_element_type=f32)
        o = o.astype(bf16).reshape(-1, q_cols)
        middle = residual + scatter_sum(*split_product(o, wo, dot))
        scale_m = rms(middle)
        xm = gather_tokens((middle * scale_m * gain_m[layer]).astype(bf16))
        gu = dot(xm, wgu).reshape(xm.shape[0], 2, 2, ff_part)
        gate, up = gu[:, :, 0], gu[:, :, 1]
        act = (gate * jax.nn.sigmoid(gate) * up).astype(bf16).reshape(-1, 2 * ff_part)
        result = middle + scatter_sum(*split_product(act, wd, dot))
        kept = (residual, scale_a, xa, q_raw, k_raw, q, keys, values, lse, o, middle, scale_m, xm, gate, up, act)
        return result, kept

    def reduce_blocks(own, other, axis):
        def blocks(value):
            shape = value.shape[:axis] + (2, 2, groups, rb) + value.shape[axis + 1 :]
            return jnp.moveaxis(value.reshape(shape), (axis, axis + 1, axis + 2), (0, 1, 2))

        total = blocks(own + swap(other.astype(bf16), "y").astype(f32))
        if groups > 1:
            total = lax.psum_scatter(total.astype(bf16), "g", scatter_dimension=2, tiled=True).astype(f32)
        total = total[:, :, 0]
        return take(total, h) + swap(take(total, 1 - h).astype(bf16), "h").astype(f32)

    def back(own, other, axis):
        total = reduce_blocks(own, other, axis).astype(bf16)
        return pair(t, take(total, t), swap(take(total, 1 - t), "t"))

    def back_kv(own, other):
        def blocks(value):
            return value.reshape(2, 2, groups, rb, -1)

        total = jnp.stack([blocks(own), blocks(other)])
        total = take(total, t, 2) + swap(take(total, 1 - t, 2).astype(bf16), "t").astype(f32)
        total = total[0] + swap(total[1].astype(bf16), "y").astype(f32)
        if groups > 1:
            total = lax.psum_scatter(total.astype(bf16), "g", scatter_dimension=1, tiled=True).astype(f32)
        total = total[:, 0]
        total = take(total, h) + swap(take(total, 1 - h).astype(bf16), "h").astype(f32)
        return total.astype(bf16)

    def backward(layer, grad_top, kept):
        w_in, wo, wgu, wd = weights[layer]
        (residual, scale_a, xa, q_raw, k_raw, q, keys, values, lse, o, middle, scale_m, xm, gate, up, act) = kept
        g3 = gather_tokens(grad_top.astype(bf16))
        d_down = t_dot(act, g3)
        d_act = dot_t(g3, wd).reshape(-1, 2, ff_part)
        sig = jax.nn.sigmoid(gate)
        d_gate = (d_act * up * sig * (1 + gate * (1 - sig))).astype(bf16)
        d_up = (d_act * gate * sig).astype(bf16)
        d_gu = jnp.stack([d_gate, d_up], 2).reshape(-1, 4 * ff_part)
        d_xm = scatter_sum(*split_product(d_gu, wgu, dot_t))
        grad_gu = t_dot(xm, d_gu)
        half = 2 * ff_part
        home_down = back(d_down[:ff_part], d_down[ff_part:], 1)
        home_gu = back(grad_gu[:, :half], grad_gu[:, half:], 0)
        d_mid, d_gain_m = norm_back(middle, scale_m, gain_m[layer], d_xm)
        d_mid = grad_top + d_mid
        g2 = gather_tokens(d_mid.astype(bf16))
        d_out = t_dot(o, g2)
        home_out = back(d_out[:q_part], d_out[q_part:], 1)
        d_o = heads_of(dot_t(g2, wo).astype(bf16))
        mixing = jnp.exp(scores_of(q, keys) - lse)
        d_mix = jnp.einsum("qhd,khd->hqk", d_o, values, preferred_element_type=f32)
        inner = jnp.sum(mixing * d_mix, axis=2, keepdims=True)
        d_scores = (mixing * (d_mix - inner)).astype(bf16)
        d_q = jnp.einsum("hqk,khd->qhd", d_scores, keys, preferred_element_type=f32) * scale_qk
        d_k = jnp.einsum("hqk,qhd->khd", d_scores, q, preferred_element_type=f32) * scale_qk
        d_v = jnp.einsum("hqk,qhd->khd", mixing.astype(bf16), d_o, preferred_element_type=f32)
        d_k, d_v = sum_keys(d_k), sum_keys(d_v)
        _, pull_q = jax.vjp(lambda raw, gain: rotate(raw, gain, cosine, sine), q_raw, gain_q[layer])
        _, pull_k = jax.vjp(lambda raw, gain: rotate(raw, gain, cosine, sine), k_raw, gain_k[layer])
        d_q_raw, d_gain_q = pull_q(d_q)
        d_k_raw, d_gain_k = pull_k(d_k)
        d_raw = jnp.concatenate(
            [value.astype(bf16).reshape(-1, q_cols) for value in (d_q_raw, d_k_raw, d_v)], 1
        )
        d_xa = scatter_sum(*split_product(d_raw, w_in, dot_t))
        grad_in = t_dot(xa, d_raw)
        home_q = back(grad_in[:, :head], grad_in[:, head:q_cols], 0)
        grad_k0, grad_k1 = grad_in[:, 2 * head : 3 * head], grad_in[:, 3 * head : 4 * head]
        grad_v0, grad_v1 = grad_in[:, 4 * head : 5 * head], grad_in[:, 5 * head :]
        home_kv = back_kv(
            jnp.concatenate([grad_k0, grad_v0], 1), jnp.concatenate([grad_k1, grad_v1], 1)
        )
        d_res, d_gain_a = norm_back(residual, scale_a, gain_a[layer], d_xa)
        homes = (home_q, home_kv, home_out, home_gu, home_down)
        return d_mid + d_res, homes, (d_gain_a, d_gain_m, d_gain_q, d_gain_k)

    middle, kept0 = forward(0, entering)
    output, kept1 = forward(1, middle.astype(bf16).astype(f32))
    grad, homes1, gains1 = backward(1, cotangent * valid[:, None], kept1)
    grad, homes0, gains0 = backward(0, grad.astype(bf16).astype(f32), kept0)

    def home(index):
        low, high = homes0[index], homes1[index]
        mine = jnp.where(s == 0, low, high)
        other = swap(jnp.where(s == 0, high, low), "s")
        return pair(s, mine, other)

    full_q = home(0).transpose(2, 0, 1, 3).reshape(rb, -1)
    full_kv = home(1).reshape(2, rb, 2, head).transpose(2, 1, 0, 3).reshape(2, rb, -1)
    full_out = home(2).reshape(-1, rb)
    full_gu = home(3).reshape(2, 2, rb, 2, ff_part).transpose(3, 2, 0, 1, 4).reshape(2, rb, -1)
    full_down = home(4).reshape(-1, rb)

    low, high = grad.astype(bf16), output.astype(bf16)
    keep = jnp.where(s == 0, low, high)
    passed = swap(jnp.where(s == 0, high, low), "s")
    mine = jnp.where(s == h, keep, passed)
    other = swap(jnp.where(s == h, passed, keep), "h")
    rows = pair(h, mine, other).reshape(2, tok // 2, cols, width).transpose(2, 0, 1, 3)
    rows = lax.all_to_all(rows, ("y", "k"), 0, 0, tiled=True)
    rows = rows.reshape(2, 2, 2, tok // 2, width).transpose(0, 2, 1, 3, 4)
    section_out = rows.reshape(micro, tok, width)

    sums = jnp.concatenate([value for gains in (gains0, gains1) for value in gains])
    sums = take(lax.psum(sums, ("s", "h", "t", "g", "y", "k")).reshape(2, -1), s)
    return (
        section_out.astype(f32)[None],
        full_q.astype(f32)[None],
        full_kv[0].astype(f32)[None],
        full_kv[1].astype(f32)[None],
        full_out.astype(f32)[None],
        full_gu[0].astype(f32)[None],
        full_gu[1].astype(f32)[None],
        full_down.astype(f32)[None],
        sums[None, :model],
        sums[None, model : 2 * model],
        sums[None, 2 * model : 2 * model + head],
        sums[None, 2 * model + head :],
    )


def solution(mesh):
    sections, row_count, col_count = (mesh.shape[name] for name in ("section", "row", "col"))
    shape = (sections, 2, 2, row_count // 4, 2, col_count // 2)
    mesh = Mesh(np.asarray(mesh.devices).reshape(shape), ("s", "h", "t", "g", "y", "k"))
    row, col = ("h", "t", "g"), ("y", "k")
    in_row, in_col = P("s", row, col), P("s", col, row)
    return jax.shard_map(
        body,
        mesh=mesh,
        in_specs=(
            P("s", None, row, col), P(), in_row, in_row, in_row, in_col, in_row, in_row, in_col,
            P("s", col), P("s", col), P("s", None), P("s", None),
        ),
        out_specs=(
            P("s", None, row, col), in_row, in_row, in_row, in_col, in_row, in_row, in_col,
            P("s", None), P("s", None), P("s", None), P("s", None),
        ),
        check_vma=False,
    )
```

time: 2390 us -> 1520 us (0.64)
  waiting for transfers between devices: 1160 us -> 721 us
  blocking collectives: 449 us -> 97.4 us
  matrix products: 373 us -> 113 us
  starting transfers between devices: 22.9 us -> 172 us
  local copies, waits for them, and re-layouts: 103 us -> 237 us
  other arithmetic: 247 us -> 161 us
    ppermute x8 -> x170, waiting for transfers between devices: 21.1 us -> 716 us  [swap(): return lax.ppermute(value, axis, [(0, 1), (1, 0)])]
    reduce_scatter x32 -> x0, waiting for transfers between devices: 667 us -> none  [the longest x20 332 us: narrow(): lax.psum_scatter(partial_value, 'col', scatter_dimension=1, tiled=True)]
    all_gather x7 -> x0, waiting for transfers between devices: 406 us -> none  [the longest x1 111 us: body(): lax.all_gather(w_up[0], 'row', axis=0, tiled=True)]
    dot_general x140 -> x43, matrix products: 373 us -> 109 us  [the longest x12 42.4 us: dot(): return jnp.dot(left, right, preferred_element_type=f32)]
    all_gather x30 -> x1, blocking collectives: 294 us -> 51.8 us  [body(): lax.all_gather(packed, ('s', 'y', 'k'), axis=0).reshape(2, cols, -1)]
    ppermute x8 -> x170, starting transfers between devices: 19.6 us -> 164 us  [swap(): return lax.ppermute(value, axis, [(0, 1), (1, 0)])]
    psum x16 -> x1, blocking collectives: 155 us -> 45.6 us  [body(): lax.psum(sums, ('s', 'h', 't', 'g', 'y', 'k')).reshape(2, -1)]
    unnamed x567 -> x605, local copies, waits for them, and re-layouts: 26.7 us -> 99.3 us
  transfers between devices with their start and end apart: 52 -> 172, of which waited for: 41 -> 87; matrix products, arithmetic and copies ran while one was open for 17% -> 28% of each run, Pallas kernels for 0% -> 0%
where the time goes in v1:
time: 1520 us; the launch traced here: 1510 us
  waiting for transfers between devices  721 us (47%)
  local copies, waits for them, and re-layouts  237 us (16%)
  starting transfers between devices  172 us (11%)
  other arithmetic  161 us (11%)
  matrix products  113 us (7%)
  blocking collectives  97.4 us (6%)
    ppermute x170, waiting for transfers between devices, swap(): return lax.ppermute(value, axis, [(0, 1), (1, 0)])  716 us
    ppermute x170, starting transfers between devices, swap(): return lax.ppermute(value, axis, [(0, 1), (1, 0)])  164 us
    unnamed x605, local copies, waits for them, and re-layouts  99.3 us
    all_gather x1, blocking collectives, body(): lax.all_gather(packed, ('s', 'y', 'k'), axis=0).reshape(2, cols, -1)  51.8 us
    psum x1, blocking collectives, body(): lax.psum(sums, ('s', 'h', 't', 'g', 'y', 'k')).reshape(2, -1)  45.6 us
    dot_general x12, matrix products, dot(): return jnp.dot(left, right, preferred_element_type=f32)  42.4 us
    another operation x51, other arithmetic, pair(): return jnp.stack([low, high], axis)  38.3 us
    dot_general x11, matrix products, dot_t(): lax.dot_general(left, right, (((1,), (1,)), ((), ())), preferred_element_...  37.6 us
  transfers between devices with their start and end apart: 172, of which 87 were waited for; matrix products, arithmetic and copies ran while one was open for 28% of the time, Pallas kernels for 0%

profile of v1, /device:TPU:0, one launch (start us, length us, event | category | flops | bytes accessed | tf_op | source)
XLA Modules:
  0.0 1507.4 jit_solution(12105729584198697750)
XLA Ops:
  27.8 51.8 %all-gather.1 = bf16[8,1,1280]{2,1,0:T(2,128)(2,1)S(1)} all-gather(bf16[1,1,1280]{2,1,0:T(2,128)(2,1)S(1)} %reshape.1148), channel_id=2, replica_groups=mesh['s'=2,'h'=2,'t'=2,'g'=1,'y'=2,'k'=2] {'s','y','k'}, dimensions={0}, use_global_device_ids=true | all-gather | bytes 23040 | tf_op jit(solution)/shard_map/all_gather | solution.py:124
  104.9 4.9 collective-permute-done.53
  112.3 5.3 collective-permute-done.10
  120.9 5.8 collective-permute-done.18
  128.3 3.9 collective-permute-done.59
  143.0 15.6 %collective-permute-done.54 = bf16[2,512,128]{1,2,0:T(8,128)(2,1)} collective-permute-done((bf16[2,512,128]{1,2,0:T(8,128)(2,1)}, bf16[2,512,128]{1,2,0:T(8,128)(2,1)}, u32[]{:S(2)}, u32[]{:S(2)}) %collective-permute-start.54) | collective-permute-done | bytes 262176 | tf_op jit(solution)/shard_map/ppermute | solution.py:15
  159.6 10.1 collective-permute-done.11
  181.7 5.0 collective-permute-done.60
  263.0 4.3 collective-permute-done.69
  274.2 17.9 %collective-permute-done.16 = bf16[2,2,512,256]{3,2,1,0:T(8,128)(2,1)S(1)} collective-permute-done((bf16[2,2,512,256]{3,2,1,0:T(8,128)(2,1)S(1)}, bf16[2,2,512,256]{3,2,1,0:T(8,128)(2,1)S(1)}, u32[]{:S(2)}, u32[]{:S(2)}) %collective-permute-start.16) | collective-permute-done | bytes 1048608 | tf_op jit(solution)/shard_map/ppermute | solution.py:15
  299.5 4.6 fusion.307
  325.3 20.9 %collective-permute-done.39 = bf16[2,384,512]{2,1,0:T(8,128)(2,1)} collective-permute-done((bf16[2,384,512]{2,1,0:T(8,128)(2,1)}, bf16[2,384,512]{2,1,0:T(8,128)(2,1)}, u32[]{:S(2)}, u32[]{:S(2)}) %collective-permute-start.39) | collective-permute-done | bytes 786464 | tf_op jit(solution)/shard_map/ppermute | solution.py:15
  350.3 19.2 %collective-permute-done.34 = bf16[512,768]{1,0:T(8,128)(2,1)S(1)} collective-permute-done((bf16[512,768]{1,0:T(8,128)(2,1)S(1)}, bf16[512,768]{1,0:T(8,128)(2,1)S(1)}, u32[]{:S(2)}, u32[]{:S(2)}) %collective-permute-start.34) | collective-permute-done | bytes 786464 | tf_op jit(solution)/shard_map/ppermute | solution.py:15
  370.6 4.2 collective-permute-done.22
  381.7 32.1 %collective-permute-done.25 = bf16[32,2048]{1,0:T(8,128)(2,1)S(1)} collective-permute-done((bf16[32,2048]{1,0:T(8,128)(2,1)S(1)}, bf16[32,2048]{1,0:T(8,128)(2,1)S(1)}, u32[]{:S(2)}, u32[]{:S(2)}) %collective-permute-start.25) | collective-permute-done | bytes 131104 | tf_op jit(solution)/shard_map/ppermute | solution.py:15
  414.1 32.2 %collective-permute-done.35 = bf16[2,512,768]{2,1,0:T(8,128)(2,1)S(1)} collective-permute-done((bf16[2,512,768]{2,1,0:T(8,128)(2,1)S(1)}, bf16[2,512,768]{2,1,0:T(8,128)(2,1)S(1)}, u32[]{:S(2)}, u32[]{:S(2)}) %collective-permute-start.35) | collective-permute-done | bytes 1572896 | tf_op jit(solution)/shard_map/ppermute | solution.py:15
  459.0 4.0 collective-permute-done.28
  469.9 47.8 %collective-permute-done.36 = bf16[4,512,768]{2,1,0:T(8,128)(2,1)} collective-permute-done((bf16[4,512,768]{2,1,0:T(8,128)(2,1)}, bf16[4,512,768]{2,1,0:T(8,128)(2,1)}, u32[]{:S(2)}, u32[]{:S(2)}) %collective-permute-start.36) | collective-permute-done | bytes 3145760 | tf_op jit(solution)/shard_map/ppermute | solution.py:15
  519.0 8.5 fusion.17
  531.3 4.1 fusion.268
  543.8 8.5 collective-permute-done.40
  552.3 4.0 convolution_convert_fusion.7
  568.8 5.4 collective-permute-done.42
  593.9 5.2 collective-permute-done.48
  622.7 14.3 collective-permute-done.76
  637.0 5.4 fusion.56
  656.6 32.7 %collective-permute-done.85 = bf16[2,512,768]{2,1,0:T(8,128)(2,1)} collective-permute-done((bf16[2,512,768]{2,1,0:T(8,128)(2,1)}, bf16[2,512,768]{2,1,0:T(8,128)(2,1)}, u32[]{:S(2)}, u32[]{:S(2)}) %collective-permute-start.85) | collective-permute-done | bytes 1572896 | tf_op jit(solution)/shard_map/ppermute | solution.py:15
  715.0 4.7 collective-permute-done.79
  722.0 43.5 %collective-permute-done.86 = bf16[4,512,768]{2,1,0:T(8,128)(2,1)S(1)} collective-permute-done((bf16[4,512,768]{2,1,0:T(8,128)(2,1)S(1)}, bf16[4,512,768]{2,1,0:T(8,128)(2,1)S(1)}, u32[]{:S(2)}, u32[]{:S(2)}) %collective-permute-start.86) | collective-permute-done | bytes 3145760 | tf_op jit(solution)/shard_map/ppermute | solution.py:15
  767.2 5.1 fusion.16
  772.3 5.2 reshape.1100
  777.5 7.3 fusion.267
  784.8 4.8 copy.854
  789.6 4.8 copy.855
  824.3 7.4 fusion.302
  849.2 4.1 collective-permute-done.89
  864.7 4.0 slice_add_fusion.2
  868.7 5.6 reshape.1117
  876.5 4.0 collective-permute-start.167
  886.5 16.6 %collective-permute-done.94 = bf16[64,2048]{1,0:T(8,128)(2,1)S(1)} collective-permute-done((bf16[64,2048]{1,0:T(8,128)(2,1)S(1)}, bf16[64,2048]{1,0:T(8,128)(2,1)S(1)}, u32[]{:S(2)}, u32[]{:S(2)}) %collective-permute-start.94) | collective-permute-done | bytes 262176 | tf_op jit(solution)/shard_map/ppermute | solution.py:15
  904.8 10.2 collective-permute-done.167
  936.3 6.3 collective-permute-done.152
  947.6 6.0 collective-permute-done.138
  977.5 52.3 %collective-permute-done.100 = bf16[64,2048]{1,0:T(8,128)(2,1)S(1)} collective-permute-done((bf16[64,2048]{1,0:T(8,128)(2,1)S(1)}, bf16[64,2048]{1,0:T(8,128)(2,1)S(1)}, u32[]{:S(2)}, u32[]{:S(2)}) %collective-permute-start.100) | collective-permute-done | bytes 262176 | tf_op jit(solution)/shard_map/ppermute | solution.py:15
  1042.4 4.6 collective-permute-done.140
  1060.0 6.4 collective-permute-done.106
  1074.1 4.8 convolution_convert_fusion
  1086.0 4.2 fusion.304
  1096.7 17.9 %collective-permute-done.112 = bf16[64,2048]{1,0:T(8,128)(2,1)S(1)} collective-permute-done((bf16[64,2048]{1,0:T(8,128)(2,1)S(1)}, bf16[64,2048]{1,0:T(8,128)(2,1)S(1)}, u32[]{:S(2)}, u32[]{:S(2)}) %collective-permute-start.112) | collective-permute-done | bytes 262176 | tf_op jit(solution)/shard_map/ppermute | solution.py:15
  1133.9 6.0 reshape.1116
  1155.6 31.6 %collective-permute-done.164 = bf16[2,384,512]{2,1,0:T(8,128)(2,1)S(1)} collective-permute-done((bf16[2,384,512]{2,1,0:T(8,128)(2,1)S(1)}, bf16[2,384,512]{2,1,0:T(8,128)(2,1)S(1)}, u32[]{:S(2)}, u32[]{:S(2)}) %collective-permute-start.164) | collective-permute-done | bytes 786464 | tf_op jit(solution)/shard_map/ppermute | solution.py:15
  1208.8 6.6 collective-permute-done.149
  1220.9 3.9 collective-permute-done.135
  1245.1 14.8 collective-permute-done.136
  1259.9 4.5 collective-permute-start.151
  1287.3 26.3 %collective-permute-done.124 = bf16[64,2048]{1,0:T(8,128)(2,1)S(1)} collective-permute-done((bf16[64,2048]{1,0:T(8,128)(2,1)S(1)}, bf16[64,2048]{1,0:T(8,128)(2,1)S(1)}, u32[]{:S(2)}, u32[]{:S(2)}) %collective-permute-start.124) | collective-permute-done | bytes 262176 | tf_op jit(solution)/shard_map/ppermute | solution.py:15
  1315.8 5.9 collective-permute-done.126
  1330.1 16.7 %collective-permute-done.127 = bf16[32,2048]{1,0:T(8,128)(2,1)} collective-permute-done((bf16[32,2048]{1,0:T(8,128)(2,1)}, bf16[32,2048]{1,0:T(8,128)(2,1)}, u32[]{:S(2)}, u32[]{:S(2)}) %collective-permute-start.127) | collective-permute-done | bytes 131104 | tf_op jit(solution)/shard_map/ppermute | solution.py:15
  1356.8 45.6 %psum.7 = f32[2,4352]{1,0:T(2,128)S(1)} all-reduce(f32[2,4352]{1,0:T(2,128)S(1)} %reshape.1118), channel_id=1, replica_groups=mesh['s'=2,'h'=2,'t'=2,'g'=1,'y'=2,'k'=2] {'s','h','t','g','y','k'}, use_global_device_ids=true, to_apply=%region_32.33 | all-reduce | flops 8704 | bytes 69632 | tf_op jit(solution)/shard_map/psum | solution.py:379
  1410.5 5.6 collective-permute-done.134
  1416.7 19.4 %collective-permute-done.158 = bf16[512,768]{1,0:T(8,128)(2,1)} collective-permute-done((bf16[512,768]{1,0:T(8,128)(2,1)S(1)}, bf16[512,768]{1,0:T(8,128)(2,1)}, u32[]{:S(2)}, u32[]{:S(2)}) %collective-permute-start.158) | collective-permute-done | bytes 786464 | tf_op jit(solution)/shard_map/ppermute | solution.py:15
  1441.2 4.3 all-to-all-start.1
  1449.8 4.7 all-to-all-done.1
  1456.7 22.9 %collective-permute-done.148 = bf16[512,256]{1,0:T(8,128)(2,1)} collective-permute-done((bf16[512,256]{1,0:T(8,128)(2,1)}, bf16[512,256]{1,0:T(8,128)(2,1)}, u32[]{:S(2)}, u32[]{:S(2)}) %collective-permute-start.148) | collective-permute-done | bytes 262176 | tf_op jit(solution)/shard_map/ppermute | solution.py:15
  (1355 shorter events, 675.1 us)
Async XLA Ops:
  3.9 91.8 %collective-permute-start.13 = (bf16[512,256]{1,0:T(8,128)(2,1)}, bf16[512,256]{1,0:T(8,128)(2,1)}, u32[]{:S(2)}, u32[]{:S(2)}) collective-permute-start(bf16[512,256]{1,0:T(8,128)(2,1)} %bitcast.48), channel_id=1, source_target_pairs={{0,16},{16,0},{1,17},{17,1},{2,18},{18,2},{3,19},{19,3},{4,20},{20... | collective-permute-start | bytes 786440 | tf_op jit(solution)/shard_map/ppermute | solution.py:15
  7.8 92.2 %collective-permute-start.9 = (bf16[2,512,128]{1,2,0:T(8,128)(2,1)}, bf16[2,512,128]{1,2,0:T(8,128)(2,1)}, u32[]{:S(2)}, u32[]{:S(2)}) collective-permute-start(bf16[2,512,128]{1,2,0:T(8,128)(2,1)} %dynamic-slice_bitcast_fusion.10), channel_id=1, source_target_pairs={{0,16},{16,0},{1,17},{17,1},{2,18},{18,2},{3,19},{19,3},{4,20},{20... | collective-permute-start | bytes 786440 | tf_op jit(solution)/shard_map/ppermute | solution.py:15
  16.5 305.7 %collective-permute-start.33 = (bf16[2,512,768]{2,1,0:T(8,128)(2,1)}, bf16[2,512,768]{2,1,0:T(8,128)(2,1)}, u32[]{:S(2)}, u32[]{:S(2)}) collective-permute-start(bf16[2,512,768]{2,1,0:T(8,128)(2,1)} %bitcast.86), channel_id=1, source_target_pairs={{0,16},{16,0},{1,17},{17,1},{2,18},{18,2},{3,19},{19,3},{4,20},{20... | collective-permute-start | bytes 4718600 | tf_op jit(solution)/shard_map/ppermute | solution.py:15
  20.5 114.7 %all-to-all-start = ((bf16[4,2,64,512]{3,2,1,0:T(8,128)(2,1)}), bf16[4,2,64,512]{3,2,1,0:T(8,128)(2,1)S(1)}, u32[]{:S(2)}, u32[]{:S(2)}) async-start(bf16[4,2,64,512]{3,2,1,0:T(8,128)(2,1)} %bitcast.2), calls=%async_computation | async-start | bytes 1048576 | tf_op jit(solution)/shard_map/all_to_all | solution.py:131
  24.8 78.0 %collective-permute-start.17 = (bf16[2,128,512]{2,1,0:T(8,128)(2,1)}, bf16[2,128,512]{2,1,0:T(8,128)(2,1)S(1)}, u32[]{:S(2)}, u32[]{:S(2)}) collective-permute-start(bf16[2,128,512]{2,1,0:T(8,128)(2,1)} %dynamic-slice_bitcast_fusion.9), channel_id=1, source_target_pairs={{0,16},{16,0},{1,17},{17,1},{2,18},{18,2},{3,19},{19,3},{4,20},{20... | collective-permute-start | bytes 786440 | tf_op jit(solution)/shard_map/ppermute | solution.py:15
  25.8 173.9 %collective-permute-start.37 = (bf16[2,384,512]{2,1,0:T(8,128)(2,1)}, bf16[2,384,512]{2,1,0:T(8,128)(2,1)}, u32[]{:S(2)}, u32[]{:S(2)}) collective-permute-start(bf16[2,384,512]{2,1,0:T(8,128)(2,1)} %dynamic-slice_bitcast_fusion.3), channel_id=1, source_target_pairs={{0,16},{16,0},{1,17},{17,1},{2,18},{18,2},{3,19},{19,3},{4,20},{20... | collective-permute-start | bytes 2359304 | tf_op jit(solution)/shard_map/ppermute | solution.py:15
  97.4 38.6 %collective-permute-start.56 = (bf16[512,256]{1,0:T(8,128)(2,1)}, bf16[512,256]{1,0:T(8,128)(2,1)}, u32[]{:S(2)}, u32[]{:S(2)}) collective-permute-start(bf16[512,256]{1,0:T(8,128)(2,1)} %get-tuple-element.286), channel_id=1, source_target_pairs={{0,8},{8,0},{1,9},{9,1},{2,10},{10,2},{3,11},{11,3},{4,12},{12,4},... | collective-permute-start | bytes 786440 | tf_op jit(solution)/shard_map/ppermute | solution.py:15
  103.4 34.3 %collective-permute-start.14 = (bf16[512,256]{1,0:T(8,128)(2,1)}, bf16[512,256]{1,0:T(8,128)(2,1)S(1)}, u32[]{:S(2)}, u32[]{:S(2)}) collective-permute-start(bf16[512,256]{1,0:T(8,128)(2,1)} %get-tuple-element.287), channel_id=1, source_target_pairs={{0,8},{8,0},{1,9},{9,1},{2,10},{10,2},{3,11},{11,3},{4,12},{12,4},... | collective-permute-start | bytes 786440 | tf_op jit(solution)/shard_map/ppermute | solution.py:15
  136.0 33.7 %collective-permute-start.11 = (bf16[2,512,128]{1,2,0:T(8,128)(2,1)}, bf16[2,512,128]{1,2,0:T(8,128)(2,1)S(1)}, u32[]{:S(2)}, u32[]{:S(2)}) collective-permute-start(bf16[2,512,128]{1,2,0:T(8,128)(2,1)} %pad_maximum_fusion.86), channel_id=1, source_target_pairs={{0,8},{8,0},{1,9},{9,1},{2,10},{10,2},{3,11},{11,3},{4,12},{12,4},... | collective-permute-start | bytes 786440 | tf_op jit(solution)/shard_map/ppermute | solution.py:15
  137.8 37.6 %collective-permute-start.19 = (bf16[2,128,512]{2,1,0:T(8,128)(2,1)}, bf16[2,128,512]{2,1,0:T(8,128)(2,1)S(1)}, u32[]{:S(2)}, u32[]{:S(2)}) collective-permute-start(bf16[2,128,512]{2,1,0:T(8,128)(2,1)} %pad_maximum_fusion.89), channel_id=1, source_target_pairs={{0,8},{8,0},{1,9},{9,1},{2,10},{10,2},{3,11},{11,3},{4,12},{12,4},... | collective-permute-start | bytes 786440 | tf_op jit(solution)/shard_map/ppermute | solution.py:15
  158.6 28.1 %collective-permute-start.60 = (bf16[2,128,512]{2,1,0:T(8,128)(2,1)}, bf16[2,128,512]{2,1,0:T(8,128)(2,1)}, u32[]{:S(2)}, u32[]{:S(2)}) collective-permute-start(bf16[2,128,512]{2,1,0:T(8,128)(2,1)} %pad_maximum_fusion.93), channel_id=1, source_target_pairs={{0,8},{8,0},{1,9},{9,1},{2,10},{10,2},{3,11},{11,3},{4,12},{12,4},... | collective-permute-start | bytes 786440 | tf_op jit(solution)/shard_map/ppermute | solution.py:15
  169.8 28.4 %collective-permute-start = (bf16[64,2048]{1,0:T(8,128)(2,1)}, bf16[64,2048]{1,0:T(8,128)(2,1)}, u32[]{:S(2)}, u32[]{:S(2)}) collective-permute-start(bf16[64,2048]{1,0:T(8,128)(2,1)} %dynamic-slice_bitcast_fusion.11), channel_id=1, source_target_pairs={{0,8},{8,0},{1,9},{9,1},{2,10},{10,2},{3,11},{11,3},{4,12},{12,4},... | collective-permute-start | bytes 786440 | tf_op jit(solution)/shard_map/ppermute | solution.py:15
  175.4 51.0 %collective-permute-start.57 = (bf16[2,512,256]{2,1,0:T(8,128)(2,1)}, bf16[2,512,256]{2,1,0:T(8,128)(2,1)}, u32[]{:S(2)}, u32[]{:S(2)}) collective-permute-start(bf16[2,512,256]{2,1,0:T(8,128)(2,1)} %get-tuple-element.283), channel_id=1, source_target_pairs={{0,2},{2,0},{1,3},{3,1},{4,6},{6,4},{5,7},{7,5},{8,10},{10,8},{9,1... | collective-permute-start | bytes 1572872 | tf_op jit(solution)/shard_map/ppermute | solution.py:15
  186.7 47.1 %collective-permute-start.15 = (bf16[2,512,256]{2,1,0:T(8,128)(2,1)}, bf16[2,512,256]{2,1,0:T(8,128)(2,1)}, u32[]{:S(2)}, u32[]{:S(2)}) collective-permute-start(bf16[2,512,256]{2,1,0:T(8,128)(2,1)} %get-tuple-element.299), channel_id=1, source_target_pairs={{0,2},{2,0},{1,3},{3,1},{4,6},{6,4},{5,7},{7,5},{8,10},{10,8},{9,1... | collective-permute-start | bytes 1572872 | tf_op jit(solution)/shard_map/ppermute | solution.py:15
  198.2 41.0 %collective-permute-start.55 = (bf16[4,512,128]{1,2,0:T(8,128)(2,1)}, bf16[4,512,128]{1,2,0:T(8,128)(2,1)S(1)}, u32[]{:S(2)}, u32[]{:S(2)}) collective-permute-start(bf16[4,512,128]{1,2,0:T(8,128)(2,1)} %bitcast.924), channel_id=1, source_target_pairs={{0,2},{2,0},{1,3},{3,1},{4,6},{6,4},{5,7},{7,5},{8,10},{10,8},{9,1... | collective-permute-start | bytes 1572872 | tf_op jit(solution)/shard_map/ppermute | solution.py:15
  232.7 86.0 %collective-permute-start.20 = (bf16[4,128,512]{1,2,0:T(8,128)(2,1)}, bf16[4,128,512]{1,2,0:T(8,128)(2,1)}, u32[]{:S(2)}, u32[]{:S(2)}) collective-permute-start(bf16[4,128,512]{1,2,0:T(8,128)(2,1)} %bitcast.75), channel_id=1, source_target_pairs={{0,2},{2,0},{1,3},{3,1},{4,6},{6,4},{5,7},{7,5},{8,10},{10,8},{9,1... | collective-permute-start | bytes 1572872 | tf_op jit(solution)/shard_map/ppermute | solution.py:15
  269.9 342.7 %collective-permute-start.61 = (bf16[4,128,512]{1,2,0:T(8,128)(2,1)}, bf16[4,128,512]{1,2,0:T(8,128)(2,1)}, u32[]{:S(2)}, u32[]{:S(2)}) collective-permute-start(bf16[4,128,512]{1,2,0:T(8,128)(2,1)} %bitcast.147), channel_id=1, source_target_pairs={{0,2},{2,0},{1,3},{3,1},{4,6},{6,4},{5,7},{7,5},{8,10},{10,8},{9,1... | collective-permute-start | bytes 1572872 | tf_op jit(solution)/shard_map/ppermute | solution.py:15
  273.1 47.4 %collective-permute-start.72 = (bf16[64,2048]{1,0:T(8,128)(2,1)}, bf16[64,2048]{1,0:T(8,128)(2,1)}, u32[]{:S(2)}, u32[]{:S(2)}) collective-permute-start(bf16[64,2048]{1,0:T(8,128)(2,1)} %get-tuple-element.369), channel_id=1, source_target_pairs={{0,1},{1,0},{2,3},{3,2},{4,5},{5,4},{6,7},{7,6},{8,9},{9,8},{10,11... | collective-permute-start | bytes 786440 | tf_op jit(solution)/shard_map/ppermute | solution.py:15
  292.0 54.1 %collective-permute-start.39 = (bf16[2,384,512]{2,1,0:T(8,128)(2,1)}, bf16[2,384,512]{2,1,0:T(8,128)(2,1)}, u32[]{:S(2)}, u32[]{:S(2)}) collective-permute-start(bf16[2,384,512]{2,1,0:T(8,128)(2,1)} %pad_maximum_fusion.37), channel_id=1, source_target_pairs={{0,8},{8,0},{1,9},{9,1},{2,10},{10,2},{3,11},{11,3},{4,12},{12,4},... | collective-permute-start | bytes 2359304 | tf_op jit(solution)/shard_map/ppermute | solution.py:15
  318.7 61.7 %collective-permute-start.75 = (bf16[2,384,512]{2,1,0:T(8,128)(2,1)S(1)}, bf16[2,384,512]{2,1,0:T(8,128)(2,1)S(1)}, u32[]{:S(2)}, u32[]{:S(2)}) collective-permute-start(bf16[2,384,512]{2,1,0:T(8,128)(2,1)S(1)} %copy-done.163), channel_id=1, source_target_pairs={{0,8},{8,0},{1,9},{9,1},{2,10},{10,2},{3,11},{11,3},{4,12},{12,4},... | collective-permute-start | bytes 2359304 | tf_op jit(solution)/shard_map/ppermute | solution.py:15
  320.5 27.0 %collective-permute-start.21 = (bf16[256,2048]{1,0:T(8,128)(2,1)S(1)}, bf16[256,2048]{1,0:T(8,128)(2,1)S(1)}, u32[]{:S(2)}, u32[]{:S(2)}) collective-permute-start(bf16[256,2048]{1,0:T(8,128)(2,1)S(1)} %convolution_convert_fusion.3), channel_id=1, source_target_pairs={{0,1},{1,0},{2,3},{3,2},{4,5},{5,4},{6,7},{7,6},{8,9},{9,8},{10,11... | collective-permute-start | bytes 3145736 | tf_op jit(solution)/shard_map/ppermute | solution.py:15
  324.0 45.6 %collective-permute-start.34 = (bf16[512,768]{1,0:T(8,128)(2,1)S(1)}, bf16[512,768]{1,0:T(8,128)(2,1)S(1)}, u32[]{:S(2)}, u32[]{:S(2)}) collective-permute-start(bf16[512,768]{1,0:T(8,128)(2,1)S(1)} %dynamic-slice_bitcast_fusion.4), channel_id=1, source_target_pairs={{0,4},{4,0},{1,5},{5,1},{2,6},{6,2},{3,7},{7,3},{8,12},{12,8},{9,1... | collective-permute-start | bytes 2359304 | tf_op jit(solution)/shard_map/ppermute | solution.py:15
  375.9 70.4 %collective-permute-start.35 = (bf16[2,512,768]{2,1,0:T(8,128)(2,1)S(1)}, bf16[2,512,768]{2,1,0:T(8,128)(2,1)S(1)}, u32[]{:S(2)}, u32[]{:S(2)}) collective-permute-start(bf16[2,512,768]{2,1,0:T(8,128)(2,1)S(1)} %pad_maximum_fusion.20), channel_id=1, source_target_pairs={{0,8},{8,0},{1,9},{9,1},{2,10},{10,2},{3,11},{11,3},{4,12},{12,4},... | collective-permute-start | bytes 4718600 | tf_op jit(solution)/shard_map/ppermute | solution.py:15
  380.1 33.7 %collective-permute-start.25 = (bf16[32,2048]{1,0:T(8,128)(2,1)S(1)}, bf16[32,2048]{1,0:T(8,128)(2,1)S(1)}, u32[]{:S(2)}, u32[]{:S(2)}) collective-permute-start(bf16[32,2048]{1,0:T(8,128)(2,1)S(1)} %get-tuple-element.207), channel_id=1, source_target_pairs={{0,4},{4,0},{1,5},{5,1},{2,6},{6,2},{3,7},{7,3},{8,12},{12,8},{9,1... | collective-permute-start | bytes 393224 | tf_op jit(solution)/shard_map/ppermute | solution.py:15
  448.5 69.2 %collective-permute-start.36 = (bf16[4,512,768]{2,1,0:T(8,128)(2,1)}, bf16[4,512,768]{2,1,0:T(8,128)(2,1)}, u32[]{:S(2)}, u32[]{:S(2)}) collective-permute-start(bf16[4,512,768]{2,1,0:T(8,128)(2,1)} %bitcast.94), channel_id=1, source_target_pairs={{0,2},{2,0},{1,3},{3,1},{4,6},{6,4},{5,7},{7,5},{8,10},{10,8},{9,1... | collective-permute-start | bytes 9437192 | tf_op jit(solution)/shard_map/ppermute | solution.py:15
  465.4 92.9 %collective-permute-start.58 = (bf16[2,2,512,256]{3,2,1,0:T(8,128)(2,1)}, bf16[2,2,512,256]{3,2,1,0:T(8,128)(2,1)}, u32[]{:S(2)}, u32[]{:S(2)}) collective-permute-start(bf16[2,2,512,256]{3,2,1,0:T(8,128)(2,1)} %pad_maximum_fusion.29), channel_id=1, source_target_pairs={{0,4},{4,0},{1,5},{5,1},{2,6},{6,2},{3,7},{7,3},{8,12},{12,8},{9,1... | collective-permute-start | bytes 3145736 | tf_op jit(solution)/shard_map/ppermute | solution.py:15
  467.3 152.9 %collective-permute-start.73 = (bf16[128,2048]{1,0:T(8,128)(2,1)}, bf16[128,2048]{1,0:T(8,128)(2,1)}, u32[]{:S(2)}, u32[]{:S(2)}) collective-permute-start(bf16[128,2048]{1,0:T(8,128)(2,1)} %pad_maximum_fusion.53), channel_id=1, source_target_pairs={{0,1},{1,0},{2,3},{3,2},{4,5},{5,4},{6,7},{7,6},{8,9},{9,8},{10,11... | collective-permute-start | bytes 1572872 | tf_op jit(solution)/shard_map/ppermute | solution.py:15
  468.2 119.9 %collective-permute-start.84 = (bf16[512,768]{1,0:T(8,128)(2,1)}, bf16[512,768]{1,0:T(8,128)(2,1)}, u32[]{:S(2)}, u32[]{:S(2)}) collective-permute-start(bf16[512,768]{1,0:T(8,128)(2,1)} %dynamic-slice_bitcast_fusion.2), channel_id=1, source_target_pairs={{0,4},{4,0},{1,5},{5,1},{2,6},{6,2},{3,7},{7,3},{8,12},{12,8},{9,1... | collective-permute-start | bytes 2359304 | tf_op jit(solution)/shard_map/ppermute | solution.py:15
  517.7 34.6 %collective-permute-start.40 = (bf16[4,384,512]{1,2,0:T(8,128)(2,1)}, bf16[4,384,512]{1,2,0:T(8,128)(2,1)}, u32[]{:S(2)}, u32[]{:S(2)}) collective-permute-start(bf16[4,384,512]{1,2,0:T(8,128)(2,1)} %bitcast.108), channel_id=1, source_target_pairs={{0,2},{2,0},{1,3},{3,1},{4,6},{6,4},{5,7},{7,5},{8,10},{10,8},{9,1... | collective-permute-start | bytes 4718600 | tf_op jit(solution)/shard_map/ppermute | solution.py:15
  599.9 37.1 %collective-permute-start.76 = (bf16[4,384,512]{1,2,0:T(8,128)(2,1)}, bf16[4,384,512]{1,2,0:T(8,128)(2,1)}, u32[]{:S(2)}, u32[]{:S(2)}) collective-permute-start(bf16[4,384,512]{1,2,0:T(8,128)(2,1)} %bitcast.159), channel_id=1, source_target_pairs={{0,2},{2,0},{1,3},{3,1},{4,6},{6,4},{5,7},{7,5},{8,10},{10,8},{9,1... | collective-permute-start | bytes 4718600 | tf_op jit(solution)/shard_map/ppermute | solution.py:15
  615.3 37.8 %collective-permute-start.62 = (bf16[256,2048]{1,0:T(8,128)(2,1)}, bf16[256,2048]{1,0:T(8,128)(2,1)}, u32[]{:S(2)}, u32[]{:S(2)}) collective-permute-start(bf16[256,2048]{1,0:T(8,128)(2,1)} %convolution_convert_fusion.2), channel_id=1, source_target_pairs={{0,1},{1,0},{2,3},{3,2},{4,5},{5,4},{6,7},{7,6},{8,9},{9,8},{10,11... | collective-permute-start | bytes 3145736 | tf_op jit(solution)/shard_map/ppermute | solution.py:15
  616.8 72.4 %collective-permute-start.85 = (bf16[2,512,768]{2,1,0:T(8,128)(2,1)}, bf16[2,512,768]{2,1,0:T(8,128)(2,1)}, u32[]{:S(2)}, u32[]{:S(2)}) collective-permute-start(bf16[2,512,768]{2,1,0:T(8,128)(2,1)} %pad_maximum_fusion.23), channel_id=1, source_target_pairs={{0,8},{8,0},{1,9},{9,1},{2,10},{10,2},{3,11},{11,3},{4,12},{12,4},... | collective-permute-start | bytes 4718600 | tf_op jit(solution)/shard_map/ppermute | solution.py:15
  655.2 39.4 %collective-permute-start.63 = (bf16[64,2048]{1,0:T(8,128)(2,1)S(1)}, bf16[64,2048]{1,0:T(8,128)(2,1)S(1)}, u32[]{:S(2)}, u32[]{:S(2)}) collective-permute-start(bf16[64,2048]{1,0:T(8,128)(2,1)S(1)} %get-tuple-element.242), channel_id=1, source_target_pairs={{0,4},{4,0},{1,5},{5,1},{2,6},{6,2},{3,7},{7,3},{8,12},{12,8},{9,1... | collective-permute-start | bytes 786440 | tf_op jit(solution)/shard_map/ppermute | solution.py:15
  695.7 69.8 %collective-permute-start.86 = (bf16[4,512,768]{2,1,0:T(8,128)(2,1)S(1)}, bf16[4,512,768]{2,1,0:T(8,128)(2,1)S(1)}, u32[]{:S(2)}, u32[]{:S(2)}) collective-permute-start(bf16[4,512,768]{2,1,0:T(8,128)(2,1)S(1)} %bitcast.903), channel_id=1, source_target_pairs={{0,2},{2,0},{1,3},{3,1},{4,6},{6,4},{5,7},{7,5},{8,10},{10,8},{9,1... | collective-permute-start | bytes 9437192 | tf_op jit(solution)/shard_map/ppermute | solution.py:15
  809.4 55.4 %collective-permute-start.166 = (bf16[384,2048]{1,0:T(8,128)(2,1)S(1)}, bf16[384,2048]{1,0:T(8,128)(2,1)}, u32[]{:S(2)}, u32[]{:S(2)}) collective-permute-start(bf16[384,2048]{1,0:T(8,128)(2,1)S(1)} %slice.1305), channel_id=1, source_target_pairs={{0,2},{2,0},{1,3},{3,1},{4,6},{6,4},{5,7},{7,5},{8,10},{10,8},{9,1... | collective-permute-start | bytes 4718600 | tf_op jit(solution)/shard_map/ppermute | solution.py:15
  822.3 141.2 %collective-permute-start.159 = (bf16[2048,768]{1,0:T(8,128)(2,1)}, bf16[2048,768]{1,0:T(8,128)(2,1)}, u32[]{:S(2)}, u32[]{:S(2)}) collective-permute-start(bf16[2048,768]{1,0:T(8,128)(2,1)} %slice.1303), channel_id=1, source_target_pairs={{0,2},{2,0},{1,3},{3,1},{4,6},{6,4},{5,7},{7,5},{8,10},{10,8},{9,1... | collective-permute-start | bytes 9437192 | tf_op jit(solution)/shard_map/ppermute | solution.py:15
  861.8 42.0 %collective-permute-start.96 = (bf16[64,2048]{1,0:T(8,128)(2,1)}, bf16[64,2048]{1,0:T(8,128)(2,1)}, u32[]{:S(2)}, u32[]{:S(2)}) collective-permute-start(bf16[64,2048]{1,0:T(8,128)(2,1)} %get-tuple-element.129), channel_id=1, source_target_pairs={{0,1},{1,0},{2,3},{3,2},{4,5},{5,4},{6,7},{7,6},{8,9},{9,8},{10,11... | collective-permute-start | bytes 786440 | tf_op jit(solution)/shard_map/ppermute | solution.py:15
  876.5 38.5 %collective-permute-start.167 = (bf16[2,384,512]{2,1,0:T(8,128)(2,1)S(1)}, bf16[2,384,512]{2,1,0:T(8,128)(2,1)S(1)}, u32[]{:S(2)}, u32[]{:S(2)}) collective-permute-start(bf16[2,384,512]{2,1,0:T(8,128)(2,1)S(1)} %bitcast.949), channel_id=1, source_target_pairs={{0,8},{8,0},{1,9},{9,1},{2,10},{10,2},{3,11},{11,3},{4,12},{12,4},... | collective-permute-start | bytes 2359304 | tf_op jit(solution)/shard_map/ppermute | solution.py:15
  927.0 42.2 %collective-permute-start.99 = (bf16[256,2048]{1,0:T(8,128)(2,1)}, bf16[256,2048]{1,0:T(8,128)(2,1)}, u32[]{:S(2)}, u32[]{:S(2)}) collective-permute-start(bf16[256,2048]{1,0:T(8,128)(2,1)} %convolution_convert_fusion.6), channel_id=1, source_target_pairs={{0,1},{1,0},{2,3},{3,2},{4,5},{5,4},{6,7},{7,6},{8,9},{9,8},{10,11... | collective-permute-start | bytes 3145736 | tf_op jit(solution)/shard_map/ppermute | solution.py:15
  944.7 29.6 %collective-permute-start.153 = (bf16[2,128,512]{2,1,0:T(8,128)(2,1)}, bf16[2,128,512]{2,1,0:T(8,128)(2,1)}, u32[]{:S(2)}, u32[]{:S(2)}) collective-permute-start(bf16[2,128,512]{2,1,0:T(8,128)(2,1)} %bitcast.860), channel_id=1, source_target_pairs={{0,8},{8,0},{1,9},{9,1},{2,10},{10,2},{3,11},{11,3},{4,12},{12,4},... | collective-permute-start | bytes 786440 | tf_op jit(solution)/shard_map/ppermute | solution.py:15
  959.0 94.1 %collective-permute-start.145 = (bf16[2,2,1,512,256]{4,3,1,2,0:T(8,128)(2,1)}, bf16[2,2,1,512,256]{4,3,1,2,0:T(8,128)(2,1)}, u32[]{:S(2)}, u32[]{:S(2)}) collective-permute-start(bf16[2,2,1,512,256]{4,3,1,2,0:T(8,128)(2,1)} %fusion.51), channel_id=1, source_target_pairs={{0,4},{4,0},{1,5},{5,1},{2,6},{6,2},{3,7},{7,3},{8,12},{12,8},{9,1... | collective-permute-start | bytes 3145736 | tf_op jit(solution)/shard_map/ppermute | solution.py:15
  961.1 70.2 %collective-permute-start.139 = (bf16[2,512,128]{2,1,0:T(8,128)(2,1)S(1)}, bf16[2,512,128]{2,1,0:T(8,128)(2,1)S(1)}, u32[]{:S(2)}, u32[]{:S(2)}) collective-permute-start(bf16[2,512,128]{2,1,0:T(8,128)(2,1)S(1)} %fusion.142), channel_id=1, source_target_pairs={{0,8},{8,0},{1,9},{9,1},{2,10},{10,2},{3,11},{11,3},{4,12},{12,4},... | collective-permute-start | bytes 786440 | tf_op jit(solution)/shard_map/ppermute | solution.py:15
  967.8 115.5 %collective-permute-start.160 = (bf16[2,512,768]{2,1,0:T(8,128)(2,1)}, bf16[2,512,768]{2,1,0:T(8,128)(2,1)}, u32[]{:S(2)}, u32[]{:S(2)}) collective-permute-start(bf16[2,512,768]{2,1,0:T(8,128)(2,1)} %fusion.21), channel_id=1, source_target_pairs={{0,8},{8,0},{1,9},{9,1},{2,10},{10,2},{3,11},{11,3},{4,12},{12,4},... | collective-permute-start | bytes 4718600 | tf_op jit(solution)/shard_map/ppermute | solution.py:15
  973.7 56.1 %collective-permute-start.100 = (bf16[64,2048]{1,0:T(8,128)(2,1)S(1)}, bf16[64,2048]{1,0:T(8,128)(2,1)S(1)}, u32[]{:S(2)}, u32[]{:S(2)}) collective-permute-start(bf16[64,2048]{1,0:T(8,128)(2,1)S(1)} %get-tuple-element.238), channel_id=1, source_target_pairs={{0,4},{4,0},{1,5},{5,1},{2,6},{6,2},{3,7},{7,3},{8,12},{12,8},{9,1... | collective-permute-start | bytes 786440 | tf_op jit(solution)/shard_map/ppermute | solution.py:15
  976.1 103.1 %collective-permute-start.154 = (bf16[128,512]{1,0:T(8,128)(2,1)}, bf16[128,512]{1,0:T(8,128)(2,1)}, u32[]{:S(2)}, u32[]{:S(2)}) collective-permute-start(bf16[128,512]{1,0:T(8,128)(2,1)} %dynamic-slice_bitcast_fusion.12), channel_id=1, source_target_pairs={{0,4},{4,0},{1,5},{5,1},{2,6},{6,2},{3,7},{7,3},{8,12},{12,8},{9,1... | collective-permute-start | bytes 393224 | tf_op jit(solution)/shard_map/ppermute | solution.py:15
  1082.2 364.7 %collective-permute-start.147 = (bf16[512,256]{1,0:T(8,128)(2,1)}, bf16[512,256]{1,0:T(8,128)(2,1)}, u32[]{:S(2)}, u32[]{:S(2)}) collective-permute-start(bf16[512,256]{1,0:T(8,128)(2,1)} %fusion.144), channel_id=1, source_target_pairs={{0,8},{8,0},{1,9},{9,1},{2,10},{10,2},{3,11},{11,3},{4,12},{12,4},... | collective-permute-start | bytes 786440 | tf_op jit(solution)/shard_map/ppermute | solution.py:15
  1085.3 38.1 %collective-permute-start.161 = (bf16[512,768]{1,0:T(8,128)(2,1)S(1)}, bf16[512,768]{1,0:T(8,128)(2,1)S(1)}, u32[]{:S(2)}, u32[]{:S(2)}) collective-permute-start(bf16[512,768]{1,0:T(8,128)(2,1)S(1)} %dynamic-slice_bitcast_fusion), channel_id=1, source_target_pairs={{0,4},{4,0},{1,5},{5,1},{2,6},{6,2},{3,7},{7,3},{8,12},{12,8},{9,1... | collective-permute-start | bytes 2359304 | tf_op jit(solution)/shard_map/ppermute | solution.py:15
  1093.8 37.4 %collective-permute-start.163 = (bf16[384,2048]{1,0:T(8,128)(2,1)S(1)}, bf16[384,2048]{1,0:T(8,128)(2,1)S(1)}, u32[]{:S(2)}, u32[]{:S(2)}) collective-permute-start(bf16[384,2048]{1,0:T(8,128)(2,1)S(1)} %slice.1306), channel_id=1, source_target_pairs={{0,2},{2,0},{1,3},{3,1},{4,6},{6,4},{5,7},{7,5},{8,10},{10,8},{9,1... | collective-permute-start | bytes 4718600 | tf_op jit(solution)/shard_map/ppermute | solution.py:15
  1095.2 26.6 %collective-permute-start.114 = (bf16[64,2048]{1,0:T(8,128)(2,1)S(1)}, bf16[64,2048]{1,0:T(8,128)(2,1)S(1)}, u32[]{:S(2)}, u32[]{:S(2)}) collective-permute-start(bf16[64,2048]{1,0:T(8,128)(2,1)S(1)} %get-tuple-element.237), channel_id=1, source_target_pairs={{0,16},{16,0},{1,17},{17,1},{2,18},{18,2},{3,19},{19,3},{4,20},{20... | collective-permute-start | bytes 786440 | tf_op jit(solution)/shard_map/ppermute | solution.py:15
  1121.8 111.6 %collective-permute-start.156 = (bf16[2048,768]{1,0:T(8,128)(2,1)}, bf16[2048,768]{1,0:T(8,128)(2,1)}, u32[]{:S(2)}, u32[]{:S(2)}) collective-permute-start(bf16[2048,768]{1,0:T(8,128)(2,1)} %slice.1304), channel_id=1, source_target_pairs={{0,2},{2,0},{1,3},{3,1},{4,6},{6,4},{5,7},{7,5},{8,10},{10,8},{9,1... | collective-permute-start | bytes 9437192 | tf_op jit(solution)/shard_map/ppermute | solution.py:15
  1150.9 36.3 %collective-permute-start.164 = (bf16[2,384,512]{2,1,0:T(8,128)(2,1)S(1)}, bf16[2,384,512]{2,1,0:T(8,128)(2,1)S(1)}, u32[]{:S(2)}, u32[]{:S(2)}) collective-permute-start(bf16[2,384,512]{2,1,0:T(8,128)(2,1)S(1)} %bitcast.950), channel_id=1, source_target_pairs={{0,8},{8,0},{1,9},{9,1},{2,10},{10,2},{3,11},{11,3},{4,12},{12,4},... | collective-permute-start | bytes 2359304 | tf_op jit(solution)/shard_map/ppermute | solution.py:15
  1154.0 33.7 %collective-permute-start.122 = (bf16[128,2048]{1,0:T(8,128)(2,1)S(1)}, bf16[128,2048]{1,0:T(8,128)(2,1)S(1)}, u32[]{:S(2)}, u32[]{:S(2)}) collective-permute-start(bf16[128,2048]{1,0:T(8,128)(2,1)S(1)} %pad_maximum_fusion.60), channel_id=1, source_target_pairs={{0,1},{1,0},{2,3},{3,2},{4,5},{5,4},{6,7},{7,6},{8,9},{9,8},{10,11... | collective-permute-start | bytes 1572872 | tf_op jit(solution)/shard_map/ppermute | solution.py:15
  1205.8 75.0 %collective-permute-start.123 = (bf16[256,2048]{1,0:T(8,128)(2,1)}, bf16[256,2048]{1,0:T(8,128)(2,1)}, u32[]{:S(2)}, u32[]{:S(2)}) collective-permute-start(bf16[256,2048]{1,0:T(8,128)(2,1)} %convolution_convert_fusion.5), channel_id=1, source_target_pairs={{0,1},{1,0},{2,3},{3,2},{4,5},{5,4},{6,7},{7,6},{8,9},{9,8},{10,11... | collective-permute-start | bytes 3145736 | tf_op jit(solution)/shard_map/ppermute | solution.py:15
  1215.4 61.1 %collective-permute-start.169 = (bf16[2,384,512]{2,1,0:T(8,128)(2,1)}, bf16[2,384,512]{2,1,0:T(8,128)(2,1)}, u32[]{:S(2)}, u32[]{:S(2)}) collective-permute-start(bf16[2,384,512]{2,1,0:T(8,128)(2,1)} %broadcast_select_fusion.4), channel_id=1, source_target_pairs={{0,16},{16,0},{1,17},{17,1},{2,18},{18,2},{3,19},{19,3},{4,20},{20... | collective-permute-start | bytes 2359304 | tf_op jit(solution)/shard_map/ppermute | solution.py:15
  1233.4 119.9 %collective-permute-start.142 = (bf16[2,2,1,512,256]{4,3,1,2,0:T(8,128)(2,1)}, bf16[2,2,1,512,256]{4,3,1,2,0:T(8,128)(2,1)}, u32[]{:S(2)}, u32[]{:S(2)}) collective-permute-start(bf16[2,2,1,512,256]{4,3,1,2,0:T(8,128)(2,1)} %fusion.50), channel_id=1, source_target_pairs={{0,4},{4,0},{1,5},{5,1},{2,6},{6,2},{3,7},{7,3},{8,12},{12,8},{9,1... | collective-permute-start | bytes 3145736 | tf_op jit(solution)/shard_map/ppermute | solution.py:15
  1274.5 128.8 %collective-permute-start.157 = (bf16[2,512,768]{2,1,0:T(8,128)(2,1)}, bf16[2,512,768]{2,1,0:T(8,128)(2,1)}, u32[]{:S(2)}, u32[]{:S(2)}) collective-permute-start(bf16[2,512,768]{2,1,0:T(8,128)(2,1)} %fusion.20), channel_id=1, source_target_pairs={{0,8},{8,0},{1,9},{9,1},{2,10},{10,2},{3,11},{11,3},{4,12},{12,4},... | collective-permute-start | bytes 4718600 | tf_op jit(solution)/shard_map/ppermute | solution.py:15
  1280.9 33.3 %collective-permute-start.141 = (bf16[2,512,128]{1,2,0:T(8,128)(2,1)S(1)}, bf16[2,512,128]{1,2,0:T(8,128)(2,1)S(1)}, u32[]{:S(2)}, u32[]{:S(2)}) collective-permute-start(bf16[2,512,128]{1,2,0:T(8,128)(2,1)S(1)} %broadcast_select_fusion.12), channel_id=1, source_target_pairs={{0,16},{16,0},{1,17},{17,1},{2,18},{18,2},{3,19},{19,3},{4,20},{20... | collective-permute-start | bytes 786440 | tf_op jit(solution)/shard_map/ppermute | solution.py:15
  1285.5 28.0 %collective-permute-start.124 = (bf16[64,2048]{1,0:T(8,128)(2,1)S(1)}, bf16[64,2048]{1,0:T(8,128)(2,1)S(1)}, u32[]{:S(2)}, u32[]{:S(2)}) collective-permute-start(bf16[64,2048]{1,0:T(8,128)(2,1)S(1)} %get-tuple-element.234), channel_id=1, source_target_pairs={{0,4},{4,0},{1,5},{5,1},{2,6},{6,2},{3,7},{7,3},{8,12},{12,8},{9,1... | collective-permute-start | bytes 786440 | tf_op jit(solution)/shard_map/ppermute | solution.py:15
  1352.8 49.6 %collective-permute-start.133 = (bf16[64,2048]{1,0:T(8,128)(2,1)}, bf16[64,2048]{1,0:T(8,128)(2,1)S(1)}, u32[]{:S(2)}, u32[]{:S(2)}) collective-permute-start(bf16[64,2048]{1,0:T(8,128)(2,1)} %get-tuple-element.117), channel_id=1, source_target_pairs={{0,16},{16,0},{1,17},{17,1},{2,18},{18,2},{3,19},{19,3},{4,20},{20... | collective-permute-start | bytes 786440 | tf_op jit(solution)/shard_map/ppermute | solution.py:15
  1356.3 52.1 %collective-permute-start.143 = (bf16[2,1,512,256]{3,2,1,0:T(8,128)(2,1)S(1)}, bf16[2,1,512,256]{3,2,1,0:T(8,128)(2,1)S(1)}, u32[]{:S(2)}, u32[]{:S(2)}) collective-permute-start(bf16[2,1,512,256]{3,2,1,0:T(8,128)(2,1)S(1)} %fusion.76), channel_id=1, source_target_pairs={{0,2},{2,0},{1,3},{3,1},{4,6},{6,4},{5,7},{7,5},{8,10},{10,8},{9,1... | collective-permute-start | bytes 1572872 | tf_op jit(solution)/shard_map/ppermute | solution.py:15
  1406.2 29.9 %collective-permute-start.158 = (bf16[512,768]{1,0:T(8,128)(2,1)S(1)}, bf16[512,768]{1,0:T(8,128)(2,1)}, u32[]{:S(2)}, u32[]{:S(2)}) collective-permute-start(bf16[512,768]{1,0:T(8,128)(2,1)S(1)} %dynamic-slice_bitcast_fusion.1), channel_id=1, source_target_pairs={{0,4},{4,0},{1,5},{5,1},{2,6},{6,2},{3,7},{7,3},{8,12},{12,8},{9,1... | collective-permute-start | bytes 2359304 | tf_op jit(solution)/shard_map/ppermute | solution.py:15
  1409.6 37.3 %collective-permute-start.144 = (bf16[512,256]{1,0:T(8,128)(2,1)}, bf16[512,256]{1,0:T(8,128)(2,1)}, u32[]{:S(2)}, u32[]{:S(2)}) collective-permute-start(bf16[512,256]{1,0:T(8,128)(2,1)} %fusion.143), channel_id=1, source_target_pairs={{0,8},{8,0},{1,9},{9,1},{2,10},{10,2},{3,11},{11,3},{4,12},{12,4},... | collective-permute-start | bytes 786440 | tf_op jit(solution)/shard_map/ppermute | solution.py:15
  1439.0 56.5 %collective-permute-start.162 = (bf16[2,512,768]{2,1,0:T(8,128)(2,1)}, bf16[2,512,768]{2,1,0:T(8,128)(2,1)}, u32[]{:S(2)}, u32[]{:S(2)}) collective-permute-start(bf16[2,512,768]{2,1,0:T(8,128)(2,1)} %broadcast_select_fusion.2), channel_id=1, source_target_pairs={{0,16},{16,0},{1,17},{17,1},{2,18},{18,2},{3,19},{19,3},{4,20},{20... | collective-permute-start | bytes 4718600 | tf_op jit(solution)/shard_map/ppermute | solution.py:15
  1449.2 30.5 %collective-permute-start.148 = (bf16[512,256]{1,0:T(8,128)(2,1)}, bf16[512,256]{1,0:T(8,128)(2,1)}, u32[]{:S(2)}, u32[]{:S(2)}) collective-permute-start(bf16[512,256]{1,0:T(8,128)(2,1)} %get-tuple-element.112), channel_id=1, source_target_pairs={{0,16},{16,0},{1,17},{17,1},{2,18},{18,2},{3,19},{19,3},{4,20},{20... | collective-permute-start | bytes 786440 | tf_op jit(solution)/shard_map/ppermute | solution.py:15
  (366 other events, 4198.3 us)

commit v2 on v1

v2 whole, which is shorter than its diff:
```python
import jax
import jax.numpy as jnp
import numpy as np
from jax import lax
from jax.experimental.layout import Layout, with_layout_constraint
from jax.sharding import Mesh
from jax.sharding import PartitionSpec as P

EPS = 1e-06
THETA = 1000000.0
f32 = jnp.float32
bf16 = jnp.bfloat16


def swap(value, axis):
    return lax.ppermute(value, axis, [(0, 1), (1, 0)])


def exchange(value, axes):
    return lax.all_to_all(value, axes, 0, 0, tiled=True)


def take(value, index, axis=0):
    return lax.dynamic_index_in_dim(value, index, axis, keepdims=False)


def pair(bit, mine, other, axis=0):
    low = jnp.where(bit == 0, mine, other)
    high = jnp.where(bit == 0, other, mine)
    return jnp.stack([low, high], axis)


def plain(value):
    return with_layout_constraint(value, Layout(major_to_minor=tuple(range(value.ndim))))


def dot(left, right):
    return jnp.dot(left, right, preferred_element_type=f32)


def dot_t(left, right):
    return lax.dot_general(left, right, (((1,), (1,)), ((), ())), preferred_element_type=f32)


def t_dot(left, right):
    return lax.dot_general(left, right, (((0,), (0,)), ((), ())), preferred_element_type=f32)


def cross(value):
    return lax.ppermute(value, ("s", "t"), [(i, 3 - i) for i in range(4)])


def gather_tokens(mine, middle):
    core = jnp.concatenate([mine, swap(mine, "s"), swap(mine, "t"), cross(mine)])
    core = middle(core)
    return jnp.concatenate([core, swap(core, "k")])


def slots_of(s, t, k, g, groups, part):
    pieces = []
    for dk in (0, 1):
        for ds, dt in ((0, 0), (1, 0), (0, 1), (1, 1)):
            block = ((s ^ ds) * 2 + (t ^ dt)) * groups + g
            start = block * (2 * part) + (k ^ dk) * part
            pieces.append(start + jnp.arange(part, dtype=jnp.int32))
    return jnp.concatenate(pieces)


def scatter_sum(near, far, middle):
    total = near + swap(far, "k").astype(f32)
    part = total.shape[0] // 4
    total, far = middle((total[:part], total[part:].astype(bf16)))
    pieces = [swap(far[:part], "s"), swap(far[part : 2 * part], "t"), cross(far[2 * part :])]
    return total + sum(piece.astype(f32) for piece in pieces)


def split_product(lefts, rights):
    half = lefts[0].shape[0] // 2
    far = sum(dot_t(left[half:], right) for left, right in zip(lefts, rights)).astype(bf16)
    near = sum(dot_t(left[:half], right) for left, right in zip(lefts, rights))
    return near, far


class Clock:
    def __init__(self):
        self.plans, self.flying, self.ready = {}, {}, {}

    def add(self, name, begin, end, make, send):
        self.plans[name] = (begin, end, make, send)

    def point(self, label, chain):
        ends = [name for name, plan in self.plans.items() if plan[1] == label]
        if ends:
            chain, arrived = lax.optimization_barrier((chain, [self.flying[name] for name in ends]))
            self.ready.update(zip(ends, arrived))
        begins = [name for name, plan in self.plans.items() if plan[0] == label]
        if begins:
            values = [self.plans[name][2]() for name in begins]
            chain, values = lax.optimization_barrier((chain, values))
            for name, value in zip(begins, values):
                self.flying[name] = self.plans[name][3](value)
        return chain


def rms(residual):
    return lax.rsqrt(jnp.mean(residual * residual, axis=1, keepdims=True) + EPS)


def norm_back(residual, scale, gain, grad):
    lifted = grad * gain
    inner = jnp.mean(lifted * residual, axis=1, keepdims=True)
    grad_residual = scale * lifted - residual * (scale**3 * inner)
    return grad_residual, jnp.sum(grad * residual * scale, axis=0)


def rotate(raw, gain, cosine, sine):
    scaled = raw * lax.rsqrt(jnp.mean(raw * raw, axis=2, keepdims=True) + EPS) * gain
    half = raw.shape[2] // 2
    turned = jnp.concatenate([-scaled[:, :, half:], scaled[:, :, :half]], axis=2)
    return scaled * cosine[:, None, :] + turned * sine[:, None, :]


FETCH = {
    "a": ("in", "rows"),
    "m0": ("c1", "c2"),
    "m1": ("c2", "F03"),
}
SPREAD = {
    "a00": ("rows", "c1", "c1", "c2"),
    "a10": ("c1", "c2", "c2", "c3"),
    "m00": ("c2", "c3", "c3", "F03"),
    "m20": ("c3", "F03", "F03", "F05"),
    "m10": ("F03", "F05", "F05", "F06"),
    "m30": ("F05", "F06", "F06", "F07"),
    "a01": ("F06", "F07", "F07", "F10"),
    "a11": ("F07", "F10", "F10", "F11"),
    "m01": ("F10", "F11", "F11", "F13"),
    "m21": ("F11", "F13", "F13", "F15"),
    "m11": ("F13", "F15", "F15", "F16"),
    "m31": ("F15", "F16", "F16", "F17"),
}
RETURN = {
    "m01": ("B14", "B15", "B15", "B16"),
    "m21": ("B15", "B16", "B16", "B18"),
    "m11": ("B16", "B18", "B18", "B00"),
    "m31": ("B18", "B00", "B00", "B01"),
    "a01": ("B00", "B01", "B01", "B03"),
    "a11": ("B01", "B03", "B04", "B05"),
    "m00": ("B04", "B05", "B05", "B06"),
    "m20": ("B05", "B06", "B06", "B08"),
    "m10": ("B06", "B08", "B08", "E0"),
    "m30": ("B08", "E0", "E0", "E1"),
    "a00": ("E0", "E1", "E1", "E2"),
    "a10": ("E1", "E2", "E2", "E3"),
}
HOME = {
    "m0": ("E0", "E1"),
    "m1": ("E1", "E3"),
}


def body(
    boundary, segment_ids, w_query, key_projection, value_projection, w_out, w_gate, w_up, w_down,
    attn_gain, mlp_gain, query_gain, key_norm_gain,
):
    s, h, t, g, y, k = (lax.axis_index(name) for name in ("s", "h", "t", "g", "y", "k"))
    groups = lax.axis_size("g")
    micro, tok, width = boundary.shape[1:]
    cols = lax.axis_size("y") * lax.axis_size("k")
    model = width * cols
    head = query_gain.shape[1]
    span = segment_ids.shape[1]
    rb = w_query.shape[1]
    ff = w_gate.shape[2] // 4
    scale_qk = head ** (-0.5)
    clock = Clock()

    packed = jnp.concatenate([attn_gain[0], mlp_gain[0], query_gain[0], key_norm_gain[0]])[None]

    sent = boundary[0].reshape(2, 2, 2, tok // 2, width).transpose(0, 2, 1, 3, 4)
    sent = exchange(sent.reshape(cols, 2, tok // 2, width), ("y", "k"))
    rows = sent.transpose(1, 2, 0, 3).reshape(2, tok // 2, model)

    def quarters(weight):
        size = weight.shape[1] // 4
        return [weight[:, i * size : (i + 1) * size] for i in range(4)]

    def to_groups(value):
        return exchange(value, ("s", "t"))

    a_home = []
    for i, (q, o) in enumerate(zip(quarters(w_query[0]), quarters(w_out[0].T))):
        low = (i // 2) * head
        kv = [w[0, :, low : low + head] for w in (key_projection, value_projection)]
        a_home.append(jnp.concatenate([q, o] + kv, 1))
    a_home, w_gate, w_up, w_down = lax.optimization_barrier((plain(jnp.stack(a_home)), w_gate, w_up, w_down))
    m_home = [
        jnp.concatenate(pieces, 1)
        for pieces in zip(quarters(w_gate[0]), quarters(w_up[0]), quarters(w_down[0].T))
    ]
    homes = {
        "a": a_home,
        "m0": plain(jnp.stack([value[: rb // 2] for value in m_home])),
        "m1": plain(jnp.stack([value[rb // 2 :] for value in m_home])),
    }

    def rolled(value):
        half = value.shape[-1] // 2
        return jnp.where(h == 0, value, jnp.concatenate([value[..., half:], value[..., :half]], -1))

    def fetch(name):
        clock.add(name, *FETCH[name], lambda: homes[name], to_groups)

    def spread(name):
        i, layer = int(name[1]), int(name[2])
        source, block = ("a", i) if name[0] == "a" else (f"m{i % 2}", i // 2)
        plan = SPREAD[name]

        def start():
            return clock.ready[source][2 * layer + block]

        def onward():
            value = [start(), clock.ready[name + "h"]]
            if groups > 1:
                value = [lax.all_gather(half, "g", axis=0, tiled=True) for half in value]
            clock.ready[name] = jnp.concatenate(value)
            return clock.ready[name]

        clock.add(name + "h", plan[0], plan[1], start, lambda value: swap(value, "h"))
        clock.add(name + "y", plan[2], plan[3], onward, lambda value: swap(value, "y"))

    def places_of(kind):
        count = 2 if kind == "m" else 1
        size = rb // count
        for i in range(4 * groups):
            half, block, group = i // (2 * groups), i // groups % 2, i % groups
            for j in range(count):
                yield block * count + j, (half * groups + group) * size, size

    def weight(kind, layer):
        return [
            jnp.concatenate(
                [
                    clock.ready[f"{kind}{part}{layer}{step}"][low : low + size]
                    for part, low, size in places_of(kind)
                ]
            )
            for step in ("", "y")
        ]

    for name in FETCH:
        fetch(name)
    for name in SPREAD:
        spread(name)

    rows, packed = clock.point("in", (rows, packed))
    own_rows = take(rows, h)
    other_rows = swap(take(rows, 1 - h), "h")
    keep = jnp.where(s == h, own_rows, other_rows)
    passed = swap(jnp.where(s == h, other_rows, own_rows), "s")
    entering = jnp.where(s == 0, keep, passed)
    cotangent = rolled(jnp.where(s == 0, passed, keep))
    entering = rolled(entering)
    packed = pair(k, packed, swap(packed, "k"), 1)
    packed = pair(s, packed, swap(packed, "s"))
    packed = pair(y, packed, swap(packed, "y"), 1).reshape(2, cols, -1).astype(f32)
    gain_a = rolled(packed[:, :, :width].reshape(2, model))
    gain_m = rolled(packed[:, :, width : 2 * width].reshape(2, model))
    gain_q = packed[:, 0, 2 * width : 2 * width + head]
    gain_k = packed[:, 0, 2 * width + head :]

    segments = take(segment_ids, 2 * y + h)
    part = tok // 2
    slots = slots_of(s, t, k, g, groups, part)
    first_run = jnp.sum((segments == 0).astype(jnp.int32))
    filled = jnp.sum((segments >= 0).astype(jnp.int32))

    def segments_at(places):
        return jnp.where(places < first_run, 0, jnp.where(places < filled, 1, -1))

    my_segments = segments_at(slots)
    offsets = slots - jnp.where(slots < first_run, 0, jnp.where(slots < filled, first_run, filled))
    inv_freq = THETA ** (-jnp.arange(0, head, 2, dtype=f32) / head)
    angles = offsets.astype(f32)[:, None] * inv_freq[None, :]
    cosine = jnp.concatenate([jnp.cos(angles)] * 2, 1)
    sine = jnp.concatenate([jnp.sin(angles)] * 2, 1)
    valid = (my_segments[:part] >= 0).astype(f32)
    key_slots = lax.all_gather(slots, "g", axis=0, tiled=True) if groups > 1 else slots
    key_segments = segments_at(key_slots)
    allowed = (my_segments[:, None] == key_segments[None, :]) & (
        key_slots[None, :] <= slots[:, None]
    )

    def all_keys(value):
        return lax.all_gather(value, "g", axis=0, tiled=True) if groups > 1 else value

    def sum_keys(value):
        if groups > 1:
            return lax.psum_scatter(value.astype(bf16), "g", scatter_dimension=0, tiled=True).astype(f32)
        return value

    def scores_of(q, keys):
        scores = jnp.einsum("qhd,khd->hqk", q, keys, preferred_element_type=f32) * scale_qk
        return jnp.where(allowed[None], scores, -1e30)

    entering, cotangent = clock.point("rows", (entering, cotangent))
    top = cotangent.astype(f32) * valid[:, None]
    kept = {}

    def forward(layer, residual):
        def at(place):
            return lambda chain: clock.point(f"F{layer}{place}", chain)

        scale_a = rms(residual)
        normed = (residual * scale_a * gain_a[layer]).astype(bf16)
        xa = at(2)(gather_tokens(at(0)(normed), at(1)))
        if layer == 0:
            for label in ("c1", "c2", "c3"):
                xa = clock.point(label, xa)
        wa = weight("a", layer)
        q_raw = jnp.stack([dot(xa, w[:, :head]) for w in wa], 1)
        raw = jnp.stack([dot(xa, w[:, 2 * head :]) for w in wa], 1)
        k_raw = raw[:, :, :head]
        v = raw[:, :, head:].astype(bf16)
        q = rotate(q_raw, gain_q[layer], cosine, sine).astype(bf16)
        keys = rotate(k_raw, gain_k[layer], cosine, sine).astype(bf16)
        keys, values = all_keys(keys), all_keys(v)
        scores = scores_of(q, keys)
        peak = jnp.max(scores, axis=2, keepdims=True)
        exps = jnp.exp(scores - peak)
        denom = jnp.sum(exps, axis=2, keepdims=True)
        mixing = (exps / denom).astype(bf16)
        lse = peak + jnp.log(denom)
        o = jnp.einsum("hqk,khd->qhd", mixing, values, preferred_element_type=f32)
        o = o.astype(bf16)
        near, far = at(3)(split_product((o[:, 0], o[:, 1]), [w[:, head : 2 * head] for w in wa]))
        middle = at(5)(residual + scatter_sum(near, far, at(4)))
        scale_m = rms(middle)
        normed = (middle * scale_m * gain_m[layer]).astype(bf16)
        xm = at(7)(gather_tokens(normed, at(6)))
        if layer == 0:
            xm, grad = lax.optimization_barrier((xm, top.astype(bf16)))
            xm, kept["g3"] = lax.optimization_barrier((xm, gather_tokens(grad, lambda value: value)))
        wm = weight("m", layer)
        hidden = []
        for w in wm:
            both = dot(xm, w[:, : 2 * ff])
            hidden.append((both[:, :ff], both[:, ff:]))
        act = [(gate * jax.nn.sigmoid(gate) * up).astype(bf16) for gate, up in hidden]
        kept[layer] = (residual, scale_a, xa, q_raw, k_raw, q, keys, values, lse, o, middle, scale_m, xm, hidden, act, wa, wm)

    def project(layer, act):
        return split_product(act, [w[:, 2 * ff :] for w in kept[layer][-1]])

    partial = {}

    def back(name):
        plan = RETURN[name]
        part, layer = int(name[1]), name[2]

        def rows_of(i):
            value = partial[name[0] + layer][i]
            rows = rb // (2 if name[0] == "m" else 1)
            lows = [
                j * rows for j, (index, _, _) in enumerate(places_of(name[0])) if index == part
            ]
            return jnp.concatenate([value[low : low + rows] for low in lows])

        def onward():
            total = rows_of(0).astype(f32) + clock.ready["back_y" + name].astype(f32)
            count = total.shape[0] // 2
            mine, other = total[:count], total[count:]
            if groups > 1:
                mine, other = (
                    lax.psum_scatter(half.astype(bf16), "g", scatter_dimension=0, tiled=True)
                    for half in (mine, other)
                )
            partial["sum" + name] = mine.astype(bf16)
            return other.astype(bf16)

        clock.add("back_y" + name, plan[0], plan[1], lambda: rows_of(1), lambda value: swap(value, "y"))
        clock.add("back_h" + name, plan[2], plan[3], onward, lambda value: swap(value, "h"))

    def summed(name):
        return (partial["sum" + name].astype(f32) + clock.ready["back_h" + name].astype(f32)).astype(bf16)

    def both_layers(name):
        names = ("a0", "a1") if name == "a" else (name, f"m{int(name[1]) + 2}")
        return plain(jnp.stack([summed(f"{part}{layer}") for layer in (0, 1) for part in names]))

    for name in RETURN:
        back(name)
    for name, plan in HOME.items():
        clock.add("home" + name, *plan, lambda name=name: both_layers(name), to_groups)

    def backward(layer, grad_top, g3):
        def at(place):
            return lambda chain: clock.point(f"B{layer}{place}", chain)

        (
            residual, scale_a, xa, q_raw, k_raw, q, keys, values, lse, o, middle, scale_m, xm, hidden,
            act, wa, wm,
        ) = kept[layer]
        d_act = [dot(g3, w[:, 2 * ff :]) for w in wm]
        d_hidden = []
        for grad, (gate, up) in zip(d_act, hidden):
            sig = jax.nn.sigmoid(gate)
            d_gate = (grad * up * sig * (1 + gate * (1 - sig))).astype(bf16)
            d_up = (grad * gate * sig).astype(bf16)
            d_hidden.append(jnp.concatenate([d_gate, d_up], 1))
        near, far = split_product(d_hidden, [w[:, : 2 * ff] for w in wm])
        partial[f"m{layer}"] = [
            plain(jnp.concatenate([t_dot(xm, d).astype(bf16), t_dot(g3, a).astype(bf16)], 1))
            for d, a in zip(d_hidden, act)
        ]
        near, far = at(3)((near, far))
        def after_core(chain):
            chain, partial[f"m{layer}"] = lax.optimization_barrier((chain, partial[f"m{layer}"]))
            return at(4)(chain)

        d_xm = at(5)(scatter_sum(near, far, after_core))
        d_mid, d_gain_m = norm_back(middle, scale_m, gain_m[layer], d_xm)
        d_mid = grad_top + d_mid
        g2 = at(7)(gather_tokens(d_mid.astype(bf16), at(6)))
        d_o = jnp.stack([dot(g2, w[:, head : 2 * head]).astype(bf16) for w in wa], 1)
        mixing = jnp.exp(scores_of(q, keys) - lse)
        d_mix = jnp.einsum("qhd,khd->hqk", d_o, values, preferred_element_type=f32)
        inner = jnp.sum(mixing * d_mix, axis=2, keepdims=True)
        d_scores = (mixing * (d_mix - inner)).astype(bf16)
        d_q = jnp.einsum("hqk,khd->qhd", d_scores, keys, preferred_element_type=f32) * scale_qk
        d_k = jnp.einsum("hqk,qhd->khd", d_scores, q, preferred_element_type=f32) * scale_qk
        d_v = jnp.einsum("hqk,qhd->khd", mixing.astype(bf16), d_o, preferred_element_type=f32)
        d_k, d_v = sum_keys(d_k), sum_keys(d_v)
        _, pull_q = jax.vjp(lambda raw, gain: rotate(raw, gain, cosine, sine), q_raw, gain_q[layer])
        _, pull_k = jax.vjp(lambda raw, gain: rotate(raw, gain, cosine, sine), k_raw, gain_k[layer])
        d_q_raw, d_gain_q = pull_q(d_q)
        d_k_raw, d_gain_k = pull_k(d_k)
        d_q_raw, d_kv_raw = d_q_raw.astype(bf16), jnp.concatenate([d_k_raw, d_v], 2).astype(bf16)
        d_raw = [d_q_raw[:, 0], d_q_raw[:, 1], d_kv_raw[:, 0], d_kv_raw[:, 1]]
        near, far = at(8)(split_product(d_raw, [w[:, :head] for w in wa] + [w[:, 2 * head :] for w in wa]))
        partial[f"a{layer}"] = [
            plain(
                jnp.concatenate(
                    [
                        value.astype(bf16)
                        for value in (t_dot(xa, d_q_raw[:, i]), t_dot(g2, o[:, i]), t_dot(xa, d_kv_raw[:, i]))
                    ],
                    1,
                )
            )
            for i in (0, 1)
        ]
        d_xa = scatter_sum(near, far, at(9))
        d_res, d_gain_a = norm_back(residual, scale_a, gain_a[layer], d_xa)
        return d_mid + d_res, (d_gain_a, d_gain_m, d_gain_q, d_gain_k)

    forward(0, entering.astype(f32))
    act = kept[0][14]
    near, far = clock.point("F09", project(0, act))
    middle = kept[0][10] + scatter_sum(near, far, lambda value: value)
    forward(1, middle.astype(bf16).astype(f32))
    grad, gains1 = backward(1, top, kept["g3"])
    grad = clock.point("B00", grad.astype(bf16))
    g3 = clock.point("B02", gather_tokens(grad, lambda value: clock.point("B01", value)))
    grad, gains0 = backward(0, grad.astype(f32), g3)
    grad = clock.point("E0", grad)

    act, grad = lax.optimization_barrier((kept[1][14], grad))
    near, far = project(1, act)
    sums = []
    for gains in (gains0, gains1):
        sums += [rolled(gains[0]), rolled(gains[1]), gains[2], gains[3]]
    sums = jnp.concatenate(sums).reshape(2, -1)
    sums = sums + swap(sums, "k")
    output = kept[1][10] + scatter_sum(near, far, lambda value: value)

    grad, output, sums = clock.point("E1", (grad, output, sums))
    low, high = rolled(grad.astype(bf16)), rolled(output.astype(bf16))
    keep = jnp.where(s == 0, low, high)
    passed = swap(jnp.where(s == 0, high, low), "s")
    sums = sums + swap(sums, "y")
    sums = sums + swap(sums, "t")
    mine = jnp.where(s == h, keep, passed)
    other = swap(jnp.where(s == h, passed, keep), "h")
    mine, other, sums = clock.point("E2", (mine, other, sums))
    mine, other, sums = clock.point("E3", (mine, other, sums))
    rows = pair(h, mine, other).reshape(2, tok // 2, cols, width).transpose(2, 0, 1, 3)
    rows = exchange(rows, ("y", "k"))
    sums = sums + swap(sums, "s")
    sums = sums + swap(sums, "h")
    rows = rows.reshape(2, 2, 2, tok // 2, width).transpose(0, 2, 1, 3, 4)
    section_out = rows.reshape(micro, tok, width)
    if groups > 1:
        sums = lax.psum(sums, "g")
    sums = take(sums, s)

    def columns(value):
        return jnp.concatenate([value[i] for i in range(4)], 1).astype(f32)

    full_a = to_groups(both_layers("a"))
    full_m = jnp.concatenate([clock.ready["homem0"], clock.ready["homem1"]], 1)
    full_gate, full_up = columns(full_m[..., :ff]), columns(full_m[..., ff : 2 * ff])
    full_down = columns(full_m[..., 2 * ff :]).T
    full_q = columns(full_a[..., :head])
    full_out = columns(full_a[..., head : 2 * head]).T
    full_kv = full_a[..., 2 * head :].astype(f32)
    full_kv = [full_kv[0] + full_kv[1], full_kv[2] + full_kv[3]]
    full_k, full_v = (
        jnp.concatenate([half[:, i * head : (i + 1) * head] for half in full_kv], 1) for i in (0, 1)
    )
    return (
        section_out.astype(f32)[None],
        full_q[None],
        full_k[None],
        full_v[None],
        full_out[None],
        full_gate[None],
        full_up[None],
        full_down[None],
        sums[None, :model],
        sums[None, model : 2 * model],
        sums[None, 2 * model : 2 * model + head],
        sums[None, 2 * model + head :],
    )


def solution(mesh):
    sections, row_count, col_count = (mesh.shape[name] for name in ("section", "row", "col"))
    shape = (sections, 2, 2, row_count // 4, 2, col_count // 2)
    mesh = Mesh(np.asarray(mesh.devices).reshape(shape), ("s", "h", "t", "g", "y", "k"))
    row, col = ("h", "t", "g"), ("y", "k")
    in_row, in_col = P("s", row, col), P("s", col, row)
    return jax.shard_map(
        body,
        mesh=mesh,
        in_specs=(
            P("s", None, row, col), P(), in_row, in_row, in_row, in_col, in_row, in_row, in_col,
            P("s", col), P("s", col), P("s", None), P("s", None),
        ),
        out_specs=(
            P("s", None, row, col), in_row, in_row, in_row, in_col, in_row, in_row, in_col,
            P("s", None), P("s", None), P("s", None), P("s", None),
        ),
        check_vma=False,
    )
```

time: 1520 us -> 1110 us (0.73)
  local copies, waits for them, and re-layouts: 237 us -> 89.9 us
  blocking collectives: 97.4 us -> 0 us
  other arithmetic: 161 us -> 92.3 us
  waiting for transfers between devices: 721 us -> 673 us
  starting transfers between devices: 172 us -> 148 us
  matrix products: 113 us -> 95.2 us
    ppermute x170 -> x108, waiting for transfers between devices: 716 us -> 456 us  [swap(): return lax.ppermute(value, axis, [(0, 1), (1, 0)])]
    ppermute x0 -> x16, waiting for transfers between devices: none -> 211 us  [cross(): return lax.ppermute(value, ('s', 't'), [(i, 3 - i) for i in range(4)])]
    ppermute x170 -> x108, starting transfers between devices: 164 us -> 90.1 us  [swap(): return lax.ppermute(value, axis, [(0, 1), (1, 0)])]
    all_gather x1 -> x0, blocking collectives: 51.8 us -> none  [body(): lax.all_gather(packed, ('s', 'y', 'k'), axis=0).reshape(2, cols, -1)]
    unnamed x605 -> x413, local copies, waits for them, and re-layouts: 99.3 us -> 52.5 us
    psum x1 -> x0, blocking collectives: 45.6 us -> none  [body(): lax.psum(sums, ('s', 'h', 't', 'g', 'y', 'k')).reshape(2, -1)]
    another operation x51 -> x5, other arithmetic: 38.3 us -> 0.11 us  [pair(): return jnp.stack([low, high], axis)]
    reshape x18 -> x1, local copies, waits for them, and re-layouts: 37.2 us -> 0.79 us  [body(): sums = jnp.concatenate(sums).reshape(2, -1)]
  transfers between devices with their start and end apart: 172 -> 132, of which waited for: 87 -> 81; matrix products, arithmetic and copies ran while one was open for 28% -> 16% of each run, Pallas kernels for 0% -> 0%
where the time goes in v2:
time: 1110 us; the launch traced here: 1100 us
  waiting for transfers between devices  673 us (61%)
  starting transfers between devices  148 us (13%)
  matrix products  95.2 us (9%)
  other arithmetic  92.3 us (8%)
  local copies, waits for them, and re-layouts  89.9 us (8%)
    ppermute x108, waiting for transfers between devices, swap(): return lax.ppermute(value, axis, [(0, 1), (1, 0)])  456 us
    ppermute x16, waiting for transfers between devices, cross(): return lax.ppermute(value, ('s', 't'), [(i, 3 - i) for i in range(4)])  211 us
    ppermute x108, starting transfers between devices, swap(): return lax.ppermute(value, axis, [(0, 1), (1, 0)])  90.1 us
    unnamed x413, local copies, waits for them, and re-layouts  52.5 us
    dot_general x40, matrix products, dot_t(): lax.dot_general(left, right, (((1,), (1,)), ((), ())), preferred_element_...  39.6 us
    all_to_all x8, starting transfers between devices, exchange(): return lax.all_to_all(value, axes, 0, 0, tiled=True)  33.8 us
    dot_general x20, matrix products, t_dot(): lax.dot_general(left, right, (((0,), (0,)), ((), ())), preferred_element_...  26.6 us
    ppermute x16, starting transfers between devices, cross(): return lax.ppermute(value, ('s', 't'), [(i, 3 - i) for i in range(4)])  24.1 us
  transfers between devices with their start and end apart: 132, of which 81 were waited for; matrix products, arithmetic and copies ran while one was open for 16% of the time, Pallas kernels for 0%

profile of v2, /device:TPU:0, one launch (start us, length us, event | category | flops | bytes accessed | tf_op | source)
XLA Modules:
  0.0 1103.7 jit_solution(10282851899670216904)
XLA Ops:
  2.7 4.4 all-to-all-start
  27.4 3.8 all-to-all-start.1
  31.3 7.0 collective-permute-done
  40.0 20.3 %collective-permute-done.1 = bf16[64,2048]{1,0:T(8,128)(2,1)S(1)} collective-permute-done((bf16[64,2048]{1,0:T(8,128)(2,1)S(1)}, bf16[64,2048]{1,0:T(8,128)(2,1)S(1)}, u32[]{:S(2)}, u32[]{:S(2)}) %collective-permute-start.1) | collective-permute-done | bytes 262176 | tf_op jit(solution)/shard_map/ppermute | solution.py:16
  67.0 5.1 collective-permute-done.5
  73.1 3.9 collective-permute-done.7
  84.8 22.9 %collective-permute-done.9 = bf16[512,512]{1,0:T(8,128)(2,1)S(1)} collective-permute-done((bf16[512,512]{1,0:T(8,128)(2,1)S(1)}, bf16[512,512]{1,0:T(8,128)(2,1)S(1)}, u32[]{:S(2)}, u32[]{:S(2)}) %collective-permute-start.9) | collective-permute-done | bytes 524320 | tf_op jit(solution)/shard_map/ppermute | solution.py:16
  109.5 4.5 all-to-all-start.2
  124.6 26.5 %collective-permute-done.11 = bf16[512,512]{1,0:T(8,128)(2,1)S(1)} collective-permute-done((bf16[512,512]{1,0:T(8,128)(2,1)S(1)}, bf16[512,512]{1,0:T(8,128)(2,1)S(1)}, u32[]{:S(2)}, u32[]{:S(2)}) %collective-permute-start.11) | collective-permute-done | bytes 524320 | tf_op jit(solution)/shard_map/ppermute | solution.py:16
  164.7 4.7 all-to-all-start.3
  171.9 16.6 %collective-permute-done.13 = bf16[256,1152]{1,0:T(8,128)(2,1)} collective-permute-done((bf16[256,1152]{1,0:T(8,128)(2,1)}, bf16[256,1152]{1,0:T(8,128)(2,1)}, u32[]{:S(2)}, u32[]{:S(2)}) %collective-permute-start.13) | collective-permute-done | bytes 589856 | tf_op jit(solution)/shard_map/ppermute | solution.py:16
  204.7 21.0 %collective-permute-done.15 = bf16[256,1152]{1,0:T(8,128)(2,1)S(1)} collective-permute-done((bf16[256,1152]{1,0:T(8,128)(2,1)S(1)}, bf16[256,1152]{1,0:T(8,128)(2,1)S(1)}, u32[]{:S(2)}, u32[]{:S(2)}) %collective-permute-start.15) | collective-permute-done | bytes 589856 | tf_op jit(solution)/shard_map/ppermute | solution.py:16
  243.9 16.9 %collective-permute-done.19 = bf16[64,2048]{1,0:T(8,128)(2,1)S(1)} collective-permute-done((bf16[64,2048]{1,0:T(8,128)(2,1)S(1)}, bf16[64,2048]{1,0:T(8,128)(2,1)S(1)}, u32[]{:S(2)}, u32[]{:S(2)}) %collective-permute-start.19) | collective-permute-done | bytes 262176 | tf_op jit(solution)/shard_map/ppermute | solution.py:50
  260.7 4.6 collective-permute-done.18
  271.2 14.8 %collective-permute-done.24 = bf16[64,2048]{1,0:T(8,128)(2,1)S(1)} collective-permute-done((bf16[64,2048]{1,0:T(8,128)(2,1)S(1)}, bf16[64,2048]{1,0:T(8,128)(2,1)S(1)}, u32[]{:S(2)}, u32[]{:S(2)}) %collective-permute-start.24) | collective-permute-done | bytes 262176 | tf_op jit(solution)/shard_map/ppermute | solution.py:50
  288.2 9.8 collective-permute-done.26
  301.2 22.3 %collective-permute-done.29 = bf16[512,512]{1,0:T(8,128)(2,1)S(1)} collective-permute-done((bf16[512,512]{1,0:T(8,128)(2,1)S(1)}, bf16[512,512]{1,0:T(8,128)(2,1)S(1)}, u32[]{:S(2)}, u32[]{:S(2)}) %collective-permute-start.29) | collective-permute-done | bytes 524320 | tf_op jit(solution)/shard_map/ppermute | solution.py:16
  331.6 3.5 collective-permute-done.30
  336.6 4.8 collective-permute-done.32
  359.3 13.9 %collective-permute-done.37 = bf16[64,2048]{1,0:T(8,128)(2,1)S(1)} collective-permute-done((bf16[64,2048]{1,0:T(8,128)(2,1)S(1)}, bf16[64,2048]{1,0:T(8,128)(2,1)S(1)}, u32[]{:S(2)}, u32[]{:S(2)}) %collective-permute-start.37) | collective-permute-done | bytes 262176 | tf_op jit(solution)/shard_map/ppermute | solution.py:50
  373.2 4.2 collective-permute-done.36
  377.8 6.5 collective-permute-done.39
  389.6 14.4 %collective-permute-done.42 = bf16[64,2048]{1,0:T(8,128)(2,1)S(1)} collective-permute-done((bf16[64,2048]{1,0:T(8,128)(2,1)S(1)}, bf16[64,2048]{1,0:T(8,128)(2,1)S(1)}, u32[]{:S(2)}, u32[]{:S(2)}) %collective-permute-start.42) | collective-permute-done | bytes 262176 | tf_op jit(solution)/shard_map/ppermute | solution.py:50
  404.9 10.3 collective-permute-done.44
  426.7 16.9 %collective-permute-done.47 = bf16[256,1152]{1,0:T(8,128)(2,1)S(1)} collective-permute-done((bf16[256,1152]{1,0:T(8,128)(2,1)S(1)}, bf16[256,1152]{1,0:T(8,128)(2,1)S(1)}, u32[]{:S(2)}, u32[]{:S(2)}) %collective-permute-start.47) | collective-permute-done | bytes 589856 | tf_op jit(solution)/shard_map/ppermute | solution.py:16
  451.4 14.0 %collective-permute-done.51 = bf16[64,2048]{1,0:T(8,128)(2,1)S(1)} collective-permute-done((bf16[64,2048]{1,0:T(8,128)(2,1)S(1)}, bf16[64,2048]{1,0:T(8,128)(2,1)S(1)}, u32[]{:S(2)}, u32[]{:S(2)}) %collective-permute-start.51) | collective-permute-done | bytes 262176 | tf_op jit(solution)/shard_map/ppermute | solution.py:50
  465.4 5.2 collective-permute-done.50
  470.8 4.3 collective-permute-done.53
  480.7 14.5 %collective-permute-done.56 = bf16[64,2048]{1,0:T(8,128)(2,1)S(1)} collective-permute-done((bf16[64,2048]{1,0:T(8,128)(2,1)S(1)}, bf16[64,2048]{1,0:T(8,128)(2,1)S(1)}, u32[]{:S(2)}, u32[]{:S(2)}) %collective-permute-start.56) | collective-permute-done | bytes 262176 | tf_op jit(solution)/shard_map/ppermute | solution.py:50
  497.7 9.7 collective-permute-done.58
  510.3 25.6 %collective-permute-done.60 = bf16[512,1152]{1,0:T(8,128)(2,1)S(1)} collective-permute-done((bf16[512,1152]{1,0:T(8,128)(2,1)S(1)}, bf16[512,1152]{1,0:T(8,128)(2,1)S(1)}, u32[]{:S(2)}, u32[]{:S(2)}) %collective-permute-start.60) | collective-permute-done | bytes 1179680 | tf_op jit(solution)/shard_map/ppermute | solution.py:16
  554.7 5.2 convolution_convert_fusion.2
  572.9 4.6 collective-permute-done.64
  577.5 4.6 collective-permute-done.63
  582.8 15.7 %collective-permute-done.65 = bf16[512,1152]{1,0:T(8,128)(2,1)S(1)} collective-permute-done((bf16[512,1152]{1,0:T(8,128)(2,1)S(1)}, bf16[512,1152]{1,0:T(8,128)(2,1)S(1)}, u32[]{:S(2)}, u32[]{:S(2)}) %collective-permute-start.65) | collective-permute-done | bytes 1179680 | tf_op jit(solution)/shard_map/ppermute | solution.py:16
  604.7 14.1 %collective-permute-done.68 = bf16[64,2048]{1,0:T(8,128)(2,1)S(1)} collective-permute-done((bf16[64,2048]{1,0:T(8,128)(2,1)S(1)}, bf16[64,2048]{1,0:T(8,128)(2,1)S(1)}, u32[]{:S(2)}, u32[]{:S(2)}) %collective-permute-start.68) | collective-permute-done | bytes 262176 | tf_op jit(solution)/shard_map/ppermute | solution.py:50
  618.8 8.0 collective-permute-done.67
  647.0 9.7 collective-permute-done.72
  665.9 14.2 %collective-permute-done.77 = bf16[64,2048]{1,0:T(8,128)(2,1)S(1)} collective-permute-done((bf16[64,2048]{1,0:T(8,128)(2,1)S(1)}, bf16[64,2048]{1,0:T(8,128)(2,1)S(1)}, u32[]{:S(2)}, u32[]{:S(2)}) %collective-permute-start.77) | collective-permute-done | bytes 262176 | tf_op jit(solution)/shard_map/ppermute | solution.py:50
  684.4 8.4 collective-permute-done.78
  698.2 14.7 %collective-permute-done.82 = bf16[64,2048]{1,0:T(8,128)(2,1)S(1)} collective-permute-done((bf16[64,2048]{1,0:T(8,128)(2,1)S(1)}, bf16[64,2048]{1,0:T(8,128)(2,1)S(1)}, u32[]{:S(2)}, u32[]{:S(2)}) %collective-permute-start.82) | collective-permute-done | bytes 262176 | tf_op jit(solution)/shard_map/ppermute | solution.py:50
  713.9 10.3 collective-permute-done.83
  741.2 8.7 collective-permute-done.86
  765.9 12.3 %collective-permute-done.91 = bf16[64,2048]{1,0:T(8,128)(2,1)S(1)} collective-permute-done((bf16[64,2048]{1,0:T(8,128)(2,1)S(1)}, bf16[64,2048]{1,0:T(8,128)(2,1)S(1)}, u32[]{:S(2)}, u32[]{:S(2)}) %collective-permute-start.91) | collective-permute-done | bytes 262176 | tf_op jit(solution)/shard_map/ppermute | solution.py:50
  778.2 4.7 collective-permute-done.90
  783.0 4.8 collective-permute-done.92
  787.8 3.9 collective-permute-done.93
  798.2 14.6 %collective-permute-done.96 = bf16[64,2048]{1,0:T(8,128)(2,1)S(1)} collective-permute-done((bf16[64,2048]{1,0:T(8,128)(2,1)S(1)}, bf16[64,2048]{1,0:T(8,128)(2,1)S(1)}, u32[]{:S(2)}, u32[]{:S(2)}) %collective-permute-start.96) | collective-permute-done | bytes 262176 | tf_op jit(solution)/shard_map/ppermute | solution.py:50
  816.0 4.0 collective-permute-done.97
  845.7 4.1 collective-permute-done.100
  861.5 12.3 %collective-permute-done.105 = bf16[64,2048]{1,0:T(8,128)(2,1)S(1)} collective-permute-done((bf16[64,2048]{1,0:T(8,128)(2,1)S(1)}, bf16[64,2048]{1,0:T(8,128)(2,1)S(1)}, u32[]{:S(2)}, u32[]{:S(2)}) %collective-permute-start.105) | collective-permute-done | bytes 262176 | tf_op jit(solution)/shard_map/ppermute | solution.py:50
  873.8 8.9 collective-permute-done.104
  891.8 3.9 all-to-all-start.4
  917.0 26.8 %collective-permute-done.111 = bf16[64,2048]{1,0:T(8,128)(2,1)S(1)} collective-permute-done((bf16[64,2048]{1,0:T(8,128)(2,1)S(1)}, bf16[64,2048]{1,0:T(8,128)(2,1)S(1)}, u32[]{:S(2)}, u32[]{:S(2)}) %collective-permute-start.111) | collective-permute-done | bytes 262176 | tf_op jit(solution)/shard_map/ppermute | solution.py:50
  943.8 4.4 collective-permute-done.110
  956.0 4.6 all-to-all-start.5
  965.9 20.5 %collective-permute-done.117 = f32[2,4352]{1,0:T(2,128)S(1)} collective-permute-done((f32[2,4352]{1,0:T(2,128)S(1)}, f32[2,4352]{1,0:T(2,128)S(1)}, u32[]{:S(2)}, u32[]{:S(2)}) %collective-permute-start.117) | collective-permute-done | bytes 34848 | tf_op jit(solution)/shard_map/ppermute | solution.py:16
  988.2 6.0 collective-permute-done.115
  997.2 3.6 collective-permute-done.118
  1000.9 9.9 collective-permute-done.116
  1015.4 23.7 %collective-permute-done.121 = bf16[512,512]{1,0:T(8,128)(2,1)} collective-permute-done((bf16[512,512]{1,0:T(8,128)(2,1)S(1)}, bf16[512,512]{1,0:T(8,128)(2,1)}, u32[]{:S(2)}, u32[]{:S(2)}) %collective-permute-start.121) | collective-permute-done | bytes 524320 | tf_op jit(solution)/shard_map/ppermute | solution.py:16
  1052.2 4.7 all-to-all-done.6
  1057.7 4.5 all-to-all-start.7
  1071.2 16.6 %collective-permute-done.122 = f32[2,4352]{1,0:T(2,128)S(1)} collective-permute-done((f32[2,4352]{1,0:T(2,128)S(1)}, f32[2,4352]{1,0:T(2,128)S(1)}, u32[]{:S(2)}, u32[]{:S(2)}) %collective-permute-start.122) | collective-permute-done | bytes 34848 | tf_op jit(solution)/shard_map/ppermute | solution.py:16
  (1014 shorter events, 424.7 us)
Async XLA Ops:
  27.4 33.9 %all-to-all-start.1 = ((bf16[4,512,512]{2,1,0:T(8,128)(2,1)}), bf16[4,512,512]{2,1,0:T(8,128)(2,1)S(1)}, u32[]{:S(2)}, u32[]{:S(2)}) async-start(bf16[4,512,512]{2,1,0:T(8,128)(2,1)} %pad_maximum_fusion.8), calls=%async_computation.1 | async-start | bytes 4194304 | tf_op jit(solution)/shard_map/all_to_all | solution.py:20
  81.2 26.4 %collective-permute-start.9 = (bf16[512,512]{1,0:T(8,128)(2,1)S(1)}, bf16[512,512]{1,0:T(8,128)(2,1)S(1)}, u32[]{:S(2)}, u32[]{:S(2)}) collective-permute-start(bf16[512,512]{1,0:T(8,128)(2,1)S(1)} %get-tuple-element.223), channel_id=1, source_target_pairs={{0,8},{8,0},{1,9},{9,1},{2,10},{10,2},{3,11},{11,3},{4,12},{12,4},... | collective-permute-start | bytes 1572872 | tf_op jit(solution)/shard_map/ppermute | solution.py:16
  109.5 44.0 %all-to-all-start.2 = ((bf16[4,256,1152]{2,1,0:T(8,128)(2,1)}), bf16[4,256,1152]{2,1,0:T(8,128)(2,1)}, u32[]{:S(2)}, u32[]{:S(2)}) async-start(bf16[4,256,1152]{2,1,0:T(8,128)(2,1)} %pad_maximum_fusion.4), calls=%async_computation.2 | async-start | bytes 4718592 | tf_op jit(solution)/shard_map/all_to_all | solution.py:20
  123.2 28.7 %collective-permute-start.10 = (bf16[1024,512]{1,0:T(8,128)(2,1)S(1)}, bf16[1024,512]{1,0:T(8,128)(2,1)}, u32[]{:S(2)}, u32[]{:S(2)}) collective-permute-start(bf16[1024,512]{1,0:T(8,128)(2,1)S(1)} %copy-done.124), channel_id=1, source_target_pairs={{0,2},{2,0},{1,3},{3,1},{4,6},{6,4},{5,7},{7,5},{8,10},{10,8},{9,1... | collective-permute-start | bytes 3145736 | tf_op jit(solution)/shard_map/ppermute | solution.py:16
  123.7 27.4 %collective-permute-start.11 = (bf16[512,512]{1,0:T(8,128)(2,1)S(1)}, bf16[512,512]{1,0:T(8,128)(2,1)S(1)}, u32[]{:S(2)}, u32[]{:S(2)}) collective-permute-start(bf16[512,512]{1,0:T(8,128)(2,1)S(1)} %get-tuple-element.232), channel_id=1, source_target_pairs={{0,8},{8,0},{1,9},{9,1},{2,10},{10,2},{3,11},{11,3},{4,12},{12,4},... | collective-permute-start | bytes 1572872 | tf_op jit(solution)/shard_map/ppermute | solution.py:16
  158.7 29.8 %collective-permute-start.12 = (bf16[1024,512]{1,0:T(8,128)(2,1)}, bf16[1024,512]{1,0:T(8,128)(2,1)}, u32[]{:S(2)}, u32[]{:S(2)}) collective-permute-start(bf16[1024,512]{1,0:T(8,128)(2,1)} %pad_maximum_fusion.42), channel_id=1, source_target_pairs={{0,2},{2,0},{1,3},{3,1},{4,6},{6,4},{5,7},{7,5},{8,10},{10,8},{9,1... | collective-permute-start | bytes 3145736 | tf_op jit(solution)/shard_map/ppermute | solution.py:16
  160.4 28.1 %collective-permute-start.13 = (bf16[256,1152]{1,0:T(8,128)(2,1)}, bf16[256,1152]{1,0:T(8,128)(2,1)}, u32[]{:S(2)}, u32[]{:S(2)}) collective-permute-start(bf16[256,1152]{1,0:T(8,128)(2,1)} %get-tuple-element.238), channel_id=1, source_target_pairs={{0,8},{8,0},{1,9},{9,1},{2,10},{10,2},{3,11},{11,3},{4,12},{12,4},... | collective-permute-start | bytes 1769480 | tf_op jit(solution)/shard_map/ppermute | solution.py:16
  164.7 61.8 %all-to-all-start.3 = ((bf16[4,256,1152]{2,1,0:T(8,128)(2,1)}), bf16[4,256,1152]{2,1,0:T(8,128)(2,1)}, u32[]{:S(2)}, u32[]{:S(2)}) async-start(bf16[4,256,1152]{2,1,0:T(8,128)(2,1)} %pad_maximum_fusion.5), calls=%async_computation.3 | async-start | bytes 4718592 | tf_op jit(solution)/shard_map/all_to_all | solution.py:20
  196.5 30.0 %collective-permute-start.14 = (bf16[512,1152]{1,0:T(8,128)(2,1)S(1)}, bf16[512,1152]{1,0:T(8,128)(2,1)}, u32[]{:S(2)}, u32[]{:S(2)}) collective-permute-start(bf16[512,1152]{1,0:T(8,128)(2,1)S(1)} %pad_maximum_fusion.24), channel_id=1, source_target_pairs={{0,2},{2,0},{1,3},{3,1},{4,6},{6,4},{5,7},{7,5},{8,10},{10,8},{9,1... | collective-permute-start | bytes 3538952 | tf_op jit(solution)/shard_map/ppermute | solution.py:16
  198.3 27.3 %collective-permute-start.15 = (bf16[256,1152]{1,0:T(8,128)(2,1)S(1)}, bf16[256,1152]{1,0:T(8,128)(2,1)S(1)}, u32[]{:S(2)}, u32[]{:S(2)}) collective-permute-start(bf16[256,1152]{1,0:T(8,128)(2,1)S(1)} %copy-done.71), channel_id=1, source_target_pairs={{0,8},{8,0},{1,9},{9,1},{2,10},{10,2},{3,11},{11,3},{4,12},{12,4},... | collective-permute-start | bytes 1769480 | tf_op jit(solution)/shard_map/ppermute | solution.py:16
  229.6 35.9 %collective-permute-start.20 = (bf16[512,1152]{1,0:T(8,128)(2,1)S(1)}, bf16[512,1152]{1,0:T(8,128)(2,1)S(1)}, u32[]{:S(2)}, u32[]{:S(2)}) collective-permute-start(bf16[512,1152]{1,0:T(8,128)(2,1)S(1)} %pad_maximum_fusion.25), channel_id=1, source_target_pairs={{0,2},{2,0},{1,3},{3,1},{4,6},{6,4},{5,7},{7,5},{8,10},{10,8},{9,1... | collective-permute-start | bytes 3538952 | tf_op jit(solution)/shard_map/ppermute | solution.py:16
  230.4 35.1 %collective-permute-start.21 = (bf16[256,1152]{1,0:T(8,128)(2,1)S(1)}, bf16[256,1152]{1,0:T(8,128)(2,1)S(1)}, u32[]{:S(2)}, u32[]{:S(2)}) collective-permute-start(bf16[256,1152]{1,0:T(8,128)(2,1)S(1)} %get-tuple-element.254), channel_id=1, source_target_pairs={{0,8},{8,0},{1,9},{9,1},{2,10},{10,2},{3,11},{11,3},{4,12},{12,4},... | collective-permute-start | bytes 1769480 | tf_op jit(solution)/shard_map/ppermute | solution.py:16
  240.4 24.9 %collective-permute-start.18 = (bf16[64,2048]{1,0:T(8,128)(2,1)S(1)}, bf16[64,2048]{1,0:T(8,128)(2,1)S(1)}, u32[]{:S(2)}, u32[]{:S(2)}) collective-permute-start(bf16[64,2048]{1,0:T(8,128)(2,1)S(1)} %get-tuple-element.660), channel_id=1, source_target_pairs={{0,4},{4,0},{1,5},{5,1},{2,6},{6,2},{3,7},{7,3},{8,12},{12,8},{9,1... | collective-permute-start | bytes 786440 | tf_op jit(solution)/shard_map/ppermute | solution.py:16
  240.8 24.5 %collective-permute-start.17 = (bf16[64,2048]{1,0:T(8,128)(2,1)S(1)}, bf16[64,2048]{1,0:T(8,128)(2,1)S(1)}, u32[]{:S(2)}, u32[]{:S(2)}) collective-permute-start(bf16[64,2048]{1,0:T(8,128)(2,1)S(1)} %get-tuple-element.658), channel_id=1, source_target_pairs={{0,16},{16,0},{1,17},{17,1},{2,18},{18,2},{3,19},{19,3},{4,20},{20... | collective-permute-start | bytes 786440 | tf_op jit(solution)/shard_map/ppermute | solution.py:16
  265.8 32.3 %collective-permute-start.25 = (bf16[512,1152]{1,0:T(8,128)(2,1)S(1)}, bf16[512,1152]{1,0:T(8,128)(2,1)S(1)}, u32[]{:S(2)}, u32[]{:S(2)}) collective-permute-start(bf16[512,1152]{1,0:T(8,128)(2,1)S(1)} %pad_maximum_fusion.26), channel_id=1, source_target_pairs={{0,2},{2,0},{1,3},{3,1},{4,6},{6,4},{5,7},{7,5},{8,10},{10,8},{9,1... | collective-permute-start | bytes 3538952 | tf_op jit(solution)/shard_map/ppermute | solution.py:16
  271.0 27.0 %collective-permute-start.26 = (bf16[256,1152]{1,0:T(8,128)(2,1)S(1)}, bf16[256,1152]{1,0:T(8,128)(2,1)S(1)}, u32[]{:S(2)}, u32[]{:S(2)}) collective-permute-start(bf16[256,1152]{1,0:T(8,128)(2,1)S(1)} %get-tuple-element.259), channel_id=1, source_target_pairs={{0,8},{8,0},{1,9},{9,1},{2,10},{10,2},{3,11},{11,3},{4,12},{12,4},... | collective-permute-start | bytes 1769480 | tf_op jit(solution)/shard_map/ppermute | solution.py:16
  298.2 28.4 %collective-permute-start.28 = (bf16[512,1152]{1,0:T(8,128)(2,1)S(1)}, bf16[512,1152]{1,0:T(8,128)(2,1)S(1)}, u32[]{:S(2)}, u32[]{:S(2)}) collective-permute-start(bf16[512,1152]{1,0:T(8,128)(2,1)S(1)} %pad_maximum_fusion.27), channel_id=1, source_target_pairs={{0,2},{2,0},{1,3},{3,1},{4,6},{6,4},{5,7},{7,5},{8,10},{10,8},{9,1... | collective-permute-start | bytes 3538952 | tf_op jit(solution)/shard_map/ppermute | solution.py:16
  298.8 24.6 %collective-permute-start.29 = (bf16[512,512]{1,0:T(8,128)(2,1)S(1)}, bf16[512,512]{1,0:T(8,128)(2,1)S(1)}, u32[]{:S(2)}, u32[]{:S(2)}) collective-permute-start(bf16[512,512]{1,0:T(8,128)(2,1)S(1)} %copy-done.33), channel_id=1, source_target_pairs={{0,8},{8,0},{1,9},{9,1},{2,10},{10,2},{3,11},{11,3},{4,12},{12,4},... | collective-permute-start | bytes 1572872 | tf_op jit(solution)/shard_map/ppermute | solution.py:16
  358.7 25.6 %collective-permute-start.38 = (bf16[1024,512]{1,0:T(8,128)(2,1)S(1)}, bf16[1024,512]{1,0:T(8,128)(2,1)S(1)}, u32[]{:S(2)}, u32[]{:S(2)}) collective-permute-start(bf16[1024,512]{1,0:T(8,128)(2,1)S(1)} %pad_maximum_fusion.44), channel_id=1, source_target_pairs={{0,2},{2,0},{1,3},{3,1},{4,6},{6,4},{5,7},{7,5},{8,10},{10,8},{9,1... | collective-permute-start | bytes 3145736 | tf_op jit(solution)/shard_map/ppermute | solution.py:16
  359.3 25.0 %collective-permute-start.39 = (bf16[512,512]{1,0:T(8,128)(2,1)S(1)}, bf16[512,512]{1,0:T(8,128)(2,1)S(1)}, u32[]{:S(2)}, u32[]{:S(2)}) collective-permute-start(bf16[512,512]{1,0:T(8,128)(2,1)S(1)} %copy-done.32), channel_id=1, source_target_pairs={{0,8},{8,0},{1,9},{9,1},{2,10},{10,2},{3,11},{11,3},{4,12},{12,4},... | collective-permute-start | bytes 1572872 | tf_op jit(solution)/shard_map/ppermute | solution.py:16
  384.4 30.9 %collective-permute-start.43 = (bf16[1024,512]{1,0:T(8,128)(2,1)S(1)}, bf16[1024,512]{1,0:T(8,128)(2,1)S(1)}, u32[]{:S(2)}, u32[]{:S(2)}) collective-permute-start(bf16[1024,512]{1,0:T(8,128)(2,1)S(1)} %pad_maximum_fusion.46), channel_id=1, source_target_pairs={{0,2},{2,0},{1,3},{3,1},{4,6},{6,4},{5,7},{7,5},{8,10},{10,8},{9,1... | collective-permute-start | bytes 3145736 | tf_op jit(solution)/shard_map/ppermute | solution.py:16
  389.4 25.8 %collective-permute-start.44 = (bf16[256,1152]{1,0:T(8,128)(2,1)S(1)}, bf16[256,1152]{1,0:T(8,128)(2,1)S(1)}, u32[]{:S(2)}, u32[]{:S(2)}) collective-permute-start(bf16[256,1152]{1,0:T(8,128)(2,1)S(1)} %copy-done.64), channel_id=1, source_target_pairs={{0,8},{8,0},{1,9},{9,1},{2,10},{10,2},{3,11},{11,3},{4,12},{12,4},... | collective-permute-start | bytes 1769480 | tf_op jit(solution)/shard_map/ppermute | solution.py:16
  415.5 28.4 %collective-permute-start.46 = (bf16[512,1152]{1,0:T(8,128)(2,1)S(1)}, bf16[512,1152]{1,0:T(8,128)(2,1)S(1)}, u32[]{:S(2)}, u32[]{:S(2)}) collective-permute-start(bf16[512,1152]{1,0:T(8,128)(2,1)S(1)} %pad_maximum_fusion.28), channel_id=1, source_target_pairs={{0,2},{2,0},{1,3},{3,1},{4,6},{6,4},{5,7},{7,5},{8,10},{10,8},{9,1... | collective-permute-start | bytes 3538952 | tf_op jit(solution)/shard_map/ppermute | solution.py:16
  416.4 27.3 %collective-permute-start.47 = (bf16[256,1152]{1,0:T(8,128)(2,1)S(1)}, bf16[256,1152]{1,0:T(8,128)(2,1)S(1)}, u32[]{:S(2)}, u32[]{:S(2)}) collective-permute-start(bf16[256,1152]{1,0:T(8,128)(2,1)S(1)} %copy-done.63), channel_id=1, source_target_pairs={{0,8},{8,0},{1,9},{9,1},{2,10},{10,2},{3,11},{11,3},{4,12},{12,4},... | collective-permute-start | bytes 1769480 | tf_op jit(solution)/shard_map/ppermute | solution.py:16
  444.8 30.2 %collective-permute-start.52 = (bf16[512,1152]{1,0:T(8,128)(2,1)S(1)}, bf16[512,1152]{1,0:T(8,128)(2,1)S(1)}, u32[]{:S(2)}, u32[]{:S(2)}) collective-permute-start(bf16[512,1152]{1,0:T(8,128)(2,1)S(1)} %pad_maximum_fusion.29), channel_id=1, source_target_pairs={{0,2},{2,0},{1,3},{3,1},{4,6},{6,4},{5,7},{7,5},{8,10},{10,8},{9,1... | collective-permute-start | bytes 3538952 | tf_op jit(solution)/shard_map/ppermute | solution.py:16
  446.1 28.9 %collective-permute-start.53 = (bf16[256,1152]{1,0:T(8,128)(2,1)S(1)}, bf16[256,1152]{1,0:T(8,128)(2,1)S(1)}, u32[]{:S(2)}, u32[]{:S(2)}) collective-permute-start(bf16[256,1152]{1,0:T(8,128)(2,1)S(1)} %get-tuple-element.296), channel_id=1, source_target_pairs={{0,8},{8,0},{1,9},{9,1},{2,10},{10,2},{3,11},{11,3},{4,12},{12,4},... | collective-permute-start | bytes 1769480 | tf_op jit(solution)/shard_map/ppermute | solution.py:16
  475.3 32.1 %collective-permute-start.57 = (bf16[512,1152]{1,0:T(8,128)(2,1)S(1)}, bf16[512,1152]{1,0:T(8,128)(2,1)S(1)}, u32[]{:S(2)}, u32[]{:S(2)}) collective-permute-start(bf16[512,1152]{1,0:T(8,128)(2,1)S(1)} %pad_maximum_fusion.30), channel_id=1, source_target_pairs={{0,2},{2,0},{1,3},{3,1},{4,6},{6,4},{5,7},{7,5},{8,10},{10,8},{9,1... | collective-permute-start | bytes 3538952 | tf_op jit(solution)/shard_map/ppermute | solution.py:16
  480.4 27.0 %collective-permute-start.58 = (bf16[256,1152]{1,0:T(8,128)(2,1)S(1)}, bf16[256,1152]{1,0:T(8,128)(2,1)S(1)}, u32[]{:S(2)}, u32[]{:S(2)}) collective-permute-start(bf16[256,1152]{1,0:T(8,128)(2,1)S(1)} %get-tuple-element.301), channel_id=1, source_target_pairs={{0,8},{8,0},{1,9},{9,1},{2,10},{10,2},{3,11},{11,3},{4,12},{12,4},... | collective-permute-start | bytes 1769480 | tf_op jit(solution)/shard_map/ppermute | solution.py:16
  507.5 28.4 %collective-permute-start.60 = (bf16[512,1152]{1,0:T(8,128)(2,1)S(1)}, bf16[512,1152]{1,0:T(8,128)(2,1)S(1)}, u32[]{:S(2)}, u32[]{:S(2)}) collective-permute-start(bf16[512,1152]{1,0:T(8,128)(2,1)S(1)} %pad_maximum_fusion.31), channel_id=1, source_target_pairs={{0,2},{2,0},{1,3},{3,1},{4,6},{6,4},{5,7},{7,5},{8,10},{10,8},{9,1... | collective-permute-start | bytes 3538952 | tf_op jit(solution)/shard_map/ppermute | solution.py:16
  570.9 27.5 %collective-permute-start.65 = (bf16[512,1152]{1,0:T(8,128)(2,1)S(1)}, bf16[512,1152]{1,0:T(8,128)(2,1)S(1)}, u32[]{:S(2)}, u32[]{:S(2)}) collective-permute-start(bf16[512,1152]{1,0:T(8,128)(2,1)S(1)} %pad_maximum_fusion.32), channel_id=1, source_target_pairs={{0,2},{2,0},{1,3},{3,1},{4,6},{6,4},{5,7},{7,5},{8,10},{10,8},{9,1... | collective-permute-start | bytes 3538952 | tf_op jit(solution)/shard_map/ppermute | solution.py:16
  599.0 27.9 %collective-permute-start.69 = (bf16[256,1152]{1,0:T(8,128)(2,1)S(1)}, bf16[256,1152]{1,0:T(8,128)(2,1)S(1)}, u32[]{:S(2)}, u32[]{:S(2)}) collective-permute-start(bf16[256,1152]{1,0:T(8,128)(2,1)S(1)} %slice.1705), channel_id=1, source_target_pairs={{0,8},{8,0},{1,9},{9,1},{2,10},{10,2},{3,11},{11,3},{4,12},{12,4},... | collective-permute-start | bytes 1769480 | tf_op jit(solution)/shard_map/ppermute | solution.py:16
  599.4 27.5 %collective-permute-start.70 = (bf16[512,1152]{1,0:T(8,128)(2,1)S(1)}, bf16[512,1152]{1,0:T(8,128)(2,1)S(1)}, u32[]{:S(2)}, u32[]{:S(2)}) collective-permute-start(bf16[512,1152]{1,0:T(8,128)(2,1)S(1)} %pad_maximum_fusion.33), channel_id=1, source_target_pairs={{0,2},{2,0},{1,3},{3,1},{4,6},{6,4},{5,7},{7,5},{8,10},{10,8},{9,1... | collective-permute-start | bytes 3538952 | tf_op jit(solution)/shard_map/ppermute | solution.py:16
  603.7 23.1 %collective-permute-start.67 = (bf16[64,2048]{1,0:T(8,128)(2,1)S(1)}, bf16[64,2048]{1,0:T(8,128)(2,1)S(1)}, u32[]{:S(2)}, u32[]{:S(2)}) collective-permute-start(bf16[64,2048]{1,0:T(8,128)(2,1)S(1)} %get-tuple-element.497), channel_id=1, source_target_pairs={{0,4},{4,0},{1,5},{5,1},{2,6},{6,2},{3,7},{7,3},{8,12},{12,8},{9,1... | collective-permute-start | bytes 786440 | tf_op jit(solution)/shard_map/ppermute | solution.py:16
  627.5 29.3 %collective-permute-start.72 = (bf16[256,1152]{1,0:T(8,128)(2,1)S(1)}, bf16[256,1152]{1,0:T(8,128)(2,1)S(1)}, u32[]{:S(2)}, u32[]{:S(2)}) collective-permute-start(bf16[256,1152]{1,0:T(8,128)(2,1)S(1)} %slice.1706), channel_id=1, source_target_pairs={{0,8},{8,0},{1,9},{9,1},{2,10},{10,2},{3,11},{11,3},{4,12},{12,4},... | collective-permute-start | bytes 1769480 | tf_op jit(solution)/shard_map/ppermute | solution.py:16
  629.0 28.1 %collective-permute-start.73 = (bf16[512,1152]{1,0:T(8,128)(2,1)S(1)}, bf16[512,1152]{1,0:T(8,128)(2,1)S(1)}, u32[]{:S(2)}, u32[]{:S(2)}) collective-permute-start(bf16[512,1152]{1,0:T(8,128)(2,1)S(1)} %pad_maximum_fusion.34), channel_id=1, source_target_pairs={{0,2},{2,0},{1,3},{3,1},{4,6},{6,4},{5,7},{7,5},{8,10},{10,8},{9,1... | collective-permute-start | bytes 3538952 | tf_op jit(solution)/shard_map/ppermute | solution.py:16
  658.8 34.0 %collective-permute-start.79 = (bf16[512,1152]{1,0:T(8,128)(2,1)S(1)}, bf16[512,1152]{1,0:T(8,128)(2,1)S(1)}, u32[]{:S(2)}, u32[]{:S(2)}) collective-permute-start(bf16[512,1152]{1,0:T(8,128)(2,1)S(1)} %pad_maximum_fusion.35), channel_id=1, source_target_pairs={{0,2},{2,0},{1,3},{3,1},{4,6},{6,4},{5,7},{7,5},{8,10},{10,8},{9,1... | collective-permute-start | bytes 3538952 | tf_op jit(solution)/shard_map/ppermute | solution.py:16
  664.5 28.3 %collective-permute-start.78 = (bf16[256,1152]{1,0:T(8,128)(2,1)S(1)}, bf16[256,1152]{1,0:T(8,128)(2,1)S(1)}, u32[]{:S(2)}, u32[]{:S(2)}) collective-permute-start(bf16[256,1152]{1,0:T(8,128)(2,1)S(1)} %slice.1719), channel_id=1, source_target_pairs={{0,8},{8,0},{1,9},{9,1},{2,10},{10,2},{3,11},{11,3},{4,12},{12,4},... | collective-permute-start | bytes 1769480 | tf_op jit(solution)/shard_map/ppermute | solution.py:16
  693.1 31.1 %collective-permute-start.84 = (bf16[1024,512]{1,0:T(8,128)(2,1)S(1)}, bf16[1024,512]{1,0:T(8,128)(2,1)S(1)}, u32[]{:S(2)}, u32[]{:S(2)}) collective-permute-start(bf16[1024,512]{1,0:T(8,128)(2,1)S(1)} %pad_maximum_fusion.50), channel_id=1, source_target_pairs={{0,2},{2,0},{1,3},{3,1},{4,6},{6,4},{5,7},{7,5},{8,10},{10,8},{9,1... | collective-permute-start | bytes 3145736 | tf_op jit(solution)/shard_map/ppermute | solution.py:16
  698.0 26.1 %collective-permute-start.83 = (bf16[256,1152]{1,0:T(8,128)(2,1)S(1)}, bf16[256,1152]{1,0:T(8,128)(2,1)S(1)}, u32[]{:S(2)}, u32[]{:S(2)}) collective-permute-start(bf16[256,1152]{1,0:T(8,128)(2,1)S(1)} %slice.1724), channel_id=1, source_target_pairs={{0,8},{8,0},{1,9},{9,1},{2,10},{10,2},{3,11},{11,3},{4,12},{12,4},... | collective-permute-start | bytes 1769480 | tf_op jit(solution)/shard_map/ppermute | solution.py:16
  724.8 25.1 %collective-permute-start.86 = (bf16[512,512]{1,0:T(8,128)(2,1)S(1)}, bf16[512,512]{1,0:T(8,128)(2,1)S(1)}, u32[]{:S(2)}, u32[]{:S(2)}) collective-permute-start(bf16[512,512]{1,0:T(8,128)(2,1)S(1)} %slice.1735), channel_id=1, source_target_pairs={{0,8},{8,0},{1,9},{9,1},{2,10},{10,2},{3,11},{11,3},{4,12},{12,4},... | collective-permute-start | bytes 1572872 | tf_op jit(solution)/shard_map/ppermute | solution.py:16
  724.8 25.6 %collective-permute-start.87 = (bf16[1024,512]{1,0:T(8,128)(2,1)S(1)}, bf16[1024,512]{1,0:T(8,128)(2,1)S(1)}, u32[]{:S(2)}, u32[]{:S(2)}) collective-permute-start(bf16[1024,512]{1,0:T(8,128)(2,1)S(1)} %pad_maximum_fusion.52), channel_id=1, source_target_pairs={{0,2},{2,0},{1,3},{3,1},{4,6},{6,4},{5,7},{7,5},{8,10},{10,8},{9,1... | collective-permute-start | bytes 3145736 | tf_op jit(solution)/shard_map/ppermute | solution.py:16
  761.9 25.9 %collective-permute-start.92 = (bf16[512,512]{1,0:T(8,128)(2,1)}, bf16[512,512]{1,0:T(8,128)(2,1)S(1)}, u32[]{:S(2)}, u32[]{:S(2)}) collective-permute-start(bf16[512,512]{1,0:T(8,128)(2,1)} %slice.1750), channel_id=1, source_target_pairs={{0,8},{8,0},{1,9},{9,1},{2,10},{10,2},{3,11},{11,3},{4,12},{12,4},... | collective-permute-start | bytes 1572872 | tf_op jit(solution)/shard_map/ppermute | solution.py:16
  764.5 27.3 %collective-permute-start.93 = (bf16[512,1152]{1,0:T(8,128)(2,1)S(1)}, bf16[512,1152]{1,0:T(8,128)(2,1)S(1)}, u32[]{:S(2)}, u32[]{:S(2)}) collective-permute-start(bf16[512,1152]{1,0:T(8,128)(2,1)S(1)} %pad_maximum_fusion.36), channel_id=1, source_target_pairs={{0,2},{2,0},{1,3},{3,1},{4,6},{6,4},{5,7},{7,5},{8,10},{10,8},{9,1... | collective-permute-start | bytes 3538952 | tf_op jit(solution)/shard_map/ppermute | solution.py:16
  793.0 27.0 %collective-permute-start.97 = (bf16[256,1152]{1,0:T(8,128)(2,1)S(1)}, bf16[256,1152]{1,0:T(8,128)(2,1)S(1)}, u32[]{:S(2)}, u32[]{:S(2)}) collective-permute-start(bf16[256,1152]{1,0:T(8,128)(2,1)S(1)} %slice.1751), channel_id=1, source_target_pairs={{0,8},{8,0},{1,9},{9,1},{2,10},{10,2},{3,11},{11,3},{4,12},{12,4},... | collective-permute-start | bytes 1769480 | tf_op jit(solution)/shard_map/ppermute | solution.py:16
  793.4 26.6 %collective-permute-start.98 = (bf16[512,1152]{1,0:T(8,128)(2,1)S(1)}, bf16[512,1152]{1,0:T(8,128)(2,1)S(1)}, u32[]{:S(2)}, u32[]{:S(2)}) collective-permute-start(bf16[512,1152]{1,0:T(8,128)(2,1)S(1)} %pad_maximum_fusion.37), channel_id=1, source_target_pairs={{0,2},{2,0},{1,3},{3,1},{4,6},{6,4},{5,7},{7,5},{8,10},{10,8},{9,1... | collective-permute-start | bytes 3538952 | tf_op jit(solution)/shard_map/ppermute | solution.py:16
  820.5 29.3 %collective-permute-start.100 = (bf16[256,1152]{1,0:T(8,128)(2,1)S(1)}, bf16[256,1152]{1,0:T(8,128)(2,1)S(1)}, u32[]{:S(2)}, u32[]{:S(2)}) collective-permute-start(bf16[256,1152]{1,0:T(8,128)(2,1)S(1)} %slice.1752), channel_id=1, source_target_pairs={{0,8},{8,0},{1,9},{9,1},{2,10},{10,2},{3,11},{11,3},{4,12},{12,4},... | collective-permute-start | bytes 1769480 | tf_op jit(solution)/shard_map/ppermute | solution.py:16
  822.6 28.1 %collective-permute-start.101 = (bf16[512,1152]{1,0:T(8,128)(2,1)S(1)}, bf16[512,1152]{1,0:T(8,128)(2,1)S(1)}, u32[]{:S(2)}, u32[]{:S(2)}) collective-permute-start(bf16[512,1152]{1,0:T(8,128)(2,1)S(1)} %pad_maximum_fusion.38), channel_id=1, source_target_pairs={{0,2},{2,0},{1,3},{3,1},{4,6},{6,4},{5,7},{7,5},{8,10},{10,8},{9,1... | collective-permute-start | bytes 3538952 | tf_op jit(solution)/shard_map/ppermute | solution.py:16
  853.6 30.6 %collective-permute-start.106 = (bf16[256,1152]{1,0:T(8,128)(2,1)S(1)}, bf16[256,1152]{1,0:T(8,128)(2,1)S(1)}, u32[]{:S(2)}, u32[]{:S(2)}) collective-permute-start(bf16[256,1152]{1,0:T(8,128)(2,1)S(1)} %slice.1765), channel_id=1, source_target_pairs={{0,8},{8,0},{1,9},{9,1},{2,10},{10,2},{3,11},{11,3},{4,12},{12,4},... | collective-permute-start | bytes 1769480 | tf_op jit(solution)/shard_map/ppermute | solution.py:16
  854.5 29.7 %collective-permute-start.107 = (bf16[512,1152]{1,0:T(8,128)(2,1)S(1)}, bf16[512,1152]{1,0:T(8,128)(2,1)S(1)}, u32[]{:S(2)}, u32[]{:S(2)}) collective-permute-start(bf16[512,1152]{1,0:T(8,128)(2,1)S(1)} %pad_maximum_fusion.39), channel_id=1, source_target_pairs={{0,2},{2,0},{1,3},{3,1},{4,6},{6,4},{5,7},{7,5},{8,10},{10,8},{9,1... | collective-permute-start | bytes 3538952 | tf_op jit(solution)/shard_map/ppermute | solution.py:16
  858.2 24.6 %collective-permute-start.104 = (bf16[64,2048]{1,0:T(8,128)(2,1)S(1)}, bf16[64,2048]{1,0:T(8,128)(2,1)S(1)}, u32[]{:S(2)}, u32[]{:S(2)}) collective-permute-start(bf16[64,2048]{1,0:T(8,128)(2,1)S(1)} %get-tuple-element.644), channel_id=1, source_target_pairs={{0,4},{4,0},{1,5},{5,1},{2,6},{6,2},{3,7},{7,3},{8,12},{12,8},{9,1... | collective-permute-start | bytes 786440 | tf_op jit(solution)/shard_map/ppermute | solution.py:16
  858.5 24.3 %collective-permute-start.103 = (bf16[64,2048]{1,0:T(8,128)(2,1)S(1)}, bf16[64,2048]{1,0:T(8,128)(2,1)S(1)}, u32[]{:S(2)}, u32[]{:S(2)}) collective-permute-start(bf16[64,2048]{1,0:T(8,128)(2,1)S(1)} %get-tuple-element.642), channel_id=1, source_target_pairs={{0,16},{16,0},{1,17},{17,1},{2,18},{18,2},{3,19},{19,3},{4,20},{20... | collective-permute-start | bytes 786440 | tf_op jit(solution)/shard_map/ppermute | solution.py:16
  891.8 58.1 %all-to-all-start.4 = ((bf16[4,256,1152]{2,1,0:T(8,128)(2,1)}), bf16[4,256,1152]{2,1,0:T(8,128)(2,1)S(1)}, u32[]{:S(2)}, u32[]{:S(2)}) async-start(bf16[4,256,1152]{2,1,0:T(8,128)(2,1)} %pad_maximum_fusion.6), calls=%async_computation.4 | async-start | bytes 4718592 | tf_op jit(solution)/shard_map/all_to_all | solution.py:20
  906.0 43.0 %collective-permute-start.113 = (bf16[256,1152]{1,0:T(8,128)(2,1)}, bf16[256,1152]{1,0:T(8,128)(2,1)S(1)}, u32[]{:S(2)}, u32[]{:S(2)}) collective-permute-start(bf16[256,1152]{1,0:T(8,128)(2,1)} %slice.1770), channel_id=1, source_target_pairs={{0,8},{8,0},{1,9},{9,1},{2,10},{10,2},{3,11},{11,3},{4,12},{12,4},... | collective-permute-start | bytes 1769480 | tf_op jit(solution)/shard_map/ppermute | solution.py:16
  906.4 43.4 %collective-permute-start.114 = (bf16[1024,512]{1,0:T(8,128)(2,1)}, bf16[1024,512]{1,0:T(8,128)(2,1)}, u32[]{:S(2)}, u32[]{:S(2)}) collective-permute-start(bf16[1024,512]{1,0:T(8,128)(2,1)} %pad_maximum_fusion.54), channel_id=1, source_target_pairs={{0,2},{2,0},{1,3},{3,1},{4,6},{6,4},{5,7},{7,5},{8,10},{10,8},{9,1... | collective-permute-start | bytes 3145736 | tf_op jit(solution)/shard_map/ppermute | solution.py:16
  912.5 31.3 %collective-permute-start.111 = (bf16[64,2048]{1,0:T(8,128)(2,1)S(1)}, bf16[64,2048]{1,0:T(8,128)(2,1)S(1)}, u32[]{:S(2)}, u32[]{:S(2)}) collective-permute-start(bf16[64,2048]{1,0:T(8,128)(2,1)S(1)} %get-tuple-element.640), channel_id=1, source_target_pairs={{0,20},{4,16},{16,4},{20,0},{1,21},{5,17},{17,5},{21,1},{2,22},{6,... | collective-permute-start | bytes 786440 | tf_op jit(solution)/shard_map/ppermute | solution.py:50
  915.3 32.8 %collective-permute-start.110 = (bf16[64,2048]{1,0:T(8,128)(2,1)S(1)}, bf16[64,2048]{1,0:T(8,128)(2,1)S(1)}, u32[]{:S(2)}, u32[]{:S(2)}) collective-permute-start(bf16[64,2048]{1,0:T(8,128)(2,1)S(1)} %get-tuple-element.641), channel_id=1, source_target_pairs={{0,4},{4,0},{1,5},{5,1},{2,6},{6,2},{3,7},{7,3},{8,12},{12,8},{9,1... | collective-permute-start | bytes 786440 | tf_op jit(solution)/shard_map/ppermute | solution.py:16
  915.9 32.3 %collective-permute-start.109 = (bf16[64,2048]{1,0:T(8,128)(2,1)S(1)}, bf16[64,2048]{1,0:T(8,128)(2,1)S(1)}, u32[]{:S(2)}, u32[]{:S(2)}) collective-permute-start(bf16[64,2048]{1,0:T(8,128)(2,1)S(1)} %get-tuple-element.639), channel_id=1, source_target_pairs={{0,16},{16,0},{1,17},{17,1},{2,18},{18,2},{3,19},{19,3},{4,20},{20... | collective-permute-start | bytes 786440 | tf_op jit(solution)/shard_map/ppermute | solution.py:16
  956.0 83.0 %all-to-all-start.5 = ((bf16[4,256,1152]{2,1,0:T(8,128)(2,1)}), bf16[4,256,1152]{2,1,0:T(8,128)(2,1)}, u32[]{:S(2)}, u32[]{:S(2)}) async-start(bf16[4,256,1152]{2,1,0:T(8,128)(2,1)} %pad_maximum_fusion.7), calls=%async_computation.5 | async-start | bytes 4718592 | tf_op jit(solution)/shard_map/all_to_all | solution.py:20
  960.6 50.1 %collective-permute-start.120 = (bf16[1024,512]{1,0:T(8,128)(2,1)}, bf16[1024,512]{1,0:T(8,128)(2,1)}, u32[]{:S(2)}, u32[]{:S(2)}) collective-permute-start(bf16[1024,512]{1,0:T(8,128)(2,1)} %pad_maximum_fusion.55), channel_id=1, source_target_pairs={{0,2},{2,0},{1,3},{3,1},{4,6},{6,4},{5,7},{7,5},{8,10},{10,8},{9,1... | collective-permute-start | bytes 3145736 | tf_op jit(solution)/shard_map/ppermute | solution.py:16
  962.7 31.4 %collective-permute-start.115 = (bf16[64,2048]{1,0:T(8,128)(2,1)}, bf16[64,2048]{1,0:T(8,128)(2,1)}, u32[]{:S(2)}, u32[]{:S(2)}) collective-permute-start(bf16[64,2048]{1,0:T(8,128)(2,1)} %get-tuple-element.484), channel_id=1, source_target_pairs={{0,16},{16,0},{1,17},{17,1},{2,18},{18,2},{3,19},{19,3},{4,20},{20... | collective-permute-start | bytes 786440 | tf_op jit(solution)/shard_map/ppermute | solution.py:16
  965.6 45.2 %collective-permute-start.119 = (bf16[512,512]{1,0:T(8,128)(2,1)}, bf16[512,512]{1,0:T(8,128)(2,1)S(1)}, u32[]{:S(2)}, u32[]{:S(2)}) collective-permute-start(bf16[512,512]{1,0:T(8,128)(2,1)} %slice.1797), channel_id=1, source_target_pairs={{0,8},{8,0},{1,9},{9,1},{2,10},{10,2},{3,11},{11,3},{4,12},{12,4},... | collective-permute-start | bytes 1572872 | tf_op jit(solution)/shard_map/ppermute | solution.py:16
  1013.3 25.7 %collective-permute-start.121 = (bf16[512,512]{1,0:T(8,128)(2,1)S(1)}, bf16[512,512]{1,0:T(8,128)(2,1)}, u32[]{:S(2)}, u32[]{:S(2)}) collective-permute-start(bf16[512,512]{1,0:T(8,128)(2,1)S(1)} %slice.1810), channel_id=1, source_target_pairs={{0,8},{8,0},{1,9},{9,1},{2,10},{10,2},{3,11},{11,3},{4,12},{12,4},... | collective-permute-start | bytes 1572872 | tf_op jit(solution)/shard_map/ppermute | solution.py:16
  1057.7 38.4 %all-to-all-start.7 = ((bf16[4,512,512]{2,1,0:T(8,128)(2,1)}), bf16[4,512,512]{2,1,0:T(8,128)(2,1)}, u32[]{:S(2)}, u32[]{:S(2)}) async-start(bf16[4,512,512]{2,1,0:T(8,128)(2,1)} %pad_maximum_fusion.19), calls=%async_computation.7 | async-start | bytes 4194304 | tf_op jit(solution)/shard_map/all_to_all | solution.py:20
  1062.4 25.4 %collective-permute-start.122 = (f32[2,4352]{1,0:T(2,128)S(1)}, f32[2,4352]{1,0:T(2,128)S(1)}, u32[]{:S(2)}, u32[]{:S(2)}) collective-permute-start(f32[2,4352]{1,0:T(2,128)S(1)} %add.761), channel_id=1, source_target_pairs={{0,16},{16,0},{1,17},{17,1},{2,18},{18,2},{3,19},{19,3},{4,20},{20... | collective-permute-start | bytes 104456 | tf_op jit(solution)/shard_map/ppermute | solution.py:16
  (254 other events, 3028.7 us)

commit v3 on v2

v3 whole, which is shorter than its diff:
```python
import jax
import jax.numpy as jnp
import numpy as np
from jax import lax
from jax.experimental.layout import Layout, with_layout_constraint
from jax.sharding import Mesh
from jax.sharding import PartitionSpec as P

EPS = 1e-06
THETA = 1000000.0
f32 = jnp.float32
bf16 = jnp.bfloat16


def swap(value, axis):
    return lax.ppermute(value, axis, [(0, 1), (1, 0)])


def exchange(value, axes):
    return lax.all_to_all(value, axes, 0, 0, tiled=True)


def take(value, index, axis=0):
    return lax.dynamic_index_in_dim(value, index, axis, keepdims=False)


def pair(bit, mine, other, axis=0):
    low = jnp.where(bit == 0, mine, other)
    high = jnp.where(bit == 0, other, mine)
    return jnp.stack([low, high], axis)


def plain(value):
    return with_layout_constraint(value, Layout(major_to_minor=tuple(range(value.ndim))))


def dot(left, right):
    return jnp.dot(left, right, preferred_element_type=f32)


def dot_t(left, right):
    return lax.dot_general(left, right, (((1,), (1,)), ((), ())), preferred_element_type=f32)


def t_dot(left, right):
    return lax.dot_general(left, right, (((0,), (0,)), ((), ())), preferred_element_type=f32)


def cross(value):
    return lax.ppermute(value, ("s", "t"), [(i, 3 - i) for i in range(4)])


def gather_near(mine):
    return [mine, swap(mine, "s"), swap(mine, "t"), cross(mine)]


def gather_core(pieces):
    core = jnp.concatenate(pieces)
    return jnp.concatenate([core, swap(core, "k")])


def gather_tokens(mine, middle):
    return gather_core(middle(gather_near(mine)))


def slots_of(s, t, k, g, groups, part):
    pieces = []
    for dk in (0, 1):
        for ds, dt in ((0, 0), (1, 0), (0, 1), (1, 1)):
            block = ((s ^ ds) * 2 + (t ^ dt)) * groups + g
            start = block * (2 * part) + (k ^ dk) * part
            pieces.append(start + jnp.arange(part, dtype=jnp.int32))
    return jnp.concatenate(pieces)


def scatter_sum(near, far, middle, last):
    total = near + swap(far, "k").astype(f32)
    part = total.shape[0] // 4
    total, far = middle((total[:part], total[part:].astype(bf16)))
    pieces = [swap(far[:part], "s"), swap(far[part : 2 * part], "t"), cross(far[2 * part :])]
    total, pieces = last((total, pieces))
    return total + sum(piece.astype(f32) for piece in pieces)


def split_product(lefts, rights):
    half = lefts[0].shape[0] // 2
    far = sum(dot_t(left[half:], right) for left, right in zip(lefts, rights)).astype(bf16)
    near = sum(dot_t(left[:half], right) for left, right in zip(lefts, rights))
    return near, far


class Clock:
    def __init__(self):
        self.plans, self.flying, self.ready, self.loose = {}, {}, {}, {}

    def add(self, name, begin, end, make, send):
        self.plans[name] = (begin, end, make, send)

    def split(self, name, value):
        self.ready[name] = [value[i] for i in range(value.shape[0])]
        self.loose[name] = self.ready[name]

    def point(self, label, chain):
        ends = [name for name, plan in self.plans.items() if plan[1] == label]
        if ends or self.loose:
            flying = [self.flying[name] for name in ends]
            chain, arrived, loose = lax.optimization_barrier((chain, flying, self.loose))
            self.ready.update(loose)
            self.loose = {}
            for name, value in zip(ends, arrived):
                if name in FETCH or name == "a":
                    self.split(name, value)
                else:
                    self.ready[name] = value
        begins = [name for name, plan in self.plans.items() if plan[0] == label]
        if begins:
            values = [self.plans[name][2]() for name in begins]
            passed, values = lax.optimization_barrier((chain, values))
            if label[0] == "E":
                chain = passed
            for name, value in zip(begins, values):
                self.flying[name] = self.plans[name][3](value)
        return chain


def rms(residual):
    return lax.rsqrt(jnp.mean(residual * residual, axis=1, keepdims=True) + EPS)


def norm_back(residual, scale, gain, grad):
    lifted = grad * gain
    inner = jnp.mean(lifted * residual, axis=1, keepdims=True)
    grad_residual = scale * lifted - residual * (scale**3 * inner)
    return grad_residual, jnp.sum(grad * residual * scale, axis=0)


def rotate(raw, gain, cosine, sine):
    scaled = raw * lax.rsqrt(jnp.mean(raw * raw, axis=2, keepdims=True) + EPS) * gain
    half = raw.shape[2] // 2
    turned = jnp.concatenate([-scaled[:, :, half:], scaled[:, :, :half]], axis=2)
    return scaled * cosine[:, None, :] + turned * sine[:, None, :]


FETCH = {
    "m0": ("F01", "c1"),
    "m1": ("c1", "F03"),
}
SPREAD = {
    "a00": ("p0", "F01", "F01", "c1"),
    "a10": ("F01", "c1", "c1", "c2"),
    "m00": ("c1", "c2", "c2", "F03"),
    "m20": ("c2", "F03", "F03", "F05"),
    "m10": ("F03", "F05", "F05", "F06"),
    "m30": ("F05", "F06", "F06", "F07"),
    "a01": ("F06", "F07", "F07", "F09"),
    "a11": ("F07", "F09", "F09", "F10"),
    "m01": ("F09", "F10", "F10", "F11"),
    "m21": ("F10", "F11", "F11", "F13"),
    "m11": ("F11", "F13", "F13", "F15"),
    "m31": ("F13", "F15", "F15", "F16"),
}
RETURN = {
    "m01": ("B12", "B13", "B13", "B15"),
    "m21": ("B13", "B15", "B15", "B16"),
    "m11": ("B15", "B16", "B16", "B18"),
    "m31": ("B16", "B18", "B18", "B1X"),
    "a01": ("B18", "B1X", "B1X", "B01"),
    "a11": ("B1X", "B01", "B01", "B02"),
    "m00": ("B02", "B04", "B04", "B05"),
    "m20": ("B04", "B05", "B05", "B06"),
    "m10": ("B05", "B06", "B06", "B08"),
    "m30": ("B06", "B08", "B08", "B0X"),
    "a00": ("B08", "B0X", "B0X", "E1"),
    "a10": ("B0X", "E1", "E1", "E2"),
}
HOME = {
    "m0": ("B06", "B0X"),
    "m1": ("B0X", "E2"),
}


def body(
    boundary, segment_ids, w_query, key_projection, value_projection, w_out, w_gate, w_up, w_down,
    attn_gain, mlp_gain, query_gain, key_norm_gain,
):
    s, h, t, g, y, k = (lax.axis_index(name) for name in ("s", "h", "t", "g", "y", "k"))
    groups = lax.axis_size("g")
    micro, tok, width = boundary.shape[1:]
    cols = lax.axis_size("y") * lax.axis_size("k")
    model = width * cols
    head = query_gain.shape[1]
    span = segment_ids.shape[1]
    rb = w_query.shape[1]
    ff = w_gate.shape[2] // 4
    scale_qk = head ** (-0.5)
    clock = Clock()

    packed = jnp.concatenate([attn_gain[0], mlp_gain[0], query_gain[0], key_norm_gain[0]])[None]
    packed = pair(s, packed, swap(packed, "s"))

    segments = take(segment_ids, 2 * y + h)
    part = tok // 2
    slots = slots_of(s, t, k, g, groups, part)
    first_run = jnp.sum((segments == 0).astype(jnp.int32))
    filled = jnp.sum((segments >= 0).astype(jnp.int32))

    def segments_at(places):
        return jnp.where(places < first_run, 0, jnp.where(places < filled, 1, -1))

    my_segments = segments_at(slots)
    offsets = slots - jnp.where(slots < first_run, 0, jnp.where(slots < filled, first_run, filled))
    inv_freq = THETA ** (-jnp.arange(0, head, 2, dtype=f32) / head)
    angles = offsets.astype(f32)[:, None] * inv_freq[None, :]
    cosine = jnp.concatenate([jnp.cos(angles)] * 2, 1)
    sine = jnp.concatenate([jnp.sin(angles)] * 2, 1)
    valid = (my_segments[:part] >= 0).astype(f32)
    key_slots = lax.all_gather(slots, "g", axis=0, tiled=True) if groups > 1 else slots
    key_segments = segments_at(key_slots)
    allowed = (my_segments[:, None] == key_segments[None, :]) & (
        key_slots[None, :] <= slots[:, None]
    )

    rows = boundary[0].reshape(2, 2 * tok, width)
    rows = pair(y, take(rows, y), swap(take(rows, 1 - y), "y")).reshape(2, 2, 2, tok // 2, width)
    rows = pair(k, take(rows, k, 2), swap(take(rows, 1 - k, 2), "k"))
    rows = jnp.stack(
        [jnp.concatenate([rows[j, i, m] for i in (0, 1) for j in (0, 1)], 1) for m in (0, 1)]
    )

    def quarters(weight):
        size = weight.shape[1] // 4
        return [weight[:, i * size : (i + 1) * size] for i in range(4)]

    def to_groups(value):
        return exchange(value, ("s", "t"))

    a_home = []
    for i, (q, o) in enumerate(zip(quarters(w_query[0]), quarters(w_out[0].T))):
        low = (i // 2) * head
        kv = [w[0, :, low : low + head] for w in (key_projection, value_projection)]
        a_home.append(jnp.concatenate([q, o] + kv, 1))
    a_home, packed = lax.optimization_barrier((plain(jnp.stack(a_home)), packed))
    fetched_a = to_groups(a_home)
    def rolled(value):
        half = value.shape[-1] // 2
        return jnp.where(h == 0, value, jnp.concatenate([value[..., half:], value[..., :half]], -1))

    homes = {}

    def fetch(name):
        clock.add(name, *FETCH[name], lambda: homes[name], to_groups)

    def spread(name):
        i, layer = int(name[1]), int(name[2])
        source, block = ("a", i) if name[0] == "a" else (f"m{i % 2}", i // 2)
        plan = SPREAD[name]

        def start():
            return clock.ready[source][2 * layer + block]

        def onward():
            value = [start(), clock.ready[name + "h"]]
            if groups > 1:
                value = [lax.all_gather(half, "g", axis=0, tiled=True) for half in value]
            clock.ready[name] = jnp.concatenate(value)
            return clock.ready[name]

        clock.add(name + "h", plan[0], plan[1], start, lambda value: swap(value, "h"))
        clock.add(name + "y", plan[2], plan[3], onward, lambda value: swap(value, "y"))

    def places_of(kind):
        count = 2 if kind == "m" else 1
        size = rb // count
        for i in range(4 * groups):
            half, block, group = i // (2 * groups), i // groups % 2, i % groups
            for j in range(count):
                yield block * count + j, (half * groups + group) * size, size

    def weight(kind, layer):
        return [
            jnp.concatenate(
                [
                    clock.ready[f"{kind}{part}{layer}{step}"][low : low + size]
                    for part, low, size in places_of(kind)
                ]
            )
            for step in ("", "y")
        ]

    for name in FETCH:
        fetch(name)
    for name in SPREAD:
        spread(name)

    rows, w_gate, w_up, w_down = lax.optimization_barrier((rows, w_gate, w_up, w_down))
    m_home = [
        jnp.concatenate(pieces, 1)
        for pieces in zip(quarters(w_gate[0]), quarters(w_up[0]), quarters(w_down[0].T))
    ]
    homes.update({
        "m0": plain(jnp.stack([value[: rb // 2] for value in m_home])),
        "m1": plain(jnp.stack([value[rb // 2 :] for value in m_home])),
    })

    own_rows = take(rows, h)
    other_rows = swap(take(rows, 1 - h), "h")
    keep = jnp.where(s == h, own_rows, other_rows)
    passed = jnp.where(s == h, other_rows, own_rows)
    passed = swap(passed, "s")
    entering = rolled(jnp.where(s == 0, keep, passed))
    cotangent = rolled(jnp.where(s == 0, passed, keep))
    packed = pair(k, packed, swap(packed, "k"), 1)
    packed = pair(y, packed, swap(packed, "y"), 1).reshape(2, cols, -1).astype(f32)
    gain_a = rolled(packed[:, :, :width].reshape(2, model))
    gain_m = rolled(packed[:, :, width : 2 * width].reshape(2, model))
    gain_q = packed[:, 0, 2 * width : 2 * width + head]
    gain_k = packed[:, 0, 2 * width + head :]
    clock.flying["a"] = fetched_a
    clock.plans["a"] = (None, "p0", None, None)
    entering, cotangent, gain_a, gain_m, homes["m0"], homes["m1"] = clock.point(
        "p0", (entering, cotangent, gain_a, gain_m, homes["m0"], homes["m1"])
    )
    top = cotangent.astype(f32) * valid[:, None]
    kept = {}

    def all_keys(value):
        return lax.all_gather(value, "g", axis=0, tiled=True) if groups > 1 else value

    def sum_keys(value):
        if groups > 1:
            return lax.psum_scatter(value.astype(bf16), "g", scatter_dimension=0, tiled=True).astype(f32)
        return value

    def scores_of(q, keys):
        scores = jnp.einsum("qhd,khd->hqk", q, keys, preferred_element_type=f32) * scale_qk
        return jnp.where(allowed[None], scores, -1e30)

    def forward(layer, residual):
        def at(place):
            return lambda chain: clock.point(f"F{layer}{place}", chain)

        scale_a = rms(residual)
        normed = (residual * scale_a * gain_a[layer]).astype(bf16)
        def head_start(pieces):
            pieces = at(1)(pieces)
            if layer == 0:
                for label in ("c1", "c2"):
                    pieces = clock.point(label, pieces)
            return pieces

        xa = at(2)(gather_tokens(normed, head_start))
        wa = weight("a", layer)
        q_raw = jnp.stack([dot(xa, w[:, :head]) for w in wa], 1)
        raw = jnp.stack([dot(xa, w[:, 2 * head :]) for w in wa], 1)
        k_raw = raw[:, :, :head]
        v = raw[:, :, head:].astype(bf16)
        q = rotate(q_raw, gain_q[layer], cosine, sine).astype(bf16)
        keys = rotate(k_raw, gain_k[layer], cosine, sine).astype(bf16)
        keys, values = all_keys(keys), all_keys(v)
        scores = scores_of(q, keys)
        peak = jnp.max(scores, axis=2, keepdims=True)
        exps = jnp.exp(scores - peak)
        denom = jnp.sum(exps, axis=2, keepdims=True)
        mixing = (exps / denom).astype(bf16)
        lse = peak + jnp.log(denom)
        o = jnp.einsum("hqk,khd->qhd", mixing, values, preferred_element_type=f32)
        o = o.astype(bf16)
        near, far = at(3)(split_product((o[:, 0], o[:, 1]), [w[:, head : 2 * head] for w in wa]))
        middle = residual + scatter_sum(near, far, at(4), at(5))
        scale_m = rms(middle)
        normed = (middle * scale_m * gain_m[layer]).astype(bf16)
        xm = gather_tokens(normed, at(6))
        if layer == 1:
            xm, pieces = lax.optimization_barrier((xm, kept["g3"]))
            xm, kept["g3"] = lax.optimization_barrier((xm, gather_core(pieces)))
        xm = at(7)(xm)
        if layer == 0:
            xm, grad = lax.optimization_barrier((xm, top.astype(bf16)))
            kept["g3"] = gather_near(grad)
        wm = weight("m", layer)
        hidden = []
        for w in wm:
            both = dot(xm, w[:, : 2 * ff])
            hidden.append((both[:, :ff], both[:, ff:]))
        act = [(gate * jax.nn.sigmoid(gate) * up).astype(bf16) for gate, up in hidden]
        kept[layer] = (residual, scale_a, xa, q_raw, k_raw, q, keys, values, lse, o, middle, scale_m, xm, hidden, act, wa, wm)

    def project(layer, act):
        return split_product(act, [w[:, 2 * ff :] for w in kept[layer][-1]])

    partial = {}

    def back(name):
        plan = RETURN[name]
        part, layer = int(name[1]), name[2]

        def rows_of(i):
            rows = rb // (2 if name[0] == "m" else 1)
            lows = [j * rows for j, (index, _, _) in enumerate(places_of(name[0])) if index == part]
            return [
                t_dot(jnp.concatenate([left[:, low : low + rows] for low in lows], 1), right)
                for left, right in partial[name[0] + layer][i]
            ]

        def other():
            return plain(jnp.concatenate([value.astype(bf16) for value in rows_of(1)], 1))

        def onward():
            total, low = [], 0
            for value in rows_of(0):
                high = low + value.shape[1]
                total.append((value + clock.ready["back_y" + name][:, low:high].astype(f32)).astype(bf16))
                low = high
            total = plain(jnp.concatenate(total, 1))
            count = total.shape[0] // 2
            mine, other = total[:count], total[count:]
            if groups > 1:
                mine, other = (
                    lax.psum_scatter(half, "g", scatter_dimension=0, tiled=True) for half in (mine, other)
                )
            partial["sum" + name] = mine
            return other

        clock.add("back_y" + name, plan[0], plan[1], other, lambda value: swap(value, "y"))
        clock.add("back_h" + name, plan[2], plan[3], onward, lambda value: swap(value, "h"))

    def summed(name):
        return (partial["sum" + name].astype(f32) + clock.ready["back_h" + name].astype(f32)).astype(bf16)

    def both_layers(name):
        names = ("a0", "a1") if name == "a" else (name, f"m{int(name[1]) + 2}")
        return plain(jnp.stack([summed(f"{part}{layer}") for layer in (0, 1) for part in names]))

    for name in RETURN:
        back(name)
    for name, plan in HOME.items():
        clock.add("home" + name, *plan, lambda name=name: both_layers(name), to_groups)

    def backward(layer, grad_top, g3):
        def at(place):
            return lambda chain: clock.point(f"B{layer}{place}", chain)

        (
            residual, scale_a, xa, q_raw, k_raw, q, keys, values, lse, o, middle, scale_m, xm, hidden,
            act, wa, wm,
        ) = kept[layer]
        d_act = [dot(g3, w[:, 2 * ff :]) for w in wm]
        d_hidden = []
        for grad, (gate, up) in zip(d_act, hidden):
            sig = jax.nn.sigmoid(gate)
            d_gate = (grad * up * sig * (1 + gate * (1 - sig))).astype(bf16)
            d_up = (grad * gate * sig).astype(bf16)
            d_hidden.append(jnp.concatenate([d_gate, d_up], 1))
        partial[f"m{layer}"] = [((xm, d), (g3, a)) for d, a in zip(d_hidden, act)]
        d_hidden = at(2)(d_hidden)
        near, far = split_product(d_hidden, [w[:, : 2 * ff] for w in wm])
        near, far = at(3)((near, far))
        d_xm = scatter_sum(near, far, at(4), at(5))
        d_mid, d_gain_m = norm_back(middle, scale_m, gain_m[layer], d_xm)
        d_mid = grad_top + d_mid
        g2 = at(7)(gather_tokens(d_mid.astype(bf16), at(6)))
        d_o = jnp.stack([dot(g2, w[:, head : 2 * head]).astype(bf16) for w in wa], 1)
        mixing = jnp.exp(scores_of(q, keys) - lse)
        d_mix = jnp.einsum("qhd,khd->hqk", d_o, values, preferred_element_type=f32)
        inner = jnp.sum(mixing * d_mix, axis=2, keepdims=True)
        d_scores = (mixing * (d_mix - inner)).astype(bf16)
        d_q = jnp.einsum("hqk,khd->qhd", d_scores, keys, preferred_element_type=f32) * scale_qk
        d_k = jnp.einsum("hqk,qhd->khd", d_scores, q, preferred_element_type=f32) * scale_qk
        d_v = jnp.einsum("hqk,qhd->khd", mixing.astype(bf16), d_o, preferred_element_type=f32)
        d_k, d_v = sum_keys(d_k), sum_keys(d_v)
        _, pull_q = jax.vjp(lambda raw, gain: rotate(raw, gain, cosine, sine), q_raw, gain_q[layer])
        _, pull_k = jax.vjp(lambda raw, gain: rotate(raw, gain, cosine, sine), k_raw, gain_k[layer])
        d_q_raw, d_gain_q = pull_q(d_q)
        d_k_raw, d_gain_k = pull_k(d_k)
        d_q_raw, d_kv_raw = d_q_raw.astype(bf16), jnp.concatenate([d_k_raw, d_v], 2).astype(bf16)
        d_raw = [d_q_raw[:, 0], d_q_raw[:, 1], d_kv_raw[:, 0], d_kv_raw[:, 1]]
        partial[f"a{layer}"] = [
            ((xa, d_q_raw[:, i]), (g2, o[:, i]), (xa, d_kv_raw[:, i])) for i in (0, 1)
        ]
        near, far = at(8)(split_product(d_raw, [w[:, :head] for w in wa] + [w[:, 2 * head :] for w in wa]))
        d_xa = scatter_sum(near, far, at(9), lambda value: clock.point(f"B{layer}X", value))
        d_res, d_gain_a = norm_back(residual, scale_a, gain_a[layer], d_xa)
        return d_mid + d_res, (d_gain_a, d_gain_m, d_gain_q, d_gain_k)

    forward(0, entering.astype(f32))
    act = kept[0][14]
    near, far, kept["g3"] = clock.point("F09", (*project(0, act), kept["g3"]))
    middle = kept[0][10] + scatter_sum(near, far, lambda value: value, lambda value: clock.point("F10", value))
    forward(1, middle.astype(bf16).astype(f32))
    grad, gains1 = backward(1, top, kept["g3"])
    grad = grad.astype(bf16)
    pieces = clock.point("B01", gather_near(grad))
    pieces, act = lax.optimization_barrier((pieces, kept[1][14]))
    near, far = project(1, act)
    output = kept[1][10] + scatter_sum(near, far, lambda value: value, lambda value: value)
    g3, kept["output"] = lax.optimization_barrier((gather_core(pieces), output))
    grad, gains0 = backward(0, grad.astype(f32), g3)

    low, high = rolled(grad.astype(bf16)), rolled(kept["output"].astype(bf16))
    keep = jnp.where(s == 0, low, high)
    passed = swap(jnp.where(s == 0, high, low), "s")
    (keep, passed), gains0, gains1 = clock.point("E1", ((keep, passed), gains0, gains1))
    sums = []
    for gains in (gains0, gains1):
        sums += [rolled(gains[0]), rolled(gains[1]), gains[2], gains[3]]
    sums = jnp.concatenate(sums)
    sums = sums.reshape(-1, head)
    sums = sums + swap(sums, "k")
    sums = sums + swap(sums, "t")
    keep, passed, sums = clock.point("E2", (keep, passed, sums))
    last = both_layers("a")
    ready = {name: clock.ready["home" + name] for name in HOME}
    last, keep, passed, sums, ready = lax.optimization_barrier((last, keep, passed, sums, ready))
    full_a = to_groups(last)
    mine = jnp.where(s == h, keep, passed)
    other = swap(jnp.where(s == h, passed, keep), "h")
    sums = sums + swap(sums, "y")
    rows = pair(h, mine, other)
    blocks = [jnp.stack([rows[..., (2 * i + j) * width : (2 * i + j + 1) * width] for i in (0, 1)]) for j in (0, 1)]
    mine, other = (jnp.where(k == j, blocks[0], blocks[1]) for j in (0, 1))
    rows = pair(k, mine, swap(other, "k"), 2).reshape(2, 2, tok, width)
    rows = pair(y, take(rows, y), swap(take(rows, 1 - y), "y"))
    section_out = rows.reshape(micro, tok, width)
    sums = sums + swap(sums, "s")
    sums = sums + swap(sums, "h")
    if groups > 1:
        sums = lax.psum(sums, "g")
    sums = take(sums.reshape(2, -1), s)

    def columns(value):
        return jnp.concatenate([value[i] for i in range(4)], 1).astype(f32)

    full_m = jnp.concatenate([ready["m0"], ready["m1"]], 1)
    full_gate, full_up = columns(full_m[..., :ff]), columns(full_m[..., ff : 2 * ff])
    full_down = columns(full_m[..., 2 * ff :]).T
    full_q = columns(full_a[..., :head])
    full_out = columns(full_a[..., head : 2 * head]).T
    full_kv = full_a[..., 2 * head :].astype(f32)
    full_kv = [full_kv[0] + full_kv[1], full_kv[2] + full_kv[3]]
    full_k, full_v = (
        jnp.concatenate([half[:, i * head : (i + 1) * head] for half in full_kv], 1) for i in (0, 1)
    )
    return (
        section_out.astype(f32)[None],
        full_q[None],
        full_k[None],
        full_v[None],
        full_out[None],
        full_gate[None],
        full_up[None],
        full_down[None],
        sums[None, :model],
        sums[None, model : 2 * model],
        sums[None, 2 * model : 2 * model + head],
        sums[None, 2 * model + head :],
    )


def solution(mesh):
    sections, row_count, col_count = (mesh.shape[name] for name in ("section", "row", "col"))
    shape = (sections, 2, 2, row_count // 4, 2, col_count // 2)
    mesh = Mesh(np.asarray(mesh.devices).reshape(shape), ("s", "h", "t", "g", "y", "k"))
    row, col = ("h", "t", "g"), ("y", "k")
    in_row, in_col = P("s", row, col), P("s", col, row)
    return jax.shard_map(
        body,
        mesh=mesh,
        in_specs=(
            P("s", None, row, col), P(), in_row, in_row, in_row, in_col, in_row, in_row, in_col,
            P("s", col), P("s", col), P("s", None), P("s", None),
        ),
        out_specs=(
            P("s", None, row, col), in_row, in_row, in_row, in_col, in_row, in_row, in_col,
            P("s", None), P("s", None), P("s", None), P("s", None),
        ),
        check_vma=False,
    )
```

time: 1110 us -> 1030 us (0.928)
  waiting for transfers between devices: 673 us -> 585 us
  matrix products: 95.2 us -> 114 us
  other arithmetic: 92.3 us -> 79.6 us
    ppermute x16, waiting for transfers between devices: 211 us -> 67.6 us  [cross(): return lax.ppermute(value, ('s', 't'), [(i, 3 - i) for i in range(4)])]
    ppermute x108 -> x112, waiting for transfers between devices: 456 us -> 516 us  [swap(): return lax.ppermute(value, axis, [(0, 1), (1, 0)])]
    ppermute x108 -> x112, starting transfers between devices: 90.1 us -> 114 us  [swap(): return lax.ppermute(value, axis, [(0, 1), (1, 0)])]
    dot_general x20 -> x56, matrix products: 26.6 us -> 43.6 us  [t_dot(): lax.dot_general(left, right, (((0,), (0,)), ((), ())), preferred_element_...]
    all_to_all x8 -> x6, starting transfers between devices: 33.8 us -> 25.7 us  [exchange(): return lax.all_to_all(value, axes, 0, 0, tiled=True)]
    unnamed x413 -> x585, local copies, waits for them, and re-layouts: 52.5 us -> 45.8 us
  transfers between devices with their start and end apart: 132 -> 134, of which waited for: 81 -> 74; matrix products, arithmetic and copies ran while one was open for 16% -> 19% of each run, Pallas kernels for 0% -> 0%
where the time goes in v3:
time: 1030 us; the launch traced here: 1020 us
  waiting for transfers between devices  585 us (57%)
  starting transfers between devices  154 us (15%)
  matrix products  114 us (11%)
  other arithmetic  79.6 us (8%)
  local copies, waits for them, and re-layouts  79 us (8%)
    ppermute x112, waiting for transfers between devices, swap(): return lax.ppermute(value, axis, [(0, 1), (1, 0)])  516 us
    ppermute x112, starting transfers between devices, swap(): return lax.ppermute(value, axis, [(0, 1), (1, 0)])  114 us
    ppermute x16, waiting for transfers between devices, cross(): return lax.ppermute(value, ('s', 't'), [(i, 3 - i) for i in range(4)])  67.6 us
    unnamed x585, local copies, waits for them, and re-layouts  45.8 us
    dot_general x56, matrix products, t_dot(): lax.dot_general(left, right, (((0,), (0,)), ((), ())), preferred_element_...  43.6 us
    dot_general x40, matrix products, dot_t(): lax.dot_general(left, right, (((1,), (1,)), ((), ())), preferred_element_...  37.5 us
    dot_general x20, matrix products, dot(): return jnp.dot(left, right, preferred_element_type=f32)  26.7 us
    all_to_all x6, starting transfers between devices, exchange(): return lax.all_to_all(value, axes, 0, 0, tiled=True)  25.7 us
  transfers between devices with their start and end apart: 134, of which 74 were waited for; matrix products, arithmetic and copies ran while one was open for 19% of the time, Pallas kernels for 0%

profile of v3, /device:TPU:0, one launch (start us, length us, event | category | flops | bytes accessed | tf_op | source)
XLA Modules:
  0.0 1018.5 jit_solution(11413444974871758492)
XLA Ops:
  2.8 3.0 collective-permute-start.4
  14.6 3.6 all-to-all-start
  18.4 3.8 collective-permute-done
  35.2 11.3 %collective-permute-done.2 = bf16[64,2048]{1,0:T(8,128)(2,1)S(1)} collective-permute-done((bf16[64,2048]{1,0:T(8,128)(2,1)S(1)}, bf16[64,2048]{1,0:T(8,128)(2,1)S(1)}, u32[]{:S(2)}, u32[]{:S(2)}) %collective-permute-start.2) | collective-permute-done | bytes 262176 | tf_op jit(solution)/shard_map/ppermute | solution.py:16
  50.1 3.8 collective-permute-done.3
  56.1 3.4 collective-permute-start.10
  63.3 3.7 collective-permute-done.7
  67.0 10.5 %collective-permute-done.8 = bf16[64,2048]{1,0:T(8,128)(2,1)S(1)} collective-permute-done((bf16[64,2048]{1,0:T(8,128)(2,1)S(1)}, bf16[64,2048]{1,0:T(8,128)(2,1)S(1)}, u32[]{:S(2)}, u32[]{:S(2)}) %collective-permute-start.8) | collective-permute-done | bytes 262176 | tf_op jit(solution)/shard_map/ppermute | solution.py:16
  82.9 4.7 all-to-all-start.1
  96.7 4.6 collective-permute-start.12
  103.1 19.2 %collective-permute-done.12 = bf16[512,512]{1,0:T(8,128)(2,1)S(1)} collective-permute-done((bf16[512,512]{1,0:T(8,128)(2,1)S(1)}, bf16[512,512]{1,0:T(8,128)(2,1)S(1)}, u32[]{:S(2)}, u32[]{:S(2)}) %collective-permute-start.12) | collective-permute-done | bytes 524320 | tf_op jit(solution)/shard_map/ppermute | solution.py:16
  133.3 4.7 all-to-all-start.2
  141.2 14.0 %collective-permute-done.14 = bf16[256,1152]{1,0:T(8,128)(2,1)} collective-permute-done((bf16[256,1152]{1,0:T(8,128)(2,1)}, bf16[256,1152]{1,0:T(8,128)(2,1)}, u32[]{:S(2)}, u32[]{:S(2)}) %collective-permute-start.14) | collective-permute-done | bytes 589856 | tf_op jit(solution)/shard_map/ppermute | solution.py:16
  174.5 14.6 %collective-permute-done.17 = bf16[256,1152]{1,0:T(8,128)(2,1)S(1)} collective-permute-done((bf16[256,1152]{1,0:T(8,128)(2,1)S(1)}, bf16[256,1152]{1,0:T(8,128)(2,1)S(1)}, u32[]{:S(2)}, u32[]{:S(2)}) %collective-permute-start.17) | collective-permute-done | bytes 589856 | tf_op jit(solution)/shard_map/ppermute | solution.py:16
  198.4 3.2 collective-permute-start.20
  204.2 18.9 %collective-permute-done.23 = bf16[256,1152]{1,0:T(8,128)(2,1)S(1)} collective-permute-done((bf16[256,1152]{1,0:T(8,128)(2,1)S(1)}, bf16[256,1152]{1,0:T(8,128)(2,1)S(1)}, u32[]{:S(2)}, u32[]{:S(2)}) %collective-permute-start.23) | collective-permute-done | bytes 589856 | tf_op jit(solution)/shard_map/ppermute | solution.py:16
  223.2 3.0 collective-permute-done.21
  231.6 4.5 collective-permute-done.24
  236.1 11.1 %collective-permute-done.25 = bf16[64,2048]{1,0:T(8,128)(2,1)S(1)} collective-permute-done((bf16[64,2048]{1,0:T(8,128)(2,1)S(1)}, bf16[64,2048]{1,0:T(8,128)(2,1)S(1)}, u32[]{:S(2)}, u32[]{:S(2)}) %collective-permute-start.25) | collective-permute-done | bytes 262176 | tf_op jit(solution)/shard_map/ppermute | solution.py:16
  247.2 3.7 collective-permute-done.26
  250.8 3.3 collective-permute-done.28
  257.1 24.3 %collective-permute-done.31 = bf16[512,512]{1,0:T(8,128)(2,1)S(1)} collective-permute-done((bf16[512,512]{1,0:T(8,128)(2,1)S(1)}, bf16[512,512]{1,0:T(8,128)(2,1)S(1)}, u32[]{:S(2)}, u32[]{:S(2)}) %collective-permute-start.31) | collective-permute-done | bytes 524320 | tf_op jit(solution)/shard_map/ppermute | solution.py:16
  298.6 20.1 %collective-permute-done.36 = bf16[512,512]{1,0:T(8,128)(2,1)S(1)} collective-permute-done((bf16[512,512]{1,0:T(8,128)(2,1)S(1)}, bf16[512,512]{1,0:T(8,128)(2,1)S(1)}, u32[]{:S(2)}, u32[]{:S(2)}) %collective-permute-start.36) | collective-permute-done | bytes 524320 | tf_op jit(solution)/shard_map/ppermute | solution.py:16
  328.1 23.0 %collective-permute-done.42 = bf16[256,1152]{1,0:T(8,128)(2,1)S(1)} collective-permute-done((bf16[256,1152]{1,0:T(8,128)(2,1)S(1)}, bf16[256,1152]{1,0:T(8,128)(2,1)S(1)}, u32[]{:S(2)}, u32[]{:S(2)}) %collective-permute-start.42) | collective-permute-done | bytes 589856 | tf_op jit(solution)/shard_map/ppermute | solution.py:16
  358.1 3.3 collective-permute-done.43
  361.4 11.3 %collective-permute-done.44 = bf16[64,2048]{1,0:T(8,128)(2,1)S(1)} collective-permute-done((bf16[64,2048]{1,0:T(8,128)(2,1)S(1)}, bf16[64,2048]{1,0:T(8,128)(2,1)S(1)}, u32[]{:S(2)}, u32[]{:S(2)}) %collective-permute-start.44) | collective-permute-done | bytes 262176 | tf_op jit(solution)/shard_map/ppermute | solution.py:16
  372.7 3.2 collective-permute-done.45
  375.9 8.8 collective-permute-done.47
  400.4 13.0 %collective-permute-done.50 = bf16[256,1152]{1,0:T(8,128)(2,1)S(1)} collective-permute-done((bf16[256,1152]{1,0:T(8,128)(2,1)S(1)}, bf16[256,1152]{1,0:T(8,128)(2,1)S(1)}, u32[]{:S(2)}, u32[]{:S(2)}) %collective-permute-start.50) | collective-permute-done | bytes 589856 | tf_op jit(solution)/shard_map/ppermute | solution.py:16
  422.3 23.7 %collective-permute-done.56 = bf16[256,1152]{1,0:T(8,128)(2,1)S(1)} collective-permute-done((bf16[256,1152]{1,0:T(8,128)(2,1)S(1)}, bf16[256,1152]{1,0:T(8,128)(2,1)S(1)}, u32[]{:S(2)}, u32[]{:S(2)}) %collective-permute-start.56) | collective-permute-done | bytes 589856 | tf_op jit(solution)/shard_map/ppermute | solution.py:16
  457.3 4.2 collective-permute-done.59
  461.5 15.7 %collective-permute-done.60 = bf16[512,1152]{1,0:T(8,128)(2,1)S(1)} collective-permute-done((bf16[512,1152]{1,0:T(8,128)(2,1)S(1)}, bf16[512,1152]{1,0:T(8,128)(2,1)S(1)}, u32[]{:S(2)}, u32[]{:S(2)}) %collective-permute-start.60) | collective-permute-done | bytes 1179680 | tf_op jit(solution)/shard_map/ppermute | solution.py:16
  502.5 3.6 fusion.1
  506.1 14.3 %collective-permute-done.63 = bf16[512,1152]{1,0:T(8,128)(2,1)} collective-permute-done((bf16[512,1152]{1,0:T(8,128)(2,1)S(1)}, bf16[512,1152]{1,0:T(8,128)(2,1)}, u32[]{:S(2)}, u32[]{:S(2)}) %collective-permute-start.63) | collective-permute-done | bytes 1179680 | tf_op jit(solution)/shard_map/ppermute | solution.py:16
  530.3 23.7 %collective-permute-done.68 = bf16[256,1152]{1,0:T(8,128)(2,1)S(1)} collective-permute-done((bf16[256,1152]{1,0:T(8,128)(2,1)S(1)}, bf16[256,1152]{1,0:T(8,128)(2,1)S(1)}, u32[]{:S(2)}, u32[]{:S(2)}) %collective-permute-start.68) | collective-permute-done | bytes 589856 | tf_op jit(solution)/shard_map/ppermute | solution.py:16
  565.0 4.7 collective-permute-done.70
  569.7 9.8 collective-permute-done.71
  579.5 8.3 collective-permute-done.72
  610.8 7.7 collective-permute-done.76
  632.4 20.5 %collective-permute-done.82 = bf16[256,1152]{1,0:T(8,128)(2,1)S(1)} collective-permute-done((bf16[256,1152]{1,0:T(8,128)(2,1)S(1)}, bf16[256,1152]{1,0:T(8,128)(2,1)S(1)}, u32[]{:S(2)}, u32[]{:S(2)}) %collective-permute-start.82) | collective-permute-done | bytes 589856 | tf_op jit(solution)/shard_map/ppermute | solution.py:16
  662.4 3.4 collective-permute-done.84
  665.8 9.9 collective-permute-done.85
  675.7 7.0 collective-permute-done.86
  693.4 13.6 %collective-permute-done.93 = bf16[64,2048]{1,0:T(8,128)(2,1)S(1)} collective-permute-done((bf16[64,2048]{1,0:T(8,128)(2,1)S(1)}, bf16[64,2048]{1,0:T(8,128)(2,1)S(1)}, u32[]{:S(2)}, u32[]{:S(2)}) %collective-permute-start.93) | collective-permute-done | bytes 262176 | tf_op jit(solution)/shard_map/ppermute | solution.py:50
  707.0 4.6 collective-permute-done.92
  715.0 3.1 collective-permute-done.94
  728.6 24.0 %collective-permute-done.96 = bf16[512,1152]{1,0:T(8,128)(2,1)S(1)} collective-permute-done((bf16[512,1152]{1,0:T(8,128)(2,1)S(1)}, bf16[512,1152]{1,0:T(8,128)(2,1)S(1)}, u32[]{:S(2)}, u32[]{:S(2)}) %collective-permute-start.96) | collective-permute-done | bytes 1179680 | tf_op jit(solution)/shard_map/ppermute | solution.py:16
  757.6 2.8 collective-permute-start.98
  763.9 11.7 %collective-permute-done.98 = bf16[64,2048]{1,0:T(8,128)(2,1)S(1)} collective-permute-done((bf16[64,2048]{1,0:T(8,128)(2,1)S(1)}, bf16[64,2048]{1,0:T(8,128)(2,1)S(1)}, u32[]{:S(2)}, u32[]{:S(2)}) %collective-permute-start.98) | collective-permute-done | bytes 262176 | tf_op jit(solution)/shard_map/ppermute | solution.py:16
  775.6 4.3 collective-permute-done.99
  779.9 4.1 collective-permute-done.100
  791.3 4.3 collective-permute-done.102
  795.5 10.0 collective-permute-done.103
  805.6 9.4 collective-permute-done.104
  822.7 3.8 all-to-all-start.3
  864.8 20.1 %collective-permute-done.114 = bf16[256,1152]{1,0:T(8,128)(2,1)S(1)} collective-permute-done((bf16[256,1152]{1,0:T(8,128)(2,1)S(1)}, bf16[256,1152]{1,0:T(8,128)(2,1)S(1)}, u32[]{:S(2)}, u32[]{:S(2)}) %collective-permute-start.114) | collective-permute-done | bytes 589856 | tf_op jit(solution)/shard_map/ppermute | solution.py:16
  886.9 4.3 collective-permute-done.113
  904.9 4.5 all-to-all-start.4
  911.0 13.6 %collective-permute-done.117 = bf16[512,512]{1,0:T(8,128)(2,1)} collective-permute-done((bf16[512,512]{1,0:T(8,128)(2,1)}, bf16[512,512]{1,0:T(8,128)(2,1)}, u32[]{:S(2)}, u32[]{:S(2)}) %collective-permute-start.117) | collective-permute-done | bytes 524320 | tf_op jit(solution)/shard_map/ppermute | solution.py:16
  937.2 22.1 %collective-permute-done.120 = f32[68,128]{1,0:T(8,128)S(1)} collective-permute-done((f32[68,128]{1,0:T(8,128)S(1)}, f32[68,128]{1,0:T(8,128)S(1)}, u32[]{:S(2)}, u32[]{:S(2)}) %collective-permute-start.120) | collective-permute-done | bytes 34848 | tf_op jit(solution)/shard_map/ppermute | solution.py:16
  960.5 3.0 pad_maximum_fusion.7
  963.7 4.4 all-to-all-start.5
  979.1 12.9 %collective-permute-done.126 = f32[68,128]{1,0:T(8,128)S(1)} collective-permute-done((f32[68,128]{1,0:T(8,128)S(1)}, f32[68,128]{1,0:T(8,128)S(1)}, u32[]{:S(2)}, u32[]{:S(2)}) %collective-permute-start.126) | collective-permute-done | bytes 34848 | tf_op jit(solution)/shard_map/ppermute | solution.py:16
  1003.4 6.3 collective-permute-done.124
  (1222 shorter events, 408.8 us)
Async XLA Ops:
  14.6 40.3 %all-to-all-start = ((bf16[4,512,512]{2,1,0:T(8,128)(2,1)}), bf16[4,512,512]{2,1,0:T(8,128)(2,1)S(1)}, u32[]{:S(2)}, u32[]{:S(2)}) async-start(bf16[4,512,512]{2,1,0:T(8,128)(2,1)} %pad_maximum_fusion.4), calls=%async_computation | async-start | bytes 4194304 | tf_op jit(solution)/shard_map/all_to_all | solution.py:20
  82.9 41.6 %all-to-all-start.1 = ((bf16[4,256,1152]{2,1,0:T(8,128)(2,1)}), bf16[4,256,1152]{2,1,0:T(8,128)(2,1)S(1)}, u32[]{:S(2)}, u32[]{:S(2)}) async-start(bf16[4,256,1152]{2,1,0:T(8,128)(2,1)} %pad_maximum_fusion), calls=%async_computation.1 | async-start | bytes 4718592 | tf_op jit(solution)/shard_map/all_to_all | solution.py:20
  91.5 31.6 %collective-permute-start.11 = (bf16[1024,512]{1,0:T(8,128)(2,1)}, bf16[1024,512]{1,0:T(8,128)(2,1)}, u32[]{:S(2)}, u32[]{:S(2)}) collective-permute-start(bf16[1024,512]{1,0:T(8,128)(2,1)} %pad_maximum_fusion.28), channel_id=1, source_target_pairs={{0,2},{2,0},{1,3},{3,1},{4,6},{6,4},{5,7},{7,5},{8,10},{10,8},{9,1... | collective-permute-start | bytes 3145736 | tf_op jit(solution)/shard_map/ppermute | solution.py:16
  96.7 25.6 %collective-permute-start.12 = (bf16[512,512]{1,0:T(8,128)(2,1)S(1)}, bf16[512,512]{1,0:T(8,128)(2,1)S(1)}, u32[]{:S(2)}, u32[]{:S(2)}) collective-permute-start(bf16[512,512]{1,0:T(8,128)(2,1)S(1)} %get-tuple-element.297), channel_id=1, source_target_pairs={{0,8},{8,0},{1,9},{9,1},{2,10},{10,2},{3,11},{11,3},{4,12},{12,4},... | collective-permute-start | bytes 1572872 | tf_op jit(solution)/shard_map/ppermute | solution.py:16
  127.8 27.4 %collective-permute-start.13 = (bf16[1024,512]{1,0:T(8,128)(2,1)}, bf16[1024,512]{1,0:T(8,128)(2,1)}, u32[]{:S(2)}, u32[]{:S(2)}) collective-permute-start(bf16[1024,512]{1,0:T(8,128)(2,1)} %pad_maximum_fusion.29), channel_id=1, source_target_pairs={{0,2},{2,0},{1,3},{3,1},{4,6},{6,4},{5,7},{7,5},{8,10},{10,8},{9,1... | collective-permute-start | bytes 3145736 | tf_op jit(solution)/shard_map/ppermute | solution.py:16
  129.5 25.7 %collective-permute-start.14 = (bf16[256,1152]{1,0:T(8,128)(2,1)}, bf16[256,1152]{1,0:T(8,128)(2,1)}, u32[]{:S(2)}, u32[]{:S(2)}) collective-permute-start(bf16[256,1152]{1,0:T(8,128)(2,1)} %get-tuple-element.313), channel_id=1, source_target_pairs={{0,8},{8,0},{1,9},{9,1},{2,10},{10,2},{3,11},{11,3},{4,12},{12,4},... | collective-permute-start | bytes 1769480 | tf_op jit(solution)/shard_map/ppermute | solution.py:16
  133.3 56.7 %all-to-all-start.2 = ((bf16[4,256,1152]{2,1,0:T(8,128)(2,1)}), bf16[4,256,1152]{2,1,0:T(8,128)(2,1)}, u32[]{:S(2)}, u32[]{:S(2)}) async-start(bf16[4,256,1152]{2,1,0:T(8,128)(2,1)} %pad_maximum_fusion.1), calls=%async_computation.2 | async-start | bytes 4718592 | tf_op jit(solution)/shard_map/all_to_all | solution.py:20
  158.9 31.0 %collective-permute-start.16 = (bf16[512,1152]{1,0:T(8,128)(2,1)S(1)}, bf16[512,1152]{1,0:T(8,128)(2,1)}, u32[]{:S(2)}, u32[]{:S(2)}) collective-permute-start(bf16[512,1152]{1,0:T(8,128)(2,1)S(1)} %pad_maximum_fusion.12), channel_id=1, source_target_pairs={{0,2},{2,0},{1,3},{3,1},{4,6},{6,4},{5,7},{7,5},{8,10},{10,8},{9,1... | collective-permute-start | bytes 3538952 | tf_op jit(solution)/shard_map/ppermute | solution.py:16
  160.2 28.9 %collective-permute-start.17 = (bf16[256,1152]{1,0:T(8,128)(2,1)S(1)}, bf16[256,1152]{1,0:T(8,128)(2,1)S(1)}, u32[]{:S(2)}, u32[]{:S(2)}) collective-permute-start(bf16[256,1152]{1,0:T(8,128)(2,1)S(1)} %copy-done.26), channel_id=1, source_target_pairs={{0,8},{8,0},{1,9},{9,1},{2,10},{10,2},{3,11},{11,3},{4,12},{12,4},... | collective-permute-start | bytes 1769480 | tf_op jit(solution)/shard_map/ppermute | solution.py:16
  193.1 30.0 %collective-permute-start.22 = (bf16[512,1152]{1,0:T(8,128)(2,1)S(1)}, bf16[512,1152]{1,0:T(8,128)(2,1)S(1)}, u32[]{:S(2)}, u32[]{:S(2)}) collective-permute-start(bf16[512,1152]{1,0:T(8,128)(2,1)S(1)} %pad_maximum_fusion.13), channel_id=1, source_target_pairs={{0,2},{2,0},{1,3},{3,1},{4,6},{6,4},{5,7},{7,5},{8,10},{10,8},{9,1... | collective-permute-start | bytes 3538952 | tf_op jit(solution)/shard_map/ppermute | solution.py:16
  194.0 29.1 %collective-permute-start.23 = (bf16[256,1152]{1,0:T(8,128)(2,1)S(1)}, bf16[256,1152]{1,0:T(8,128)(2,1)S(1)}, u32[]{:S(2)}, u32[]{:S(2)}) collective-permute-start(bf16[256,1152]{1,0:T(8,128)(2,1)S(1)} %get-tuple-element.330), channel_id=1, source_target_pairs={{0,8},{8,0},{1,9},{9,1},{2,10},{10,2},{3,11},{11,3},{4,12},{12,4},... | collective-permute-start | bytes 1769480 | tf_op jit(solution)/shard_map/ppermute | solution.py:16
  197.0 26.2 %collective-permute-start.19 = (bf16[64,2048]{1,0:T(8,128)(2,1)S(1)}, bf16[64,2048]{1,0:T(8,128)(2,1)S(1)}, u32[]{:S(2)}, u32[]{:S(2)}) collective-permute-start(bf16[64,2048]{1,0:T(8,128)(2,1)S(1)} %get-tuple-element.765), channel_id=1, source_target_pairs={{0,16},{16,0},{1,17},{17,1},{2,18},{18,2},{3,19},{19,3},{4,20},{20... | collective-permute-start | bytes 786440 | tf_op jit(solution)/shard_map/ppermute | solution.py:16
  226.6 27.5 %collective-permute-start.27 = (bf16[512,1152]{1,0:T(8,128)(2,1)S(1)}, bf16[512,1152]{1,0:T(8,128)(2,1)S(1)}, u32[]{:S(2)}, u32[]{:S(2)}) collective-permute-start(bf16[512,1152]{1,0:T(8,128)(2,1)S(1)} %pad_maximum_fusion.14), channel_id=1, source_target_pairs={{0,2},{2,0},{1,3},{3,1},{4,6},{6,4},{5,7},{7,5},{8,10},{10,8},{9,1... | collective-permute-start | bytes 3538952 | tf_op jit(solution)/shard_map/ppermute | solution.py:16
  227.7 26.4 %collective-permute-start.28 = (bf16[256,1152]{1,0:T(8,128)(2,1)S(1)}, bf16[256,1152]{1,0:T(8,128)(2,1)S(1)}, u32[]{:S(2)}, u32[]{:S(2)}) collective-permute-start(bf16[256,1152]{1,0:T(8,128)(2,1)S(1)} %get-tuple-element.334), channel_id=1, source_target_pairs={{0,8},{8,0},{1,9},{9,1},{2,10},{10,2},{3,11},{11,3},{4,12},{12,4},... | collective-permute-start | bytes 1769480 | tf_op jit(solution)/shard_map/ppermute | solution.py:16
  254.5 28.4 %collective-permute-start.30 = (bf16[512,1152]{1,0:T(8,128)(2,1)S(1)}, bf16[512,1152]{1,0:T(8,128)(2,1)S(1)}, u32[]{:S(2)}, u32[]{:S(2)}) collective-permute-start(bf16[512,1152]{1,0:T(8,128)(2,1)S(1)} %pad_maximum_fusion.15), channel_id=1, source_target_pairs={{0,2},{2,0},{1,3},{3,1},{4,6},{6,4},{5,7},{7,5},{8,10},{10,8},{9,1... | collective-permute-start | bytes 3538952 | tf_op jit(solution)/shard_map/ppermute | solution.py:16
  255.6 25.9 %collective-permute-start.31 = (bf16[512,512]{1,0:T(8,128)(2,1)S(1)}, bf16[512,512]{1,0:T(8,128)(2,1)S(1)}, u32[]{:S(2)}, u32[]{:S(2)}) collective-permute-start(bf16[512,512]{1,0:T(8,128)(2,1)S(1)} %copy-done.33), channel_id=1, source_target_pairs={{0,8},{8,0},{1,9},{9,1},{2,10},{10,2},{3,11},{11,3},{4,12},{12,4},... | collective-permute-start | bytes 1572872 | tf_op jit(solution)/shard_map/ppermute | solution.py:16
  292.8 25.9 %collective-permute-start.35 = (bf16[1024,512]{1,0:T(8,128)(2,1)S(1)}, bf16[1024,512]{1,0:T(8,128)(2,1)S(1)}, u32[]{:S(2)}, u32[]{:S(2)}) collective-permute-start(bf16[1024,512]{1,0:T(8,128)(2,1)S(1)} %pad_maximum_fusion.33), channel_id=1, source_target_pairs={{0,2},{2,0},{1,3},{3,1},{4,6},{6,4},{5,7},{7,5},{8,10},{10,8},{9,1... | collective-permute-start | bytes 3145736 | tf_op jit(solution)/shard_map/ppermute | solution.py:16
  321.2 29.9 %collective-permute-start.41 = (bf16[1024,512]{1,0:T(8,128)(2,1)S(1)}, bf16[1024,512]{1,0:T(8,128)(2,1)S(1)}, u32[]{:S(2)}, u32[]{:S(2)}) collective-permute-start(bf16[1024,512]{1,0:T(8,128)(2,1)S(1)} %pad_maximum_fusion.34), channel_id=1, source_target_pairs={{0,2},{2,0},{1,3},{3,1},{4,6},{6,4},{5,7},{7,5},{8,10},{10,8},{9,1... | collective-permute-start | bytes 3145736 | tf_op jit(solution)/shard_map/ppermute | solution.py:16
  322.3 28.8 %collective-permute-start.42 = (bf16[256,1152]{1,0:T(8,128)(2,1)S(1)}, bf16[256,1152]{1,0:T(8,128)(2,1)S(1)}, u32[]{:S(2)}, u32[]{:S(2)}) collective-permute-start(bf16[256,1152]{1,0:T(8,128)(2,1)S(1)} %copy-done.25), channel_id=1, source_target_pairs={{0,8},{8,0},{1,9},{9,1},{2,10},{10,2},{3,11},{11,3},{4,12},{12,4},... | collective-permute-start | bytes 1769480 | tf_op jit(solution)/shard_map/ppermute | solution.py:16
  323.7 27.5 %collective-permute-start.38 = (bf16[64,2048]{1,0:T(8,128)(2,1)S(1)}, bf16[64,2048]{1,0:T(8,128)(2,1)S(1)}, u32[]{:S(2)}, u32[]{:S(2)}) collective-permute-start(bf16[64,2048]{1,0:T(8,128)(2,1)S(1)} %get-tuple-element.747), channel_id=1, source_target_pairs={{0,16},{16,0},{1,17},{17,1},{2,18},{18,2},{3,19},{19,3},{4,20},{20... | collective-permute-start | bytes 786440 | tf_op jit(solution)/shard_map/ppermute | solution.py:16
  324.9 26.2 %collective-permute-start.39 = (bf16[64,2048]{1,0:T(8,128)(2,1)S(1)}, bf16[64,2048]{1,0:T(8,128)(2,1)S(1)}, u32[]{:S(2)}, u32[]{:S(2)}) collective-permute-start(bf16[64,2048]{1,0:T(8,128)(2,1)S(1)} %get-tuple-element.746), channel_id=1, source_target_pairs={{0,4},{4,0},{1,5},{5,1},{2,6},{6,2},{3,7},{7,3},{8,12},{12,8},{9,1... | collective-permute-start | bytes 786440 | tf_op jit(solution)/shard_map/ppermute | solution.py:16
  327.5 24.9 %collective-permute-start.40 = (bf16[64,2048]{1,0:T(8,128)(2,1)S(1)}, bf16[64,2048]{1,0:T(8,128)(2,1)S(1)}, u32[]{:S(2)}, u32[]{:S(2)}) collective-permute-start(bf16[64,2048]{1,0:T(8,128)(2,1)S(1)} %get-tuple-element.745), channel_id=1, source_target_pairs={{0,20},{4,16},{16,4},{20,0},{1,21},{5,17},{17,5},{21,1},{2,22},{6,... | collective-permute-start | bytes 786440 | tf_op jit(solution)/shard_map/ppermute | solution.py:50
  352.8 31.8 %collective-permute-start.46 = (bf16[512,1152]{1,0:T(8,128)(2,1)S(1)}, bf16[512,1152]{1,0:T(8,128)(2,1)S(1)}, u32[]{:S(2)}, u32[]{:S(2)}) collective-permute-start(bf16[512,1152]{1,0:T(8,128)(2,1)S(1)} %pad_maximum_fusion.16), channel_id=1, source_target_pairs={{0,2},{2,0},{1,3},{3,1},{4,6},{6,4},{5,7},{7,5},{8,10},{10,8},{9,1... | collective-permute-start | bytes 3538952 | tf_op jit(solution)/shard_map/ppermute | solution.py:16
  357.6 27.0 %collective-permute-start.47 = (bf16[256,1152]{1,0:T(8,128)(2,1)S(1)}, bf16[256,1152]{1,0:T(8,128)(2,1)S(1)}, u32[]{:S(2)}, u32[]{:S(2)}) collective-permute-start(bf16[256,1152]{1,0:T(8,128)(2,1)S(1)} %get-tuple-element.371), channel_id=1, source_target_pairs={{0,8},{8,0},{1,9},{9,1},{2,10},{10,2},{3,11},{11,3},{4,12},{12,4},... | collective-permute-start | bytes 1769480 | tf_op jit(solution)/shard_map/ppermute | solution.py:16
  384.9 28.4 %collective-permute-start.49 = (bf16[512,1152]{1,0:T(8,128)(2,1)S(1)}, bf16[512,1152]{1,0:T(8,128)(2,1)S(1)}, u32[]{:S(2)}, u32[]{:S(2)}) collective-permute-start(bf16[512,1152]{1,0:T(8,128)(2,1)S(1)} %pad_maximum_fusion.17), channel_id=1, source_target_pairs={{0,2},{2,0},{1,3},{3,1},{4,6},{6,4},{5,7},{7,5},{8,10},{10,8},{9,1... | collective-permute-start | bytes 3538952 | tf_op jit(solution)/shard_map/ppermute | solution.py:16
  385.9 27.5 %collective-permute-start.50 = (bf16[256,1152]{1,0:T(8,128)(2,1)S(1)}, bf16[256,1152]{1,0:T(8,128)(2,1)S(1)}, u32[]{:S(2)}, u32[]{:S(2)}) collective-permute-start(bf16[256,1152]{1,0:T(8,128)(2,1)S(1)} %get-tuple-element.381), channel_id=1, source_target_pairs={{0,8},{8,0},{1,9},{9,1},{2,10},{10,2},{3,11},{11,3},{4,12},{12,4},... | collective-permute-start | bytes 1769480 | tf_op jit(solution)/shard_map/ppermute | solution.py:16
  415.9 30.1 %collective-permute-start.55 = (bf16[512,1152]{1,0:T(8,128)(2,1)}, bf16[512,1152]{1,0:T(8,128)(2,1)}, u32[]{:S(2)}, u32[]{:S(2)}) collective-permute-start(bf16[512,1152]{1,0:T(8,128)(2,1)} %pad_maximum_fusion.18), channel_id=1, source_target_pairs={{0,2},{2,0},{1,3},{3,1},{4,6},{6,4},{5,7},{7,5},{8,10},{10,8},{9,1... | collective-permute-start | bytes 3538952 | tf_op jit(solution)/shard_map/ppermute | solution.py:16
  416.9 29.1 %collective-permute-start.56 = (bf16[256,1152]{1,0:T(8,128)(2,1)S(1)}, bf16[256,1152]{1,0:T(8,128)(2,1)S(1)}, u32[]{:S(2)}, u32[]{:S(2)}) collective-permute-start(bf16[256,1152]{1,0:T(8,128)(2,1)S(1)} %get-tuple-element.387), channel_id=1, source_target_pairs={{0,8},{8,0},{1,9},{9,1},{2,10},{10,2},{3,11},{11,3},{4,12},{12,4},... | collective-permute-start | bytes 1769480 | tf_op jit(solution)/shard_map/ppermute | solution.py:16
  417.4 28.6 %collective-permute-start.52 = (bf16[64,2048]{1,0:T(8,128)(2,1)S(1)}, bf16[64,2048]{1,0:T(8,128)(2,1)S(1)}, u32[]{:S(2)}, u32[]{:S(2)}) collective-permute-start(bf16[64,2048]{1,0:T(8,128)(2,1)S(1)} %get-tuple-element.740), channel_id=1, source_target_pairs={{0,16},{16,0},{1,17},{17,1},{2,18},{18,2},{3,19},{19,3},{4,20},{20... | collective-permute-start | bytes 786440 | tf_op jit(solution)/shard_map/ppermute | solution.py:16
  419.1 26.9 %collective-permute-start.53 = (bf16[64,2048]{1,0:T(8,128)(2,1)S(1)}, bf16[64,2048]{1,0:T(8,128)(2,1)S(1)}, u32[]{:S(2)}, u32[]{:S(2)}) collective-permute-start(bf16[64,2048]{1,0:T(8,128)(2,1)S(1)} %get-tuple-element.739), channel_id=1, source_target_pairs={{0,4},{4,0},{1,5},{5,1},{2,6},{6,2},{3,7},{7,3},{8,12},{12,8},{9,1... | collective-permute-start | bytes 786440 | tf_op jit(solution)/shard_map/ppermute | solution.py:16
  450.1 27.1 %collective-permute-start.60 = (bf16[512,1152]{1,0:T(8,128)(2,1)S(1)}, bf16[512,1152]{1,0:T(8,128)(2,1)S(1)}, u32[]{:S(2)}, u32[]{:S(2)}) collective-permute-start(bf16[512,1152]{1,0:T(8,128)(2,1)S(1)} %pad_maximum_fusion.19), channel_id=1, source_target_pairs={{0,2},{2,0},{1,3},{3,1},{4,6},{6,4},{5,7},{7,5},{8,10},{10,8},{9,1... | collective-permute-start | bytes 3538952 | tf_op jit(solution)/shard_map/ppermute | solution.py:16
  492.2 28.2 %collective-permute-start.63 = (bf16[512,1152]{1,0:T(8,128)(2,1)S(1)}, bf16[512,1152]{1,0:T(8,128)(2,1)}, u32[]{:S(2)}, u32[]{:S(2)}) collective-permute-start(bf16[512,1152]{1,0:T(8,128)(2,1)S(1)} %pad_maximum_fusion.20), channel_id=1, source_target_pairs={{0,2},{2,0},{1,3},{3,1},{4,6},{6,4},{5,7},{7,5},{8,10},{10,8},{9,1... | collective-permute-start | bytes 3538952 | tf_op jit(solution)/shard_map/ppermute | solution.py:16
  524.9 29.2 %collective-permute-start.68 = (bf16[256,1152]{1,0:T(8,128)(2,1)S(1)}, bf16[256,1152]{1,0:T(8,128)(2,1)S(1)}, u32[]{:S(2)}, u32[]{:S(2)}) collective-permute-start(bf16[256,1152]{1,0:T(8,128)(2,1)S(1)} %fusion.106), channel_id=1, source_target_pairs={{0,8},{8,0},{1,9},{9,1},{2,10},{10,2},{3,11},{11,3},{4,12},{12,4},... | collective-permute-start | bytes 1769480 | tf_op jit(solution)/shard_map/ppermute | solution.py:16
  525.1 28.9 %collective-permute-start.69 = (bf16[512,1152]{1,0:T(8,128)(2,1)}, bf16[512,1152]{1,0:T(8,128)(2,1)}, u32[]{:S(2)}, u32[]{:S(2)}) collective-permute-start(bf16[512,1152]{1,0:T(8,128)(2,1)} %pad_maximum_fusion.21), channel_id=1, source_target_pairs={{0,2},{2,0},{1,3},{3,1},{4,6},{6,4},{5,7},{7,5},{8,10},{10,8},{9,1... | collective-permute-start | bytes 3538952 | tf_op jit(solution)/shard_map/ppermute | solution.py:16
  526.6 27.4 %collective-permute-start.65 = (bf16[64,2048]{1,0:T(8,128)(2,1)S(1)}, bf16[64,2048]{1,0:T(8,128)(2,1)S(1)}, u32[]{:S(2)}, u32[]{:S(2)}) collective-permute-start(bf16[64,2048]{1,0:T(8,128)(2,1)S(1)} %get-tuple-element.737), channel_id=1, source_target_pairs={{0,16},{16,0},{1,17},{17,1},{2,18},{18,2},{3,19},{19,3},{4,20},{20... | collective-permute-start | bytes 786440 | tf_op jit(solution)/shard_map/ppermute | solution.py:16
  528.1 25.9 %collective-permute-start.66 = (bf16[64,2048]{1,0:T(8,128)(2,1)S(1)}, bf16[64,2048]{1,0:T(8,128)(2,1)S(1)}, u32[]{:S(2)}, u32[]{:S(2)}) collective-permute-start(bf16[64,2048]{1,0:T(8,128)(2,1)S(1)} %get-tuple-element.736), channel_id=1, source_target_pairs={{0,4},{4,0},{1,5},{5,1},{2,6},{6,2},{3,7},{7,3},{8,12},{12,8},{9,1... | collective-permute-start | bytes 786440 | tf_op jit(solution)/shard_map/ppermute | solution.py:16
  558.5 29.2 %collective-permute-start.73 = (bf16[256,1152]{1,0:T(8,128)(2,1)S(1)}, bf16[256,1152]{1,0:T(8,128)(2,1)S(1)}, u32[]{:S(2)}, u32[]{:S(2)}) collective-permute-start(bf16[256,1152]{1,0:T(8,128)(2,1)S(1)} %fusion.105), channel_id=1, source_target_pairs={{0,8},{8,0},{1,9},{9,1},{2,10},{10,2},{3,11},{11,3},{4,12},{12,4},... | collective-permute-start | bytes 1769480 | tf_op jit(solution)/shard_map/ppermute | solution.py:16
  560.1 27.7 %collective-permute-start.74 = (bf16[512,1152]{1,0:T(8,128)(2,1)S(1)}, bf16[512,1152]{1,0:T(8,128)(2,1)S(1)}, u32[]{:S(2)}, u32[]{:S(2)}) collective-permute-start(bf16[512,1152]{1,0:T(8,128)(2,1)S(1)} %pad_maximum_fusion.22), channel_id=1, source_target_pairs={{0,2},{2,0},{1,3},{3,1},{4,6},{6,4},{5,7},{7,5},{8,10},{10,8},{9,1... | collective-permute-start | bytes 3538952 | tf_op jit(solution)/shard_map/ppermute | solution.py:16
  589.2 29.3 %collective-permute-start.76 = (bf16[256,1152]{1,0:T(8,128)(2,1)S(1)}, bf16[256,1152]{1,0:T(8,128)(2,1)}, u32[]{:S(2)}, u32[]{:S(2)}) collective-permute-start(bf16[256,1152]{1,0:T(8,128)(2,1)S(1)} %fusion.104), channel_id=1, source_target_pairs={{0,8},{8,0},{1,9},{9,1},{2,10},{10,2},{3,11},{11,3},{4,12},{12,4},... | collective-permute-start | bytes 1769480 | tf_op jit(solution)/shard_map/ppermute | solution.py:16
  590.6 28.2 %collective-permute-start.77 = (bf16[512,1152]{1,0:T(8,128)(2,1)S(1)}, bf16[512,1152]{1,0:T(8,128)(2,1)}, u32[]{:S(2)}, u32[]{:S(2)}) collective-permute-start(bf16[512,1152]{1,0:T(8,128)(2,1)S(1)} %pad_maximum_fusion.23), channel_id=1, source_target_pairs={{0,2},{2,0},{1,3},{3,1},{4,6},{6,4},{5,7},{7,5},{8,10},{10,8},{9,1... | collective-permute-start | bytes 3538952 | tf_op jit(solution)/shard_map/ppermute | solution.py:16
  623.7 29.2 %collective-permute-start.82 = (bf16[256,1152]{1,0:T(8,128)(2,1)S(1)}, bf16[256,1152]{1,0:T(8,128)(2,1)S(1)}, u32[]{:S(2)}, u32[]{:S(2)}) collective-permute-start(bf16[256,1152]{1,0:T(8,128)(2,1)S(1)} %fusion.103), channel_id=1, source_target_pairs={{0,8},{8,0},{1,9},{9,1},{2,10},{10,2},{3,11},{11,3},{4,12},{12,4},... | collective-permute-start | bytes 1769480 | tf_op jit(solution)/shard_map/ppermute | solution.py:16
  625.4 27.6 %collective-permute-start.83 = (bf16[1024,512]{1,0:T(8,128)(2,1)S(1)}, bf16[1024,512]{1,0:T(8,128)(2,1)S(1)}, u32[]{:S(2)}, u32[]{:S(2)}) collective-permute-start(bf16[1024,512]{1,0:T(8,128)(2,1)S(1)} %pad_maximum_fusion.41), channel_id=1, source_target_pairs={{0,2},{2,0},{1,3},{3,1},{4,6},{6,4},{5,7},{7,5},{8,10},{10,8},{9,1... | collective-permute-start | bytes 3145736 | tf_op jit(solution)/shard_map/ppermute | solution.py:16
  626.8 26.1 %collective-permute-start.79 = (bf16[64,2048]{1,0:T(8,128)(2,1)S(1)}, bf16[64,2048]{1,0:T(8,128)(2,1)S(1)}, u32[]{:S(2)}, u32[]{:S(2)}) collective-permute-start(bf16[64,2048]{1,0:T(8,128)(2,1)S(1)} %get-tuple-element.734), channel_id=1, source_target_pairs={{0,16},{16,0},{1,17},{17,1},{2,18},{18,2},{3,19},{19,3},{4,20},{20... | collective-permute-start | bytes 786440 | tf_op jit(solution)/shard_map/ppermute | solution.py:16
  628.8 25.6 %collective-permute-start.81 = (bf16[64,2048]{1,0:T(8,128)(2,1)S(1)}, bf16[64,2048]{1,0:T(8,128)(2,1)S(1)}, u32[]{:S(2)}, u32[]{:S(2)}) collective-permute-start(bf16[64,2048]{1,0:T(8,128)(2,1)S(1)} %get-tuple-element.732), channel_id=1, source_target_pairs={{0,20},{4,16},{16,4},{20,0},{1,21},{5,17},{17,5},{21,1},{2,22},{6,... | collective-permute-start | bytes 786440 | tf_op jit(solution)/shard_map/ppermute | solution.py:50
  656.8 26.0 %collective-permute-start.88 = (bf16[1024,512]{1,0:T(8,128)(2,1)S(1)}, bf16[1024,512]{1,0:T(8,128)(2,1)S(1)}, u32[]{:S(2)}, u32[]{:S(2)}) collective-permute-start(bf16[1024,512]{1,0:T(8,128)(2,1)S(1)} %pad_maximum_fusion.45), channel_id=1, source_target_pairs={{0,2},{2,0},{1,3},{3,1},{4,6},{6,4},{5,7},{7,5},{8,10},{10,8},{9,1... | collective-permute-start | bytes 3145736 | tf_op jit(solution)/shard_map/ppermute | solution.py:16
  657.7 25.1 %collective-permute-start.87 = (bf16[512,512]{1,0:T(8,128)(2,1)S(1)}, bf16[512,512]{1,0:T(8,128)(2,1)S(1)}, u32[]{:S(2)}, u32[]{:S(2)}) collective-permute-start(bf16[512,512]{1,0:T(8,128)(2,1)S(1)} %slice.1937), channel_id=1, source_target_pairs={{0,8},{8,0},{1,9},{9,1},{2,10},{10,2},{3,11},{11,3},{4,12},{12,4},... | collective-permute-start | bytes 1572872 | tf_op jit(solution)/shard_map/ppermute | solution.py:16
  692.6 25.5 %collective-permute-start.94 = (bf16[512,512]{1,0:T(8,128)(2,1)S(1)}, bf16[512,512]{1,0:T(8,128)(2,1)S(1)}, u32[]{:S(2)}, u32[]{:S(2)}) collective-permute-start(bf16[512,512]{1,0:T(8,128)(2,1)S(1)} %slice.1946), channel_id=1, source_target_pairs={{0,8},{8,0},{1,9},{9,1},{2,10},{10,2},{3,11},{11,3},{4,12},{12,4},... | collective-permute-start | bytes 1572872 | tf_op jit(solution)/shard_map/ppermute | solution.py:16
  724.2 28.4 %collective-permute-start.96 = (bf16[512,1152]{1,0:T(8,128)(2,1)S(1)}, bf16[512,1152]{1,0:T(8,128)(2,1)S(1)}, u32[]{:S(2)}, u32[]{:S(2)}) collective-permute-start(bf16[512,1152]{1,0:T(8,128)(2,1)S(1)} %pad_maximum_fusion.24), channel_id=1, source_target_pairs={{0,2},{2,0},{1,3},{3,1},{4,6},{6,4},{5,7},{7,5},{8,10},{10,8},{9,1... | collective-permute-start | bytes 3538952 | tf_op jit(solution)/shard_map/ppermute | solution.py:16
  753.7 30.3 %collective-permute-start.101 = (bf16[512,1152]{1,0:T(8,128)(2,1)S(1)}, bf16[512,1152]{1,0:T(8,128)(2,1)S(1)}, u32[]{:S(2)}, u32[]{:S(2)}) collective-permute-start(bf16[512,1152]{1,0:T(8,128)(2,1)S(1)} %pad_maximum_fusion.25), channel_id=1, source_target_pairs={{0,2},{2,0},{1,3},{3,1},{4,6},{6,4},{5,7},{7,5},{8,10},{10,8},{9,1... | collective-permute-start | bytes 3538952 | tf_op jit(solution)/shard_map/ppermute | solution.py:16
  756.1 27.9 %collective-permute-start.100 = (bf16[256,1152]{1,0:T(8,128)(2,1)S(1)}, bf16[256,1152]{1,0:T(8,128)(2,1)S(1)}, u32[]{:S(2)}, u32[]{:S(2)}) collective-permute-start(bf16[256,1152]{1,0:T(8,128)(2,1)S(1)} %fusion.102), channel_id=1, source_target_pairs={{0,8},{8,0},{1,9},{9,1},{2,10},{10,2},{3,11},{11,3},{4,12},{12,4},... | collective-permute-start | bytes 1769480 | tf_op jit(solution)/shard_map/ppermute | solution.py:16
  786.2 28.8 %collective-permute-start.105 = (bf16[256,1152]{1,0:T(8,128)(2,1)S(1)}, bf16[256,1152]{1,0:T(8,128)(2,1)S(1)}, u32[]{:S(2)}, u32[]{:S(2)}) collective-permute-start(bf16[256,1152]{1,0:T(8,128)(2,1)S(1)} %fusion.101), channel_id=1, source_target_pairs={{0,8},{8,0},{1,9},{9,1},{2,10},{10,2},{3,11},{11,3},{4,12},{12,4},... | collective-permute-start | bytes 1769480 | tf_op jit(solution)/shard_map/ppermute | solution.py:16
  786.2 28.7 %collective-permute-start.106 = (bf16[512,1152]{1,0:T(8,128)(2,1)S(1)}, bf16[512,1152]{1,0:T(8,128)(2,1)S(1)}, u32[]{:S(2)}, u32[]{:S(2)}) collective-permute-start(bf16[512,1152]{1,0:T(8,128)(2,1)S(1)} %pad_maximum_fusion.26), channel_id=1, source_target_pairs={{0,2},{2,0},{1,3},{3,1},{4,6},{6,4},{5,7},{7,5},{8,10},{10,8},{9,1... | collective-permute-start | bytes 3538952 | tf_op jit(solution)/shard_map/ppermute | solution.py:16
  820.0 29.7 %collective-permute-start.108 = (bf16[256,1152]{1,0:T(8,128)(2,1)}, bf16[256,1152]{1,0:T(8,128)(2,1)}, u32[]{:S(2)}, u32[]{:S(2)}) collective-permute-start(bf16[256,1152]{1,0:T(8,128)(2,1)} %fusion.100), channel_id=1, source_target_pairs={{0,8},{8,0},{1,9},{9,1},{2,10},{10,2},{3,11},{11,3},{4,12},{12,4},... | collective-permute-start | bytes 1769480 | tf_op jit(solution)/shard_map/ppermute | solution.py:16
  821.8 28.4 %collective-permute-start.109 = (bf16[512,1152]{1,0:T(8,128)(2,1)}, bf16[512,1152]{1,0:T(8,128)(2,1)}, u32[]{:S(2)}, u32[]{:S(2)}) collective-permute-start(bf16[512,1152]{1,0:T(8,128)(2,1)} %pad_maximum_fusion.27), channel_id=1, source_target_pairs={{0,2},{2,0},{1,3},{3,1},{4,6},{6,4},{5,7},{7,5},{8,10},{10,8},{9,1... | collective-permute-start | bytes 3538952 | tf_op jit(solution)/shard_map/ppermute | solution.py:16
  822.7 68.5 %all-to-all-start.3 = ((bf16[4,256,1152]{2,1,0:T(8,128)(2,1)}), bf16[4,256,1152]{2,1,0:T(8,128)(2,1)S(1)}, u32[]{:S(2)}, u32[]{:S(2)}) async-start(bf16[4,256,1152]{2,1,0:T(8,128)(2,1)} %pad_maximum_fusion.2), calls=%async_computation.3 | async-start | bytes 4718592 | tf_op jit(solution)/shard_map/all_to_all | solution.py:20
  855.4 29.5 %collective-permute-start.114 = (bf16[256,1152]{1,0:T(8,128)(2,1)S(1)}, bf16[256,1152]{1,0:T(8,128)(2,1)S(1)}, u32[]{:S(2)}, u32[]{:S(2)}) collective-permute-start(bf16[256,1152]{1,0:T(8,128)(2,1)S(1)} %fusion.99), channel_id=1, source_target_pairs={{0,8},{8,0},{1,9},{9,1},{2,10},{10,2},{3,11},{11,3},{4,12},{12,4},... | collective-permute-start | bytes 1769480 | tf_op jit(solution)/shard_map/ppermute | solution.py:16
  856.6 28.3 %collective-permute-start.115 = (bf16[1024,512]{1,0:T(8,128)(2,1)S(1)}, bf16[1024,512]{1,0:T(8,128)(2,1)S(1)}, u32[]{:S(2)}, u32[]{:S(2)}) collective-permute-start(bf16[1024,512]{1,0:T(8,128)(2,1)S(1)} %pad_maximum_fusion.50), channel_id=1, source_target_pairs={{0,2},{2,0},{1,3},{3,1},{4,6},{6,4},{5,7},{7,5},{8,10},{10,8},{9,1... | collective-permute-start | bytes 3145736 | tf_op jit(solution)/shard_map/ppermute | solution.py:16
  858.4 26.6 %collective-permute-start.111 = (bf16[64,2048]{1,0:T(8,128)(2,1)S(1)}, bf16[64,2048]{1,0:T(8,128)(2,1)S(1)}, u32[]{:S(2)}, u32[]{:S(2)}) collective-permute-start(bf16[64,2048]{1,0:T(8,128)(2,1)S(1)} %get-tuple-element.728), channel_id=1, source_target_pairs={{0,16},{16,0},{1,17},{17,1},{2,18},{18,2},{3,19},{19,3},{4,20},{20... | collective-permute-start | bytes 786440 | tf_op jit(solution)/shard_map/ppermute | solution.py:16
  859.7 26.0 %collective-permute-start.112 = (bf16[64,2048]{1,0:T(8,128)(2,1)S(1)}, bf16[64,2048]{1,0:T(8,128)(2,1)S(1)}, u32[]{:S(2)}, u32[]{:S(2)}) collective-permute-start(bf16[64,2048]{1,0:T(8,128)(2,1)S(1)} %get-tuple-element.727), channel_id=1, source_target_pairs={{0,4},{4,0},{1,5},{5,1},{2,6},{6,2},{3,7},{7,3},{8,12},{12,8},{9,1... | collective-permute-start | bytes 786440 | tf_op jit(solution)/shard_map/ppermute | solution.py:16
  860.9 30.2 %collective-permute-start.113 = (bf16[64,2048]{1,0:T(8,128)(2,1)S(1)}, bf16[64,2048]{1,0:T(8,128)(2,1)}, u32[]{:S(2)}, u32[]{:S(2)}) collective-permute-start(bf16[64,2048]{1,0:T(8,128)(2,1)S(1)} %get-tuple-element.726), channel_id=1, source_target_pairs={{0,20},{4,16},{16,4},{20,0},{1,21},{5,17},{17,5},{21,1},{2,22},{6,... | collective-permute-start | bytes 786440 | tf_op jit(solution)/shard_map/ppermute | solution.py:50
  904.9 54.4 %all-to-all-start.4 = ((bf16[4,256,1152]{2,1,0:T(8,128)(2,1)}), bf16[4,256,1152]{2,1,0:T(8,128)(2,1)}, u32[]{:S(2)}, u32[]{:S(2)}) async-start(bf16[4,256,1152]{2,1,0:T(8,128)(2,1)} %pad_maximum_fusion.3), calls=%async_computation.4 | async-start | bytes 4718592 | tf_op jit(solution)/shard_map/all_to_all | solution.py:20
  932.5 26.8 %collective-permute-start.121 = (bf16[512,512]{1,0:T(8,128)(2,1)S(1)}, bf16[512,512]{1,0:T(8,128)(2,1)}, u32[]{:S(2)}, u32[]{:S(2)}) collective-permute-start(bf16[512,512]{1,0:T(8,128)(2,1)S(1)} %slice.1992), channel_id=1, source_target_pairs={{0,8},{8,0},{1,9},{9,1},{2,10},{10,2},{3,11},{11,3},{4,12},{12,4},... | collective-permute-start | bytes 1572872 | tf_op jit(solution)/shard_map/ppermute | solution.py:16
  963.6 31.7 %collective-permute-start.122 = (bf16[64,2048]{1,0:T(8,128)(2,1)S(1)}, bf16[64,2048]{1,0:T(8,128)(2,1)S(1)}, u32[]{:S(2)}, u32[]{:S(2)}) collective-permute-start(bf16[64,2048]{1,0:T(8,128)(2,1)S(1)} %broadcast_select_fusion.5), channel_id=1, source_target_pairs={{0,8},{8,0},{1,9},{9,1},{2,10},{10,2},{3,11},{11,3},{4,12},{12,4},... | collective-permute-start | bytes 786440 | tf_op jit(solution)/shard_map/ppermute | solution.py:16
  963.7 47.2 %all-to-all-start.5 = ((bf16[4,512,512]{2,1,0:T(8,128)(2,1)}), bf16[4,512,512]{2,1,0:T(8,128)(2,1)}, u32[]{:S(2)}, u32[]{:S(2)}) async-start(bf16[4,512,512]{2,1,0:T(8,128)(2,1)} %pad_maximum_fusion.7), calls=%async_computation.5 | async-start | bytes 4194304 | tf_op jit(solution)/shard_map/all_to_all | solution.py:20
  (328 other events, 3448.4 us)

commit v4 on v3

--- a/solution.py
+++ b/solution.py
@@ -73,13 +73,23 @@
     return jnp.concatenate(pieces)
 
 
-def scatter_sum(near, far, middle, last):
+def scatter_core(near, far):
     total = near + swap(far, "k").astype(f32)
     part = total.shape[0] // 4
-    total, far = middle((total[:part], total[part:].astype(bf16)))
-    pieces = [swap(far[:part], "s"), swap(far[part : 2 * part], "t"), cross(far[2 * part :])]
-    total, pieces = last((total, pieces))
+    return total[:part], total[part:].astype(bf16)
+
+
+def scatter_near(total, far):
+    part = total.shape[0]
+    return total, [swap(far[:part], "s"), swap(far[part : 2 * part], "t"), cross(far[2 * part :])]
+
+
+def added(total, pieces):
     return total + sum(piece.astype(f32) for piece in pieces)
+
+
+def scatter_sum(near, far, middle, last):
+    return added(*last(scatter_near(*middle(scatter_core(near, far)))))
 
 
 def split_product(lefts, rights):
@@ -165,7 +175,7 @@
     "m11": ("B15", "B16", "B16", "B18"),
     "m31": ("B16", "B18", "B18", "B1X"),
     "a01": ("B18", "B1X", "B1X", "B01"),
-    "a11": ("B1X", "B01", "B01", "B02"),
+    "a11": ("B1X", "B01", "B02", "B04"),
     "m00": ("B02", "B04", "B04", "B05"),
     "m20": ("B04", "B05", "B05", "B06"),
     "m10": ("B05", "B06", "B06", "B08"),
@@ -198,6 +208,81 @@
     packed = jnp.concatenate([attn_gain[0], mlp_gain[0], query_gain[0], key_norm_gain[0]])[None]
     packed = pair(s, packed, swap(packed, "s"))
 
+    rows = boundary[0].reshape(2, 2 * tok, width)
+    rows = pair(y, take(rows, y), swap(take(rows, 1 - y), "y")).reshape(2, 2, 2, tok // 2, width)
+    rows = pair(k, take(rows, k, 2), swap(take(rows, 1 - k, 2), "k"))
+    rows = jnp.stack(
+        [jnp.concatenate([rows[j, i, m] for i in (0, 1) for j in (0, 1)], 1) for m in (0, 1)]
+    )
+
+    def quarters(weight):
+        size = weight.shape[1] // 4
+        return [weight[:, i * size : (i + 1) * size] for i in range(4)]
+
+    def to_groups(value):
+        return exchange(value, ("s", "t"))
+
+    a_home = []
+    for i, (q, o) in enumerate(zip(quarters(w_query[0]), quarters(w_out[0].T))):
+        low = (i // 2) * head
+        kv = [w[0, :, low : low + head] for w in (key_projection, value_projection)]
+        a_home.append(jnp.concatenate([q, o] + kv, 1))
+    a_home, packed = lax.optimization_barrier((plain(jnp.stack(a_home)), packed))
+    fetched_a = to_groups(a_home)
+    def rolled(value):
+        half = value.shape[-1] // 2
+        return jnp.where(h == 0, value, jnp.concatenate([value[..., half:], value[..., :half]], -1))
+
+    homes = {}
+
+    def fetch(name):
+        clock.add(name, *FETCH[name], lambda: homes[name], to_groups)
+
+    def spread(name):
+        i, layer = int(name[1]), int(name[2])
+        source, block = ("a", i) if name[0] == "a" else (f"m{i % 2}", i // 2)
+        plan = SPREAD[name]
+
+        def start():
+            return clock.ready[source][2 * layer + block]
+
+        def onward():
+            value = [start(), clock.ready[name + "h"]]
+            if groups > 1:
+                value = [lax.all_gather(half, "g", axis=0, tiled=True) for half in value]
+            clock.ready[name] = jnp.concatenate(value)
+            return clock.ready[name]
+
+        clock.add(name + "h", plan[0], plan[1], start, lambda value: swap(value, "h"))
+        clock.add(name + "y", plan[2], plan[3], onward, lambda value: swap(value, "y"))
+
+    def places_of(kind):
+        count = 2 if kind == "m" else 1
+        size = rb // count
+        for i in range(4 * groups):
+            half, block, group = i // (2 * groups), i // groups % 2, i % groups
+            for j in range(count):
+                yield block * count + j, (half * groups + group) * size, size
+
+    def weight(kind, layer):
+        return [
+            jnp.concatenate(
+                [
+                    clock.ready[f"{kind}{part}{layer}{step}"][low : low + size]
+                    for part, low, size in places_of(kind)
+                ]
+            )
+            for step in ("", "y")
+        ]
+
+    for name in FETCH:
+        fetch(name)
+    for name in SPREAD:
+        spread(name)
+
+    rows, w_gate, w_up, w_down, segment_ids = lax.optimization_barrier(
+        (rows, w_gate, w_up, w_down, segment_ids)
+    )
     segments = take(segment_ids, 2 * y + h)
     part = tok // 2
     slots = slots_of(s, t, k, g, groups, part)
@@ -220,79 +305,6 @@
         key_slots[None, :] <= slots[:, None]
     )
 
-    rows = boundary[0].reshape(2, 2 * tok, width)
-    rows = pair(y, take(rows, y), swap(take(rows, 1 - y), "y")).reshape(2, 2, 2, tok // 2, width)
-    rows = pair(k, take(rows, k, 2), swap(take(rows, 1 - k, 2), "k"))
-    rows = jnp.stack(
-        [jnp.concatenate([rows[j, i, m] for i in (0, 1) for j in (0, 1)], 1) for m in (0, 1)]
-    )
-
-    def quarters(weight):
-        size = weight.shape[1] // 4
-        return [weight[:, i * size : (i + 1) * size] for i in range(4)]
-
-    def to_groups(value):
-        return exchange(value, ("s", "t"))
-
-    a_home = []
-    for i, (q, o) in enumerate(zip(quarters(w_query[0]), quarters(w_out[0].T))):
-        low = (i // 2) * head
-        kv = [w[0, :, low : low + head] for w in (key_projection, value_projection)]
-        a_home.append(jnp.concatenate([q, o] + kv, 1))
-    a_home, packed = lax.optimization_barrier((plain(jnp.stack(a_home)), packed))
-    fetched_a = to_groups(a_home)
-    def rolled(value):
-        half = value.shape[-1] // 2
-        return jnp.where(h == 0, value, jnp.concatenate([value[..., half:], value[..., :half]], -1))
-
-    homes = {}
-
-    def fetch(name):
-        clock.add(name, *FETCH[name], lambda: homes[name], to_groups)
-
-    def spread(name):
-        i, layer = int(name[1]), int(name[2])
-        source, block = ("a", i) if name[0] == "a" else (f"m{i % 2}", i // 2)
-        plan = SPREAD[name]
-
-        def start():
-            return clock.ready[source][2 * layer + block]
-
-        def onward():
-            value = [start(), clock.ready[name + "h"]]
-            if groups > 1:
-                value = [lax.all_gather(half, "g", axis=0, tiled=True) for half in value]
-            clock.ready[name] = jnp.concatenate(value)
-            return clock.ready[name]
-
-        clock.add(name + "h", plan[0], plan[1], start, lambda value: swap(value, "h"))
-        clock.add(name + "y", plan[2], plan[3], onward, lambda value: swap(value, "y"))
-
-    def places_of(kind):
-        count = 2 if kind == "m" else 1
-        size = rb // count
-        for i in range(4 * groups):
-            half, block, group = i // (2 * groups), i // groups % 2, i % groups
-            for j in range(count):
-                yield block * count + j, (half * groups + group) * size, size
-
-    def weight(kind, layer):
-        return [
-            jnp.concatenate(
-                [
-                    clock.ready[f"{kind}{part}{layer}{step}"][low : low + size]
-                    for part, low, size in places_of(kind)
-                ]
-            )
-            for step in ("", "y")
-        ]
-
-    for name in FETCH:
-        fetch(name)
-    for name in SPREAD:
-        spread(name)
-
-    rows, w_gate, w_up, w_down = lax.optimization_barrier((rows, w_gate, w_up, w_down))
     m_home = [
         jnp.concatenate(pieces, 1)
         for pieces in zip(quarters(w_gate[0]), quarters(w_up[0]), quarters(w_down[0].T))
@@ -322,6 +334,7 @@
     )
     top = cotangent.astype(f32) * valid[:, None]
     kept = {}
+    geometry = [cosine, sine, allowed]
 
     def all_keys(value):
         return lax.all_gather(value, "g", axis=0, tiled=True) if groups > 1 else value
@@ -333,7 +346,7 @@
 
     def scores_of(q, keys):
         scores = jnp.einsum("qhd,khd->hqk", q, keys, preferred_element_type=f32) * scale_qk
-        return jnp.where(allowed[None], scores, -1e30)
+        return jnp.where(geometry[2][None], scores, -1e30)
 
     def forward(layer, residual):
         def at(place):
@@ -342,7 +355,11 @@
         scale_a = rms(residual)
         normed = (residual * scale_a * gain_a[layer]).astype(bf16)
         def head_start(pieces):
-            pieces = at(1)(pieces)
+            if layer == 0:
+                pieces, cosine, sine, allowed = at(1)((pieces, *geometry))
+                geometry[:] = [cosine, sine, allowed]
+            else:
+                pieces = at(1)(pieces)
             if layer == 0:
                 for label in ("c1", "c2"):
                     pieces = clock.point(label, pieces)
@@ -354,8 +371,8 @@
         raw = jnp.stack([dot(xa, w[:, 2 * head :]) for w in wa], 1)
         k_raw = raw[:, :, :head]
         v = raw[:, :, head:].astype(bf16)
-        q = rotate(q_raw, gain_q[layer], cosine, sine).astype(bf16)
-        keys = rotate(k_raw, gain_k[layer], cosine, sine).astype(bf16)
+        q = rotate(q_raw, gain_q[layer], *geometry[:2]).astype(bf16)
+        keys = rotate(k_raw, gain_k[layer], *geometry[:2]).astype(bf16)
         keys, values = all_keys(keys), all_keys(v)
         scores = scores_of(q, keys)
         peak = jnp.max(scores, axis=2, keepdims=True)
@@ -402,16 +419,25 @@
                 for left, right in partial[name[0] + layer][i]
             ]
 
+        def packed_rows(i):
+            return plain(jnp.concatenate([value.astype(bf16) for value in rows_of(i)], 1))
+
         def other():
-            return plain(jnp.concatenate([value.astype(bf16) for value in rows_of(1)], 1))
+            if name in ("a00", "a10"):
+                clock.ready["own" + name] = clock.loose["own" + name] = packed_rows(0)
+            return packed_rows(1)
 
         def onward():
-            total, low = [], 0
-            for value in rows_of(0):
-                high = low + value.shape[1]
-                total.append((value + clock.ready["back_y" + name][:, low:high].astype(f32)).astype(bf16))
-                low = high
-            total = plain(jnp.concatenate(total, 1))
+            received = clock.ready["back_y" + name].astype(f32)
+            if "own" + name in clock.ready:
+                total = (clock.ready["own" + name].astype(f32) + received).astype(bf16)
+            else:
+                total, low = [], 0
+                for value in rows_of(0):
+                    high = low + value.shape[1]
+                    total.append((value + received[:, low:high]).astype(bf16))
+                    low = high
+                total = plain(jnp.concatenate(total, 1))
             count = total.shape[0] // 2
             mine, other = total[:count], total[count:]
             if groups > 1:
@@ -452,10 +478,19 @@
             d_up = (grad * gate * sig).astype(bf16)
             d_hidden.append(jnp.concatenate([d_gate, d_up], 1))
         partial[f"m{layer}"] = [((xm, d), (g3, a)) for d, a in zip(d_hidden, act)]
-        d_hidden = at(2)(d_hidden)
+        beside = at(4)
+        if layer == 0:
+            d_hidden, output = at(2)((d_hidden, kept["output"]))
+            output = scatter_near(*output)
+
+            def beside(chain):
+                chain, kept["output"] = lax.optimization_barrier((chain, output))
+                return at(4)(chain)
+        else:
+            d_hidden = at(2)(d_hidden)
         near, far = split_product(d_hidden, [w[:, : 2 * ff] for w in wm])
         near, far = at(3)((near, far))
-        d_xm = scatter_sum(near, far, at(4), at(5))
+        d_xm = scatter_sum(near, far, beside, at(5))
         d_mid, d_gain_m = norm_back(middle, scale_m, gain_m[layer], d_xm)
         d_mid = grad_top + d_mid
         g2 = at(7)(gather_tokens(d_mid.astype(bf16), at(6)))
@@ -468,8 +503,8 @@
         d_k = jnp.einsum("hqk,qhd->khd", d_scores, q, preferred_element_type=f32) * scale_qk
         d_v = jnp.einsum("hqk,qhd->khd", mixing.astype(bf16), d_o, preferred_element_type=f32)
         d_k, d_v = sum_keys(d_k), sum_keys(d_v)
-        _, pull_q = jax.vjp(lambda raw, gain: rotate(raw, gain, cosine, sine), q_raw, gain_q[layer])
-        _, pull_k = jax.vjp(lambda raw, gain: rotate(raw, gain, cosine, sine), k_raw, gain_k[layer])
+        _, pull_q = jax.vjp(lambda raw, gain: rotate(raw, gain, *geometry[:2]), q_raw, gain_q[layer])
+        _, pull_k = jax.vjp(lambda raw, gain: rotate(raw, gain, *geometry[:2]), k_raw, gain_k[layer])
         d_q_raw, d_gain_q = pull_q(d_q)
         d_k_raw, d_gain_k = pull_k(d_k)
         d_q_raw, d_kv_raw = d_q_raw.astype(bf16), jnp.concatenate([d_k_raw, d_v], 2).astype(bf16)
@@ -483,20 +518,19 @@
         return d_mid + d_res, (d_gain_a, d_gain_m, d_gain_q, d_gain_k)
 
     forward(0, entering.astype(f32))
-    act = kept[0][14]
-    near, far, kept["g3"] = clock.point("F09", (*project(0, act), kept["g3"]))
+    act, kept["g3"] = clock.point("F09", (kept[0][14], kept["g3"]))
+    near, far = project(0, act)
     middle = kept[0][10] + scatter_sum(near, far, lambda value: value, lambda value: clock.point("F10", value))
     forward(1, middle.astype(bf16).astype(f32))
     grad, gains1 = backward(1, top, kept["g3"])
     grad = grad.astype(bf16)
     pieces = clock.point("B01", gather_near(grad))
     pieces, act = lax.optimization_barrier((pieces, kept[1][14]))
-    near, far = project(1, act)
-    output = kept[1][10] + scatter_sum(near, far, lambda value: value, lambda value: value)
-    g3, kept["output"] = lax.optimization_barrier((gather_core(pieces), output))
+    kept["output"] = scatter_core(*project(1, act))
+    g3 = gather_core(pieces)
     grad, gains0 = backward(0, grad.astype(f32), g3)
 
-    low, high = rolled(grad.astype(bf16)), rolled(kept["output"].astype(bf16))
+    low, high = rolled(grad.astype(bf16)), rolled((kept[1][10] + added(*kept["output"])).astype(bf16))
     keep = jnp.where(s == 0, low, high)
     passed = swap(jnp.where(s == 0, high, low), "s")
     (keep, passed), gains0, gains1 = clock.point("E1", ((keep, passed), gains0, gains1))
@@ -506,6 +540,7 @@
     sums = jnp.concatenate(sums)
     sums = sums.reshape(-1, head)
     sums = sums + swap(sums, "k")
+    sums = sums + swap(sums, "s")
     sums = sums + swap(sums, "t")
     keep, passed, sums = clock.point("E2", (keep, passed, sums))
     last = both_layers("a")
@@ -521,7 +556,6 @@
     rows = pair(k, mine, swap(other, "k"), 2).reshape(2, 2, tok, width)
     rows = pair(y, take(rows, y), swap(take(rows, 1 - y), "y"))
     section_out = rows.reshape(micro, tok, width)
-    sums = sums + swap(sums, "s")
     sums = sums + swap(sums, "h")
     if groups > 1:
         sums = lax.psum(sums, "g")

time: 1030 us -> 1000 us (0.971)
  waiting for transfers between devices: 585 us -> 540 us
  starting transfers between devices: 154 us -> 167 us
  matrix products: 114 us -> 103 us
  other arithmetic: 79.6 us -> 90.5 us
    ppermute x112, waiting for transfers between devices: 516 us -> 482 us  [swap(): return lax.ppermute(value, axis, [(0, 1), (1, 0)])]
    ppermute x112, starting transfers between devices: 114 us -> 126 us  [swap(): return lax.ppermute(value, axis, [(0, 1), (1, 0)])]
    ppermute x16, waiting for transfers between devices: 67.6 us -> 55.4 us  [cross(): return lax.ppermute(value, ('s', 't'), [(i, 3 - i) for i in range(4)])]
    dot_general x56, matrix products: 43.6 us -> 31.7 us  [t_dot(): lax.dot_general(left, right, (((0,), (0,)), ((), ())), preferred_element_...]
    unnamed x585 -> x611, local copies, waits for them, and re-layouts: 45.8 us -> 46.5 us
  transfers between devices with their start and end apart: 134 -> 134, of which waited for: 74 -> 70; matrix products, arithmetic and copies ran while one was open for 19% -> 20% of each run, Pallas kernels for 0% -> 0%
where the time goes in v4:
time: 1000 us; the launch traced here: 991 us
  waiting for transfers between devices  540 us (54%)
  starting transfers between devices  167 us (17%)
  matrix products  103 us (10%)
  other arithmetic  90.5 us (9%)
  local copies, waits for them, and re-layouts  84.5 us (8%)
    ppermute x112, waiting for transfers between devices, swap(): return lax.ppermute(value, axis, [(0, 1), (1, 0)])  482 us
    ppermute x112, starting transfers between devices, swap(): return lax.ppermute(value, axis, [(0, 1), (1, 0)])  126 us
    ppermute x16, waiting for transfers between devices, cross(): return lax.ppermute(value, ('s', 't'), [(i, 3 - i) for i in range(4)])  55.4 us
    unnamed x611, local copies, waits for them, and re-layouts  46.5 us
    dot_general x40, matrix products, dot_t(): lax.dot_general(left, right, (((1,), (1,)), ((), ())), preferred_element_...  37.7 us
    dot_general x56, matrix products, t_dot(): lax.dot_general(left, right, (((0,), (0,)), ((), ())), preferred_element_...  31.7 us
    all_to_all x6, starting transfers between devices, exchange(): return lax.all_to_all(value, axes, 0, 0, tiled=True)  28.3 us
    dot_general x20, matrix products, dot(): return jnp.dot(left, right, preferred_element_type=f32)  26.7 us
  transfers between devices with their start and end apart: 134, of which 70 were waited for; matrix products, arithmetic and copies ran while one was open for 20% of the time, Pallas kernels for 0%

profile of v4, /device:TPU:0, one launch (start us, length us, event | category | flops | bytes accessed | tf_op | source)
XLA Modules:
  0.0 990.9 jit_solution(18011665111474169465)
XLA Ops:
  1.7 3.0 collective-permute-start
  15.7 3.7 all-to-all-start
  37.2 10.9 %collective-permute-done.2 = bf16[64,2048]{1,0:T(8,128)(2,1)S(1)} collective-permute-done((bf16[64,2048]{1,0:T(8,128)(2,1)S(1)}, bf16[64,2048]{1,0:T(8,128)(2,1)S(1)}, u32[]{:S(2)}, u32[]{:S(2)}) %collective-permute-start.2) | collective-permute-done | bytes 262176 | tf_op jit(solution)/shard_map/ppermute | solution.py:16
  51.5 4.1 collective-permute-done.3
  58.5 3.4 collective-permute-start.10
  68.7 11.2 %collective-permute-done.8 = bf16[64,2048]{1,0:T(8,128)(2,1)S(1)} collective-permute-done((bf16[64,2048]{1,0:T(8,128)(2,1)S(1)}, bf16[64,2048]{1,0:T(8,128)(2,1)S(1)}, u32[]{:S(2)}, u32[]{:S(2)}) %collective-permute-start.8) | collective-permute-done | bytes 262176 | tf_op jit(solution)/shard_map/ppermute | solution.py:16
  79.8 3.0 collective-permute-done.9
  84.7 4.6 all-to-all-start.1
  93.2 4.4 collective-permute-start.12
  98.3 26.0 %collective-permute-done.12 = bf16[512,512]{1,0:T(8,128)(2,1)S(1)} collective-permute-done((bf16[512,512]{1,0:T(8,128)(2,1)S(1)}, bf16[512,512]{1,0:T(8,128)(2,1)S(1)}, u32[]{:S(2)}, u32[]{:S(2)}) %collective-permute-start.12) | collective-permute-done | bytes 524320 | tf_op jit(solution)/shard_map/ppermute | solution.py:16
  138.1 5.4 all-to-all-start.2
  146.8 15.5 %collective-permute-done.14 = bf16[256,1152]{1,0:T(8,128)(2,1)} collective-permute-done((bf16[256,1152]{1,0:T(8,128)(2,1)}, bf16[256,1152]{1,0:T(8,128)(2,1)}, u32[]{:S(2)}, u32[]{:S(2)}) %collective-permute-start.14) | collective-permute-done | bytes 589856 | tf_op jit(solution)/shard_map/ppermute | solution.py:16
  180.9 14.6 %collective-permute-done.17 = bf16[256,1152]{1,0:T(8,128)(2,1)S(1)} collective-permute-done((bf16[256,1152]{1,0:T(8,128)(2,1)S(1)}, bf16[256,1152]{1,0:T(8,128)(2,1)S(1)}, u32[]{:S(2)}, u32[]{:S(2)}) %collective-permute-start.17) | collective-permute-done | bytes 589856 | tf_op jit(solution)/shard_map/ppermute | solution.py:16
  212.5 16.7 %collective-permute-done.23 = bf16[256,1152]{1,0:T(8,128)(2,1)S(1)} collective-permute-done((bf16[256,1152]{1,0:T(8,128)(2,1)S(1)}, bf16[256,1152]{1,0:T(8,128)(2,1)S(1)}, u32[]{:S(2)}, u32[]{:S(2)}) %collective-permute-start.23) | collective-permute-done | bytes 589856 | tf_op jit(solution)/shard_map/ppermute | solution.py:16
  229.3 3.1 collective-permute-done.20
  232.3 4.3 collective-permute-done.21
  245.4 12.4 %collective-permute-done.25 = bf16[64,2048]{1,0:T(8,128)(2,1)S(1)} collective-permute-done((bf16[64,2048]{1,0:T(8,128)(2,1)S(1)}, bf16[64,2048]{1,0:T(8,128)(2,1)S(1)}, u32[]{:S(2)}, u32[]{:S(2)}) %collective-permute-start.25) | collective-permute-done | bytes 262176 | tf_op jit(solution)/shard_map/ppermute | solution.py:16
  257.8 3.4 collective-permute-done.26
  261.2 4.2 collective-permute-done.28
  268.3 24.0 %collective-permute-done.31 = bf16[512,512]{1,0:T(8,128)(2,1)S(1)} collective-permute-done((bf16[512,512]{1,0:T(8,128)(2,1)S(1)}, bf16[512,512]{1,0:T(8,128)(2,1)S(1)}, u32[]{:S(2)}, u32[]{:S(2)}) %collective-permute-start.31) | collective-permute-done | bytes 524320 | tf_op jit(solution)/shard_map/ppermute | solution.py:16
  305.2 5.5 collective-permute-done.33
  310.7 3.2 collective-permute-done.34
  313.9 11.4 %collective-permute-done.36 = bf16[512,512]{1,0:T(8,128)(2,1)S(1)} collective-permute-done((bf16[512,512]{1,0:T(8,128)(2,1)S(1)}, bf16[512,512]{1,0:T(8,128)(2,1)S(1)}, u32[]{:S(2)}, u32[]{:S(2)}) %collective-permute-start.36) | collective-permute-done | bytes 524320 | tf_op jit(solution)/shard_map/ppermute | solution.py:16
  336.6 21.8 %collective-permute-done.42 = bf16[256,1152]{1,0:T(8,128)(2,1)S(1)} collective-permute-done((bf16[256,1152]{1,0:T(8,128)(2,1)S(1)}, bf16[256,1152]{1,0:T(8,128)(2,1)S(1)}, u32[]{:S(2)}, u32[]{:S(2)}) %collective-permute-start.42) | collective-permute-done | bytes 589856 | tf_op jit(solution)/shard_map/ppermute | solution.py:16
  369.6 13.0 %collective-permute-done.44 = bf16[64,2048]{1,0:T(8,128)(2,1)S(1)} collective-permute-done((bf16[64,2048]{1,0:T(8,128)(2,1)S(1)}, bf16[64,2048]{1,0:T(8,128)(2,1)S(1)}, u32[]{:S(2)}, u32[]{:S(2)}) %collective-permute-start.44) | collective-permute-done | bytes 262176 | tf_op jit(solution)/shard_map/ppermute | solution.py:16
  384.9 7.8 collective-permute-done.47
  408.5 14.2 %collective-permute-done.50 = bf16[256,1152]{1,0:T(8,128)(2,1)S(1)} collective-permute-done((bf16[256,1152]{1,0:T(8,128)(2,1)S(1)}, bf16[256,1152]{1,0:T(8,128)(2,1)S(1)}, u32[]{:S(2)}, u32[]{:S(2)}) %collective-permute-start.50) | collective-permute-done | bytes 589856 | tf_op jit(solution)/shard_map/ppermute | solution.py:16
  430.6 23.7 %collective-permute-done.56 = bf16[256,1152]{1,0:T(8,128)(2,1)S(1)} collective-permute-done((bf16[256,1152]{1,0:T(8,128)(2,1)S(1)}, bf16[256,1152]{1,0:T(8,128)(2,1)S(1)}, u32[]{:S(2)}, u32[]{:S(2)}) %collective-permute-start.56) | collective-permute-done | bytes 589856 | tf_op jit(solution)/shard_map/ppermute | solution.py:16
  459.7 3.4 collective-permute-done.57
  465.8 4.0 collective-permute-done.59
  469.8 15.7 %collective-permute-done.60 = bf16[512,1152]{1,0:T(8,128)(2,1)S(1)} collective-permute-done((bf16[512,1152]{1,0:T(8,128)(2,1)S(1)}, bf16[512,1152]{1,0:T(8,128)(2,1)S(1)}, u32[]{:S(2)}, u32[]{:S(2)}) %collective-permute-start.60) | collective-permute-done | bytes 1179680 | tf_op jit(solution)/shard_map/ppermute | solution.py:16
  509.6 3.6 fusion.1
  513.2 15.4 %collective-permute-done.63 = bf16[512,1152]{1,0:T(8,128)(2,1)S(1)} collective-permute-done((bf16[512,1152]{1,0:T(8,128)(2,1)S(1)}, bf16[512,1152]{1,0:T(8,128)(2,1)S(1)}, u32[]{:S(2)}, u32[]{:S(2)}) %collective-permute-start.63) | collective-permute-done | bytes 1179680 | tf_op jit(solution)/shard_map/ppermute | solution.py:16
  539.2 22.9 %collective-permute-done.68 = bf16[256,1152]{1,0:T(8,128)(2,1)} collective-permute-done((bf16[256,1152]{1,0:T(8,128)(2,1)S(1)}, bf16[256,1152]{1,0:T(8,128)(2,1)}, u32[]{:S(2)}, u32[]{:S(2)}) %collective-permute-start.68) | collective-permute-done | bytes 589856 | tf_op jit(solution)/shard_map/ppermute | solution.py:16
  573.0 3.6 collective-permute-done.70
  576.6 9.7 collective-permute-done.71
  586.4 4.0 collective-permute-done.72
  590.4 3.4 collective-permute-done.73
  619.3 7.2 collective-permute-done.76
  637.9 20.7 %collective-permute-done.82 = bf16[256,1152]{1,0:T(8,128)(2,1)S(1)} collective-permute-done((bf16[256,1152]{1,0:T(8,128)(2,1)S(1)}, bf16[256,1152]{1,0:T(8,128)(2,1)S(1)}, u32[]{:S(2)}, u32[]{:S(2)}) %collective-permute-start.82) | collective-permute-done | bytes 589856 | tf_op jit(solution)/shard_map/ppermute | solution.py:16
  666.9 3.3 collective-permute-start.85
  671.3 3.4 collective-permute-done.84
  674.6 9.4 collective-permute-done.85
  684.0 6.6 collective-permute-done.86
  718.7 11.1 %collective-permute-done.94 = bf16[64,2048]{1,0:T(8,128)(2,1)S(1)} collective-permute-done((bf16[64,2048]{1,0:T(8,128)(2,1)S(1)}, bf16[64,2048]{1,0:T(8,128)(2,1)S(1)}, u32[]{:S(2)}, u32[]{:S(2)}) %collective-permute-start.94) | collective-permute-done | bytes 262176 | tf_op jit(solution)/shard_map/ppermute | solution.py:50
  729.8 4.4 collective-permute-done.95
  734.2 3.3 collective-permute-done.96
  747.0 12.7 %collective-permute-done.98 = bf16[64,2048]{1,0:T(8,128)(2,1)S(1)} collective-permute-done((bf16[64,2048]{1,0:T(8,128)(2,1)S(1)}, bf16[64,2048]{1,0:T(8,128)(2,1)S(1)}, u32[]{:S(2)}, u32[]{:S(2)}) %collective-permute-start.98) | collective-permute-done | bytes 262176 | tf_op jit(solution)/shard_map/ppermute | solution.py:16
  759.7 4.0 collective-permute-done.99
  763.6 7.0 collective-permute-done.100
  774.9 3.0 collective-permute-start.103
  778.9 4.9 collective-permute-done.102
  783.8 5.9 collective-permute-done.103
  789.7 6.4 collective-permute-done.104
  804.4 4.8 all-to-all-start.3
  850.3 19.4 %collective-permute-done.114 = bf16[256,1152]{1,0:T(8,128)(2,1)S(1)} collective-permute-done((bf16[256,1152]{1,0:T(8,128)(2,1)S(1)}, bf16[256,1152]{1,0:T(8,128)(2,1)S(1)}, u32[]{:S(2)}, u32[]{:S(2)}) %collective-permute-start.114) | collective-permute-done | bytes 589856 | tf_op jit(solution)/shard_map/ppermute | solution.py:16
  885.4 4.8 all-to-all-start.4
  890.2 14.3 %collective-permute-done.117 = bf16[512,512]{1,0:T(8,128)(2,1)} collective-permute-done((bf16[512,512]{1,0:T(8,128)(2,1)}, bf16[512,512]{1,0:T(8,128)(2,1)}, u32[]{:S(2)}, u32[]{:S(2)}) %collective-permute-start.117) | collective-permute-done | bytes 524320 | tf_op jit(solution)/shard_map/ppermute | solution.py:16
  914.5 4.8 collective-permute-start.121
  921.2 18.7 %collective-permute-done.121 = f32[68,128]{1,0:T(8,128)S(1)} collective-permute-done((f32[68,128]{1,0:T(8,128)S(1)}, f32[68,128]{1,0:T(8,128)S(1)}, u32[]{:S(2)}, u32[]{:S(2)}) %collective-permute-start.121) | collective-permute-done | bytes 34848 | tf_op jit(solution)/shard_map/ppermute | solution.py:16
  941.2 3.0 pad_maximum_fusion.7
  944.3 5.0 all-to-all-start.5
  964.4 8.4 collective-permute-done.127
  977.3 4.8 collective-permute-done.125
  (1260 shorter events, 418.6 us)
Async XLA Ops:
  15.7 41.0 %all-to-all-start = ((bf16[4,512,512]{2,1,0:T(8,128)(2,1)}), bf16[4,512,512]{2,1,0:T(8,128)(2,1)S(1)}, u32[]{:S(2)}, u32[]{:S(2)}) async-start(bf16[4,512,512]{2,1,0:T(8,128)(2,1)} %pad_maximum_fusion.4), calls=%async_computation | async-start | bytes 4194304 | tf_op jit(solution)/shard_map/all_to_all | solution.py:20
  22.1 25.9 %collective-permute-start.2 = (bf16[64,2048]{1,0:T(8,128)(2,1)S(1)}, bf16[64,2048]{1,0:T(8,128)(2,1)S(1)}, u32[]{:S(2)}, u32[]{:S(2)}) collective-permute-start(bf16[64,2048]{1,0:T(8,128)(2,1)S(1)} %dynamic-slice_bitcast_fusion.1), channel_id=1, source_target_pairs={{0,8},{8,0},{1,9},{9,1},{2,10},{10,2},{3,11},{11,3},{4,12},{12,4},... | collective-permute-start | bytes 786440 | tf_op jit(solution)/shard_map/ppermute | solution.py:16
  58.5 25.1 %collective-permute-start.10 = (bf16[512,512]{1,0:T(8,128)(2,1)S(1)}, bf16[512,512]{1,0:T(8,128)(2,1)S(1)}, u32[]{:S(2)}, u32[]{:S(2)}) collective-permute-start(bf16[512,512]{1,0:T(8,128)(2,1)S(1)} %get-tuple-element.306), channel_id=1, source_target_pairs={{0,8},{8,0},{1,9},{9,1},{2,10},{10,2},{3,11},{11,3},{4,12},{12,4},... | collective-permute-start | bytes 1572872 | tf_op jit(solution)/shard_map/ppermute | solution.py:16
  84.7 42.4 %all-to-all-start.1 = ((bf16[4,256,1152]{2,1,0:T(8,128)(2,1)}), bf16[4,256,1152]{2,1,0:T(8,128)(2,1)}, u32[]{:S(2)}, u32[]{:S(2)}) async-start(bf16[4,256,1152]{2,1,0:T(8,128)(2,1)} %pad_maximum_fusion), calls=%async_computation.1 | async-start | bytes 4718592 | tf_op jit(solution)/shard_map/all_to_all | solution.py:20
  90.8 34.3 %collective-permute-start.11 = (bf16[1024,512]{1,0:T(8,128)(2,1)}, bf16[1024,512]{1,0:T(8,128)(2,1)}, u32[]{:S(2)}, u32[]{:S(2)}) collective-permute-start(bf16[1024,512]{1,0:T(8,128)(2,1)} %pad_maximum_fusion.28), channel_id=1, source_target_pairs={{0,2},{2,0},{1,3},{3,1},{4,6},{6,4},{5,7},{7,5},{8,10},{10,8},{9,1... | collective-permute-start | bytes 3145736 | tf_op jit(solution)/shard_map/ppermute | solution.py:16
  93.2 31.1 %collective-permute-start.12 = (bf16[512,512]{1,0:T(8,128)(2,1)S(1)}, bf16[512,512]{1,0:T(8,128)(2,1)S(1)}, u32[]{:S(2)}, u32[]{:S(2)}) collective-permute-start(bf16[512,512]{1,0:T(8,128)(2,1)S(1)} %get-tuple-element.311), channel_id=1, source_target_pairs={{0,8},{8,0},{1,9},{9,1},{2,10},{10,2},{3,11},{11,3},{4,12},{12,4},... | collective-permute-start | bytes 1572872 | tf_op jit(solution)/shard_map/ppermute | solution.py:16
  132.1 30.1 %collective-permute-start.13 = (bf16[1024,512]{1,0:T(8,128)(2,1)}, bf16[1024,512]{1,0:T(8,128)(2,1)}, u32[]{:S(2)}, u32[]{:S(2)}) collective-permute-start(bf16[1024,512]{1,0:T(8,128)(2,1)} %pad_maximum_fusion.29), channel_id=1, source_target_pairs={{0,2},{2,0},{1,3},{3,1},{4,6},{6,4},{5,7},{7,5},{8,10},{10,8},{9,1... | collective-permute-start | bytes 3145736 | tf_op jit(solution)/shard_map/ppermute | solution.py:16
  136.1 26.2 %collective-permute-start.14 = (bf16[256,1152]{1,0:T(8,128)(2,1)}, bf16[256,1152]{1,0:T(8,128)(2,1)}, u32[]{:S(2)}, u32[]{:S(2)}) collective-permute-start(bf16[256,1152]{1,0:T(8,128)(2,1)} %get-tuple-element.327), channel_id=1, source_target_pairs={{0,8},{8,0},{1,9},{9,1},{2,10},{10,2},{3,11},{11,3},{4,12},{12,4},... | collective-permute-start | bytes 1769480 | tf_op jit(solution)/shard_map/ppermute | solution.py:16
  138.1 58.2 %all-to-all-start.2 = ((bf16[4,256,1152]{2,1,0:T(8,128)(2,1)}), bf16[4,256,1152]{2,1,0:T(8,128)(2,1)}, u32[]{:S(2)}, u32[]{:S(2)}) async-start(bf16[4,256,1152]{2,1,0:T(8,128)(2,1)} %pad_maximum_fusion.1), calls=%async_computation.2 | async-start | bytes 4718592 | tf_op jit(solution)/shard_map/all_to_all | solution.py:20
  165.9 30.4 %collective-permute-start.16 = (bf16[512,1152]{1,0:T(8,128)(2,1)S(1)}, bf16[512,1152]{1,0:T(8,128)(2,1)}, u32[]{:S(2)}, u32[]{:S(2)}) collective-permute-start(bf16[512,1152]{1,0:T(8,128)(2,1)S(1)} %pad_maximum_fusion.12), channel_id=1, source_target_pairs={{0,2},{2,0},{1,3},{3,1},{4,6},{6,4},{5,7},{7,5},{8,10},{10,8},{9,1... | collective-permute-start | bytes 3538952 | tf_op jit(solution)/shard_map/ppermute | solution.py:16
  166.4 29.0 %collective-permute-start.17 = (bf16[256,1152]{1,0:T(8,128)(2,1)S(1)}, bf16[256,1152]{1,0:T(8,128)(2,1)S(1)}, u32[]{:S(2)}, u32[]{:S(2)}) collective-permute-start(bf16[256,1152]{1,0:T(8,128)(2,1)S(1)} %copy-done.26), channel_id=1, source_target_pairs={{0,8},{8,0},{1,9},{9,1},{2,10},{10,2},{3,11},{11,3},{4,12},{12,4},... | collective-permute-start | bytes 1769480 | tf_op jit(solution)/shard_map/ppermute | solution.py:16
  199.4 29.8 %collective-permute-start.22 = (bf16[512,1152]{1,0:T(8,128)(2,1)S(1)}, bf16[512,1152]{1,0:T(8,128)(2,1)S(1)}, u32[]{:S(2)}, u32[]{:S(2)}) collective-permute-start(bf16[512,1152]{1,0:T(8,128)(2,1)S(1)} %pad_maximum_fusion.13), channel_id=1, source_target_pairs={{0,2},{2,0},{1,3},{3,1},{4,6},{6,4},{5,7},{7,5},{8,10},{10,8},{9,1... | collective-permute-start | bytes 3538952 | tf_op jit(solution)/shard_map/ppermute | solution.py:16
  201.0 28.2 %collective-permute-start.23 = (bf16[256,1152]{1,0:T(8,128)(2,1)S(1)}, bf16[256,1152]{1,0:T(8,128)(2,1)S(1)}, u32[]{:S(2)}, u32[]{:S(2)}) collective-permute-start(bf16[256,1152]{1,0:T(8,128)(2,1)S(1)} %get-tuple-element.339), channel_id=1, source_target_pairs={{0,8},{8,0},{1,9},{9,1},{2,10},{10,2},{3,11},{11,3},{4,12},{12,4},... | collective-permute-start | bytes 1769480 | tf_op jit(solution)/shard_map/ppermute | solution.py:16
  237.1 28.3 %collective-permute-start.27 = (bf16[512,1152]{1,0:T(8,128)(2,1)S(1)}, bf16[512,1152]{1,0:T(8,128)(2,1)S(1)}, u32[]{:S(2)}, u32[]{:S(2)}) collective-permute-start(bf16[512,1152]{1,0:T(8,128)(2,1)S(1)} %pad_maximum_fusion.14), channel_id=1, source_target_pairs={{0,2},{2,0},{1,3},{3,1},{4,6},{6,4},{5,7},{7,5},{8,10},{10,8},{9,1... | collective-permute-start | bytes 3538952 | tf_op jit(solution)/shard_map/ppermute | solution.py:16
  237.6 27.7 %collective-permute-start.28 = (bf16[256,1152]{1,0:T(8,128)(2,1)S(1)}, bf16[256,1152]{1,0:T(8,128)(2,1)S(1)}, u32[]{:S(2)}, u32[]{:S(2)}) collective-permute-start(bf16[256,1152]{1,0:T(8,128)(2,1)S(1)} %get-tuple-element.348), channel_id=1, source_target_pairs={{0,8},{8,0},{1,9},{9,1},{2,10},{10,2},{3,11},{11,3},{4,12},{12,4},... | collective-permute-start | bytes 1769480 | tf_op jit(solution)/shard_map/ppermute | solution.py:16
  265.7 28.4 %collective-permute-start.30 = (bf16[512,1152]{1,0:T(8,128)(2,1)S(1)}, bf16[512,1152]{1,0:T(8,128)(2,1)S(1)}, u32[]{:S(2)}, u32[]{:S(2)}) collective-permute-start(bf16[512,1152]{1,0:T(8,128)(2,1)S(1)} %pad_maximum_fusion.15), channel_id=1, source_target_pairs={{0,2},{2,0},{1,3},{3,1},{4,6},{6,4},{5,7},{7,5},{8,10},{10,8},{9,1... | collective-permute-start | bytes 3538952 | tf_op jit(solution)/shard_map/ppermute | solution.py:16
  267.3 25.1 %collective-permute-start.31 = (bf16[512,512]{1,0:T(8,128)(2,1)S(1)}, bf16[512,512]{1,0:T(8,128)(2,1)S(1)}, u32[]{:S(2)}, u32[]{:S(2)}) collective-permute-start(bf16[512,512]{1,0:T(8,128)(2,1)S(1)} %copy-done.33), channel_id=1, source_target_pairs={{0,8},{8,0},{1,9},{9,1},{2,10},{10,2},{3,11},{11,3},{4,12},{12,4},... | collective-permute-start | bytes 1572872 | tf_op jit(solution)/shard_map/ppermute | solution.py:16
  299.1 26.2 %collective-permute-start.35 = (bf16[1024,512]{1,0:T(8,128)(2,1)S(1)}, bf16[1024,512]{1,0:T(8,128)(2,1)S(1)}, u32[]{:S(2)}, u32[]{:S(2)}) collective-permute-start(bf16[1024,512]{1,0:T(8,128)(2,1)S(1)} %pad_maximum_fusion.32), channel_id=1, source_target_pairs={{0,2},{2,0},{1,3},{3,1},{4,6},{6,4},{5,7},{7,5},{8,10},{10,8},{9,1... | collective-permute-start | bytes 3145736 | tf_op jit(solution)/shard_map/ppermute | solution.py:16
  300.7 24.6 %collective-permute-start.36 = (bf16[512,512]{1,0:T(8,128)(2,1)S(1)}, bf16[512,512]{1,0:T(8,128)(2,1)S(1)}, u32[]{:S(2)}, u32[]{:S(2)}) collective-permute-start(bf16[512,512]{1,0:T(8,128)(2,1)S(1)} %copy-done.31), channel_id=1, source_target_pairs={{0,8},{8,0},{1,9},{9,1},{2,10},{10,2},{3,11},{11,3},{4,12},{12,4},... | collective-permute-start | bytes 1572872 | tf_op jit(solution)/shard_map/ppermute | solution.py:16
  329.3 29.1 %collective-permute-start.41 = (bf16[1024,512]{1,0:T(8,128)(2,1)S(1)}, bf16[1024,512]{1,0:T(8,128)(2,1)S(1)}, u32[]{:S(2)}, u32[]{:S(2)}) collective-permute-start(bf16[1024,512]{1,0:T(8,128)(2,1)S(1)} %pad_maximum_fusion.33), channel_id=1, source_target_pairs={{0,2},{2,0},{1,3},{3,1},{4,6},{6,4},{5,7},{7,5},{8,10},{10,8},{9,1... | collective-permute-start | bytes 3145736 | tf_op jit(solution)/shard_map/ppermute | solution.py:16
  330.4 28.0 %collective-permute-start.42 = (bf16[256,1152]{1,0:T(8,128)(2,1)S(1)}, bf16[256,1152]{1,0:T(8,128)(2,1)S(1)}, u32[]{:S(2)}, u32[]{:S(2)}) collective-permute-start(bf16[256,1152]{1,0:T(8,128)(2,1)S(1)} %get-tuple-element.377), channel_id=1, source_target_pairs={{0,8},{8,0},{1,9},{9,1},{2,10},{10,2},{3,11},{11,3},{4,12},{12,4},... | collective-permute-start | bytes 1769480 | tf_op jit(solution)/shard_map/ppermute | solution.py:16
  332.8 25.5 %collective-permute-start.38 = (bf16[64,2048]{1,0:T(8,128)(2,1)S(1)}, bf16[64,2048]{1,0:T(8,128)(2,1)S(1)}, u32[]{:S(2)}, u32[]{:S(2)}) collective-permute-start(bf16[64,2048]{1,0:T(8,128)(2,1)S(1)} %get-tuple-element.760), channel_id=1, source_target_pairs={{0,16},{16,0},{1,17},{17,1},{2,18},{18,2},{3,19},{19,3},{4,20},{20... | collective-permute-start | bytes 786440 | tf_op jit(solution)/shard_map/ppermute | solution.py:16
  336.3 24.5 %collective-permute-start.40 = (bf16[64,2048]{1,0:T(8,128)(2,1)S(1)}, bf16[64,2048]{1,0:T(8,128)(2,1)S(1)}, u32[]{:S(2)}, u32[]{:S(2)}) collective-permute-start(bf16[64,2048]{1,0:T(8,128)(2,1)S(1)} %get-tuple-element.758), channel_id=1, source_target_pairs={{0,20},{4,16},{16,4},{20,0},{1,21},{5,17},{17,5},{21,1},{2,22},{6,... | collective-permute-start | bytes 786440 | tf_op jit(solution)/shard_map/ppermute | solution.py:50
  361.2 31.5 %collective-permute-start.46 = (bf16[512,1152]{1,0:T(8,128)(2,1)S(1)}, bf16[512,1152]{1,0:T(8,128)(2,1)S(1)}, u32[]{:S(2)}, u32[]{:S(2)}) collective-permute-start(bf16[512,1152]{1,0:T(8,128)(2,1)S(1)} %pad_maximum_fusion.16), channel_id=1, source_target_pairs={{0,2},{2,0},{1,3},{3,1},{4,6},{6,4},{5,7},{7,5},{8,10},{10,8},{9,1... | collective-permute-start | bytes 3538952 | tf_op jit(solution)/shard_map/ppermute | solution.py:16
  366.0 26.8 %collective-permute-start.47 = (bf16[256,1152]{1,0:T(8,128)(2,1)S(1)}, bf16[256,1152]{1,0:T(8,128)(2,1)S(1)}, u32[]{:S(2)}, u32[]{:S(2)}) collective-permute-start(bf16[256,1152]{1,0:T(8,128)(2,1)S(1)} %get-tuple-element.385), channel_id=1, source_target_pairs={{0,8},{8,0},{1,9},{9,1},{2,10},{10,2},{3,11},{11,3},{4,12},{12,4},... | collective-permute-start | bytes 1769480 | tf_op jit(solution)/shard_map/ppermute | solution.py:16
  393.0 29.7 %collective-permute-start.49 = (bf16[512,1152]{1,0:T(8,128)(2,1)S(1)}, bf16[512,1152]{1,0:T(8,128)(2,1)S(1)}, u32[]{:S(2)}, u32[]{:S(2)}) collective-permute-start(bf16[512,1152]{1,0:T(8,128)(2,1)S(1)} %pad_maximum_fusion.17), channel_id=1, source_target_pairs={{0,2},{2,0},{1,3},{3,1},{4,6},{6,4},{5,7},{7,5},{8,10},{10,8},{9,1... | collective-permute-start | bytes 3538952 | tf_op jit(solution)/shard_map/ppermute | solution.py:16
  394.1 28.6 %collective-permute-start.50 = (bf16[256,1152]{1,0:T(8,128)(2,1)S(1)}, bf16[256,1152]{1,0:T(8,128)(2,1)S(1)}, u32[]{:S(2)}, u32[]{:S(2)}) collective-permute-start(bf16[256,1152]{1,0:T(8,128)(2,1)S(1)} %get-tuple-element.395), channel_id=1, source_target_pairs={{0,8},{8,0},{1,9},{9,1},{2,10},{10,2},{3,11},{11,3},{4,12},{12,4},... | collective-permute-start | bytes 1769480 | tf_op jit(solution)/shard_map/ppermute | solution.py:16
  425.3 29.0 %collective-permute-start.55 = (bf16[512,1152]{1,0:T(8,128)(2,1)}, bf16[512,1152]{1,0:T(8,128)(2,1)S(1)}, u32[]{:S(2)}, u32[]{:S(2)}) collective-permute-start(bf16[512,1152]{1,0:T(8,128)(2,1)} %pad_maximum_fusion.18), channel_id=1, source_target_pairs={{0,2},{2,0},{1,3},{3,1},{4,6},{6,4},{5,7},{7,5},{8,10},{10,8},{9,1... | collective-permute-start | bytes 3538952 | tf_op jit(solution)/shard_map/ppermute | solution.py:16
  426.3 28.0 %collective-permute-start.56 = (bf16[256,1152]{1,0:T(8,128)(2,1)S(1)}, bf16[256,1152]{1,0:T(8,128)(2,1)S(1)}, u32[]{:S(2)}, u32[]{:S(2)}) collective-permute-start(bf16[256,1152]{1,0:T(8,128)(2,1)S(1)} %get-tuple-element.401), channel_id=1, source_target_pairs={{0,8},{8,0},{1,9},{9,1},{2,10},{10,2},{3,11},{11,3},{4,12},{12,4},... | collective-permute-start | bytes 1769480 | tf_op jit(solution)/shard_map/ppermute | solution.py:16
  426.8 27.5 %collective-permute-start.52 = (bf16[64,2048]{1,0:T(8,128)(2,1)S(1)}, bf16[64,2048]{1,0:T(8,128)(2,1)S(1)}, u32[]{:S(2)}, u32[]{:S(2)}) collective-permute-start(bf16[64,2048]{1,0:T(8,128)(2,1)S(1)} %get-tuple-element.753), channel_id=1, source_target_pairs={{0,16},{16,0},{1,17},{17,1},{2,18},{18,2},{3,19},{19,3},{4,20},{20... | collective-permute-start | bytes 786440 | tf_op jit(solution)/shard_map/ppermute | solution.py:16
  428.3 26.0 %collective-permute-start.53 = (bf16[64,2048]{1,0:T(8,128)(2,1)S(1)}, bf16[64,2048]{1,0:T(8,128)(2,1)S(1)}, u32[]{:S(2)}, u32[]{:S(2)}) collective-permute-start(bf16[64,2048]{1,0:T(8,128)(2,1)S(1)} %get-tuple-element.752), channel_id=1, source_target_pairs={{0,4},{4,0},{1,5},{5,1},{2,6},{6,2},{3,7},{7,3},{8,12},{12,8},{9,1... | collective-permute-start | bytes 786440 | tf_op jit(solution)/shard_map/ppermute | solution.py:16
  458.4 27.1 %collective-permute-start.60 = (bf16[512,1152]{1,0:T(8,128)(2,1)S(1)}, bf16[512,1152]{1,0:T(8,128)(2,1)S(1)}, u32[]{:S(2)}, u32[]{:S(2)}) collective-permute-start(bf16[512,1152]{1,0:T(8,128)(2,1)S(1)} %pad_maximum_fusion.19), channel_id=1, source_target_pairs={{0,2},{2,0},{1,3},{3,1},{4,6},{6,4},{5,7},{7,5},{8,10},{10,8},{9,1... | collective-permute-start | bytes 3538952 | tf_op jit(solution)/shard_map/ppermute | solution.py:16
  500.5 28.1 %collective-permute-start.63 = (bf16[512,1152]{1,0:T(8,128)(2,1)S(1)}, bf16[512,1152]{1,0:T(8,128)(2,1)S(1)}, u32[]{:S(2)}, u32[]{:S(2)}) collective-permute-start(bf16[512,1152]{1,0:T(8,128)(2,1)S(1)} %pad_maximum_fusion.20), channel_id=1, source_target_pairs={{0,2},{2,0},{1,3},{3,1},{4,6},{6,4},{5,7},{7,5},{8,10},{10,8},{9,1... | collective-permute-start | bytes 3538952 | tf_op jit(solution)/shard_map/ppermute | solution.py:16
  532.9 29.3 %collective-permute-start.68 = (bf16[256,1152]{1,0:T(8,128)(2,1)S(1)}, bf16[256,1152]{1,0:T(8,128)(2,1)}, u32[]{:S(2)}, u32[]{:S(2)}) collective-permute-start(bf16[256,1152]{1,0:T(8,128)(2,1)S(1)} %fusion.116), channel_id=1, source_target_pairs={{0,8},{8,0},{1,9},{9,1},{2,10},{10,2},{3,11},{11,3},{4,12},{12,4},... | collective-permute-start | bytes 1769480 | tf_op jit(solution)/shard_map/ppermute | solution.py:16
  534.0 28.3 %collective-permute-start.69 = (bf16[512,1152]{1,0:T(8,128)(2,1)}, bf16[512,1152]{1,0:T(8,128)(2,1)S(1)}, u32[]{:S(2)}, u32[]{:S(2)}) collective-permute-start(bf16[512,1152]{1,0:T(8,128)(2,1)} %pad_maximum_fusion.21), channel_id=1, source_target_pairs={{0,2},{2,0},{1,3},{3,1},{4,6},{6,4},{5,7},{7,5},{8,10},{10,8},{9,1... | collective-permute-start | bytes 3538952 | tf_op jit(solution)/shard_map/ppermute | solution.py:16
  535.5 26.8 %collective-permute-start.65 = (bf16[64,2048]{1,0:T(8,128)(2,1)S(1)}, bf16[64,2048]{1,0:T(8,128)(2,1)S(1)}, u32[]{:S(2)}, u32[]{:S(2)}) collective-permute-start(bf16[64,2048]{1,0:T(8,128)(2,1)S(1)} %get-tuple-element.750), channel_id=1, source_target_pairs={{0,16},{16,0},{1,17},{17,1},{2,18},{18,2},{3,19},{19,3},{4,20},{20... | collective-permute-start | bytes 786440 | tf_op jit(solution)/shard_map/ppermute | solution.py:16
  537.0 25.3 %collective-permute-start.66 = (bf16[64,2048]{1,0:T(8,128)(2,1)S(1)}, bf16[64,2048]{1,0:T(8,128)(2,1)S(1)}, u32[]{:S(2)}, u32[]{:S(2)}) collective-permute-start(bf16[64,2048]{1,0:T(8,128)(2,1)S(1)} %get-tuple-element.749), channel_id=1, source_target_pairs={{0,4},{4,0},{1,5},{5,1},{2,6},{6,2},{3,7},{7,3},{8,12},{12,8},{9,1... | collective-permute-start | bytes 786440 | tf_op jit(solution)/shard_map/ppermute | solution.py:16
  538.8 24.3 %collective-permute-start.67 = (bf16[64,2048]{1,0:T(8,128)(2,1)S(1)}, bf16[64,2048]{1,0:T(8,128)(2,1)S(1)}, u32[]{:S(2)}, u32[]{:S(2)}) collective-permute-start(bf16[64,2048]{1,0:T(8,128)(2,1)S(1)} %get-tuple-element.748), channel_id=1, source_target_pairs={{0,20},{4,16},{16,4},{20,0},{1,21},{5,17},{17,5},{21,1},{2,22},{6,... | collective-permute-start | bytes 786440 | tf_op jit(solution)/shard_map/ppermute | solution.py:50
  565.9 28.0 %collective-permute-start.73 = (bf16[256,1152]{1,0:T(8,128)(2,1)S(1)}, bf16[256,1152]{1,0:T(8,128)(2,1)S(1)}, u32[]{:S(2)}, u32[]{:S(2)}) collective-permute-start(bf16[256,1152]{1,0:T(8,128)(2,1)S(1)} %fusion.115), channel_id=1, source_target_pairs={{0,8},{8,0},{1,9},{9,1},{2,10},{10,2},{3,11},{11,3},{4,12},{12,4},... | collective-permute-start | bytes 1769480 | tf_op jit(solution)/shard_map/ppermute | solution.py:16
  567.0 27.0 %collective-permute-start.74 = (bf16[512,1152]{1,0:T(8,128)(2,1)S(1)}, bf16[512,1152]{1,0:T(8,128)(2,1)S(1)}, u32[]{:S(2)}, u32[]{:S(2)}) collective-permute-start(bf16[512,1152]{1,0:T(8,128)(2,1)S(1)} %pad_maximum_fusion.22), channel_id=1, source_target_pairs={{0,2},{2,0},{1,3},{3,1},{4,6},{6,4},{5,7},{7,5},{8,10},{10,8},{9,1... | collective-permute-start | bytes 3538952 | tf_op jit(solution)/shard_map/ppermute | solution.py:16
  596.8 29.6 %collective-permute-start.76 = (bf16[256,1152]{1,0:T(8,128)(2,1)}, bf16[256,1152]{1,0:T(8,128)(2,1)}, u32[]{:S(2)}, u32[]{:S(2)}) collective-permute-start(bf16[256,1152]{1,0:T(8,128)(2,1)} %fusion.114), channel_id=1, source_target_pairs={{0,8},{8,0},{1,9},{9,1},{2,10},{10,2},{3,11},{11,3},{4,12},{12,4},... | collective-permute-start | bytes 1769480 | tf_op jit(solution)/shard_map/ppermute | solution.py:16
  598.4 28.1 %collective-permute-start.77 = (bf16[512,1152]{1,0:T(8,128)(2,1)S(1)}, bf16[512,1152]{1,0:T(8,128)(2,1)S(1)}, u32[]{:S(2)}, u32[]{:S(2)}) collective-permute-start(bf16[512,1152]{1,0:T(8,128)(2,1)S(1)} %pad_maximum_fusion.23), channel_id=1, source_target_pairs={{0,2},{2,0},{1,3},{3,1},{4,6},{6,4},{5,7},{7,5},{8,10},{10,8},{9,1... | collective-permute-start | bytes 3538952 | tf_op jit(solution)/shard_map/ppermute | solution.py:16
  629.3 29.3 %collective-permute-start.82 = (bf16[256,1152]{1,0:T(8,128)(2,1)S(1)}, bf16[256,1152]{1,0:T(8,128)(2,1)S(1)}, u32[]{:S(2)}, u32[]{:S(2)}) collective-permute-start(bf16[256,1152]{1,0:T(8,128)(2,1)S(1)} %fusion.113), channel_id=1, source_target_pairs={{0,8},{8,0},{1,9},{9,1},{2,10},{10,2},{3,11},{11,3},{4,12},{12,4},... | collective-permute-start | bytes 1769480 | tf_op jit(solution)/shard_map/ppermute | solution.py:16
  630.7 27.9 %collective-permute-start.83 = (bf16[1024,512]{1,0:T(8,128)(2,1)S(1)}, bf16[1024,512]{1,0:T(8,128)(2,1)S(1)}, u32[]{:S(2)}, u32[]{:S(2)}) collective-permute-start(bf16[1024,512]{1,0:T(8,128)(2,1)S(1)} %pad_maximum_fusion.40), channel_id=1, source_target_pairs={{0,2},{2,0},{1,3},{3,1},{4,6},{6,4},{5,7},{7,5},{8,10},{10,8},{9,1... | collective-permute-start | bytes 3145736 | tf_op jit(solution)/shard_map/ppermute | solution.py:16
  632.2 26.4 %collective-permute-start.79 = (bf16[64,2048]{1,0:T(8,128)(2,1)S(1)}, bf16[64,2048]{1,0:T(8,128)(2,1)S(1)}, u32[]{:S(2)}, u32[]{:S(2)}) collective-permute-start(bf16[64,2048]{1,0:T(8,128)(2,1)S(1)} %get-tuple-element.747), channel_id=1, source_target_pairs={{0,16},{16,0},{1,17},{17,1},{2,18},{18,2},{3,19},{19,3},{4,20},{20... | collective-permute-start | bytes 786440 | tf_op jit(solution)/shard_map/ppermute | solution.py:16
  633.7 24.9 %collective-permute-start.80 = (bf16[64,2048]{1,0:T(8,128)(2,1)S(1)}, bf16[64,2048]{1,0:T(8,128)(2,1)S(1)}, u32[]{:S(2)}, u32[]{:S(2)}) collective-permute-start(bf16[64,2048]{1,0:T(8,128)(2,1)S(1)} %get-tuple-element.746), channel_id=1, source_target_pairs={{0,4},{4,0},{1,5},{5,1},{2,6},{6,2},{3,7},{7,3},{8,12},{12,8},{9,1... | collective-permute-start | bytes 786440 | tf_op jit(solution)/shard_map/ppermute | solution.py:16
  662.8 28.7 %collective-permute-start.88 = (bf16[1024,512]{1,0:T(8,128)(2,1)S(1)}, bf16[1024,512]{1,0:T(8,128)(2,1)S(1)}, u32[]{:S(2)}, u32[]{:S(2)}) collective-permute-start(bf16[1024,512]{1,0:T(8,128)(2,1)S(1)} %pad_maximum_fusion.44), channel_id=1, source_target_pairs={{0,2},{2,0},{1,3},{3,1},{4,6},{6,4},{5,7},{7,5},{8,10},{10,8},{9,1... | collective-permute-start | bytes 3145736 | tf_op jit(solution)/shard_map/ppermute | solution.py:16
  663.9 26.7 %collective-permute-start.87 = (bf16[512,512]{1,0:T(8,128)(2,1)S(1)}, bf16[512,512]{1,0:T(8,128)(2,1)S(1)}, u32[]{:S(2)}, u32[]{:S(2)}) collective-permute-start(bf16[512,512]{1,0:T(8,128)(2,1)S(1)} %slice.1918), channel_id=1, source_target_pairs={{0,8},{8,0},{1,9},{9,1},{2,10},{10,2},{3,11},{11,3},{4,12},{12,4},... | collective-permute-start | bytes 1572872 | tf_op jit(solution)/shard_map/ppermute | solution.py:16
  708.0 26.1 %collective-permute-start.95 = (bf16[512,512]{1,0:T(8,128)(2,1)S(1)}, bf16[512,512]{1,0:T(8,128)(2,1)S(1)}, u32[]{:S(2)}, u32[]{:S(2)}) collective-permute-start(bf16[512,512]{1,0:T(8,128)(2,1)S(1)} %slice.1940), channel_id=1, source_target_pairs={{0,8},{8,0},{1,9},{9,1},{2,10},{10,2},{3,11},{11,3},{4,12},{12,4},... | collective-permute-start | bytes 1572872 | tf_op jit(solution)/shard_map/ppermute | solution.py:16
  710.1 27.4 %collective-permute-start.96 = (bf16[512,1152]{1,0:T(8,128)(2,1)S(1)}, bf16[512,1152]{1,0:T(8,128)(2,1)S(1)}, u32[]{:S(2)}, u32[]{:S(2)}) collective-permute-start(bf16[512,1152]{1,0:T(8,128)(2,1)S(1)} %pad_maximum_fusion.24), channel_id=1, source_target_pairs={{0,2},{2,0},{1,3},{3,1},{4,6},{6,4},{5,7},{7,5},{8,10},{10,8},{9,1... | collective-permute-start | bytes 3538952 | tf_op jit(solution)/shard_map/ppermute | solution.py:16
  739.2 31.5 %collective-permute-start.101 = (bf16[512,1152]{1,0:T(8,128)(2,1)S(1)}, bf16[512,1152]{1,0:T(8,128)(2,1)S(1)}, u32[]{:S(2)}, u32[]{:S(2)}) collective-permute-start(bf16[512,1152]{1,0:T(8,128)(2,1)S(1)} %pad_maximum_fusion.25), channel_id=1, source_target_pairs={{0,2},{2,0},{1,3},{3,1},{4,6},{6,4},{5,7},{7,5},{8,10},{10,8},{9,1... | collective-permute-start | bytes 3538952 | tf_op jit(solution)/shard_map/ppermute | solution.py:16
  744.0 26.7 %collective-permute-start.100 = (bf16[256,1152]{1,0:T(8,128)(2,1)S(1)}, bf16[256,1152]{1,0:T(8,128)(2,1)S(1)}, u32[]{:S(2)}, u32[]{:S(2)}) collective-permute-start(bf16[256,1152]{1,0:T(8,128)(2,1)S(1)} %fusion.112), channel_id=1, source_target_pairs={{0,8},{8,0},{1,9},{9,1},{2,10},{10,2},{3,11},{11,3},{4,12},{12,4},... | collective-permute-start | bytes 1769480 | tf_op jit(solution)/shard_map/ppermute | solution.py:16
  801.3 33.5 %collective-permute-start.108 = (bf16[256,1152]{1,0:T(8,128)(2,1)}, bf16[256,1152]{1,0:T(8,128)(2,1)}, u32[]{:S(2)}, u32[]{:S(2)}) collective-permute-start(bf16[256,1152]{1,0:T(8,128)(2,1)} %fusion.110), channel_id=1, source_target_pairs={{0,8},{8,0},{1,9},{9,1},{2,10},{10,2},{3,11},{11,3},{4,12},{12,4},... | collective-permute-start | bytes 1769480 | tf_op jit(solution)/shard_map/ppermute | solution.py:16
  803.4 31.4 %collective-permute-start.109 = (bf16[512,1152]{1,0:T(8,128)(2,1)}, bf16[512,1152]{1,0:T(8,128)(2,1)}, u32[]{:S(2)}, u32[]{:S(2)}) collective-permute-start(bf16[512,1152]{1,0:T(8,128)(2,1)} %pad_maximum_fusion.27), channel_id=1, source_target_pairs={{0,2},{2,0},{1,3},{3,1},{4,6},{6,4},{5,7},{7,5},{8,10},{10,8},{9,1... | collective-permute-start | bytes 3538952 | tf_op jit(solution)/shard_map/ppermute | solution.py:16
  804.4 67.2 %all-to-all-start.3 = ((bf16[4,256,1152]{2,1,0:T(8,128)(2,1)}), bf16[4,256,1152]{2,1,0:T(8,128)(2,1)S(1)}, u32[]{:S(2)}, u32[]{:S(2)}) async-start(bf16[4,256,1152]{2,1,0:T(8,128)(2,1)} %pad_maximum_fusion.2), calls=%async_computation.3 | async-start | bytes 4718592 | tf_op jit(solution)/shard_map/all_to_all | solution.py:20
  840.2 29.5 %collective-permute-start.114 = (bf16[256,1152]{1,0:T(8,128)(2,1)S(1)}, bf16[256,1152]{1,0:T(8,128)(2,1)S(1)}, u32[]{:S(2)}, u32[]{:S(2)}) collective-permute-start(bf16[256,1152]{1,0:T(8,128)(2,1)S(1)} %fusion.109), channel_id=1, source_target_pairs={{0,8},{8,0},{1,9},{9,1},{2,10},{10,2},{3,11},{11,3},{4,12},{12,4},... | collective-permute-start | bytes 1769480 | tf_op jit(solution)/shard_map/ppermute | solution.py:16
  842.2 27.4 %collective-permute-start.115 = (bf16[1024,512]{1,0:T(8,128)(2,1)S(1)}, bf16[1024,512]{1,0:T(8,128)(2,1)S(1)}, u32[]{:S(2)}, u32[]{:S(2)}) collective-permute-start(bf16[1024,512]{1,0:T(8,128)(2,1)S(1)} %pad_maximum_fusion.51), channel_id=1, source_target_pairs={{0,2},{2,0},{1,3},{3,1},{4,6},{6,4},{5,7},{7,5},{8,10},{10,8},{9,1... | collective-permute-start | bytes 3145736 | tf_op jit(solution)/shard_map/ppermute | solution.py:16
  844.6 25.1 %collective-permute-start.111 = (bf16[64,2048]{1,0:T(8,128)(2,1)S(1)}, bf16[64,2048]{1,0:T(8,128)(2,1)S(1)}, u32[]{:S(2)}, u32[]{:S(2)}) collective-permute-start(bf16[64,2048]{1,0:T(8,128)(2,1)S(1)} %get-tuple-element.775), channel_id=1, source_target_pairs={{0,16},{16,0},{1,17},{17,1},{2,18},{18,2},{3,19},{19,3},{4,20},{20... | collective-permute-start | bytes 786440 | tf_op jit(solution)/shard_map/ppermute | solution.py:16
  878.3 26.1 %collective-permute-start.117 = (bf16[512,512]{1,0:T(8,128)(2,1)}, bf16[512,512]{1,0:T(8,128)(2,1)}, u32[]{:S(2)}, u32[]{:S(2)}) collective-permute-start(bf16[512,512]{1,0:T(8,128)(2,1)} %slice.1994), channel_id=1, source_target_pairs={{0,8},{8,0},{1,9},{9,1},{2,10},{10,2},{3,11},{11,3},{4,12},{12,4},... | collective-permute-start | bytes 1572872 | tf_op jit(solution)/shard_map/ppermute | solution.py:16
  879.7 24.8 %collective-permute-start.118 = (bf16[1024,512]{1,0:T(8,128)(2,1)}, bf16[1024,512]{1,0:T(8,128)(2,1)}, u32[]{:S(2)}, u32[]{:S(2)}) collective-permute-start(bf16[1024,512]{1,0:T(8,128)(2,1)} %pad_maximum_fusion.54), channel_id=1, source_target_pairs={{0,2},{2,0},{1,3},{3,1},{4,6},{6,4},{5,7},{7,5},{8,10},{10,8},{9,1... | collective-permute-start | bytes 3145736 | tf_op jit(solution)/shard_map/ppermute | solution.py:16
  885.4 54.6 %all-to-all-start.4 = ((bf16[4,256,1152]{2,1,0:T(8,128)(2,1)}), bf16[4,256,1152]{2,1,0:T(8,128)(2,1)}, u32[]{:S(2)}, u32[]{:S(2)}) async-start(bf16[4,256,1152]{2,1,0:T(8,128)(2,1)} %pad_maximum_fusion.3), calls=%async_computation.4 | async-start | bytes 4718592 | tf_op jit(solution)/shard_map/all_to_all | solution.py:20
  907.9 32.1 %collective-permute-start.122 = (bf16[512,512]{1,0:T(8,128)(2,1)S(1)}, bf16[512,512]{1,0:T(8,128)(2,1)}, u32[]{:S(2)}, u32[]{:S(2)}) collective-permute-start(bf16[512,512]{1,0:T(8,128)(2,1)S(1)} %slice.2000), channel_id=1, source_target_pairs={{0,8},{8,0},{1,9},{9,1},{2,10},{10,2},{3,11},{11,3},{4,12},{12,4},... | collective-permute-start | bytes 1572872 | tf_op jit(solution)/shard_map/ppermute | solution.py:16
  914.5 25.4 %collective-permute-start.121 = (f32[68,128]{1,0:T(8,128)S(1)}, f32[68,128]{1,0:T(8,128)S(1)}, u32[]{:S(2)}, u32[]{:S(2)}) collective-permute-start(f32[68,128]{1,0:T(8,128)S(1)} %fusion.479), channel_id=1, source_target_pairs={{0,4},{4,0},{1,5},{5,1},{2,6},{6,2},{3,7},{7,3},{8,12},{12,8},{9,1... | collective-permute-start | bytes 104456 | tf_op jit(solution)/shard_map/ppermute | solution.py:16
  944.3 39.0 %all-to-all-start.5 = ((bf16[4,512,512]{2,1,0:T(8,128)(2,1)}), bf16[4,512,512]{2,1,0:T(8,128)(2,1)}, u32[]{:S(2)}, u32[]{:S(2)}) async-start(bf16[4,512,512]{2,1,0:T(8,128)(2,1)} %pad_maximum_fusion.7), calls=%async_computation.5 | async-start | bytes 4194304 | tf_op jit(solution)/shard_map/all_to_all | solution.py:20
  (341 other events, 3582.7 us)

commit v5 on v4

--- a/solution.py
+++ b/solution.py
@@ -532,8 +532,9 @@
 
     low, high = rolled(grad.astype(bf16)), rolled((kept[1][10] + added(*kept["output"])).astype(bf16))
     keep = jnp.where(s == 0, low, high)
-    passed = swap(jnp.where(s == 0, high, low), "s")
+    passed = jnp.where(s == 0, high, low)
     (keep, passed), gains0, gains1 = clock.point("E1", ((keep, passed), gains0, gains1))
+    passed = swap(passed, "s")
     sums = []
     for gains in (gains0, gains1):
         sums += [rolled(gains[0]), rolled(gains[1]), gains[2], gains[3]]

time: 1000 us -> 998 us (level)
    unnamed x611 -> x601, local copies, waits for them, and re-layouts: 46.5 us -> 47.6 us
where the time goes in v5:
time: 998 us; the launch traced here: 988 us
  waiting for transfers between devices  537 us (54%)
  starting transfers between devices  166 us (17%)
  matrix products  101 us (10%)
  other arithmetic  91.1 us (9%)
  local copies, waits for them, and re-layouts  85.4 us (9%)
    ppermute x112, waiting for transfers between devices, swap(): return lax.ppermute(value, axis, [(0, 1), (1, 0)])  480 us
    ppermute x112, starting transfers between devices, swap(): return lax.ppermute(value, axis, [(0, 1), (1, 0)])  125 us
    ppermute x16, waiting for transfers between devices, cross(): return lax.ppermute(value, ('s', 't'), [(i, 3 - i) for i in range(4)])  55.2 us
    unnamed x601, local copies, waits for them, and re-layouts  47.6 us
    dot_general x40, matrix products, dot_t(): lax.dot_general(left, right, (((1,), (1,)), ((), ())), preferred_element_...  37.4 us
    dot_general x56, matrix products, t_dot(): lax.dot_general(left, right, (((0,), (0,)), ((), ())), preferred_element_...  30.6 us
    all_to_all x6, starting transfers between devices, exchange(): return lax.all_to_all(value, axes, 0, 0, tiled=True)  28.5 us
    dot_general x20, matrix products, dot(): return jnp.dot(left, right, preferred_element_type=f32)  26.7 us
  transfers between devices with their start and end apart: 134, of which 70 were waited for; matrix products, arithmetic and copies ran while one was open for 20% of the time, Pallas kernels for 0%

profile of v5, /device:TPU:0, one launch (start us, length us, event | category | flops | bytes accessed | tf_op | source)
XLA Modules:
  0.0 987.5 jit_solution(13579954439881995051)
XLA Ops:
  1.7 3.0 collective-permute-start
  15.7 3.7 all-to-all-start
  37.1 10.9 %collective-permute-done.2 = bf16[64,2048]{1,0:T(8,128)(2,1)S(1)} collective-permute-done((bf16[64,2048]{1,0:T(8,128)(2,1)S(1)}, bf16[64,2048]{1,0:T(8,128)(2,1)S(1)}, u32[]{:S(2)}, u32[]{:S(2)}) %collective-permute-start.2) | collective-permute-done | bytes 262176 | tf_op jit(solution)/shard_map/ppermute | solution.py:16
  51.5 4.1 collective-permute-done.3
  58.5 3.4 collective-permute-start.10
  68.7 11.2 %collective-permute-done.8 = bf16[64,2048]{1,0:T(8,128)(2,1)S(1)} collective-permute-done((bf16[64,2048]{1,0:T(8,128)(2,1)S(1)}, bf16[64,2048]{1,0:T(8,128)(2,1)S(1)}, u32[]{:S(2)}, u32[]{:S(2)}) %collective-permute-start.8) | collective-permute-done | bytes 262176 | tf_op jit(solution)/shard_map/ppermute | solution.py:16
  79.9 3.0 collective-permute-done.9
  84.8 4.6 all-to-all-start.1
  93.2 4.4 collective-permute-start.12
  98.3 26.0 %collective-permute-done.12 = bf16[512,512]{1,0:T(8,128)(2,1)S(1)} collective-permute-done((bf16[512,512]{1,0:T(8,128)(2,1)S(1)}, bf16[512,512]{1,0:T(8,128)(2,1)S(1)}, u32[]{:S(2)}, u32[]{:S(2)}) %collective-permute-start.12) | collective-permute-done | bytes 524320 | tf_op jit(solution)/shard_map/ppermute | solution.py:16
  138.2 5.4 all-to-all-start.2
  146.8 15.5 %collective-permute-done.14 = bf16[256,1152]{1,0:T(8,128)(2,1)} collective-permute-done((bf16[256,1152]{1,0:T(8,128)(2,1)}, bf16[256,1152]{1,0:T(8,128)(2,1)}, u32[]{:S(2)}, u32[]{:S(2)}) %collective-permute-start.14) | collective-permute-done | bytes 589856 | tf_op jit(solution)/shard_map/ppermute | solution.py:16
  180.8 14.7 %collective-permute-done.17 = bf16[256,1152]{1,0:T(8,128)(2,1)S(1)} collective-permute-done((bf16[256,1152]{1,0:T(8,128)(2,1)S(1)}, bf16[256,1152]{1,0:T(8,128)(2,1)S(1)}, u32[]{:S(2)}, u32[]{:S(2)}) %collective-permute-start.17) | collective-permute-done | bytes 589856 | tf_op jit(solution)/shard_map/ppermute | solution.py:16
  212.6 16.7 %collective-permute-done.23 = bf16[256,1152]{1,0:T(8,128)(2,1)S(1)} collective-permute-done((bf16[256,1152]{1,0:T(8,128)(2,1)S(1)}, bf16[256,1152]{1,0:T(8,128)(2,1)S(1)}, u32[]{:S(2)}, u32[]{:S(2)}) %collective-permute-start.23) | collective-permute-done | bytes 589856 | tf_op jit(solution)/shard_map/ppermute | solution.py:16
  229.3 3.1 collective-permute-done.20
  232.3 4.3 collective-permute-done.21
  245.4 12.4 %collective-permute-done.25 = bf16[64,2048]{1,0:T(8,128)(2,1)S(1)} collective-permute-done((bf16[64,2048]{1,0:T(8,128)(2,1)S(1)}, bf16[64,2048]{1,0:T(8,128)(2,1)S(1)}, u32[]{:S(2)}, u32[]{:S(2)}) %collective-permute-start.25) | collective-permute-done | bytes 262176 | tf_op jit(solution)/shard_map/ppermute | solution.py:16
  257.8 3.4 collective-permute-done.26
  261.2 4.2 collective-permute-done.28
  268.3 24.0 %collective-permute-done.31 = bf16[512,512]{1,0:T(8,128)(2,1)S(1)} collective-permute-done((bf16[512,512]{1,0:T(8,128)(2,1)S(1)}, bf16[512,512]{1,0:T(8,128)(2,1)S(1)}, u32[]{:S(2)}, u32[]{:S(2)}) %collective-permute-start.31) | collective-permute-done | bytes 524320 | tf_op jit(solution)/shard_map/ppermute | solution.py:16
  305.2 5.5 collective-permute-done.33
  310.7 3.2 collective-permute-done.34
  313.9 11.4 %collective-permute-done.36 = bf16[512,512]{1,0:T(8,128)(2,1)S(1)} collective-permute-done((bf16[512,512]{1,0:T(8,128)(2,1)S(1)}, bf16[512,512]{1,0:T(8,128)(2,1)S(1)}, u32[]{:S(2)}, u32[]{:S(2)}) %collective-permute-start.36) | collective-permute-done | bytes 524320 | tf_op jit(solution)/shard_map/ppermute | solution.py:16
  336.6 21.8 %collective-permute-done.42 = bf16[256,1152]{1,0:T(8,128)(2,1)S(1)} collective-permute-done((bf16[256,1152]{1,0:T(8,128)(2,1)S(1)}, bf16[256,1152]{1,0:T(8,128)(2,1)S(1)}, u32[]{:S(2)}, u32[]{:S(2)}) %collective-permute-start.42) | collective-permute-done | bytes 589856 | tf_op jit(solution)/shard_map/ppermute | solution.py:16
  369.6 13.0 %collective-permute-done.44 = bf16[64,2048]{1,0:T(8,128)(2,1)S(1)} collective-permute-done((bf16[64,2048]{1,0:T(8,128)(2,1)S(1)}, bf16[64,2048]{1,0:T(8,128)(2,1)S(1)}, u32[]{:S(2)}, u32[]{:S(2)}) %collective-permute-start.44) | collective-permute-done | bytes 262176 | tf_op jit(solution)/shard_map/ppermute | solution.py:16
  384.8 7.9 collective-permute-done.47
  408.4 14.2 %collective-permute-done.50 = bf16[256,1152]{1,0:T(8,128)(2,1)S(1)} collective-permute-done((bf16[256,1152]{1,0:T(8,128)(2,1)S(1)}, bf16[256,1152]{1,0:T(8,128)(2,1)S(1)}, u32[]{:S(2)}, u32[]{:S(2)}) %collective-permute-start.50) | collective-permute-done | bytes 589856 | tf_op jit(solution)/shard_map/ppermute | solution.py:16
  430.6 23.7 %collective-permute-done.56 = bf16[256,1152]{1,0:T(8,128)(2,1)S(1)} collective-permute-done((bf16[256,1152]{1,0:T(8,128)(2,1)S(1)}, bf16[256,1152]{1,0:T(8,128)(2,1)S(1)}, u32[]{:S(2)}, u32[]{:S(2)}) %collective-permute-start.56) | collective-permute-done | bytes 589856 | tf_op jit(solution)/shard_map/ppermute | solution.py:16
  459.6 3.4 collective-permute-done.57
  465.8 3.9 collective-permute-done.59
  469.7 15.7 %collective-permute-done.60 = bf16[512,1152]{1,0:T(8,128)(2,1)S(1)} collective-permute-done((bf16[512,1152]{1,0:T(8,128)(2,1)S(1)}, bf16[512,1152]{1,0:T(8,128)(2,1)S(1)}, u32[]{:S(2)}, u32[]{:S(2)}) %collective-permute-start.60) | collective-permute-done | bytes 1179680 | tf_op jit(solution)/shard_map/ppermute | solution.py:16
  509.6 3.6 fusion.1
  513.2 15.3 %collective-permute-done.63 = bf16[512,1152]{1,0:T(8,128)(2,1)S(1)} collective-permute-done((bf16[512,1152]{1,0:T(8,128)(2,1)S(1)}, bf16[512,1152]{1,0:T(8,128)(2,1)S(1)}, u32[]{:S(2)}, u32[]{:S(2)}) %collective-permute-start.63) | collective-permute-done | bytes 1179680 | tf_op jit(solution)/shard_map/ppermute | solution.py:16
  539.2 22.9 %collective-permute-done.68 = bf16[256,1152]{1,0:T(8,128)(2,1)} collective-permute-done((bf16[256,1152]{1,0:T(8,128)(2,1)S(1)}, bf16[256,1152]{1,0:T(8,128)(2,1)}, u32[]{:S(2)}, u32[]{:S(2)}) %collective-permute-start.68) | collective-permute-done | bytes 589856 | tf_op jit(solution)/shard_map/ppermute | solution.py:16
  573.0 3.6 collective-permute-done.70
  576.6 9.7 collective-permute-done.71
  586.3 4.0 collective-permute-done.72
  590.4 3.4 collective-permute-done.73
  619.2 7.1 collective-permute-done.76
  637.8 20.8 %collective-permute-done.82 = bf16[256,1152]{1,0:T(8,128)(2,1)S(1)} collective-permute-done((bf16[256,1152]{1,0:T(8,128)(2,1)S(1)}, bf16[256,1152]{1,0:T(8,128)(2,1)S(1)}, u32[]{:S(2)}, u32[]{:S(2)}) %collective-permute-start.82) | collective-permute-done | bytes 589856 | tf_op jit(solution)/shard_map/ppermute | solution.py:16
  666.7 3.5 collective-permute-start.85
  671.2 3.2 collective-permute-done.84
  674.4 9.6 collective-permute-done.85
  684.0 6.5 collective-permute-done.86
  718.8 11.0 %collective-permute-done.94 = bf16[64,2048]{1,0:T(8,128)(2,1)S(1)} collective-permute-done((bf16[64,2048]{1,0:T(8,128)(2,1)S(1)}, bf16[64,2048]{1,0:T(8,128)(2,1)S(1)}, u32[]{:S(2)}, u32[]{:S(2)}) %collective-permute-start.94) | collective-permute-done | bytes 262176 | tf_op jit(solution)/shard_map/ppermute | solution.py:50
  729.8 4.4 collective-permute-done.95
  734.2 3.3 collective-permute-done.96
  746.9 12.7 %collective-permute-done.98 = bf16[64,2048]{1,0:T(8,128)(2,1)S(1)} collective-permute-done((bf16[64,2048]{1,0:T(8,128)(2,1)S(1)}, bf16[64,2048]{1,0:T(8,128)(2,1)S(1)}, u32[]{:S(2)}, u32[]{:S(2)}) %collective-permute-start.98) | collective-permute-done | bytes 262176 | tf_op jit(solution)/shard_map/ppermute | solution.py:16
  759.6 4.0 collective-permute-done.99
  763.6 7.0 collective-permute-done.100
  774.9 3.0 collective-permute-start.103
  778.8 4.8 collective-permute-done.102
  783.5 5.9 collective-permute-done.103
  789.5 6.4 collective-permute-done.104
  804.2 4.8 all-to-all-start.3
  850.6 19.4 %collective-permute-done.114 = bf16[256,1152]{1,0:T(8,128)(2,1)S(1)} collective-permute-done((bf16[256,1152]{1,0:T(8,128)(2,1)S(1)}, bf16[256,1152]{1,0:T(8,128)(2,1)S(1)}, u32[]{:S(2)}, u32[]{:S(2)}) %collective-permute-start.114) | collective-permute-done | bytes 589856 | tf_op jit(solution)/shard_map/ppermute | solution.py:16
  881.8 5.1 all-to-all-start.4
  887.8 16.9 %collective-permute-done.116 = bf16[512,512]{1,0:T(8,128)(2,1)} collective-permute-done((bf16[512,512]{1,0:T(8,128)(2,1)}, bf16[512,512]{1,0:T(8,128)(2,1)}, u32[]{:S(2)}, u32[]{:S(2)}) %collective-permute-start.116) | collective-permute-done | bytes 524320 | tf_op jit(solution)/shard_map/ppermute | solution.py:16
  914.1 5.6 collective-permute-start.121
  921.6 15.7 %collective-permute-done.121 = f32[68,128]{1,0:T(8,128)S(1)} collective-permute-done((f32[68,128]{1,0:T(8,128)S(1)}, f32[68,128]{1,0:T(8,128)S(1)}, u32[]{:S(2)}, u32[]{:S(2)}) %collective-permute-start.121) | collective-permute-done | bytes 34848 | tf_op jit(solution)/shard_map/ppermute | solution.py:16
  938.5 3.0 pad_maximum_fusion.7
  942.6 4.8 all-to-all-start.5
  962.7 7.5 collective-permute-done.127
  974.6 4.1 collective-permute-done.125
  (1250 shorter events, 416.1 us)
Async XLA Ops:
  15.7 41.0 %all-to-all-start = ((bf16[4,512,512]{2,1,0:T(8,128)(2,1)}), bf16[4,512,512]{2,1,0:T(8,128)(2,1)S(1)}, u32[]{:S(2)}, u32[]{:S(2)}) async-start(bf16[4,512,512]{2,1,0:T(8,128)(2,1)} %pad_maximum_fusion.4), calls=%async_computation | async-start | bytes 4194304 | tf_op jit(solution)/shard_map/all_to_all | solution.py:20
  22.1 25.9 %collective-permute-start.2 = (bf16[64,2048]{1,0:T(8,128)(2,1)S(1)}, bf16[64,2048]{1,0:T(8,128)(2,1)S(1)}, u32[]{:S(2)}, u32[]{:S(2)}) collective-permute-start(bf16[64,2048]{1,0:T(8,128)(2,1)S(1)} %dynamic-slice_bitcast_fusion.1), channel_id=1, source_target_pairs={{0,8},{8,0},{1,9},{9,1},{2,10},{10,2},{3,11},{11,3},{4,12},{12,4},... | collective-permute-start | bytes 786440 | tf_op jit(solution)/shard_map/ppermute | solution.py:16
  58.5 25.1 %collective-permute-start.10 = (bf16[512,512]{1,0:T(8,128)(2,1)S(1)}, bf16[512,512]{1,0:T(8,128)(2,1)S(1)}, u32[]{:S(2)}, u32[]{:S(2)}) collective-permute-start(bf16[512,512]{1,0:T(8,128)(2,1)S(1)} %get-tuple-element.306), channel_id=1, source_target_pairs={{0,8},{8,0},{1,9},{9,1},{2,10},{10,2},{3,11},{11,3},{4,12},{12,4},... | collective-permute-start | bytes 1572872 | tf_op jit(solution)/shard_map/ppermute | solution.py:16
  84.8 42.4 %all-to-all-start.1 = ((bf16[4,256,1152]{2,1,0:T(8,128)(2,1)}), bf16[4,256,1152]{2,1,0:T(8,128)(2,1)}, u32[]{:S(2)}, u32[]{:S(2)}) async-start(bf16[4,256,1152]{2,1,0:T(8,128)(2,1)} %pad_maximum_fusion), calls=%async_computation.1 | async-start | bytes 4718592 | tf_op jit(solution)/shard_map/all_to_all | solution.py:20
  90.8 34.4 %collective-permute-start.11 = (bf16[1024,512]{1,0:T(8,128)(2,1)}, bf16[1024,512]{1,0:T(8,128)(2,1)}, u32[]{:S(2)}, u32[]{:S(2)}) collective-permute-start(bf16[1024,512]{1,0:T(8,128)(2,1)} %pad_maximum_fusion.28), channel_id=1, source_target_pairs={{0,2},{2,0},{1,3},{3,1},{4,6},{6,4},{5,7},{7,5},{8,10},{10,8},{9,1... | collective-permute-start | bytes 3145736 | tf_op jit(solution)/shard_map/ppermute | solution.py:16
  93.2 31.2 %collective-permute-start.12 = (bf16[512,512]{1,0:T(8,128)(2,1)S(1)}, bf16[512,512]{1,0:T(8,128)(2,1)S(1)}, u32[]{:S(2)}, u32[]{:S(2)}) collective-permute-start(bf16[512,512]{1,0:T(8,128)(2,1)S(1)} %get-tuple-element.311), channel_id=1, source_target_pairs={{0,8},{8,0},{1,9},{9,1},{2,10},{10,2},{3,11},{11,3},{4,12},{12,4},... | collective-permute-start | bytes 1572872 | tf_op jit(solution)/shard_map/ppermute | solution.py:16
  132.2 30.1 %collective-permute-start.13 = (bf16[1024,512]{1,0:T(8,128)(2,1)}, bf16[1024,512]{1,0:T(8,128)(2,1)}, u32[]{:S(2)}, u32[]{:S(2)}) collective-permute-start(bf16[1024,512]{1,0:T(8,128)(2,1)} %pad_maximum_fusion.29), channel_id=1, source_target_pairs={{0,2},{2,0},{1,3},{3,1},{4,6},{6,4},{5,7},{7,5},{8,10},{10,8},{9,1... | collective-permute-start | bytes 3145736 | tf_op jit(solution)/shard_map/ppermute | solution.py:16
  136.1 26.2 %collective-permute-start.14 = (bf16[256,1152]{1,0:T(8,128)(2,1)}, bf16[256,1152]{1,0:T(8,128)(2,1)}, u32[]{:S(2)}, u32[]{:S(2)}) collective-permute-start(bf16[256,1152]{1,0:T(8,128)(2,1)} %get-tuple-element.327), channel_id=1, source_target_pairs={{0,8},{8,0},{1,9},{9,1},{2,10},{10,2},{3,11},{11,3},{4,12},{12,4},... | collective-permute-start | bytes 1769480 | tf_op jit(solution)/shard_map/ppermute | solution.py:16
  138.2 58.1 %all-to-all-start.2 = ((bf16[4,256,1152]{2,1,0:T(8,128)(2,1)}), bf16[4,256,1152]{2,1,0:T(8,128)(2,1)}, u32[]{:S(2)}, u32[]{:S(2)}) async-start(bf16[4,256,1152]{2,1,0:T(8,128)(2,1)} %pad_maximum_fusion.1), calls=%async_computation.2 | async-start | bytes 4718592 | tf_op jit(solution)/shard_map/all_to_all | solution.py:20
  165.9 30.4 %collective-permute-start.16 = (bf16[512,1152]{1,0:T(8,128)(2,1)S(1)}, bf16[512,1152]{1,0:T(8,128)(2,1)}, u32[]{:S(2)}, u32[]{:S(2)}) collective-permute-start(bf16[512,1152]{1,0:T(8,128)(2,1)S(1)} %pad_maximum_fusion.12), channel_id=1, source_target_pairs={{0,2},{2,0},{1,3},{3,1},{4,6},{6,4},{5,7},{7,5},{8,10},{10,8},{9,1... | collective-permute-start | bytes 3538952 | tf_op jit(solution)/shard_map/ppermute | solution.py:16
  166.5 29.0 %collective-permute-start.17 = (bf16[256,1152]{1,0:T(8,128)(2,1)S(1)}, bf16[256,1152]{1,0:T(8,128)(2,1)S(1)}, u32[]{:S(2)}, u32[]{:S(2)}) collective-permute-start(bf16[256,1152]{1,0:T(8,128)(2,1)S(1)} %copy-done.22), channel_id=1, source_target_pairs={{0,8},{8,0},{1,9},{9,1},{2,10},{10,2},{3,11},{11,3},{4,12},{12,4},... | collective-permute-start | bytes 1769480 | tf_op jit(solution)/shard_map/ppermute | solution.py:16
  199.4 29.8 %collective-permute-start.22 = (bf16[512,1152]{1,0:T(8,128)(2,1)S(1)}, bf16[512,1152]{1,0:T(8,128)(2,1)S(1)}, u32[]{:S(2)}, u32[]{:S(2)}) collective-permute-start(bf16[512,1152]{1,0:T(8,128)(2,1)S(1)} %pad_maximum_fusion.13), channel_id=1, source_target_pairs={{0,2},{2,0},{1,3},{3,1},{4,6},{6,4},{5,7},{7,5},{8,10},{10,8},{9,1... | collective-permute-start | bytes 3538952 | tf_op jit(solution)/shard_map/ppermute | solution.py:16
  201.0 28.2 %collective-permute-start.23 = (bf16[256,1152]{1,0:T(8,128)(2,1)S(1)}, bf16[256,1152]{1,0:T(8,128)(2,1)S(1)}, u32[]{:S(2)}, u32[]{:S(2)}) collective-permute-start(bf16[256,1152]{1,0:T(8,128)(2,1)S(1)} %get-tuple-element.339), channel_id=1, source_target_pairs={{0,8},{8,0},{1,9},{9,1},{2,10},{10,2},{3,11},{11,3},{4,12},{12,4},... | collective-permute-start | bytes 1769480 | tf_op jit(solution)/shard_map/ppermute | solution.py:16
  237.1 28.3 %collective-permute-start.27 = (bf16[512,1152]{1,0:T(8,128)(2,1)S(1)}, bf16[512,1152]{1,0:T(8,128)(2,1)S(1)}, u32[]{:S(2)}, u32[]{:S(2)}) collective-permute-start(bf16[512,1152]{1,0:T(8,128)(2,1)S(1)} %pad_maximum_fusion.14), channel_id=1, source_target_pairs={{0,2},{2,0},{1,3},{3,1},{4,6},{6,4},{5,7},{7,5},{8,10},{10,8},{9,1... | collective-permute-start | bytes 3538952 | tf_op jit(solution)/shard_map/ppermute | solution.py:16
  237.6 27.7 %collective-permute-start.28 = (bf16[256,1152]{1,0:T(8,128)(2,1)S(1)}, bf16[256,1152]{1,0:T(8,128)(2,1)S(1)}, u32[]{:S(2)}, u32[]{:S(2)}) collective-permute-start(bf16[256,1152]{1,0:T(8,128)(2,1)S(1)} %get-tuple-element.348), channel_id=1, source_target_pairs={{0,8},{8,0},{1,9},{9,1},{2,10},{10,2},{3,11},{11,3},{4,12},{12,4},... | collective-permute-start | bytes 1769480 | tf_op jit(solution)/shard_map/ppermute | solution.py:16
  265.7 28.4 %collective-permute-start.30 = (bf16[512,1152]{1,0:T(8,128)(2,1)S(1)}, bf16[512,1152]{1,0:T(8,128)(2,1)S(1)}, u32[]{:S(2)}, u32[]{:S(2)}) collective-permute-start(bf16[512,1152]{1,0:T(8,128)(2,1)S(1)} %pad_maximum_fusion.15), channel_id=1, source_target_pairs={{0,2},{2,0},{1,3},{3,1},{4,6},{6,4},{5,7},{7,5},{8,10},{10,8},{9,1... | collective-permute-start | bytes 3538952 | tf_op jit(solution)/shard_map/ppermute | solution.py:16
  267.3 25.1 %collective-permute-start.31 = (bf16[512,512]{1,0:T(8,128)(2,1)S(1)}, bf16[512,512]{1,0:T(8,128)(2,1)S(1)}, u32[]{:S(2)}, u32[]{:S(2)}) collective-permute-start(bf16[512,512]{1,0:T(8,128)(2,1)S(1)} %copy-done.29), channel_id=1, source_target_pairs={{0,8},{8,0},{1,9},{9,1},{2,10},{10,2},{3,11},{11,3},{4,12},{12,4},... | collective-permute-start | bytes 1572872 | tf_op jit(solution)/shard_map/ppermute | solution.py:16
  299.1 26.2 %collective-permute-start.35 = (bf16[1024,512]{1,0:T(8,128)(2,1)S(1)}, bf16[1024,512]{1,0:T(8,128)(2,1)S(1)}, u32[]{:S(2)}, u32[]{:S(2)}) collective-permute-start(bf16[1024,512]{1,0:T(8,128)(2,1)S(1)} %pad_maximum_fusion.32), channel_id=1, source_target_pairs={{0,2},{2,0},{1,3},{3,1},{4,6},{6,4},{5,7},{7,5},{8,10},{10,8},{9,1... | collective-permute-start | bytes 3145736 | tf_op jit(solution)/shard_map/ppermute | solution.py:16
  300.7 24.6 %collective-permute-start.36 = (bf16[512,512]{1,0:T(8,128)(2,1)S(1)}, bf16[512,512]{1,0:T(8,128)(2,1)S(1)}, u32[]{:S(2)}, u32[]{:S(2)}) collective-permute-start(bf16[512,512]{1,0:T(8,128)(2,1)S(1)} %copy-done.27), channel_id=1, source_target_pairs={{0,8},{8,0},{1,9},{9,1},{2,10},{10,2},{3,11},{11,3},{4,12},{12,4},... | collective-permute-start | bytes 1572872 | tf_op jit(solution)/shard_map/ppermute | solution.py:16
  329.3 29.1 %collective-permute-start.41 = (bf16[1024,512]{1,0:T(8,128)(2,1)S(1)}, bf16[1024,512]{1,0:T(8,128)(2,1)S(1)}, u32[]{:S(2)}, u32[]{:S(2)}) collective-permute-start(bf16[1024,512]{1,0:T(8,128)(2,1)S(1)} %pad_maximum_fusion.33), channel_id=1, source_target_pairs={{0,2},{2,0},{1,3},{3,1},{4,6},{6,4},{5,7},{7,5},{8,10},{10,8},{9,1... | collective-permute-start | bytes 3145736 | tf_op jit(solution)/shard_map/ppermute | solution.py:16
  330.4 28.0 %collective-permute-start.42 = (bf16[256,1152]{1,0:T(8,128)(2,1)S(1)}, bf16[256,1152]{1,0:T(8,128)(2,1)S(1)}, u32[]{:S(2)}, u32[]{:S(2)}) collective-permute-start(bf16[256,1152]{1,0:T(8,128)(2,1)S(1)} %get-tuple-element.377), channel_id=1, source_target_pairs={{0,8},{8,0},{1,9},{9,1},{2,10},{10,2},{3,11},{11,3},{4,12},{12,4},... | collective-permute-start | bytes 1769480 | tf_op jit(solution)/shard_map/ppermute | solution.py:16
  332.8 25.5 %collective-permute-start.38 = (bf16[64,2048]{1,0:T(8,128)(2,1)S(1)}, bf16[64,2048]{1,0:T(8,128)(2,1)S(1)}, u32[]{:S(2)}, u32[]{:S(2)}) collective-permute-start(bf16[64,2048]{1,0:T(8,128)(2,1)S(1)} %get-tuple-element.760), channel_id=1, source_target_pairs={{0,16},{16,0},{1,17},{17,1},{2,18},{18,2},{3,19},{19,3},{4,20},{20... | collective-permute-start | bytes 786440 | tf_op jit(solution)/shard_map/ppermute | solution.py:16
  336.2 24.5 %collective-permute-start.40 = (bf16[64,2048]{1,0:T(8,128)(2,1)S(1)}, bf16[64,2048]{1,0:T(8,128)(2,1)S(1)}, u32[]{:S(2)}, u32[]{:S(2)}) collective-permute-start(bf16[64,2048]{1,0:T(8,128)(2,1)S(1)} %get-tuple-element.758), channel_id=1, source_target_pairs={{0,20},{4,16},{16,4},{20,0},{1,21},{5,17},{17,5},{21,1},{2,22},{6,... | collective-permute-start | bytes 786440 | tf_op jit(solution)/shard_map/ppermute | solution.py:50
  361.2 31.5 %collective-permute-start.46 = (bf16[512,1152]{1,0:T(8,128)(2,1)S(1)}, bf16[512,1152]{1,0:T(8,128)(2,1)S(1)}, u32[]{:S(2)}, u32[]{:S(2)}) collective-permute-start(bf16[512,1152]{1,0:T(8,128)(2,1)S(1)} %pad_maximum_fusion.16), channel_id=1, source_target_pairs={{0,2},{2,0},{1,3},{3,1},{4,6},{6,4},{5,7},{7,5},{8,10},{10,8},{9,1... | collective-permute-start | bytes 3538952 | tf_op jit(solution)/shard_map/ppermute | solution.py:16
  365.9 26.8 %collective-permute-start.47 = (bf16[256,1152]{1,0:T(8,128)(2,1)S(1)}, bf16[256,1152]{1,0:T(8,128)(2,1)S(1)}, u32[]{:S(2)}, u32[]{:S(2)}) collective-permute-start(bf16[256,1152]{1,0:T(8,128)(2,1)S(1)} %get-tuple-element.385), channel_id=1, source_target_pairs={{0,8},{8,0},{1,9},{9,1},{2,10},{10,2},{3,11},{11,3},{4,12},{12,4},... | collective-permute-start | bytes 1769480 | tf_op jit(solution)/shard_map/ppermute | solution.py:16
  393.0 29.7 %collective-permute-start.49 = (bf16[512,1152]{1,0:T(8,128)(2,1)S(1)}, bf16[512,1152]{1,0:T(8,128)(2,1)S(1)}, u32[]{:S(2)}, u32[]{:S(2)}) collective-permute-start(bf16[512,1152]{1,0:T(8,128)(2,1)S(1)} %pad_maximum_fusion.17), channel_id=1, source_target_pairs={{0,2},{2,0},{1,3},{3,1},{4,6},{6,4},{5,7},{7,5},{8,10},{10,8},{9,1... | collective-permute-start | bytes 3538952 | tf_op jit(solution)/shard_map/ppermute | solution.py:16
  394.1 28.6 %collective-permute-start.50 = (bf16[256,1152]{1,0:T(8,128)(2,1)S(1)}, bf16[256,1152]{1,0:T(8,128)(2,1)S(1)}, u32[]{:S(2)}, u32[]{:S(2)}) collective-permute-start(bf16[256,1152]{1,0:T(8,128)(2,1)S(1)} %get-tuple-element.395), channel_id=1, source_target_pairs={{0,8},{8,0},{1,9},{9,1},{2,10},{10,2},{3,11},{11,3},{4,12},{12,4},... | collective-permute-start | bytes 1769480 | tf_op jit(solution)/shard_map/ppermute | solution.py:16
  425.3 29.0 %collective-permute-start.55 = (bf16[512,1152]{1,0:T(8,128)(2,1)}, bf16[512,1152]{1,0:T(8,128)(2,1)S(1)}, u32[]{:S(2)}, u32[]{:S(2)}) collective-permute-start(bf16[512,1152]{1,0:T(8,128)(2,1)} %pad_maximum_fusion.18), channel_id=1, source_target_pairs={{0,2},{2,0},{1,3},{3,1},{4,6},{6,4},{5,7},{7,5},{8,10},{10,8},{9,1... | collective-permute-start | bytes 3538952 | tf_op jit(solution)/shard_map/ppermute | solution.py:16
  426.3 27.9 %collective-permute-start.56 = (bf16[256,1152]{1,0:T(8,128)(2,1)S(1)}, bf16[256,1152]{1,0:T(8,128)(2,1)S(1)}, u32[]{:S(2)}, u32[]{:S(2)}) collective-permute-start(bf16[256,1152]{1,0:T(8,128)(2,1)S(1)} %get-tuple-element.401), channel_id=1, source_target_pairs={{0,8},{8,0},{1,9},{9,1},{2,10},{10,2},{3,11},{11,3},{4,12},{12,4},... | collective-permute-start | bytes 1769480 | tf_op jit(solution)/shard_map/ppermute | solution.py:16
  426.7 27.5 %collective-permute-start.52 = (bf16[64,2048]{1,0:T(8,128)(2,1)S(1)}, bf16[64,2048]{1,0:T(8,128)(2,1)S(1)}, u32[]{:S(2)}, u32[]{:S(2)}) collective-permute-start(bf16[64,2048]{1,0:T(8,128)(2,1)S(1)} %get-tuple-element.753), channel_id=1, source_target_pairs={{0,16},{16,0},{1,17},{17,1},{2,18},{18,2},{3,19},{19,3},{4,20},{20... | collective-permute-start | bytes 786440 | tf_op jit(solution)/shard_map/ppermute | solution.py:16
  428.3 25.9 %collective-permute-start.53 = (bf16[64,2048]{1,0:T(8,128)(2,1)S(1)}, bf16[64,2048]{1,0:T(8,128)(2,1)S(1)}, u32[]{:S(2)}, u32[]{:S(2)}) collective-permute-start(bf16[64,2048]{1,0:T(8,128)(2,1)S(1)} %get-tuple-element.752), channel_id=1, source_target_pairs={{0,4},{4,0},{1,5},{5,1},{2,6},{6,2},{3,7},{7,3},{8,12},{12,8},{9,1... | collective-permute-start | bytes 786440 | tf_op jit(solution)/shard_map/ppermute | solution.py:16
  458.3 27.1 %collective-permute-start.60 = (bf16[512,1152]{1,0:T(8,128)(2,1)S(1)}, bf16[512,1152]{1,0:T(8,128)(2,1)S(1)}, u32[]{:S(2)}, u32[]{:S(2)}) collective-permute-start(bf16[512,1152]{1,0:T(8,128)(2,1)S(1)} %pad_maximum_fusion.19), channel_id=1, source_target_pairs={{0,2},{2,0},{1,3},{3,1},{4,6},{6,4},{5,7},{7,5},{8,10},{10,8},{9,1... | collective-permute-start | bytes 3538952 | tf_op jit(solution)/shard_map/ppermute | solution.py:16
  500.4 28.1 %collective-permute-start.63 = (bf16[512,1152]{1,0:T(8,128)(2,1)S(1)}, bf16[512,1152]{1,0:T(8,128)(2,1)S(1)}, u32[]{:S(2)}, u32[]{:S(2)}) collective-permute-start(bf16[512,1152]{1,0:T(8,128)(2,1)S(1)} %pad_maximum_fusion.20), channel_id=1, source_target_pairs={{0,2},{2,0},{1,3},{3,1},{4,6},{6,4},{5,7},{7,5},{8,10},{10,8},{9,1... | collective-permute-start | bytes 3538952 | tf_op jit(solution)/shard_map/ppermute | solution.py:16
  532.8 29.3 %collective-permute-start.68 = (bf16[256,1152]{1,0:T(8,128)(2,1)S(1)}, bf16[256,1152]{1,0:T(8,128)(2,1)}, u32[]{:S(2)}, u32[]{:S(2)}) collective-permute-start(bf16[256,1152]{1,0:T(8,128)(2,1)S(1)} %fusion.116), channel_id=1, source_target_pairs={{0,8},{8,0},{1,9},{9,1},{2,10},{10,2},{3,11},{11,3},{4,12},{12,4},... | collective-permute-start | bytes 1769480 | tf_op jit(solution)/shard_map/ppermute | solution.py:16
  534.0 28.3 %collective-permute-start.69 = (bf16[512,1152]{1,0:T(8,128)(2,1)}, bf16[512,1152]{1,0:T(8,128)(2,1)S(1)}, u32[]{:S(2)}, u32[]{:S(2)}) collective-permute-start(bf16[512,1152]{1,0:T(8,128)(2,1)} %pad_maximum_fusion.21), channel_id=1, source_target_pairs={{0,2},{2,0},{1,3},{3,1},{4,6},{6,4},{5,7},{7,5},{8,10},{10,8},{9,1... | collective-permute-start | bytes 3538952 | tf_op jit(solution)/shard_map/ppermute | solution.py:16
  535.5 26.9 %collective-permute-start.65 = (bf16[64,2048]{1,0:T(8,128)(2,1)S(1)}, bf16[64,2048]{1,0:T(8,128)(2,1)S(1)}, u32[]{:S(2)}, u32[]{:S(2)}) collective-permute-start(bf16[64,2048]{1,0:T(8,128)(2,1)S(1)} %get-tuple-element.750), channel_id=1, source_target_pairs={{0,16},{16,0},{1,17},{17,1},{2,18},{18,2},{3,19},{19,3},{4,20},{20... | collective-permute-start | bytes 786440 | tf_op jit(solution)/shard_map/ppermute | solution.py:16
  537.0 25.3 %collective-permute-start.66 = (bf16[64,2048]{1,0:T(8,128)(2,1)S(1)}, bf16[64,2048]{1,0:T(8,128)(2,1)S(1)}, u32[]{:S(2)}, u32[]{:S(2)}) collective-permute-start(bf16[64,2048]{1,0:T(8,128)(2,1)S(1)} %get-tuple-element.749), channel_id=1, source_target_pairs={{0,4},{4,0},{1,5},{5,1},{2,6},{6,2},{3,7},{7,3},{8,12},{12,8},{9,1... | collective-permute-start | bytes 786440 | tf_op jit(solution)/shard_map/ppermute | solution.py:16
  538.7 24.3 %collective-permute-start.67 = (bf16[64,2048]{1,0:T(8,128)(2,1)S(1)}, bf16[64,2048]{1,0:T(8,128)(2,1)S(1)}, u32[]{:S(2)}, u32[]{:S(2)}) collective-permute-start(bf16[64,2048]{1,0:T(8,128)(2,1)S(1)} %get-tuple-element.748), channel_id=1, source_target_pairs={{0,20},{4,16},{16,4},{20,0},{1,21},{5,17},{17,5},{21,1},{2,22},{6,... | collective-permute-start | bytes 786440 | tf_op jit(solution)/shard_map/ppermute | solution.py:50
  565.8 28.0 %collective-permute-start.73 = (bf16[256,1152]{1,0:T(8,128)(2,1)S(1)}, bf16[256,1152]{1,0:T(8,128)(2,1)S(1)}, u32[]{:S(2)}, u32[]{:S(2)}) collective-permute-start(bf16[256,1152]{1,0:T(8,128)(2,1)S(1)} %fusion.115), channel_id=1, source_target_pairs={{0,8},{8,0},{1,9},{9,1},{2,10},{10,2},{3,11},{11,3},{4,12},{12,4},... | collective-permute-start | bytes 1769480 | tf_op jit(solution)/shard_map/ppermute | solution.py:16
  566.9 27.0 %collective-permute-start.74 = (bf16[512,1152]{1,0:T(8,128)(2,1)S(1)}, bf16[512,1152]{1,0:T(8,128)(2,1)S(1)}, u32[]{:S(2)}, u32[]{:S(2)}) collective-permute-start(bf16[512,1152]{1,0:T(8,128)(2,1)S(1)} %pad_maximum_fusion.22), channel_id=1, source_target_pairs={{0,2},{2,0},{1,3},{3,1},{4,6},{6,4},{5,7},{7,5},{8,10},{10,8},{9,1... | collective-permute-start | bytes 3538952 | tf_op jit(solution)/shard_map/ppermute | solution.py:16
  596.7 29.6 %collective-permute-start.76 = (bf16[256,1152]{1,0:T(8,128)(2,1)}, bf16[256,1152]{1,0:T(8,128)(2,1)}, u32[]{:S(2)}, u32[]{:S(2)}) collective-permute-start(bf16[256,1152]{1,0:T(8,128)(2,1)} %fusion.114), channel_id=1, source_target_pairs={{0,8},{8,0},{1,9},{9,1},{2,10},{10,2},{3,11},{11,3},{4,12},{12,4},... | collective-permute-start | bytes 1769480 | tf_op jit(solution)/shard_map/ppermute | solution.py:16
  598.3 28.1 %collective-permute-start.77 = (bf16[512,1152]{1,0:T(8,128)(2,1)S(1)}, bf16[512,1152]{1,0:T(8,128)(2,1)S(1)}, u32[]{:S(2)}, u32[]{:S(2)}) collective-permute-start(bf16[512,1152]{1,0:T(8,128)(2,1)S(1)} %pad_maximum_fusion.23), channel_id=1, source_target_pairs={{0,2},{2,0},{1,3},{3,1},{4,6},{6,4},{5,7},{7,5},{8,10},{10,8},{9,1... | collective-permute-start | bytes 3538952 | tf_op jit(solution)/shard_map/ppermute | solution.py:16
  629.2 29.4 %collective-permute-start.82 = (bf16[256,1152]{1,0:T(8,128)(2,1)S(1)}, bf16[256,1152]{1,0:T(8,128)(2,1)S(1)}, u32[]{:S(2)}, u32[]{:S(2)}) collective-permute-start(bf16[256,1152]{1,0:T(8,128)(2,1)S(1)} %fusion.113), channel_id=1, source_target_pairs={{0,8},{8,0},{1,9},{9,1},{2,10},{10,2},{3,11},{11,3},{4,12},{12,4},... | collective-permute-start | bytes 1769480 | tf_op jit(solution)/shard_map/ppermute | solution.py:16
  630.7 28.0 %collective-permute-start.83 = (bf16[1024,512]{1,0:T(8,128)(2,1)S(1)}, bf16[1024,512]{1,0:T(8,128)(2,1)S(1)}, u32[]{:S(2)}, u32[]{:S(2)}) collective-permute-start(bf16[1024,512]{1,0:T(8,128)(2,1)S(1)} %pad_maximum_fusion.40), channel_id=1, source_target_pairs={{0,2},{2,0},{1,3},{3,1},{4,6},{6,4},{5,7},{7,5},{8,10},{10,8},{9,1... | collective-permute-start | bytes 3145736 | tf_op jit(solution)/shard_map/ppermute | solution.py:16
  632.2 26.4 %collective-permute-start.79 = (bf16[64,2048]{1,0:T(8,128)(2,1)S(1)}, bf16[64,2048]{1,0:T(8,128)(2,1)S(1)}, u32[]{:S(2)}, u32[]{:S(2)}) collective-permute-start(bf16[64,2048]{1,0:T(8,128)(2,1)S(1)} %get-tuple-element.747), channel_id=1, source_target_pairs={{0,16},{16,0},{1,17},{17,1},{2,18},{18,2},{3,19},{19,3},{4,20},{20... | collective-permute-start | bytes 786440 | tf_op jit(solution)/shard_map/ppermute | solution.py:16
  633.7 25.0 %collective-permute-start.80 = (bf16[64,2048]{1,0:T(8,128)(2,1)S(1)}, bf16[64,2048]{1,0:T(8,128)(2,1)S(1)}, u32[]{:S(2)}, u32[]{:S(2)}) collective-permute-start(bf16[64,2048]{1,0:T(8,128)(2,1)S(1)} %get-tuple-element.746), channel_id=1, source_target_pairs={{0,4},{4,0},{1,5},{5,1},{2,6},{6,2},{3,7},{7,3},{8,12},{12,8},{9,1... | collective-permute-start | bytes 786440 | tf_op jit(solution)/shard_map/ppermute | solution.py:16
  662.8 28.6 %collective-permute-start.88 = (bf16[1024,512]{1,0:T(8,128)(2,1)S(1)}, bf16[1024,512]{1,0:T(8,128)(2,1)S(1)}, u32[]{:S(2)}, u32[]{:S(2)}) collective-permute-start(bf16[1024,512]{1,0:T(8,128)(2,1)S(1)} %pad_maximum_fusion.44), channel_id=1, source_target_pairs={{0,2},{2,0},{1,3},{3,1},{4,6},{6,4},{5,7},{7,5},{8,10},{10,8},{9,1... | collective-permute-start | bytes 3145736 | tf_op jit(solution)/shard_map/ppermute | solution.py:16
  663.9 26.7 %collective-permute-start.87 = (bf16[512,512]{1,0:T(8,128)(2,1)S(1)}, bf16[512,512]{1,0:T(8,128)(2,1)S(1)}, u32[]{:S(2)}, u32[]{:S(2)}) collective-permute-start(bf16[512,512]{1,0:T(8,128)(2,1)S(1)} %slice.1918), channel_id=1, source_target_pairs={{0,8},{8,0},{1,9},{9,1},{2,10},{10,2},{3,11},{11,3},{4,12},{12,4},... | collective-permute-start | bytes 1572872 | tf_op jit(solution)/shard_map/ppermute | solution.py:16
  708.2 26.0 %collective-permute-start.95 = (bf16[512,512]{1,0:T(8,128)(2,1)S(1)}, bf16[512,512]{1,0:T(8,128)(2,1)S(1)}, u32[]{:S(2)}, u32[]{:S(2)}) collective-permute-start(bf16[512,512]{1,0:T(8,128)(2,1)S(1)} %slice.1940), channel_id=1, source_target_pairs={{0,8},{8,0},{1,9},{9,1},{2,10},{10,2},{3,11},{11,3},{4,12},{12,4},... | collective-permute-start | bytes 1572872 | tf_op jit(solution)/shard_map/ppermute | solution.py:16
  710.2 27.3 %collective-permute-start.96 = (bf16[512,1152]{1,0:T(8,128)(2,1)S(1)}, bf16[512,1152]{1,0:T(8,128)(2,1)S(1)}, u32[]{:S(2)}, u32[]{:S(2)}) collective-permute-start(bf16[512,1152]{1,0:T(8,128)(2,1)S(1)} %pad_maximum_fusion.24), channel_id=1, source_target_pairs={{0,2},{2,0},{1,3},{3,1},{4,6},{6,4},{5,7},{7,5},{8,10},{10,8},{9,1... | collective-permute-start | bytes 3538952 | tf_op jit(solution)/shard_map/ppermute | solution.py:16
  739.2 31.4 %collective-permute-start.101 = (bf16[512,1152]{1,0:T(8,128)(2,1)S(1)}, bf16[512,1152]{1,0:T(8,128)(2,1)S(1)}, u32[]{:S(2)}, u32[]{:S(2)}) collective-permute-start(bf16[512,1152]{1,0:T(8,128)(2,1)S(1)} %pad_maximum_fusion.25), channel_id=1, source_target_pairs={{0,2},{2,0},{1,3},{3,1},{4,6},{6,4},{5,7},{7,5},{8,10},{10,8},{9,1... | collective-permute-start | bytes 3538952 | tf_op jit(solution)/shard_map/ppermute | solution.py:16
  744.0 26.7 %collective-permute-start.100 = (bf16[256,1152]{1,0:T(8,128)(2,1)S(1)}, bf16[256,1152]{1,0:T(8,128)(2,1)S(1)}, u32[]{:S(2)}, u32[]{:S(2)}) collective-permute-start(bf16[256,1152]{1,0:T(8,128)(2,1)S(1)} %fusion.112), channel_id=1, source_target_pairs={{0,8},{8,0},{1,9},{9,1},{2,10},{10,2},{3,11},{11,3},{4,12},{12,4},... | collective-permute-start | bytes 1769480 | tf_op jit(solution)/shard_map/ppermute | solution.py:16
  801.2 34.7 %collective-permute-start.108 = (bf16[256,1152]{1,0:T(8,128)(2,1)}, bf16[256,1152]{1,0:T(8,128)(2,1)}, u32[]{:S(2)}, u32[]{:S(2)}) collective-permute-start(bf16[256,1152]{1,0:T(8,128)(2,1)} %fusion.110), channel_id=1, source_target_pairs={{0,8},{8,0},{1,9},{9,1},{2,10},{10,2},{3,11},{11,3},{4,12},{12,4},... | collective-permute-start | bytes 1769480 | tf_op jit(solution)/shard_map/ppermute | solution.py:16
  803.2 32.6 %collective-permute-start.109 = (bf16[512,1152]{1,0:T(8,128)(2,1)}, bf16[512,1152]{1,0:T(8,128)(2,1)}, u32[]{:S(2)}, u32[]{:S(2)}) collective-permute-start(bf16[512,1152]{1,0:T(8,128)(2,1)} %pad_maximum_fusion.27), channel_id=1, source_target_pairs={{0,2},{2,0},{1,3},{3,1},{4,6},{6,4},{5,7},{7,5},{8,10},{10,8},{9,1... | collective-permute-start | bytes 3538952 | tf_op jit(solution)/shard_map/ppermute | solution.py:16
  804.2 67.7 %all-to-all-start.3 = ((bf16[4,256,1152]{2,1,0:T(8,128)(2,1)}), bf16[4,256,1152]{2,1,0:T(8,128)(2,1)S(1)}, u32[]{:S(2)}, u32[]{:S(2)}) async-start(bf16[4,256,1152]{2,1,0:T(8,128)(2,1)} %pad_maximum_fusion.2), calls=%async_computation.3 | async-start | bytes 4718592 | tf_op jit(solution)/shard_map/all_to_all | solution.py:20
  840.5 29.5 %collective-permute-start.114 = (bf16[256,1152]{1,0:T(8,128)(2,1)S(1)}, bf16[256,1152]{1,0:T(8,128)(2,1)S(1)}, u32[]{:S(2)}, u32[]{:S(2)}) collective-permute-start(bf16[256,1152]{1,0:T(8,128)(2,1)S(1)} %fusion.109), channel_id=1, source_target_pairs={{0,8},{8,0},{1,9},{9,1},{2,10},{10,2},{3,11},{11,3},{4,12},{12,4},... | collective-permute-start | bytes 1769480 | tf_op jit(solution)/shard_map/ppermute | solution.py:16
  842.5 27.5 %collective-permute-start.115 = (bf16[1024,512]{1,0:T(8,128)(2,1)S(1)}, bf16[1024,512]{1,0:T(8,128)(2,1)S(1)}, u32[]{:S(2)}, u32[]{:S(2)}) collective-permute-start(bf16[1024,512]{1,0:T(8,128)(2,1)S(1)} %pad_maximum_fusion.51), channel_id=1, source_target_pairs={{0,2},{2,0},{1,3},{3,1},{4,6},{6,4},{5,7},{7,5},{8,10},{10,8},{9,1... | collective-permute-start | bytes 3145736 | tf_op jit(solution)/shard_map/ppermute | solution.py:16
  844.9 25.1 %collective-permute-start.111 = (bf16[64,2048]{1,0:T(8,128)(2,1)S(1)}, bf16[64,2048]{1,0:T(8,128)(2,1)S(1)}, u32[]{:S(2)}, u32[]{:S(2)}) collective-permute-start(bf16[64,2048]{1,0:T(8,128)(2,1)S(1)} %get-tuple-element.775), channel_id=1, source_target_pairs={{0,16},{16,0},{1,17},{17,1},{2,18},{18,2},{3,19},{19,3},{4,20},{20... | collective-permute-start | bytes 786440 | tf_op jit(solution)/shard_map/ppermute | solution.py:16
  878.6 26.1 %collective-permute-start.116 = (bf16[512,512]{1,0:T(8,128)(2,1)}, bf16[512,512]{1,0:T(8,128)(2,1)}, u32[]{:S(2)}, u32[]{:S(2)}) collective-permute-start(bf16[512,512]{1,0:T(8,128)(2,1)} %slice.1994), channel_id=1, source_target_pairs={{0,8},{8,0},{1,9},{9,1},{2,10},{10,2},{3,11},{11,3},{4,12},{12,4},... | collective-permute-start | bytes 1572872 | tf_op jit(solution)/shard_map/ppermute | solution.py:16
  879.7 25.1 %collective-permute-start.117 = (bf16[1024,512]{1,0:T(8,128)(2,1)}, bf16[1024,512]{1,0:T(8,128)(2,1)}, u32[]{:S(2)}, u32[]{:S(2)}) collective-permute-start(bf16[1024,512]{1,0:T(8,128)(2,1)} %pad_maximum_fusion.54), channel_id=1, source_target_pairs={{0,2},{2,0},{1,3},{3,1},{4,6},{6,4},{5,7},{7,5},{8,10},{10,8},{9,1... | collective-permute-start | bytes 3145736 | tf_op jit(solution)/shard_map/ppermute | solution.py:16
  881.8 55.5 %all-to-all-start.4 = ((bf16[4,256,1152]{2,1,0:T(8,128)(2,1)}), bf16[4,256,1152]{2,1,0:T(8,128)(2,1)}, u32[]{:S(2)}, u32[]{:S(2)}) async-start(bf16[4,256,1152]{2,1,0:T(8,128)(2,1)} %pad_maximum_fusion.3), calls=%async_computation.4 | async-start | bytes 4718592 | tf_op jit(solution)/shard_map/all_to_all | solution.py:20
  907.9 29.5 %collective-permute-start.122 = (bf16[512,512]{1,0:T(8,128)(2,1)S(1)}, bf16[512,512]{1,0:T(8,128)(2,1)}, u32[]{:S(2)}, u32[]{:S(2)}) collective-permute-start(bf16[512,512]{1,0:T(8,128)(2,1)S(1)} %slice.2000), channel_id=1, source_target_pairs={{0,8},{8,0},{1,9},{9,1},{2,10},{10,2},{3,11},{11,3},{4,12},{12,4},... | collective-permute-start | bytes 1572872 | tf_op jit(solution)/shard_map/ppermute | solution.py:16
  912.5 24.8 %collective-permute-start.118 = (bf16[64,2048]{1,0:T(8,128)(2,1)S(1)}, bf16[64,2048]{1,0:T(8,128)(2,1)}, u32[]{:S(2)}, u32[]{:S(2)}) collective-permute-start(bf16[64,2048]{1,0:T(8,128)(2,1)S(1)} %get-tuple-element.531), channel_id=1, source_target_pairs={{0,16},{16,0},{1,17},{17,1},{2,18},{18,2},{3,19},{19,3},{4,20},{20... | collective-permute-start | bytes 786440 | tf_op jit(solution)/shard_map/ppermute | solution.py:16
  942.6 37.3 %all-to-all-start.5 = ((bf16[4,512,512]{2,1,0:T(8,128)(2,1)}), bf16[4,512,512]{2,1,0:T(8,128)(2,1)}, u32[]{:S(2)}, u32[]{:S(2)}) async-start(bf16[4,512,512]{2,1,0:T(8,128)(2,1)} %pad_maximum_fusion.7), calls=%async_computation.5 | async-start | bytes 4194304 | tf_op jit(solution)/shard_map/all_to_all | solution.py:20
  (336 other events, 3486.3 us)
